TPU v7x, 256 devices: a whole 4x4x8 slice. The times are simulated.
256 devices in a mesh: loop: 32 (over z, y_hi, core), dp: 8 (over x, y_lo).
Axes of the slice: x: 4, y: 4 (y_hi: 2, y_lo: 2; y = y_hi * 2 + y_lo), z: 8, core: 2. Of those that a mesh axis runs over, the one named last changes fastest.
Arguments:
- sensor_feats: bfloat16 [8, 4096, 1152], P('dp', 'loop'), may hold values from -6 to 6
- text_embeds: bfloat16 [8, 4096, 1024], P('dp', 'loop'), may hold values from -6 to 6
- proj_weight: bfloat16 [1152, 1024], replicated, may hold values from -0.1875 to 0.1875
- matches: int32 [8, 4096], P('dp', 'loop'), may hold values from 0 to 4095, each once within a row
- log_scale: float32 [], replicated, may hold values from 2 to 2.6
- logit_bias: float32 [], replicated, may hold values from -3 to -1
Outputs:
- sensor_grad: bfloat16 [8, 4096, 1152], P('dp', 'loop')
- text_grad: float32 [8, 4096, 1024], P('dp', 'loop')
- weight_grad: float32 [1152, 1024], P('loop')
Inputs may be any that keep to these rules, and one draw needn't show every extreme that they name: `matches`: within each group every index appears exactly once.
All inputs are finite; a program needn't handle non-finite values.
Results may differ from a plain program's by a relative error of at most 0.0068.
Values may be sent and summed in bfloat16 or wider, within the bound.
No kernel may reach another device: no remote copies, remote signals or barrier semaphores. Data moves between devices by JAX's collectives and lax.ppermute only.
A program may use at most 64 MiB of HBM per device.

v0:
```python
import jax
import jax.numpy as jnp
from jax import lax
from jax.sharding import PartitionSpec as P


def from_behind(block, axis, distance):
    devices = range(lax.axis_size(axis))
    route = [((i - distance) % len(devices), i) for i in devices]
    return lax.ppermute(block, axis, route)


def inner_rows(left, right):
    return lax.dot_general(
        left, right, (((1,), (1,)), ((), ())), preferred_element_type=jnp.float32
    )


def inner_cols(left, right):
    return lax.dot_general(
        left, right, (((0,), (0,)), ((), ())), preferred_element_type=jnp.float32
    )


def on_device(sensor_feats, text_embeds, proj_weight, matches, log_scale, logit_bias):
    sensor = sensor_feats[0]
    texts = text_embeds[0]
    matched = matches[0]
    local_rows = sensor.shape[0]
    loop_size = lax.axis_size("loop")
    loop_index = lax.axis_index("loop")
    half_loop = loop_size // 2
    logit_scale = jnp.exp(log_scale)
    projected = jnp.dot(sensor, proj_weight, preferred_element_type=jnp.float32)
    image_inv = lax.rsqrt(jnp.sum(projected * projected, -1, keepdims=True) + 1e-06)
    image_unit = projected * image_inv
    image_emb = image_unit.astype(jnp.bfloat16)
    text_wide = texts.astype(jnp.float32)
    text_inv = lax.rsqrt(jnp.sum(text_wide * text_wide, -1, keepdims=True) + 1e-06)
    text_unit = text_wide * text_inv
    text_emb = text_unit.astype(jnp.bfloat16)

    def grad_block(piece, start):
        logits = logit_scale * inner_rows(image_emb, piece) + logit_bias
        columns = start + jnp.arange(piece.shape[0], dtype=jnp.int32)
        positive = (matched[:, None] == columns[None, :]).astype(jnp.float32)
        return (jax.nn.sigmoid(logits) - positive).astype(jnp.bfloat16)

    own_grads = grad_block(text_emb, loop_index * local_rows)
    image_acc = jnp.dot(own_grads, text_emb, preferred_element_type=jnp.float32)
    own_acc = inner_cols(own_grads, image_emb)
    zeros_acc = jnp.zeros_like(own_acc)

    def travel(offset, carry):
        ahead_text, ahead_acc, behind_text, behind_acc, image_sum = carry
        ahead_text = from_behind(ahead_text, "loop", 1)
        ahead_acc = from_behind(ahead_acc, "loop", 1)
        ahead_owner = (loop_index - offset) % loop_size
        ahead_grads = grad_block(ahead_text, ahead_owner * local_rows)
        image_sum = image_sum + jnp.dot(ahead_grads, ahead_text, preferred_element_type=jnp.float32)
        ahead_acc = ahead_acc + inner_cols(ahead_grads, image_emb)
        behind_text = from_behind(behind_text, "loop", -1)
        behind_acc = from_behind(behind_acc, "loop", -1)
        behind_owner = (loop_index + offset) % loop_size
        behind_grads = grad_block(behind_text, behind_owner * local_rows)
        weight_keep = (offset < half_loop).astype(jnp.float32)
        image_sum = image_sum + weight_keep * jnp.dot(
            behind_grads, behind_text, preferred_element_type=jnp.float32
        )
        behind_acc = behind_acc + weight_keep * inner_cols(behind_grads, image_emb)
        return (ahead_text, ahead_acc, behind_text, behind_acc, image_sum)

    final = lax.fori_loop(
        1, half_loop + 1, travel, (text_emb, zeros_acc, text_emb, zeros_acc, image_acc)
    )
    image_acc = final[4]
    ahead_home = from_behind(final[1], "loop", -half_loop)
    behind_home = from_behind(final[3], "loop", half_loop)
    text_acc = own_acc + ahead_home + behind_home
    image_grad = logit_scale * image_acc
    text_acc = logit_scale * text_acc
    proj_grad = (
        (image_grad - image_unit * jnp.sum(image_unit * image_grad, -1, keepdims=True)) * image_inv
    ).astype(jnp.bfloat16)
    text_grad = (text_acc - text_unit * jnp.sum(text_unit * text_acc, -1, keepdims=True)) * text_inv
    sensor_grad = inner_rows(proj_grad, proj_weight).astype(jnp.bfloat16)
    weight_share = lax.psum_scatter(
        inner_cols(sensor, proj_grad), "loop", scatter_dimension=0, tiled=True
    )
    weight_grad = lax.psum(weight_share, "dp") / lax.axis_size("dp")
    return (sensor_grad[None], text_grad[None], weight_grad)


def solution(mesh):
    placed = (P("dp", "loop", None), P("dp", "loop", None), P(), P("dp", "loop"), P(), P())
    return jax.shard_map(
        on_device,
        mesh=mesh,
        in_specs=placed,
        out_specs=(P("dp", "loop", None), P("dp", "loop", None), P("loop", None)),
        check_vma=False,
    )
```

profile of v0, /device:TPU:1, one launch (start us, length us, event | category | flops | bytes accessed | tf_op | source)
XLA Modules:
  0.0 822.2 jit_solution(2931896232332433311)
XLA Ops:
  15.8 417.9 %while.24 = (s32[]{:T(128)}, bf16[128,1024]{1,0:T(8,128)(2,1)}, f32[128,1024]{1,0:T(8,128)}, bf16[128,1024]{1,0:T(8,128)(2,1)}, f32[128,1024]{1,0:T(8,128)}, /*i...) while((s32[]{:T(128)}, bf16[128,1024]{1,0:T(8,128)(2,1)}, ...), condition=%wide.region_3.4_spmd.clone, body=%wide.region_2.3_spmd.clone.sunk | while | flops 202670352 | bytes 15928960 | solution.py:73
  22.4 4.6 collective-permute-start.3
  28.0 9.1 %collective-permute-done.2 = bf16[128,1024]{1,0:T(8,128)(2,1)} collective-permute-done((bf16[128,1024]{1,0:T(8,128)(2,1)}, bf16[128,1024]{1,0:T(8,128)(2,1)}, u32[]{:S(2)}, u32[]{:S(2)}) %collective-permute-start.2) | collective-permute-done | bytes 262176 | tf_op jit(solution)/shard_map/while/body/eval_jaxpr/ppermute | solution.py:10
  51.3 5.4 collective-permute-start.3
  57.6 4.6 collective-permute-done.2
  82.6 5.4 collective-permute-done.2
  108.4 5.4 collective-permute-done.2
  134.2 5.4 collective-permute-done.2
  160.1 5.4 collective-permute-done.2
  185.9 5.4 collective-permute-done.2
  211.8 5.4 collective-permute-done.2
  237.6 5.4 collective-permute-done.2
  263.4 5.4 collective-permute-done.2
  289.3 5.4 collective-permute-done.2
  315.1 5.4 collective-permute-done.2
  340.9 5.4 collective-permute-done.2
  366.8 5.4 collective-permute-done.2
  392.6 5.4 collective-permute-done.2
  418.4 5.4 collective-permute-done.2
  440.9 6.0 collective-permute-start.5
  451.6 27.1 %collective-permute-done.5 = f32[128,1024]{1,0:T(8,128)} collective-permute-done((f32[128,1024]{1,0:T(8,128)}, f32[128,1024]{1,0:T(8,128)}, u32[]{:S(2)}, u32[]{:S(2)}) %collective-permute-start.5) | collective-permute-done | bytes 524320 | tf_op jit(solution)/shard_map/ppermute | solution.py:10
  478.7 10.8 %collective-permute-done.4 = f32[128,1024]{1,0:T(8,128)} collective-permute-done((f32[128,1024]{1,0:T(8,128)S(1)}, f32[128,1024]{1,0:T(8,128)}, u32[]{:S(2)}, u32[]{:S(2)}) %collective-permute-start.4) | collective-permute-done | bytes 524320 | tf_op jit(solution)/shard_map/ppermute | solution.py:10
  491.0 245.9 %all-reduce.6.cloned.1.call-done = f32[1152,1024]{0,1:T(8,128)} async-done(((f32[1152,1024]{0,1:T(8,128)}), f32[1152,1024]{0,1:T(8,128)}) %all-reduce.6.cloned.1.call-update) | async-done | bytes 4718608
  740.2 73.2 %all-reduce.4.cloned.1.call-done = f32[36,1024]{0,1:T(8,128)} async-done(((f32[36,1024]{0,1:T(8,128)}), f32[36,1024]{0,1:T(8,128)}) %all-reduce.4.cloned.1.call-update) | async-done | bytes 147472 | tf_op jit(solution)/shard_map/psum | solution.py:90
  (346 shorter events, 343.2 us)
Async XLA Ops:
  7.2 729.7 %all-reduce.6.cloned.1.call-start = ((), (), s32[]{:S(2)}) async-start(), calls=%async_computation.1 | async-start | bytes 9437184
  21.1 21.8 %collective-permute-start.1 = (f32[128,1024]{1,0:T(8,128)}, f32[128,1024]{1,0:T(8,128)}, u32[]{:S(2)}, u32[]{:S(2)}) collective-permute-start(f32[128,1024]{1,0:T(8,128)} %broadcast_select_fusion.4), channel_id=1, source_target_pairs={{248,0},{0,8},{8,16},{16,24},{24,32},{32,40},{40,48},{48,56},{56,6... | collective-permute-start | bytes 1572872 | tf_op jit(solution)/shard_map/while/body/eval_jaxpr/ppermute | solution.py:10
  22.4 22.5 %collective-permute-start.3 = (f32[128,1024]{1,0:T(8,128)}, f32[128,1024]{1,0:T(8,128)}, u32[]{:S(2)}, u32[]{:S(2)}) collective-permute-start(f32[128,1024]{1,0:T(8,128)} %broadcast_select_fusion.5), channel_id=1, source_target_pairs={{8,0},{16,8},{24,16},{32,24},{40,32},{48,40},{56,48},{64,56},{72,6... | collective-permute-start | bytes 1572872 | tf_op jit(solution)/shard_map/while/body/eval_jaxpr/ppermute | solution.py:10
  48.9 18.9 %collective-permute-start.1 = (f32[128,1024]{1,0:T(8,128)}, f32[128,1024]{1,0:T(8,128)}, u32[]{:S(2)}, u32[]{:S(2)}) collective-permute-start(f32[128,1024]{1,0:T(8,128)} %broadcast_select_fusion.4), channel_id=1, source_target_pairs={{248,0},{0,8},{8,16},{16,24},{24,32},{32,40},{40,48},{48,56},{56,6... | collective-permute-start | bytes 1572872 | tf_op jit(solution)/shard_map/while/body/eval_jaxpr/ppermute | solution.py:10
  51.3 18.6 %collective-permute-start.3 = (f32[128,1024]{1,0:T(8,128)}, f32[128,1024]{1,0:T(8,128)}, u32[]{:S(2)}, u32[]{:S(2)}) collective-permute-start(f32[128,1024]{1,0:T(8,128)} %broadcast_select_fusion.5), channel_id=1, source_target_pairs={{8,0},{16,8},{24,16},{32,24},{40,32},{48,40},{56,48},{64,56},{72,6... | collective-permute-start | bytes 1572872 | tf_op jit(solution)/shard_map/while/body/eval_jaxpr/ppermute | solution.py:10
  74.7 18.9 %collective-permute-start.1 = (f32[128,1024]{1,0:T(8,128)}, f32[128,1024]{1,0:T(8,128)}, u32[]{:S(2)}, u32[]{:S(2)}) collective-permute-start(f32[128,1024]{1,0:T(8,128)} %broadcast_select_fusion.4), channel_id=1, source_target_pairs={{248,0},{0,8},{8,16},{16,24},{24,32},{32,40},{40,48},{48,56},{56,6... | collective-permute-start | bytes 1572872 | tf_op jit(solution)/shard_map/while/body/eval_jaxpr/ppermute | solution.py:10
  100.6 18.9 %collective-permute-start.1 = (f32[128,1024]{1,0:T(8,128)}, f32[128,1024]{1,0:T(8,128)}, u32[]{:S(2)}, u32[]{:S(2)}) collective-permute-start(f32[128,1024]{1,0:T(8,128)} %broadcast_select_fusion.4), channel_id=1, source_target_pairs={{248,0},{0,8},{8,16},{16,24},{24,32},{32,40},{40,48},{48,56},{56,6... | collective-permute-start | bytes 1572872 | tf_op jit(solution)/shard_map/while/body/eval_jaxpr/ppermute | solution.py:10
  103.0 18.6 %collective-permute-start.3 = (f32[128,1024]{1,0:T(8,128)}, f32[128,1024]{1,0:T(8,128)}, u32[]{:S(2)}, u32[]{:S(2)}) collective-permute-start(f32[128,1024]{1,0:T(8,128)} %broadcast_select_fusion.5), channel_id=1, source_target_pairs={{8,0},{16,8},{24,16},{32,24},{40,32},{48,40},{56,48},{64,56},{72,6... | collective-permute-start | bytes 1572872 | tf_op jit(solution)/shard_map/while/body/eval_jaxpr/ppermute | solution.py:10
  126.4 18.9 %collective-permute-start.1 = (f32[128,1024]{1,0:T(8,128)}, f32[128,1024]{1,0:T(8,128)}, u32[]{:S(2)}, u32[]{:S(2)}) collective-permute-start(f32[128,1024]{1,0:T(8,128)} %broadcast_select_fusion.4), channel_id=1, source_target_pairs={{248,0},{0,8},{8,16},{16,24},{24,32},{32,40},{40,48},{48,56},{56,6... | collective-permute-start | bytes 1572872 | tf_op jit(solution)/shard_map/while/body/eval_jaxpr/ppermute | solution.py:10
  152.2 18.9 %collective-permute-start.1 = (f32[128,1024]{1,0:T(8,128)}, f32[128,1024]{1,0:T(8,128)}, u32[]{:S(2)}, u32[]{:S(2)}) collective-permute-start(f32[128,1024]{1,0:T(8,128)} %broadcast_select_fusion.4), channel_id=1, source_target_pairs={{248,0},{0,8},{8,16},{16,24},{24,32},{32,40},{40,48},{48,56},{56,6... | collective-permute-start | bytes 1572872 | tf_op jit(solution)/shard_map/while/body/eval_jaxpr/ppermute | solution.py:10
  154.6 18.6 %collective-permute-start.3 = (f32[128,1024]{1,0:T(8,128)}, f32[128,1024]{1,0:T(8,128)}, u32[]{:S(2)}, u32[]{:S(2)}) collective-permute-start(f32[128,1024]{1,0:T(8,128)} %broadcast_select_fusion.5), channel_id=1, source_target_pairs={{8,0},{16,8},{24,16},{32,24},{40,32},{48,40},{56,48},{64,56},{72,6... | collective-permute-start | bytes 1572872 | tf_op jit(solution)/shard_map/while/body/eval_jaxpr/ppermute | solution.py:10
  178.1 18.9 %collective-permute-start.1 = (f32[128,1024]{1,0:T(8,128)}, f32[128,1024]{1,0:T(8,128)}, u32[]{:S(2)}, u32[]{:S(2)}) collective-permute-start(f32[128,1024]{1,0:T(8,128)} %broadcast_select_fusion.4), channel_id=1, source_target_pairs={{248,0},{0,8},{8,16},{16,24},{24,32},{32,40},{40,48},{48,56},{56,6... | collective-permute-start | bytes 1572872 | tf_op jit(solution)/shard_map/while/body/eval_jaxpr/ppermute | solution.py:10
  203.9 18.9 %collective-permute-start.1 = (f32[128,1024]{1,0:T(8,128)}, f32[128,1024]{1,0:T(8,128)}, u32[]{:S(2)}, u32[]{:S(2)}) collective-permute-start(f32[128,1024]{1,0:T(8,128)} %broadcast_select_fusion.4), channel_id=1, source_target_pairs={{248,0},{0,8},{8,16},{16,24},{24,32},{32,40},{40,48},{48,56},{56,6... | collective-permute-start | bytes 1572872 | tf_op jit(solution)/shard_map/while/body/eval_jaxpr/ppermute | solution.py:10
  229.7 18.9 %collective-permute-start.1 = (f32[128,1024]{1,0:T(8,128)}, f32[128,1024]{1,0:T(8,128)}, u32[]{:S(2)}, u32[]{:S(2)}) collective-permute-start(f32[128,1024]{1,0:T(8,128)} %broadcast_select_fusion.4), channel_id=1, source_target_pairs={{248,0},{0,8},{8,16},{16,24},{24,32},{32,40},{40,48},{48,56},{56,6... | collective-permute-start | bytes 1572872 | tf_op jit(solution)/shard_map/while/body/eval_jaxpr/ppermute | solution.py:10
  255.6 18.9 %collective-permute-start.1 = (f32[128,1024]{1,0:T(8,128)}, f32[128,1024]{1,0:T(8,128)}, u32[]{:S(2)}, u32[]{:S(2)}) collective-permute-start(f32[128,1024]{1,0:T(8,128)} %broadcast_select_fusion.4), channel_id=1, source_target_pairs={{248,0},{0,8},{8,16},{16,24},{24,32},{32,40},{40,48},{48,56},{56,6... | collective-permute-start | bytes 1572872 | tf_op jit(solution)/shard_map/while/body/eval_jaxpr/ppermute | solution.py:10
  281.4 18.9 %collective-permute-start.1 = (f32[128,1024]{1,0:T(8,128)}, f32[128,1024]{1,0:T(8,128)}, u32[]{:S(2)}, u32[]{:S(2)}) collective-permute-start(f32[128,1024]{1,0:T(8,128)} %broadcast_select_fusion.4), channel_id=1, source_target_pairs={{248,0},{0,8},{8,16},{16,24},{24,32},{32,40},{40,48},{48,56},{56,6... | collective-permute-start | bytes 1572872 | tf_op jit(solution)/shard_map/while/body/eval_jaxpr/ppermute | solution.py:10
  307.2 18.9 %collective-permute-start.1 = (f32[128,1024]{1,0:T(8,128)}, f32[128,1024]{1,0:T(8,128)}, u32[]{:S(2)}, u32[]{:S(2)}) collective-permute-start(f32[128,1024]{1,0:T(8,128)} %broadcast_select_fusion.4), channel_id=1, source_target_pairs={{248,0},{0,8},{8,16},{16,24},{24,32},{32,40},{40,48},{48,56},{56,6... | collective-permute-start | bytes 1572872 | tf_op jit(solution)/shard_map/while/body/eval_jaxpr/ppermute | solution.py:10
  333.1 18.9 %collective-permute-start.1 = (f32[128,1024]{1,0:T(8,128)}, f32[128,1024]{1,0:T(8,128)}, u32[]{:S(2)}, u32[]{:S(2)}) collective-permute-start(f32[128,1024]{1,0:T(8,128)} %broadcast_select_fusion.4), channel_id=1, source_target_pairs={{248,0},{0,8},{8,16},{16,24},{24,32},{32,40},{40,48},{48,56},{56,6... | collective-permute-start | bytes 1572872 | tf_op jit(solution)/shard_map/while/body/eval_jaxpr/ppermute | solution.py:10
  358.9 18.9 %collective-permute-start.1 = (f32[128,1024]{1,0:T(8,128)}, f32[128,1024]{1,0:T(8,128)}, u32[]{:S(2)}, u32[]{:S(2)}) collective-permute-start(f32[128,1024]{1,0:T(8,128)} %broadcast_select_fusion.4), channel_id=1, source_target_pairs={{248,0},{0,8},{8,16},{16,24},{24,32},{32,40},{40,48},{48,56},{56,6... | collective-permute-start | bytes 1572872 | tf_op jit(solution)/shard_map/while/body/eval_jaxpr/ppermute | solution.py:10
  384.8 18.9 %collective-permute-start.1 = (f32[128,1024]{1,0:T(8,128)}, f32[128,1024]{1,0:T(8,128)}, u32[]{:S(2)}, u32[]{:S(2)}) collective-permute-start(f32[128,1024]{1,0:T(8,128)} %broadcast_select_fusion.4), channel_id=1, source_target_pairs={{248,0},{0,8},{8,16},{16,24},{24,32},{32,40},{40,48},{48,56},{56,6... | collective-permute-start | bytes 1572872 | tf_op jit(solution)/shard_map/while/body/eval_jaxpr/ppermute | solution.py:10
  410.6 18.9 %collective-permute-start.1 = (f32[128,1024]{1,0:T(8,128)}, f32[128,1024]{1,0:T(8,128)}, u32[]{:S(2)}, u32[]{:S(2)}) collective-permute-start(f32[128,1024]{1,0:T(8,128)} %broadcast_select_fusion.4), channel_id=1, source_target_pairs={{248,0},{0,8},{8,16},{16,24},{24,32},{32,40},{40,48},{48,56},{56,6... | collective-permute-start | bytes 1572872 | tf_op jit(solution)/shard_map/while/body/eval_jaxpr/ppermute | solution.py:10
  440.9 372.5 %all-reduce.4.cloned.1.call-start = ((), (), s32[]{:S(2)}) async-start(), calls=%async_computation | async-start | bytes 1048576 | tf_op jit(solution)/shard_map/psum | solution.py:90
  440.9 37.7 %collective-permute-start.5 = (f32[128,1024]{1,0:T(8,128)}, f32[128,1024]{1,0:T(8,128)}, u32[]{:S(2)}, u32[]{:S(2)}) collective-permute-start(f32[128,1024]{1,0:T(8,128)} %get-tuple-element.272), channel_id=1, source_target_pairs={{128,0},{136,8},{144,16},{152,24},{160,32},{168,40},{176,48},{184,... | collective-permute-start | bytes 1572872 | tf_op jit(solution)/shard_map/ppermute | solution.py:10
  446.9 42.5 %collective-permute-start.4 = (f32[128,1024]{1,0:T(8,128)S(1)}, f32[128,1024]{1,0:T(8,128)}, u32[]{:S(2)}, u32[]{:S(2)}) collective-permute-start(f32[128,1024]{1,0:T(8,128)S(1)} %copy-done.1), channel_id=1, source_target_pairs={{128,0},{136,8},{144,16},{152,24},{160,32},{168,40},{176,48},{184,... | collective-permute-start | bytes 1572872 | tf_op jit(solution)/shard_map/ppermute | solution.py:10
  (53 other events, 672.4 us)
Sparse Core Ops, SparseCore 0:
  441.0 295.8 all-reduce.5
  739.5 73.8 all-reduce.3
where the time goes:
time: 831 us; the launch traced here: 822 us
  waiting for transfers between devices  446 us (54%)
  matrix products  146 us (18%)
  starting transfers between devices  105 us (13%)
  other arithmetic  65.3 us (8%)
  local copies, waits for them, and re-layouts  43.6 us (5%)
  between operations  16.2 us (2%)
    unnamed x3, waiting for transfers between devices  246 us
    ppermute x66, waiting for transfers between devices, from_behind(): return lax.ppermute(block, axis, route)  127 us
    ppermute x66, starting transfers between devices, from_behind(): return lax.ppermute(block, axis, route)  104 us
    psum x1, waiting for transfers between devices, on_device(): weight_grad = lax.psum(weight_share, 'dp') / lax.axis_size('dp')  73.2 us
    dot_general x34, matrix products, inner_cols(): lax.dot_general(left, right, (((0,), (0,)), ((), ())), preferred_element_...  72.2 us
    while x32, other arithmetic  58.5 us
    dot_general x34, matrix products, inner_rows(): lax.dot_general(left, right, (((1,), (1,)), ((), ())), preferred_element_...  47.6 us
    while x32, local copies, waits for them, and re-layouts  38 us
  transfers between devices with their start and end apart: 68, of which 20 were waited for; matrix products, arithmetic and copies ran while one was open for 25% of the time, Pallas kernels for 0%

commit v1 on v0

v1 whole, which is shorter than its diff:
```python
import jax
import jax.numpy as jnp
from jax import lax
from jax.sharding import PartitionSpec as P

Z, YH, CORE = 8, 2, 2
LOOP = Z * YH * CORE
DP = 8
BF16 = jnp.bfloat16
F32 = jnp.float32


def route(move):
    pairs = []
    for z in range(Z):
        for y in range(YH):
            for c in range(CORE):
                to_z, to_y, to_c = move(z, y, c)
                source = (z * YH + y) * CORE + c
                pairs.append((source, ((to_z % Z) * YH + to_y) * CORE + to_c))
    return pairs


def shift_z(block, distance):
    return lax.ppermute(block, "loop", route(lambda z, y, c: (z + distance, y, c)))


def swap_core(block):
    return lax.ppermute(block, "loop", route(lambda z, y, c: (z, y, 1 - c)))


def swap_yh(block):
    return lax.ppermute(block, "loop", route(lambda z, y, c: (z, 1 - y, c)))


def inner_rows(left, right):
    return lax.dot_general(left, right, (((1,), (1,)), ((), ())), preferred_element_type=F32)


def inner_cols(left, right):
    return lax.dot_general(left, right, (((0,), (0,)), ((), ())), preferred_element_type=F32)


def part_of(array, index, parts):
    width = array.shape[-1] // parts
    return lax.dynamic_slice_in_dim(array, index * width, width, array.ndim - 1)


def swap_blocks(array, bit, rows):
    count = array.shape[0] // rows
    blocks = [array[(s ^ bit) * rows : ((s ^ bit) + 1) * rows] for s in range(count)]
    return jnp.concatenate(blocks, 0)


def on_device(sensor_feats, text_embeds, proj_weight, matches, log_scale, logit_bias):
    sensor = sensor_feats[0]
    texts = text_embeds[0]
    rows = sensor.shape[0]
    feat, width = proj_weight.shape
    loop_index = lax.axis_index("loop")
    z = loop_index // (YH * CORE)
    yh = (loop_index // CORE) % YH
    core = loop_index % CORE
    logit_scale = jnp.exp(log_scale)

    text_wide = texts.astype(F32)
    text_inv = lax.rsqrt(jnp.sum(text_wide * text_wide, -1, keepdims=True) + 1e-06)
    text_unit = text_wide * text_inv
    text_emb = text_unit.astype(BF16)
    half = rows // 2
    slot = {0: text_emb}
    slot[1] = shift_z(text_emb, -1)
    slot[-1] = shift_z(text_emb, 1)
    slot[2] = shift_z(text_emb, -2)
    slot[-2] = shift_z(text_emb, 2)

    sensor_yh = swap_yh(sensor)
    sensor_rows = jnp.concatenate([sensor, swap_core(sensor), sensor_yh, swap_core(sensor_yh)], 0)
    match = matches.reshape(1, rows)
    match_pair = jnp.concatenate([match, swap_core(match)], 1)
    match_rows = jnp.concatenate([match_pair, swap_yh(match_pair)], 1).reshape(4 * rows, 1)

    slot[3] = shift_z(slot[2], -1)
    slot[-3] = shift_z(slot[-2], 1)
    slot[4] = jnp.concatenate([shift_z(slot[2][:half], -2), shift_z(slot[-2][half:], 2)], 0)

    projected = jnp.dot(sensor_rows, proj_weight, preferred_element_type=F32)
    image_inv = lax.rsqrt(jnp.sum(projected * projected, -1, keepdims=True) + 1e-06)
    image_unit = projected * image_inv
    image_emb = image_unit.astype(BF16)

    def grads_of(keys):
        piece = jnp.concatenate([slot[k] for k in keys], 0)
        logits = logit_scale * inner_rows(image_emb, piece) + logit_bias
        own = jnp.arange(rows, dtype=jnp.int32)
        columns = jnp.concatenate(
            [own + (((z + k) % Z) * YH * CORE + yh * CORE + core) * rows for k in keys]
        )
        positive = (match_rows == columns[None, :]).astype(F32)
        grads = (jax.nn.sigmoid(logits) - positive).astype(BF16)
        image_part = jnp.dot(grads, piece, preferred_element_type=F32)
        text_part = inner_cols(grads, image_emb)
        return image_part, {k: text_part[n * rows : (n + 1) * rows] for n, k in enumerate(keys)}

    image_near, text_acc = grads_of((-2, -1, 0, 1, 2))
    image_far, text_far = grads_of((-3, 3, 4))
    image_acc = logit_scale * (image_near + image_far)

    text_far = {k: v.astype(BF16) for k, v in text_far.items()}
    from_below = shift_z(text_far[3], 1)
    from_above = shift_z(text_far[-3], -1)
    far_below = shift_z(text_far[4][:half], 2)
    far_above = shift_z(text_far[4][half:], -2)
    beside_below = shift_z(text_acc[1].astype(BF16), 1)
    beside_above = shift_z(text_acc[-1].astype(BF16), -1)
    nil = jnp.zeros((half, width), F32)
    up = text_acc[2] + from_below.astype(F32) + jnp.concatenate([far_below.astype(F32), nil], 0)
    down = text_acc[-2] + from_above.astype(F32) + jnp.concatenate([nil, far_above.astype(F32)], 0)
    up = shift_z(up.astype(BF16), 2)
    down = shift_z(down.astype(BF16), -2)

    dot = jnp.sum(image_unit * image_acc, -1).reshape(4, rows)
    sent = part_of(image_acc, 1 - core, 2).astype(BF16)
    kept = part_of(image_acc, core, 2)
    kept = kept + swap_blocks(swap_core(sent), 1, rows).astype(F32)
    dot = dot + swap_blocks(swap_core(dot), 1, 1)
    sent = part_of(kept, 1 - yh, 2).astype(BF16)
    kept = part_of(kept, yh, 2)
    kept = kept + swap_blocks(swap_yh(sent), 2, rows).astype(F32)
    dot = dot + swap_blocks(swap_yh(dot), 2, 1)
    quarter = core * 2 + yh
    unit_part = part_of(image_unit, quarter, 4)
    proj_grad = ((kept - unit_part * dot.reshape(4 * rows, 1)) * image_inv).astype(BF16)

    per_loop = feat // LOOP
    strip = per_loop // 4
    place = jnp.arange(feat, dtype=jnp.int32)
    rest = place % (feat // 4)
    wanted = (rest // strip) * per_loop + (place // (feat // 4)) * strip + rest % strip
    permutation = (jnp.arange(feat, dtype=jnp.int32)[:, None] == wanted[None, :]).astype(BF16)
    sensor_sorted = jnp.dot(sensor_rows, permutation, preferred_element_type=F32).astype(BF16)
    weight_part = inner_cols(sensor_sorted, proj_grad).astype(BF16)
    lanes = width // 8
    weight_part = weight_part.reshape(4, feat // 4, 2, lanes).transpose(0, 2, 1, 3)
    weight_part = lax.all_to_all(weight_part.reshape(DP, feat // 4, lanes), "dp", 0, 0, tiled=True)
    weight_part = jnp.sum(weight_part.astype(F32), 0).astype(BF16)
    weight_part = weight_part.reshape(LOOP, strip, lanes)
    weight_part = lax.all_to_all(weight_part, "loop", 0, 0, tiled=True)
    weight_part = jnp.sum(weight_part.reshape(Z, YH * CORE, strip, lanes).astype(F32), 0)
    weight_part = weight_part * (1.0 / DP)
    shares = jnp.broadcast_to(weight_part[None], (DP,) + weight_part.shape)
    shares = lax.all_to_all(shares, "dp", 0, 0, tiled=True)
    shares = shares.reshape(4, 2, YH, CORE, strip, lanes).transpose(0, 4, 3, 2, 1, 5)
    weight_grad = shares.reshape(per_loop, width)

    from_yh = swap_yh(proj_grad[2 * rows :])
    mine = proj_grad[: 2 * rows]
    pair = jnp.where(
        yh == 0, jnp.concatenate([mine, from_yh], 1), jnp.concatenate([from_yh, mine], 1)
    )
    from_core = swap_core(pair[rows:])
    mine = pair[:rows]
    own_grad = jnp.where(
        core == 0, jnp.concatenate([mine, from_core], 1), jnp.concatenate([from_core, mine], 1)
    )
    sensor_grad = inner_rows(own_grad, proj_weight).astype(BF16)

    text_sum = text_acc[0] + beside_below.astype(F32) + beside_above.astype(F32)
    text_sum = logit_scale * (text_sum + up.astype(F32) + down.astype(F32))
    text_grad = (text_sum - text_unit * jnp.sum(text_unit * text_sum, -1, keepdims=True)) * text_inv
    return (sensor_grad[None], text_grad[None], weight_grad)


def solution(mesh):
    placed = (P("dp", "loop", None), P("dp", "loop", None), P(), P("dp", "loop"), P(), P())
    return jax.shard_map(
        on_device,
        mesh=mesh,
        in_specs=placed,
        out_specs=(P("dp", "loop", None), P("dp", "loop", None), P("loop", None)),
        check_vma=False,
    )
```

time: 831 us -> 146 us (0.18); the launches traced: 822 us -> 146 us
  waiting for transfers between devices: 446 us -> 47.2 us
  matrix products: 146 us -> 14.1 us
  other arithmetic: 65.3 us -> 8.08 us
  starting transfers between devices: 105 us -> 66.6 us
  local copies, waits for them, and re-layouts: 43.6 us -> 7.13 us
  between operations: 16.2 us -> 2.57 us
    unnamed x3 -> x0, waiting for transfers between devices: 246 us -> none
    ppermute x66 -> x27, waiting for transfers between devices: 127 us -> 32.9 us  [the longest x16 20.6 us: shift_z(): lax.ppermute(block, 'loop', route(lambda z, y, c: (z + distance, y, c)))]
    psum x1 -> x0, waiting for transfers between devices: 73.2 us -> none  [on_device(): weight_grad = lax.psum(weight_share, 'dp') / lax.axis_size('dp')]
    dot_general x34 -> x3, matrix products: 72.2 us -> 5.97 us  [inner_cols(): lax.dot_general(left, right, (((0,), (0,)), ((), ())), preferred_element_...]
    while x32 -> x0, other arithmetic: 58.5 us -> none
    ppermute x66 -> x27, starting transfers between devices: 104 us -> 47.5 us  [the longest x16 26.3 us: shift_z(): lax.ppermute(block, 'loop', route(lambda z, y, c: (z + distance, y, c)))]
    dot_general x34 -> x3, matrix products: 47.6 us -> 3.58 us  [inner_rows(): lax.dot_general(left, right, (((1,), (1,)), ((), ())), preferred_element_...]
    while x32 -> x0, local copies, waits for them, and re-layouts: 38 us -> none
  transfers between devices with their start and end apart: 68 -> 30, of which waited for: 20 -> 16; matrix products, arithmetic and copies ran while one was open for 25% -> 6% of each run, Pallas kernels for 0% -> 0%
where the time goes in v1:
time: 146 us
  starting transfers between devices  66.6 us (46%)
  waiting for transfers between devices  47.2 us (32%)
  matrix products  14.1 us (10%)
  other arithmetic  8.08 us (6%)
  local copies, waits for them, and re-layouts  7.13 us (5%)
  between operations  2.57 us (2%)
    ppermute x16, starting transfers between devices, shift_z(): lax.ppermute(block, 'loop', route(lambda z, y, c: (z + distance, y, c)))  26.3 us
    ppermute x16, waiting for transfers between devices, shift_z(): lax.ppermute(block, 'loop', route(lambda z, y, c: (z + distance, y, c)))  20.6 us
    ppermute x5, waiting for transfers between devices, swap_yh(): return lax.ppermute(block, 'loop', route(lambda z, y, c: (z, 1 - y, c)))  11.5 us
    ppermute x6, starting transfers between devices, swap_core(): return lax.ppermute(block, 'loop', route(lambda z, y, c: (z, y, 1 - c)))  11.2 us
    all_to_all x1, waiting for transfers between devices, on_device(): weight_part = lax.all_to_all(weight_part, 'loop', 0, 0, tiled=True)  10.4 us
    ppermute x5, starting transfers between devices, swap_yh(): return lax.ppermute(block, 'loop', route(lambda z, y, c: (z, 1 - y, c)))  9.95 us
    all_to_all x1, starting transfers between devices, on_device(): weight_part = lax.all_to_all(weight_part, 'loop', 0, 0, tiled=True)  8.3 us
    all_to_all x1, starting transfers between devices, on_device(): lax.all_to_all(weight_part.reshape(DP, feat // 4, lanes), 'dp', 0, 0, til...  6.44 us
  transfers between devices with their start and end apart: 30, of which 16 were waited for; matrix products, arithmetic and copies ran while one was open for 6% of the time, Pallas kernels for 0%

profile of v1, /device:TPU:1, one launch (start us, length us, event | category | flops | bytes accessed | tf_op | source)
XLA Modules:
  0.0 145.7 jit_solution(7476887643760072520)
XLA Ops:
  3.0 3.9 %collective-permute-start.3 = (bf16[128,1024]{1,0:T(8,128)(2,1)S(1)}, bf16[128,1024]{1,0:T(8,128)(2,1)S(1)}, u32[]{:S(2)}, u32[]{:S(2)}) collective-permute-start(bf16[128,1024]{1,0:T(8,128)(2,1)S(1)} %fusion.17), channel_id=1, source_target_pairs={{0,64},{8,72},{16,80},{24,88},{32,96},{40,104},{48,112},{56,120},{... | collective-permute-start | bytes 786440 | tf_op jit(solution)/shard_map/ppermute | solution.py:25
  6.9 3.1 %collective-permute-start.6 = (bf16[128,1024]{1,0:T(8,128)(2,1)S(1)}, bf16[128,1024]{1,0:T(8,128)(2,1)S(1)}, u32[]{:S(2)}, u32[]{:S(2)}) collective-permute-start(bf16[128,1024]{1,0:T(8,128)(2,1)S(1)} %fusion.17), channel_id=1, source_target_pairs={{0,192},{8,200},{16,208},{24,216},{32,224},{40,232},{48,240},{56,2... | collective-permute-start | bytes 786440 | tf_op jit(solution)/shard_map/ppermute | solution.py:25
  10.7 2.9 %collective-permute-start.1 = (bf16[128,1152]{1,0:T(8,128)(2,1)}, bf16[128,1152]{1,0:T(8,128)(2,1)}, u32[]{:S(2)}, u32[]{:S(2)}) collective-permute-start(bf16[128,1152]{1,0:T(8,128)(2,1)} %bitcast.53), channel_id=1, source_target_pairs={{0,16},{8,24},{16,0},{24,8},{32,48},{40,56},{48,32},{56,40},{64,80... | collective-permute-start | bytes 884744 | tf_op jit(solution)/shard_map/ppermute | solution.py:33
  18.2 3.0 %collective-permute-done.8 = s32[1,256]{1,0:T(1,128)S(1)} collective-permute-done((s32[1,256]{1,0:T(1,128)S(1)}, s32[1,256]{1,0:T(1,128)S(1)}, u32[]{:S(2)}, u32[]{:S(2)}) %collective-permute-start.8) | collective-permute-done | bytes 1056 | tf_op jit(solution)/shard_map/ppermute | solution.py:33
  28.2 2.9 %collective-permute-done.5 = bf16[128,1024]{1,0:T(8,128)(2,1)S(1)} collective-permute-done((bf16[128,1024]{1,0:T(8,128)(2,1)S(1)}, bf16[128,1024]{1,0:T(8,128)(2,1)S(1)}, u32[]{:S(2)}, u32[]{:S(2)}) %collective-permute-start.5) | collective-permute-done | bytes 262176 | tf_op jit(solution)/shard_map/ppermute | solution.py:25
  31.2 3.7 %collective-permute-start.10 = (bf16[128,1024]{1,0:T(8,128)(2,1)S(1)}, bf16[128,1024]{1,0:T(8,128)(2,1)S(1)}, u32[]{:S(2)}, u32[]{:S(2)}) collective-permute-start(bf16[128,1024]{1,0:T(8,128)(2,1)S(1)} %collective-permute-done.6), channel_id=1, source_target_pairs={{0,224},{8,232},{16,240},{24,248},{32,0},{40,8},{48,16},{56,24},{6... | collective-permute-start | bytes 786440 | tf_op jit(solution)/shard_map/ppermute | solution.py:25
  35.3 4.5 %collective-permute-start.2 = (bf16[128,1152]{1,0:T(8,128)(2,1)}, bf16[128,1152]{1,0:T(8,128)(2,1)S(1)}, u32[]{:S(2)}, u32[]{:S(2)}) collective-permute-start(bf16[128,1152]{1,0:T(8,128)(2,1)} %collective-permute-done.1), channel_id=1, source_target_pairs={{0,8},{8,0},{16,24},{24,16},{32,40},{40,32},{48,56},{56,48},{64,72... | collective-permute-start | bytes 884744 | tf_op jit(solution)/shard_map/ppermute | solution.py:29
  41.2 2.7 %multiply_reduce_fusion.1 = (f32[512]{0:T(512)S(1)}, f32[512,1024]{1,0:T(8,128)S(1)}) fusion(bf16[1152,1024]{1,0:T(8,128)(2,1)S(1)} %copy-done, bf16[128,1152]{1,0:T(8,128)(2,1)S(1)} %collective-permute-done.2, bf16[128,1152]{1,0:T(8,128)(2,1)} %collective-permute-done.1, bf16[128,1152]{1,0:T(8,128)(2,1)S(1)} %collective-permute-done, ...), kind=kOutput, calls=%fused_computation.9 | convolution fusion | flops 1213726208 | bytes 5638144 | tf_op jit(solution)/shard_map/dot_general | solution.py:87
  49.6 3.7 %collective-permute-start.15 = (f32[4,128]{1,0:T(4,128)S(1)}, f32[4,128]{1,0:T(4,128)S(1)}, u32[]{:S(2)}, u32[]{:S(2)}) collective-permute-start(f32[4,128]{1,0:T(4,128)S(1)} %bitcast.50), channel_id=1, source_target_pairs={{0,8},{8,0},{16,24},{24,16},{32,40},{40,32},{48,56},{56,48},{64,72... | collective-permute-start | bytes 6152 | tf_op jit(solution)/shard_map/ppermute | solution.py:29
  60.8 2.2 %collective-permute-done.16 = f32[4,128]{1,0:T(4,128)S(1)} collective-permute-done((f32[4,128]{1,0:T(4,128)S(1)}, f32[4,128]{1,0:T(4,128)S(1)}, u32[]{:S(2)}, u32[]{:S(2)}) %collective-permute-start.16) | collective-permute-done | bytes 2080 | tf_op jit(solution)/shard_map/ppermute | solution.py:33
  63.1 4.5 %collective-permute-done.22 = bf16[64,1024]{1,0:T(8,128)(2,1)S(1)} collective-permute-done((bf16[64,1024]{1,0:T(8,128)(2,1)S(1)}, bf16[64,1024]{1,0:T(8,128)(2,1)S(1)}, u32[]{:S(2)}, u32[]{:S(2)}) %collective-permute-start.22) | collective-permute-done | bytes 131104 | tf_op jit(solution)/shard_map/ppermute | solution.py:25
  67.6 2.1 %collective-permute-start.20 = (bf16[128,1024]{1,0:T(8,128)(2,1)S(1)}, bf16[128,1024]{1,0:T(8,128)(2,1)S(1)}, u32[]{:S(2)}, u32[]{:S(2)}) collective-permute-start(bf16[128,1024]{1,0:T(8,128)(2,1)S(1)} %get-tuple-element.10), channel_id=1, source_target_pairs={{0,224},{8,232},{16,240},{24,248},{32,0},{40,8},{48,16},{56,24},{6... | collective-permute-start | bytes 786440 | tf_op jit(solution)/shard_map/ppermute | solution.py:25
  70.8 3.9 %collective-permute-start.26 = (bf16[128,1024]{1,0:T(8,128)(2,1)S(1)}, bf16[128,1024]{1,0:T(8,128)(2,1)S(1)}, u32[]{:S(2)}, u32[]{:S(2)}) collective-permute-start(bf16[128,1024]{1,0:T(8,128)(2,1)S(1)} %get-tuple-element.8), channel_id=1, source_target_pairs={{0,192},{8,200},{16,208},{24,216},{32,224},{40,232},{48,240},{56,2... | collective-permute-start | bytes 786440 | tf_op jit(solution)/shard_map/ppermute | solution.py:25
  75.0 2.5 %collective-permute-start.14 = (bf16[512,256]{1,0:T(8,128)(2,1)S(1)}, bf16[512,256]{1,0:T(8,128)(2,1)S(1)}, u32[]{:S(2)}, u32[]{:S(2)}) collective-permute-start(bf16[512,256]{1,0:T(8,128)(2,1)S(1)} %dynamic-slice_convert_fusion.1), channel_id=1, source_target_pairs={{0,16},{8,24},{16,0},{24,8},{32,48},{40,56},{48,32},{56,40},{64,80... | collective-permute-start | bytes 786440 | tf_op jit(solution)/shard_map/ppermute | solution.py:33
  77.5 10.0 %collective-permute-done.26 = bf16[128,1024]{1,0:T(8,128)(2,1)S(1)} collective-permute-done((bf16[128,1024]{1,0:T(8,128)(2,1)S(1)}, bf16[128,1024]{1,0:T(8,128)(2,1)S(1)}, u32[]{:S(2)}, u32[]{:S(2)}) %collective-permute-start.26) | collective-permute-done | bytes 262176 | tf_op jit(solution)/shard_map/ppermute | solution.py:25
  89.6 4.5 %convolution_convert_fusion = bf16[1152,256]{1,0:T(8,128)(2,1)} fusion(bf16[512,256]{1,0:T(8,128)(2,1)S(1)} %multiply_convert_fusion, s32[1152]{0:T(1024)S(1)} %fusion.46, bf16[128,1152]{1,0:T(8,128)(2,1)} %copy-done.6, bf16[128,1152]{1,0:T(8,128)(2,1)} %collective-permute-done.1, bf16[128,1152]{1,0:T(8,128)(2,1)S(1)} %copy-done.5, ...), kind=kOutput, calls=%fused_computation.4 | convolution fusion | flops 1667874816 | bytes 2036224 | tf_op jit(solution)/shard_map/dot_general | solution.py:41
  96.8 6.4 %all-to-all-start = ((bf16[8,288,128]{2,1,0:T(8,128)(2,1)}), bf16[8,288,128]{2,1,0:T(8,128)(2,1)S(1)}, u32[]{:S(2)}, u32[]{:S(2)}) async-start(bf16[8,288,128]{2,1,0:T(8,128)(2,1)} %bitcast.47), calls=%async_computation | async-start | bytes 1179648 | tf_op jit(solution)/shard_map/all_to_all | solution.py:145
  103.2 2.7 %collective-permute-start.17 = (bf16[256,256]{1,0:T(8,128)(2,1)S(1)}, bf16[256,256]{1,0:T(8,128)(2,1)S(1)}, u32[]{:S(2)}, u32[]{:S(2)}) collective-permute-start(bf16[256,256]{1,0:T(8,128)(2,1)S(1)} %get-tuple-element.22), channel_id=1, source_target_pairs={{0,16},{8,24},{16,0},{24,8},{32,48},{40,56},{48,32},{56,40},{64,80... | collective-permute-start | bytes 393224 | tf_op jit(solution)/shard_map/ppermute | solution.py:33
  105.9 2.1 %fusion.21 = f32[1,128,1024]{2,1,0:T(8,128)} fusion(f32[128,1024]{1,0:T(8,128)} %get-tuple-element.4, bf16[1,128,1024]{2,1,0:T(8,128)(2,1)S(1)} %copy-done.1, f32[128]{0:T(128)S(1)} %get-tuple-element.3, f32[128]{0:T(128)S(1)} %add_rsqrt_fusion.1), kind=kLoop, calls=%fused_computation.37 | loop fusion | flops 655360 | bytes 1311744 | tf_op jit(solution)/shard_map/broadcast_in_dim | solution.py:171
  108.0 6.3 %collective-permute-done.17 = bf16[256,256]{1,0:T(8,128)(2,1)S(1)} collective-permute-done((bf16[256,256]{1,0:T(8,128)(2,1)S(1)}, bf16[256,256]{1,0:T(8,128)(2,1)S(1)}, u32[]{:S(2)}, u32[]{:S(2)}) %collective-permute-start.17) | collective-permute-done | bytes 131104 | tf_op jit(solution)/shard_map/ppermute | solution.py:33
  115.2 8.3 %all-to-all-start.1 = ((bf16[32,9,128]{2,1,0:T(8,128)(2,1)}), bf16[32,9,128]{2,1,0:T(8,128)(2,1)S(1)}, u32[]{:S(2)}, u32[]{:S(2)}) async-start(bf16[32,9,128]{2,1,0:T(8,128)(2,1)} %reshape.98), calls=%async_computation.1 | async-start | bytes 262144 | tf_op jit(solution)/shard_map/all_to_all | solution.py:148
  123.8 10.4 %all-to-all-done.1 = bf16[32,9,128]{2,1,0:T(8,128)(2,1)S(1)} async-done(((bf16[32,9,128]{2,1,0:T(8,128)(2,1)}), bf16[32,9,128]{2,1,0:T(8,128)(2,1)S(1)}, u32[]{:S(2)}, u32[]{:S(2)}) %all-to-all-start.1) | async-done | bytes 73760 | tf_op jit(solution)/shard_map/all_to_all | solution.py:148
  135.0 4.3 %all-to-all-start.2 = ((f32[8,4,9,128]{3,1,2,0:T(4,128)}), f32[8,4,9,128]{3,1,2,0:T(4,128)S(1)}, u32[]{:S(2)}, u32[]{:S(2)}) async-start(f32[8,4,9,128]{3,1,2,0:T(4,128)} %broadcast_in_dim.8), calls=%async_computation.2 | async-start | bytes 294912 | tf_op jit(solution)/shard_map/all_to_all | solution.py:152
  140.9 3.9 %all-to-all-done.2 = f32[8,4,9,128]{3,1,2,0:T(4,128)S(1)} async-done(((f32[8,4,9,128]{3,1,2,0:T(4,128)}), f32[8,4,9,128]{3,1,2,0:T(4,128)S(1)}, u32[]{:S(2)}, u32[]{:S(2)}) %all-to-all-start.2) | async-done | bytes 147488 | tf_op jit(solution)/shard_map/all_to_all | solution.py:152
  (117 shorter events, 38.5 us)
Async XLA Ops:
  3.0 21.8 %collective-permute-start.3 = (bf16[128,1024]{1,0:T(8,128)(2,1)S(1)}, bf16[128,1024]{1,0:T(8,128)(2,1)S(1)}, u32[]{:S(2)}, u32[]{:S(2)}) collective-permute-start(bf16[128,1024]{1,0:T(8,128)(2,1)S(1)} %fusion.17), channel_id=1, source_target_pairs={{0,64},{8,72},{16,80},{24,88},{32,96},{40,104},{48,112},{56,120},{... | collective-permute-start | bytes 786440 | tf_op jit(solution)/shard_map/ppermute | solution.py:25
  6.9 16.2 %collective-permute-start.6 = (bf16[128,1024]{1,0:T(8,128)(2,1)S(1)}, bf16[128,1024]{1,0:T(8,128)(2,1)S(1)}, u32[]{:S(2)}, u32[]{:S(2)}) collective-permute-start(bf16[128,1024]{1,0:T(8,128)(2,1)S(1)} %fusion.17), channel_id=1, source_target_pairs={{0,192},{8,200},{16,208},{24,216},{32,224},{40,232},{48,240},{56,2... | collective-permute-start | bytes 786440 | tf_op jit(solution)/shard_map/ppermute | solution.py:25
  10.0 17.2 %collective-permute-start.4 = (bf16[128,1024]{1,0:T(8,128)(2,1)S(1)}, bf16[128,1024]{1,0:T(8,128)(2,1)}, u32[]{:S(2)}, u32[]{:S(2)}) collective-permute-start(bf16[128,1024]{1,0:T(8,128)(2,1)S(1)} %fusion.17), channel_id=1, source_target_pairs={{0,32},{8,40},{16,48},{24,56},{32,64},{40,72},{48,80},{56,88},{64,... | collective-permute-start | bytes 786440 | tf_op jit(solution)/shard_map/ppermute | solution.py:25
  10.7 24.2 %collective-permute-start.1 = (bf16[128,1152]{1,0:T(8,128)(2,1)}, bf16[128,1152]{1,0:T(8,128)(2,1)}, u32[]{:S(2)}, u32[]{:S(2)}) collective-permute-start(bf16[128,1152]{1,0:T(8,128)(2,1)} %bitcast.53), channel_id=1, source_target_pairs={{0,16},{8,24},{16,0},{24,8},{32,48},{40,56},{48,32},{56,40},{64,80... | collective-permute-start | bytes 884744 | tf_op jit(solution)/shard_map/ppermute | solution.py:33
  21.2 19.9 %collective-permute-start = (bf16[128,1152]{1,0:T(8,128)(2,1)}, bf16[128,1152]{1,0:T(8,128)(2,1)S(1)}, u32[]{:S(2)}, u32[]{:S(2)}) collective-permute-start(bf16[128,1152]{1,0:T(8,128)(2,1)} %bitcast.54), channel_id=1, source_target_pairs={{0,8},{8,0},{16,24},{24,16},{32,40},{40,32},{48,56},{56,48},{64,72... | collective-permute-start | bytes 884744 | tf_op jit(solution)/shard_map/ppermute | solution.py:29
  23.1 8.1 %collective-permute-start.5 = (bf16[128,1024]{1,0:T(8,128)(2,1)S(1)}, bf16[128,1024]{1,0:T(8,128)(2,1)S(1)}, u32[]{:S(2)}, u32[]{:S(2)}) collective-permute-start(bf16[128,1024]{1,0:T(8,128)(2,1)S(1)} %fusion.17), channel_id=1, source_target_pairs={{0,224},{8,232},{16,240},{24,248},{32,0},{40,8},{48,16},{56,24},{6... | collective-permute-start | bytes 786440 | tf_op jit(solution)/shard_map/ppermute | solution.py:25
  24.8 16.1 %collective-permute-start.11 = (bf16[64,1024]{1,0:T(8,128)(2,1)S(1)}, bf16[64,1024]{1,0:T(8,128)(2,1)S(1)}, u32[]{:S(2)}, u32[]{:S(2)}) collective-permute-start(bf16[64,1024]{1,0:T(8,128)(2,1)S(1)} %slice.124), channel_id=1, source_target_pairs={{0,192},{8,200},{16,208},{24,216},{32,224},{40,232},{48,240},{56,2... | collective-permute-start | bytes 393224 | tf_op jit(solution)/shard_map/ppermute | solution.py:25
  27.1 8.1 %collective-permute-start.9 = (bf16[128,1024]{1,0:T(8,128)(2,1)S(1)}, bf16[128,1024]{1,0:T(8,128)(2,1)S(1)}, u32[]{:S(2)}, u32[]{:S(2)}) collective-permute-start(bf16[128,1024]{1,0:T(8,128)(2,1)S(1)} %collective-permute-done.3), channel_id=1, source_target_pairs={{0,32},{8,40},{16,48},{24,56},{32,64},{40,72},{48,80},{56,88},{64,... | collective-permute-start | bytes 786440 | tf_op jit(solution)/shard_map/ppermute | solution.py:25
  31.2 9.7 %collective-permute-start.10 = (bf16[128,1024]{1,0:T(8,128)(2,1)S(1)}, bf16[128,1024]{1,0:T(8,128)(2,1)S(1)}, u32[]{:S(2)}, u32[]{:S(2)}) collective-permute-start(bf16[128,1024]{1,0:T(8,128)(2,1)S(1)} %collective-permute-done.6), channel_id=1, source_target_pairs={{0,224},{8,232},{16,240},{24,248},{32,0},{40,8},{48,16},{56,24},{6... | collective-permute-start | bytes 786440 | tf_op jit(solution)/shard_map/ppermute | solution.py:25
  49.6 9.4 %collective-permute-start.15 = (f32[4,128]{1,0:T(4,128)S(1)}, f32[4,128]{1,0:T(4,128)S(1)}, u32[]{:S(2)}, u32[]{:S(2)}) collective-permute-start(f32[4,128]{1,0:T(4,128)S(1)} %bitcast.50), channel_id=1, source_target_pairs={{0,8},{8,0},{16,24},{24,16},{32,40},{40,32},{48,56},{56,48},{64,72... | collective-permute-start | bytes 6152 | tf_op jit(solution)/shard_map/ppermute | solution.py:29
  53.4 21.3 %collective-permute-start.13 = (bf16[512,512]{1,0:T(8,128)(2,1)S(1)}, bf16[512,512]{1,0:T(8,128)(2,1)S(1)}, u32[]{:S(2)}, u32[]{:S(2)}) collective-permute-start(bf16[512,512]{1,0:T(8,128)(2,1)S(1)} %dynamic-slice_convert_fusion), channel_id=1, source_target_pairs={{0,8},{8,0},{16,24},{24,16},{32,40},{40,32},{48,56},{56,48},{64,72... | collective-permute-start | bytes 1572872 | tf_op jit(solution)/shard_map/ppermute | solution.py:29
  53.5 16.2 %collective-permute-start.21 = (bf16[128,1024]{1,0:T(8,128)(2,1)S(1)}, bf16[128,1024]{1,0:T(8,128)(2,1)S(1)}, u32[]{:S(2)}, u32[]{:S(2)}) collective-permute-start(bf16[128,1024]{1,0:T(8,128)(2,1)S(1)} %get-tuple-element.13), channel_id=1, source_target_pairs={{0,32},{8,40},{16,48},{24,56},{32,64},{40,72},{48,80},{56,88},{64,... | collective-permute-start | bytes 786440 | tf_op jit(solution)/shard_map/ppermute | solution.py:25
  55.4 12.2 %collective-permute-start.22 = (bf16[64,1024]{1,0:T(8,128)(2,1)S(1)}, bf16[64,1024]{1,0:T(8,128)(2,1)S(1)}, u32[]{:S(2)}, u32[]{:S(2)}) collective-permute-start(bf16[64,1024]{1,0:T(8,128)(2,1)S(1)} %get-tuple-element.11), channel_id=1, source_target_pairs={{0,64},{8,72},{16,80},{24,88},{32,96},{40,104},{48,112},{56,120},{... | collective-permute-start | bytes 393224 | tf_op jit(solution)/shard_map/ppermute | solution.py:25
  57.4 12.3 %collective-permute-start.25 = (bf16[64,1024]{1,0:T(8,128)(2,1)S(1)}, bf16[64,1024]{1,0:T(8,128)(2,1)S(1)}, u32[]{:S(2)}, u32[]{:S(2)}) collective-permute-start(bf16[64,1024]{1,0:T(8,128)(2,1)S(1)} %get-tuple-element.12), channel_id=1, source_target_pairs={{0,192},{8,200},{16,208},{24,216},{32,224},{40,232},{48,240},{56,2... | collective-permute-start | bytes 393224 | tf_op jit(solution)/shard_map/ppermute | solution.py:25
  67.6 9.9 %collective-permute-start.20 = (bf16[128,1024]{1,0:T(8,128)(2,1)S(1)}, bf16[128,1024]{1,0:T(8,128)(2,1)S(1)}, u32[]{:S(2)}, u32[]{:S(2)}) collective-permute-start(bf16[128,1024]{1,0:T(8,128)(2,1)S(1)} %get-tuple-element.10), channel_id=1, source_target_pairs={{0,224},{8,232},{16,240},{24,248},{32,0},{40,8},{48,16},{56,24},{6... | collective-permute-start | bytes 786440 | tf_op jit(solution)/shard_map/ppermute | solution.py:25
  69.7 7.8 %collective-permute-start.19 = (bf16[128,1024]{1,0:T(8,128)(2,1)S(1)}, bf16[128,1024]{1,0:T(8,128)(2,1)S(1)}, u32[]{:S(2)}, u32[]{:S(2)}) collective-permute-start(bf16[128,1024]{1,0:T(8,128)(2,1)S(1)} %get-tuple-element.9), channel_id=1, source_target_pairs={{0,32},{8,40},{16,48},{24,56},{32,64},{40,72},{48,80},{56,88},{64,... | collective-permute-start | bytes 786440 | tf_op jit(solution)/shard_map/ppermute | solution.py:25
  70.8 16.7 %collective-permute-start.26 = (bf16[128,1024]{1,0:T(8,128)(2,1)S(1)}, bf16[128,1024]{1,0:T(8,128)(2,1)S(1)}, u32[]{:S(2)}, u32[]{:S(2)}) collective-permute-start(bf16[128,1024]{1,0:T(8,128)(2,1)S(1)} %get-tuple-element.8), channel_id=1, source_target_pairs={{0,192},{8,200},{16,208},{24,216},{32,224},{40,232},{48,240},{56,2... | collective-permute-start | bytes 786440 | tf_op jit(solution)/shard_map/ppermute | solution.py:25
  74.7 12.8 %collective-permute-start.23 = (bf16[128,1024]{1,0:T(8,128)(2,1)S(1)}, bf16[128,1024]{1,0:T(8,128)(2,1)S(1)}, u32[]{:S(2)}, u32[]{:S(2)}) collective-permute-start(bf16[128,1024]{1,0:T(8,128)(2,1)S(1)} %get-tuple-element.7), channel_id=1, source_target_pairs={{0,64},{8,72},{16,80},{24,88},{32,96},{40,104},{48,112},{56,120},{... | collective-permute-start | bytes 786440 | tf_op jit(solution)/shard_map/ppermute | solution.py:25
  75.0 13.6 %collective-permute-start.14 = (bf16[512,256]{1,0:T(8,128)(2,1)S(1)}, bf16[512,256]{1,0:T(8,128)(2,1)S(1)}, u32[]{:S(2)}, u32[]{:S(2)}) collective-permute-start(bf16[512,256]{1,0:T(8,128)(2,1)S(1)} %dynamic-slice_convert_fusion.1), channel_id=1, source_target_pairs={{0,16},{8,24},{16,0},{24,8},{32,48},{40,56},{48,32},{56,40},{64,80... | collective-permute-start | bytes 786440 | tf_op jit(solution)/shard_map/ppermute | solution.py:33
  96.8 17.6 %all-to-all-start = ((bf16[8,288,128]{2,1,0:T(8,128)(2,1)}), bf16[8,288,128]{2,1,0:T(8,128)(2,1)S(1)}, u32[]{:S(2)}, u32[]{:S(2)}) async-start(bf16[8,288,128]{2,1,0:T(8,128)(2,1)} %bitcast.47), calls=%async_computation | async-start | bytes 1179648 | tf_op jit(solution)/shard_map/all_to_all | solution.py:145
  103.2 11.0 %collective-permute-start.17 = (bf16[256,256]{1,0:T(8,128)(2,1)S(1)}, bf16[256,256]{1,0:T(8,128)(2,1)S(1)}, u32[]{:S(2)}, u32[]{:S(2)}) collective-permute-start(bf16[256,256]{1,0:T(8,128)(2,1)S(1)} %get-tuple-element.22), channel_id=1, source_target_pairs={{0,16},{8,24},{16,0},{24,8},{32,48},{40,56},{48,32},{56,40},{64,80... | collective-permute-start | bytes 393224 | tf_op jit(solution)/shard_map/ppermute | solution.py:33
  115.2 19.1 %all-to-all-start.1 = ((bf16[32,9,128]{2,1,0:T(8,128)(2,1)}), bf16[32,9,128]{2,1,0:T(8,128)(2,1)S(1)}, u32[]{:S(2)}, u32[]{:S(2)}) async-start(bf16[32,9,128]{2,1,0:T(8,128)(2,1)} %reshape.98), calls=%async_computation.1 | async-start | bytes 262144 | tf_op jit(solution)/shard_map/all_to_all | solution.py:148
  123.5 15.8 %collective-permute-start.18 = (bf16[128,512]{1,0:T(8,128)(2,1)S(1)}, bf16[128,512]{1,0:T(8,128)(2,1)S(1)}, u32[]{:S(2)}, u32[]{:S(2)}) collective-permute-start(bf16[128,512]{1,0:T(8,128)(2,1)S(1)} %get-tuple-element.20), channel_id=1, source_target_pairs={{0,8},{8,0},{16,24},{24,16},{32,40},{40,32},{48,56},{56,48},{64,72... | collective-permute-start | bytes 393224 | tf_op jit(solution)/shard_map/ppermute | solution.py:29
  135.0 9.8 %all-to-all-start.2 = ((f32[8,4,9,128]{3,1,2,0:T(4,128)}), f32[8,4,9,128]{3,1,2,0:T(4,128)S(1)}, u32[]{:S(2)}, u32[]{:S(2)}) async-start(f32[8,4,9,128]{3,1,2,0:T(4,128)} %broadcast_in_dim.8), calls=%async_computation.2 | async-start | bytes 294912 | tf_op jit(solution)/shard_map/all_to_all | solution.py:152
  (13 other events, 112.5 us)

commit v2 on v1

--- a/solution.py
+++ b/solution.py
@@ -69,20 +69,20 @@
     text_emb = text_unit.astype(BF16)
     half = rows // 2
     slot = {0: text_emb}
-    slot[1] = shift_z(text_emb, -1)
-    slot[-1] = shift_z(text_emb, 1)
-    slot[2] = shift_z(text_emb, -2)
-    slot[-2] = shift_z(text_emb, 2)
+    for k in (1, 2, 3):
+        slot[k] = shift_z(slot[k - 1], -1)
+        slot[-k] = shift_z(slot[1 - k], 1)
+    slot[4] = jnp.concatenate([shift_z(slot[3][:half], -1), shift_z(slot[-3][half:], 1)], 0)
 
-    sensor_yh = swap_yh(sensor)
-    sensor_rows = jnp.concatenate([sensor, swap_core(sensor), sensor_yh, swap_core(sensor_yh)], 0)
     match = matches.reshape(1, rows)
-    match_pair = jnp.concatenate([match, swap_core(match)], 1)
-    match_rows = jnp.concatenate([match_pair, swap_yh(match_pair)], 1).reshape(4 * rows, 1)
-
-    slot[3] = shift_z(slot[2], -1)
-    slot[-3] = shift_z(slot[-2], 1)
-    slot[4] = jnp.concatenate([shift_z(slot[2][:half], -2), shift_z(slot[-2][half:], 2)], 0)
+    digits = jnp.concatenate([match // 64, match % 64], 0).astype(BF16)
+    digits = jnp.pad(digits, ((0, 14), (0, feat - rows)))
+    packet = jnp.concatenate([sensor, digits], 0)
+    packet = jnp.concatenate([packet, swap_yh(packet)], 0)
+    packets = jnp.stack([packet.reshape(2, rows + 16, feat), swap_core(packet).reshape(2, rows + 16, feat)], 1)
+    sensor_rows = packets[:, :, :rows].reshape(4 * rows, feat)
+    digits = packets[:, :, rows : rows + 2, :rows].astype(F32)
+    match_rows = (digits[:, :, 0] * 64.0 + digits[:, :, 1]).reshape(4 * rows, 1)
 
     projected = jnp.dot(sensor_rows, proj_weight, preferred_element_type=F32)
     image_inv = lax.rsqrt(jnp.sum(projected * projected, -1, keepdims=True) + 1e-06)
@@ -96,38 +96,45 @@
         columns = jnp.concatenate(
             [own + (((z + k) % Z) * YH * CORE + yh * CORE + core) * rows for k in keys]
         )
-        positive = (match_rows == columns[None, :]).astype(F32)
+        positive = (match_rows == columns[None, :].astype(F32)).astype(F32)
         grads = (jax.nn.sigmoid(logits) - positive).astype(BF16)
         image_part = jnp.dot(grads, piece, preferred_element_type=F32)
-        text_part = inner_cols(grads, image_emb)
+        text_part = inner_cols(grads, image_emb).astype(BF16)
         return image_part, {k: text_part[n * rows : (n + 1) * rows] for n, k in enumerate(keys)}
 
-    image_near, text_acc = grads_of((-2, -1, 0, 1, 2))
-    image_far, text_far = grads_of((-3, 3, 4))
-    image_acc = logit_scale * (image_near + image_far)
+    image_acc, text_part = 0.0, {}
+    for keys in ((-1, 0, 1), (-2, 2), (-3, 3), (4,)):
+        image_part, parts = grads_of(keys)
+        image_acc = image_acc + image_part
+        text_part.update(parts)
+    image_acc = logit_scale * image_acc
 
-    text_far = {k: v.astype(BF16) for k, v in text_far.items()}
-    from_below = shift_z(text_far[3], 1)
-    from_above = shift_z(text_far[-3], -1)
-    far_below = shift_z(text_far[4][:half], 2)
-    far_above = shift_z(text_far[4][half:], -2)
-    beside_below = shift_z(text_acc[1].astype(BF16), 1)
-    beside_above = shift_z(text_acc[-1].astype(BF16), -1)
-    nil = jnp.zeros((half, width), F32)
-    up = text_acc[2] + from_below.astype(F32) + jnp.concatenate([far_below.astype(F32), nil], 0)
-    down = text_acc[-2] + from_above.astype(F32) + jnp.concatenate([nil, far_above.astype(F32)], 0)
-    up = shift_z(up.astype(BF16), 2)
-    down = shift_z(down.astype(BF16), -2)
+    turned = jnp.concatenate([text_part[k] for k in (0, 1, 2, 3, 4, -3, -2, -1)] * 2, 0)
+    turned = lax.dynamic_slice_in_dim(turned, ((Z - z) % Z) * rows, Z * rows, 0)
+    columns_of_z = [[(n * YH + y) * CORE + c for n in range(Z)] for y in range(YH) for c in range(CORE)]
+    text_sum = lax.psum_scatter(
+        turned, "loop", scatter_dimension=0, axis_index_groups=columns_of_z, tiled=True
+    )
+
+    def with_dot(block, dot):
+        high = lax.reduce_precision(dot, 8, 7)
+        digits = jnp.stack([high, dot - high]).astype(BF16).reshape(-1, block.shape[1])
+        digits = jnp.pad(digits, ((0, 16 - digits.shape[0]), (0, 0)))
+        return jnp.concatenate([block.astype(BF16), digits], 0)
+
+    def taken(packet):
+        block = packet[: 4 * rows].astype(F32)
+        digits = packet[4 * rows : 4 * rows + 8 * rows // packet.shape[1]].astype(F32)
+        digits = digits.reshape(2, 4, rows)
+        return block, digits[0] + digits[1]
 
     dot = jnp.sum(image_unit * image_acc, -1).reshape(4, rows)
-    sent = part_of(image_acc, 1 - core, 2).astype(BF16)
-    kept = part_of(image_acc, core, 2)
-    kept = kept + swap_blocks(swap_core(sent), 1, rows).astype(F32)
-    dot = dot + swap_blocks(swap_core(dot), 1, 1)
-    sent = part_of(kept, 1 - yh, 2).astype(BF16)
-    kept = part_of(kept, yh, 2)
-    kept = kept + swap_blocks(swap_yh(sent), 2, rows).astype(F32)
-    dot = dot + swap_blocks(swap_yh(dot), 2, 1)
+    other, other_dot = taken(swap_core(with_dot(part_of(image_acc, 1 - core, 2), dot)))
+    kept = part_of(image_acc, core, 2) + swap_blocks(other, 1, rows)
+    dot = dot + swap_blocks(other_dot, 1, 1)
+    other, other_dot = taken(swap_yh(with_dot(part_of(kept, 1 - yh, 2), dot)))
+    kept = part_of(kept, yh, 2) + swap_blocks(other, 2, rows)
+    dot = dot + swap_blocks(other_dot, 2, 1)
     quarter = core * 2 + yh
     unit_part = part_of(image_unit, quarter, 4)
     proj_grad = ((kept - unit_part * dot.reshape(4 * rows, 1)) * image_inv).astype(BF16)
@@ -144,6 +151,7 @@
     weight_part = weight_part.reshape(4, feat // 4, 2, lanes).transpose(0, 2, 1, 3)
     weight_part = lax.all_to_all(weight_part.reshape(DP, feat // 4, lanes), "dp", 0, 0, tiled=True)
     weight_part = jnp.sum(weight_part.astype(F32), 0).astype(BF16)
+    proj_grad, weight_part = lax.optimization_barrier((proj_grad, weight_part))
     weight_part = weight_part.reshape(LOOP, strip, lanes)
     weight_part = lax.all_to_all(weight_part, "loop", 0, 0, tiled=True)
     weight_part = jnp.sum(weight_part.reshape(Z, YH * CORE, strip, lanes).astype(F32), 0)
@@ -165,8 +173,7 @@
     )
     sensor_grad = inner_rows(own_grad, proj_weight).astype(BF16)
 
-    text_sum = text_acc[0] + beside_below.astype(F32) + beside_above.astype(F32)
-    text_sum = logit_scale * (text_sum + up.astype(F32) + down.astype(F32))
+    text_sum = logit_scale * text_sum.astype(F32)
     text_grad = (text_sum - text_unit * jnp.sum(text_unit * text_sum, -1, keepdims=True)) * text_inv
     return (sensor_grad[None], text_grad[None], weight_grad)
 

time: 146 us -> 140 us (0.959)
  starting transfers between devices: 66.6 us -> 40 us
  waiting for transfers between devices: 47.2 us -> 26.7 us
  between operations: 2.57 us -> 16 us
  blocking collectives: 0 us -> 12.3 us
  other arithmetic: 8.08 us -> 17.7 us
  local copies, waits for them, and re-layouts: 7.13 us -> 9.75 us
  matrix products: 14.1 us -> 16.5 us
    ppermute x16 -> x8, waiting for transfers between devices: 20.6 us -> 5.79 us  [shift_z(): lax.ppermute(block, 'loop', route(lambda z, y, c: (z + distance, y, c)))]
    all_to_all x0 -> x1, blocking collectives: none -> 12.3 us  [on_device(): lax.all_to_all(weight_part.reshape(DP, feat // 4, lanes), 'dp', 0, 0, til...]
    ppermute x16 -> x8, starting transfers between devices: 26.3 us -> 16 us  [shift_z(): lax.ppermute(block, 'loop', route(lambda z, y, c: (z + distance, y, c)))]
    all_to_all x1 -> x0, starting transfers between devices: 6.44 us -> none  [on_device(): lax.all_to_all(weight_part.reshape(DP, feat // 4, lanes), 'dp', 0, 0, til...]
    ppermute x6 -> x3, starting transfers between devices: 11.2 us -> 6.12 us  [swap_core(): return lax.ppermute(block, 'loop', route(lambda z, y, c: (z, y, 1 - c)))]
    ppermute x5 -> x3, waiting for transfers between devices: 11.5 us -> 7.03 us  [swap_yh(): return lax.ppermute(block, 'loop', route(lambda z, y, c: (z, 1 - y, c)))]
    convert_element_type x1 -> x9, other arithmetic: 0.21 us -> 4.23 us  [the longest x4 2.44 us: grads_of(): positive = (match_rows == columns[None, :].astype(F32)).astype(F32)]
    ppermute x5 -> x3, starting transfers between devices: 9.95 us -> 7.22 us  [swap_yh(): return lax.ppermute(block, 'loop', route(lambda z, y, c: (z, 1 - y, c)))]
  transfers between devices with their start and end apart: 30 -> 17, of which waited for: 16 -> 6; matrix products, arithmetic and copies ran while one was open for 6% -> 19% of each run, Pallas kernels for 0% -> 0%
where the time goes in v2:
time: 140 us; the launch traced here: 139 us
  starting transfers between devices  40 us (29%)
  waiting for transfers between devices  26.7 us (19%)
  other arithmetic  17.7 us (13%)
  matrix products  16.5 us (12%)
  between operations  16 us (11%)
  blocking collectives  12.3 us (9%)
  local copies, waits for them, and re-layouts  9.75 us (7%)
    ppermute x8, starting transfers between devices, shift_z(): lax.ppermute(block, 'loop', route(lambda z, y, c: (z + distance, y, c)))  16 us
    all_to_all x1, blocking collectives, on_device(): lax.all_to_all(weight_part.reshape(DP, feat // 4, lanes), 'dp', 0, 0, til...  12.3 us
    all_to_all x1, waiting for transfers between devices, on_device(): weight_part = lax.all_to_all(weight_part, 'loop', 0, 0, tiled=True)  10.3 us
    all_to_all x1, starting transfers between devices, on_device(): weight_part = lax.all_to_all(weight_part, 'loop', 0, 0, tiled=True)  7.27 us
    ppermute x3, starting transfers between devices, swap_yh(): return lax.ppermute(block, 'loop', route(lambda z, y, c: (z, 1 - y, c)))  7.22 us
    ppermute x3, waiting for transfers between devices, swap_yh(): return lax.ppermute(block, 'loop', route(lambda z, y, c: (z, 1 - y, c)))  7.03 us
    dot_general x5, matrix products, inner_cols(): lax.dot_general(left, right, (((0,), (0,)), ((), ())), preferred_element_...  6.65 us
    ppermute x3, starting transfers between devices, swap_core(): return lax.ppermute(block, 'loop', route(lambda z, y, c: (z, y, 1 - c)))  6.12 us
  transfers between devices with their start and end apart: 17, of which 6 were waited for; matrix products, arithmetic and copies ran while one was open for 19% of the time, Pallas kernels for 0%

profile of v2, /device:TPU:1, one launch (start us, length us, event | category | flops | bytes accessed | tf_op | source)
XLA Modules:
  0.0 139.0 jit_solution(3374163952909628284)
XLA Ops:
  9.6 6.5 %collective-permute-start.3 = (bf16[128,1024]{1,0:T(8,128)(2,1)S(1)}, bf16[128,1024]{1,0:T(8,128)(2,1)S(1)}, u32[]{:S(2)}, u32[]{:S(2)}) collective-permute-start(bf16[128,1024]{1,0:T(8,128)(2,1)S(1)} %fusion.35), channel_id=1, source_target_pairs={{0,224},{8,232},{16,240},{24,248},{32,0},{40,8},{48,16},{56,24},{6... | collective-permute-start | bytes 786440 | tf_op jit(solution)/shard_map/ppermute | solution.py:25
  17.7 3.0 %collective-permute-start = (bf16[144,1152]{1,0:T(8,128)(2,1)S(1)}, bf16[144,1152]{1,0:T(8,128)(2,1)}, u32[]{:S(2)}, u32[]{:S(2)}) collective-permute-start(bf16[144,1152]{1,0:T(8,128)(2,1)S(1)} %pad_maximum_fusion.3), channel_id=1, source_target_pairs={{0,16},{8,24},{16,0},{24,8},{32,48},{40,56},{48,32},{56,40},{64,80... | collective-permute-start | bytes 995336 | tf_op jit(solution)/shard_map/ppermute | solution.py:33
  22.9 2.7 %collective-permute-start.5 = (bf16[128,1024]{1,0:T(8,128)(2,1)S(1)}, bf16[128,1024]{1,0:T(8,128)(2,1)}, u32[]{:S(2)}, u32[]{:S(2)}) collective-permute-start(bf16[128,1024]{1,0:T(8,128)(2,1)S(1)} %collective-permute-done.3), channel_id=1, source_target_pairs={{0,224},{8,232},{16,240},{24,248},{32,0},{40,8},{48,16},{56,24},{6... | collective-permute-start | bytes 786440 | tf_op jit(solution)/shard_map/ppermute | solution.py:25
  29.7 3.5 %collective-permute-start.7 = (bf16[128,1024]{1,0:T(8,128)(2,1)}, bf16[128,1024]{1,0:T(8,128)(2,1)S(1)}, u32[]{:S(2)}, u32[]{:S(2)}) collective-permute-start(bf16[128,1024]{1,0:T(8,128)(2,1)} %collective-permute-done.5), channel_id=1, source_target_pairs={{0,224},{8,232},{16,240},{24,248},{32,0},{40,8},{48,16},{56,24},{6... | collective-permute-start | bytes 786440 | tf_op jit(solution)/shard_map/ppermute | solution.py:25
  34.3 2.8 %collective-permute-start.1 = (bf16[288,1152]{1,0:T(8,128)(2,1)S(1)}, bf16[288,1152]{1,0:T(8,128)(2,1)S(1)}, u32[]{:S(2)}, u32[]{:S(2)}) collective-permute-start(bf16[288,1152]{1,0:T(8,128)(2,1)S(1)} %pad_maximum_fusion.1), channel_id=1, source_target_pairs={{0,8},{8,0},{16,24},{24,16},{32,40},{40,32},{48,56},{56,48},{64,72... | collective-permute-start | bytes 1990664 | tf_op jit(solution)/shard_map/ppermute | solution.py:29
  39.0 3.0 %collective-permute-start.8 = (bf16[64,1024]{1,0:T(8,128)(2,1)S(1)}, bf16[64,1024]{1,0:T(8,128)(2,1)S(1)}, u32[]{:S(2)}, u32[]{:S(2)}) collective-permute-start(bf16[64,1024]{1,0:T(8,128)(2,1)S(1)} %slice.175), channel_id=1, source_target_pairs={{0,224},{8,232},{16,240},{24,248},{32,0},{40,8},{48,16},{56,24},{6... | collective-permute-start | bytes 393224 | tf_op jit(solution)/shard_map/ppermute | solution.py:25
  42.4 1.6 %collective-permute-done.8 = bf16[64,1024]{1,0:T(8,128)(2,1)S(1)} collective-permute-done((bf16[64,1024]{1,0:T(8,128)(2,1)S(1)}, bf16[64,1024]{1,0:T(8,128)(2,1)S(1)}, u32[]{:S(2)}, u32[]{:S(2)}) %collective-permute-start.8) | collective-permute-done | bytes 131104 | tf_op jit(solution)/shard_map/ppermute | solution.py:25
  44.0 3.3 %collective-permute-done.9 = bf16[64,1024]{1,0:T(8,128)(2,1)S(1)} collective-permute-done((bf16[64,1024]{1,0:T(8,128)(2,1)S(1)}, bf16[64,1024]{1,0:T(8,128)(2,1)S(1)}, u32[]{:S(2)}, u32[]{:S(2)}) %collective-permute-start.9) | collective-permute-done | bytes 131104 | tf_op jit(solution)/shard_map/ppermute | solution.py:25
  47.6 1.6 %multiply_reduce_fusion.1 = (f32[512]{0:T(512)S(1)}, f32[512,1024]{1,0:T(8,128)S(1)}) fusion(bf16[512,1152]{1,0:T(8,128)(2,1)S(1)} %bitcast.82, bf16[1152,1024]{1,0:T(8,128)(2,1)S(1)} %copy-done), kind=kOutput, calls=%fused_computation.9 | convolution fusion | flops 1209007616 | bytes 5638144 | tf_op jit(solution)/shard_map/dot_general | solution.py:87
  51.9 1.8 %fusion.10 = bf16[512,384]{1,0:T(8,128)(2,1)S(1)} fusion(bf16[512,1024]{1,0:T(8,128)(2,1)S(1)} %get-tuple-element.7, f32[384]{0:T(512)S(1)} %add_convert_fusion, f32[]{:T(128)S(6)} %copy.38, f32[]{:T(128)S(6)} %exp.15, f32[512]{0:T(512)S(1)} %bitcast.93, bf16[128,1024]{1,0:T(8,128)(2,1)S(1)} %collective-permute-done.3, bf16[128,1024]{1,0:T(8,128)(2,1)S(1)} %fusion.35, ...), kind=kOutput, calls=%fused_computation.22 | convolution fusion | flops 406781952 | bytes 2231816 | tf_op jit(solution)/shard_map/dot_general | solution.py:37
  55.3 1.7 %fusion.45 = f32[512,1024]{1,0:T(8,128)S(1)} fusion(bf16[512,384]{1,0:T(8,128)(2,1)S(1)} %fusion.10, bf16[128,1024]{1,0:T(8,128)(2,1)S(1)} %collective-permute-done.3, bf16[128,1024]{1,0:T(8,128)(2,1)S(1)} %fusion.35, bf16[128,1024]{1,0:T(8,128)(2,1)} %collective-permute-done.2), kind=kOutput, calls=%fused_computation.76 | convolution fusion | flops 405012480 | bytes 3276800 | tf_op jit(solution)/shard_map/dot_general | solution.py:101
  57.9 3.0 %collective-permute-start.10 = (bf16[528,512]{1,0:T(8,128)(2,1)S(1)}, bf16[528,512]{1,0:T(8,128)(2,1)S(1)}, u32[]{:S(2)}, u32[]{:S(2)}) collective-permute-start(bf16[528,512]{1,0:T(8,128)(2,1)S(1)} %pad_maximum_fusion.2), channel_id=1, source_target_pairs={{0,8},{8,0},{16,24},{24,16},{32,40},{40,32},{48,56},{56,48},{64,72... | collective-permute-start | bytes 1622024 | tf_op jit(solution)/shard_map/ppermute | solution.py:29
  65.9 1.8 %collective-permute-start.11 = (bf16[528,256]{1,0:T(8,128)(2,1)}, bf16[528,256]{1,0:T(8,128)(2,1)}, u32[]{:S(2)}, u32[]{:S(2)}) collective-permute-start(bf16[528,256]{1,0:T(8,128)(2,1)} %fusion.46), channel_id=1, source_target_pairs={{0,16},{8,24},{16,0},{24,8},{32,48},{40,56},{48,32},{56,40},{64,80... | collective-permute-start | bytes 811016 | tf_op jit(solution)/shard_map/ppermute | solution.py:33
  67.6 7.0 %collective-permute-done.11 = bf16[528,256]{1,0:T(8,128)(2,1)} collective-permute-done((bf16[528,256]{1,0:T(8,128)(2,1)}, bf16[528,256]{1,0:T(8,128)(2,1)}, u32[]{:S(2)}, u32[]{:S(2)}) %collective-permute-start.11) | collective-permute-done | bytes 270368 | tf_op jit(solution)/shard_map/ppermute | solution.py:33
  76.4 2.0 %fusion.44 = bf16[512,256]{1,0:T(8,128)(2,1)} fusion(f32[256,256]{1,0:T(8,128)S(1)} %get-tuple-element.14, f32[256,256]{1,0:T(8,128)S(1)} %get-tuple-element.13, f32[512,1024]{1,0:T(8,128)} %copy-done.1, s32[]{:T(128)S(6)} %select_n.153, f32[512,512]{1,0:T(8,128)S(1)} %maximum_add_fusion, s32[]{:T(128)S(6)} %select_n.151, f32[512]{0:T(512)S(1)} %add_rsqrt_fusion, ...), kind=kLoop, calls=%fused_computation.72 | loop fusion | flops 786432 | bytes 1839112 | tf_op jit(solution)/shard_map/convert_element_type | solution.py:140
  78.4 4.8 %convolution_convert_fusion = bf16[1152,256]{1,0:T(8,128)(2,1)} fusion(bf16[512,256]{1,0:T(8,128)(2,1)} %fusion.44, bf16[512,1152]{1,0:T(8,128)(2,1)} %bitcast.83, s32[1152]{0:T(1024)S(1)} %fusion.70), kind=kOutput, calls=%fused_computation.4 | convolution fusion | flops 1663156224 | bytes 2036224 | tf_op jit(solution)/shard_map/dot_general | solution.py:41
  83.2 1.8 %reshape.300 = bf16[4,288,2,128]{3,2,1,0:T(2,128)(2,1)S(1)} reshape(bf16[1152,256]{1,0:T(8,128)(2,1)} %convolution_convert_fusion) | data formatting | bytes 1179648 | tf_op jit(solution)/shard_map/reshape | solution.py:151
  85.1 12.3 %all_to_all.15 = bf16[8,288,128]{2,1,0:T(8,128)(2,1)S(1)} all-to-all(bf16[8,288,128]{2,1,0:T(8,128)(2,1)S(1)} %bitcast.81), channel_id=1, replica_groups=mesh['loop'=32,'dp'=8] {'dp'}, dimensions={0} | all-to-all | bytes 1179648 | tf_op jit(solution)/shard_map/all_to_all | solution.py:152
  97.6 2.5 %collective-permute-start.12 = (bf16[256,256]{1,0:T(8,128)(2,1)S(1)}, bf16[256,256]{1,0:T(8,128)(2,1)S(1)}, u32[]{:S(2)}, u32[]{:S(2)}) collective-permute-start(bf16[256,256]{1,0:T(8,128)(2,1)S(1)} %get-tuple-element.18), channel_id=1, source_target_pairs={{0,16},{8,24},{16,0},{24,8},{32,48},{40,56},{48,32},{56,40},{64,80... | collective-permute-start | bytes 393224 | tf_op jit(solution)/shard_map/ppermute | solution.py:33
  100.7 7.3 %all-to-all-start.1 = ((bf16[32,9,128]{2,1,0:T(8,128)(2,1)}), bf16[32,9,128]{2,1,0:T(8,128)(2,1)S(1)}, u32[]{:S(2)}, u32[]{:S(2)}) async-start(bf16[32,9,128]{2,1,0:T(8,128)(2,1)} %reshape.302), calls=%async_computation.2 | async-start | bytes 262144 | tf_op jit(solution)/shard_map/all_to_all | solution.py:156
  108.5 10.3 %all-to-all-done.1 = bf16[32,9,128]{2,1,0:T(8,128)(2,1)S(1)} async-done(((bf16[32,9,128]{2,1,0:T(8,128)(2,1)}), bf16[32,9,128]{2,1,0:T(8,128)(2,1)S(1)}, u32[]{:S(2)}, u32[]{:S(2)}) %all-to-all-start.1) | async-done | bytes 73760 | tf_op jit(solution)/shard_map/all_to_all | solution.py:156
  119.5 3.4 %all-to-all-start.2 = ((f32[8,4,9,128]{3,1,2,0:T(4,128)}), f32[8,4,9,128]{3,1,2,0:T(4,128)S(1)}, u32[]{:S(2)}, u32[]{:S(2)}) async-start(f32[8,4,9,128]{3,1,2,0:T(4,128)} %broadcast_in_dim.8), calls=%async_computation.3 | async-start | bytes 294912 | tf_op jit(solution)/shard_map/all_to_all | solution.py:160
  124.5 3.6 %all-to-all-done.2 = f32[8,4,9,128]{3,1,2,0:T(4,128)S(1)} async-done(((f32[8,4,9,128]{3,1,2,0:T(4,128)}), f32[8,4,9,128]{3,1,2,0:T(4,128)S(1)}, u32[]{:S(2)}, u32[]{:S(2)}) %all-to-all-start.2) | async-done | bytes 147488 | tf_op jit(solution)/shard_map/all_to_all | solution.py:160
  130.2 2.0 %fusion.40 = f32[1,128,1024]{2,1,0:T(8,128)} fusion(bf16[128,1024]{1,0:T(8,128)(2,1)} %reduce-scatter.2.cloned.1.call-done, bf16[1,128,1024]{2,1,0:T(8,128)(2,1)S(1)} %copy-done.4, f32[128]{0:T(128)S(1)} %fusion.37, f32[]{:T(128)S(6)} %exp.15, f32[128]{0:T(128)S(1)} %add_rsqrt_fusion.1), kind=kLoop, calls=%fused_computation.65 | loop fusion | flops 917504 | bytes 1049604 | tf_op jit(solution)/shard_map/broadcast_in_dim | solution.py:178
  (127 shorter events, 29.8 us)
Async XLA Ops:
  7.2 40.4 %copy-start = (bf16[1152,1024]{1,0:T(8,128)(2,1)S(1)}, bf16[1152,1024]{1,0:T(8,128)(2,1)}, u32[]{:S(2)}) copy-start(bf16[1152,1024]{1,0:T(8,128)(2,1)} %param.8) | copy-start | bytes 7077892
  7.2 26.0 %copy-start.6 = (bf16[1,128,1152]{2,1,0:T(8,128)(2,1)S(1)}, bf16[1,128,1152]{2,1,0:T(8,128)(2,1)}, u32[]{:S(2)}) copy-start(bf16[1,128,1152]{2,1,0:T(8,128)(2,1)} %param.6) | copy-start | bytes 884740
  7.2 121.8 %reduce-scatter.2.cloned.1.call-start = ((), (), s32[]{:S(2)}) async-start(), calls=%async_computation.4 | async-start | bytes 2359296 | tf_op jit(solution)/shard_map/reduce_scatter | solution.py:115
  9.6 13.4 %collective-permute-start.3 = (bf16[128,1024]{1,0:T(8,128)(2,1)S(1)}, bf16[128,1024]{1,0:T(8,128)(2,1)S(1)}, u32[]{:S(2)}, u32[]{:S(2)}) collective-permute-start(bf16[128,1024]{1,0:T(8,128)(2,1)S(1)} %fusion.35), channel_id=1, source_target_pairs={{0,224},{8,232},{16,240},{24,248},{32,0},{40,8},{48,16},{56,24},{6... | collective-permute-start | bytes 786440 | tf_op jit(solution)/shard_map/ppermute | solution.py:25
  16.1 9.5 %collective-permute-start.2 = (bf16[128,1024]{1,0:T(8,128)(2,1)S(1)}, bf16[128,1024]{1,0:T(8,128)(2,1)}, u32[]{:S(2)}, u32[]{:S(2)}) collective-permute-start(bf16[128,1024]{1,0:T(8,128)(2,1)S(1)} %fusion.35), channel_id=1, source_target_pairs={{0,32},{8,40},{16,48},{24,56},{32,64},{40,72},{48,80},{56,88},{64,... | collective-permute-start | bytes 786440 | tf_op jit(solution)/shard_map/ppermute | solution.py:25
  17.7 15.5 %collective-permute-start = (bf16[144,1152]{1,0:T(8,128)(2,1)S(1)}, bf16[144,1152]{1,0:T(8,128)(2,1)}, u32[]{:S(2)}, u32[]{:S(2)}) collective-permute-start(bf16[144,1152]{1,0:T(8,128)(2,1)S(1)} %pad_maximum_fusion.3), channel_id=1, source_target_pairs={{0,16},{8,24},{16,0},{24,8},{32,48},{40,56},{48,32},{56,40},{64,80... | collective-permute-start | bytes 995336 | tf_op jit(solution)/shard_map/ppermute | solution.py:33
  22.9 6.8 %collective-permute-start.5 = (bf16[128,1024]{1,0:T(8,128)(2,1)S(1)}, bf16[128,1024]{1,0:T(8,128)(2,1)}, u32[]{:S(2)}, u32[]{:S(2)}) collective-permute-start(bf16[128,1024]{1,0:T(8,128)(2,1)S(1)} %collective-permute-done.3), channel_id=1, source_target_pairs={{0,224},{8,232},{16,240},{24,248},{32,0},{40,8},{48,16},{56,24},{6... | collective-permute-start | bytes 786440 | tf_op jit(solution)/shard_map/ppermute | solution.py:25
  25.6 7.6 %collective-permute-start.4 = (bf16[128,1024]{1,0:T(8,128)(2,1)}, bf16[128,1024]{1,0:T(8,128)(2,1)}, u32[]{:S(2)}, u32[]{:S(2)}) collective-permute-start(bf16[128,1024]{1,0:T(8,128)(2,1)} %collective-permute-done.2), channel_id=1, source_target_pairs={{0,32},{8,40},{16,48},{24,56},{32,64},{40,72},{48,80},{56,88},{64,... | collective-permute-start | bytes 786440 | tf_op jit(solution)/shard_map/ppermute | solution.py:25
  29.7 9.3 %collective-permute-start.7 = (bf16[128,1024]{1,0:T(8,128)(2,1)}, bf16[128,1024]{1,0:T(8,128)(2,1)S(1)}, u32[]{:S(2)}, u32[]{:S(2)}) collective-permute-start(bf16[128,1024]{1,0:T(8,128)(2,1)} %collective-permute-done.5), channel_id=1, source_target_pairs={{0,224},{8,232},{16,240},{24,248},{32,0},{40,8},{48,16},{56,24},{6... | collective-permute-start | bytes 786440 | tf_op jit(solution)/shard_map/ppermute | solution.py:25
  33.2 8.9 %collective-permute-start.6 = (bf16[128,1024]{1,0:T(8,128)(2,1)}, bf16[128,1024]{1,0:T(8,128)(2,1)S(1)}, u32[]{:S(2)}, u32[]{:S(2)}) collective-permute-start(bf16[128,1024]{1,0:T(8,128)(2,1)} %collective-permute-done.4), channel_id=1, source_target_pairs={{0,32},{8,40},{16,48},{24,56},{32,64},{40,72},{48,80},{56,88},{64,... | collective-permute-start | bytes 786440 | tf_op jit(solution)/shard_map/ppermute | solution.py:25
  34.3 13.1 %collective-permute-start.1 = (bf16[288,1152]{1,0:T(8,128)(2,1)S(1)}, bf16[288,1152]{1,0:T(8,128)(2,1)S(1)}, u32[]{:S(2)}, u32[]{:S(2)}) collective-permute-start(bf16[288,1152]{1,0:T(8,128)(2,1)S(1)} %pad_maximum_fusion.1), channel_id=1, source_target_pairs={{0,8},{8,0},{16,24},{24,16},{32,40},{40,32},{48,56},{56,48},{64,72... | collective-permute-start | bytes 1990664 | tf_op jit(solution)/shard_map/ppermute | solution.py:29
  39.0 5.0 %collective-permute-start.8 = (bf16[64,1024]{1,0:T(8,128)(2,1)S(1)}, bf16[64,1024]{1,0:T(8,128)(2,1)S(1)}, u32[]{:S(2)}, u32[]{:S(2)}) collective-permute-start(bf16[64,1024]{1,0:T(8,128)(2,1)S(1)} %slice.175), channel_id=1, source_target_pairs={{0,224},{8,232},{16,240},{24,248},{32,0},{40,8},{48,16},{56,24},{6... | collective-permute-start | bytes 393224 | tf_op jit(solution)/shard_map/ppermute | solution.py:25
  42.1 5.3 %collective-permute-start.9 = (bf16[64,1024]{1,0:T(8,128)(2,1)S(1)}, bf16[64,1024]{1,0:T(8,128)(2,1)S(1)}, u32[]{:S(2)}, u32[]{:S(2)}) collective-permute-start(bf16[64,1024]{1,0:T(8,128)(2,1)S(1)} %slice.176), channel_id=1, source_target_pairs={{0,32},{8,40},{16,48},{24,56},{32,64},{40,72},{48,80},{56,88},{64,... | collective-permute-start | bytes 393224 | tf_op jit(solution)/shard_map/ppermute | solution.py:25
  47.5 1.7 %copy-start.5 = (bf16[2,2,128,1152]{3,2,1,0:T(8,128)(2,1)}, bf16[2,2,128,1152]{3,2,1,0:T(8,128)(2,1)S(1)}, u32[]{:S(2)}) copy-start(bf16[2,2,128,1152]{3,2,1,0:T(8,128)(2,1)S(1)} %fusion.25) | copy-start | bytes 3538948
  49.5 7.5 %copy-start.1 = (f32[512,1024]{1,0:T(8,128)}, f32[512,1024]{1,0:T(8,128)S(1)}, u32[]{:S(2)}) copy-start(f32[512,1024]{1,0:T(8,128)S(1)} %get-tuple-element.8) | copy-start | bytes 6291460
  57.8 3.2 %copy-start.2 = (f32[512,1024]{1,0:T(8,128)}, f32[512,1024]{1,0:T(8,128)S(1)}, u32[]{:S(2)}) copy-start(f32[512,1024]{1,0:T(8,128)S(1)} %get-tuple-element.38) | copy-start | bytes 6291460
  57.9 5.2 %collective-permute-start.10 = (bf16[528,512]{1,0:T(8,128)(2,1)S(1)}, bf16[528,512]{1,0:T(8,128)(2,1)S(1)}, u32[]{:S(2)}, u32[]{:S(2)}) collective-permute-start(bf16[528,512]{1,0:T(8,128)(2,1)S(1)} %pad_maximum_fusion.2), channel_id=1, source_target_pairs={{0,8},{8,0},{16,24},{24,16},{32,40},{40,32},{48,56},{56,48},{64,72... | collective-permute-start | bytes 1622024 | tf_op jit(solution)/shard_map/ppermute | solution.py:29
  65.9 8.8 %collective-permute-start.11 = (bf16[528,256]{1,0:T(8,128)(2,1)}, bf16[528,256]{1,0:T(8,128)(2,1)}, u32[]{:S(2)}, u32[]{:S(2)}) collective-permute-start(bf16[528,256]{1,0:T(8,128)(2,1)} %fusion.46), channel_id=1, source_target_pairs={{0,16},{8,24},{16,0},{24,8},{32,48},{40,56},{48,32},{56,40},{64,80... | collective-permute-start | bytes 811016 | tf_op jit(solution)/shard_map/ppermute | solution.py:33
  83.2 14.4 %copy-start.7 = (bf16[512,256]{1,0:T(8,128)(2,1)S(1)}, bf16[512,256]{1,0:T(8,128)(2,1)}, u32[]{:S(2)}) copy-start(bf16[512,256]{1,0:T(8,128)(2,1)} %fusion.44) | copy-start | bytes 786436
  97.6 10.4 %collective-permute-start.12 = (bf16[256,256]{1,0:T(8,128)(2,1)S(1)}, bf16[256,256]{1,0:T(8,128)(2,1)S(1)}, u32[]{:S(2)}, u32[]{:S(2)}) collective-permute-start(bf16[256,256]{1,0:T(8,128)(2,1)S(1)} %get-tuple-element.18), channel_id=1, source_target_pairs={{0,16},{8,24},{16,0},{24,8},{32,48},{40,56},{48,32},{56,40},{64,80... | collective-permute-start | bytes 393224 | tf_op jit(solution)/shard_map/ppermute | solution.py:33
  100.7 18.0 %all-to-all-start.1 = ((bf16[32,9,128]{2,1,0:T(8,128)(2,1)}), bf16[32,9,128]{2,1,0:T(8,128)(2,1)S(1)}, u32[]{:S(2)}, u32[]{:S(2)}) async-start(bf16[32,9,128]{2,1,0:T(8,128)(2,1)} %reshape.302), calls=%async_computation.2 | async-start | bytes 262144 | tf_op jit(solution)/shard_map/all_to_all | solution.py:156
  108.2 14.7 %collective-permute-start.13 = (bf16[128,512]{1,0:T(8,128)(2,1)S(1)}, bf16[128,512]{1,0:T(8,128)(2,1)S(1)}, u32[]{:S(2)}, u32[]{:S(2)}) collective-permute-start(bf16[128,512]{1,0:T(8,128)(2,1)S(1)} %get-tuple-element.16), channel_id=1, source_target_pairs={{0,8},{8,0},{16,24},{24,16},{32,40},{40,32},{48,56},{56,48},{64,72... | collective-permute-start | bytes 393224 | tf_op jit(solution)/shard_map/ppermute | solution.py:29
  119.5 8.6 %all-to-all-start.2 = ((f32[8,4,9,128]{3,1,2,0:T(4,128)}), f32[8,4,9,128]{3,1,2,0:T(4,128)S(1)}, u32[]{:S(2)}, u32[]{:S(2)}) async-start(f32[8,4,9,128]{3,1,2,0:T(4,128)} %broadcast_in_dim.8), calls=%async_computation.3 | async-start | bytes 294912 | tf_op jit(solution)/shard_map/all_to_all | solution.py:160
  122.9 6.1 %copy-start.4 = (bf16[1,128,1024]{2,1,0:T(8,128)(2,1)S(1)}, bf16[1,128,1024]{2,1,0:T(8,128)(2,1)}, u32[]{:S(2)}) copy-start(bf16[1,128,1024]{2,1,0:T(8,128)(2,1)} %param.7) | copy-start | bytes 786436
  (3 other events, 3.2 us)
Sparse Core Ops, SparseCore 0:
  63.3 34.6 reduce-scatter.1

commit v3 on v2

v3 whole, which is shorter than its diff:
```python
import functools

import jax
import jax.numpy as jnp
from jax import lax
from jax.experimental import pallas as pl
from jax.experimental.pallas import tpu as pltpu
from jax.sharding import PartitionSpec as P

Z, YH, CORE = 8, 2, 2
LOOP = Z * YH * CORE
DP = 8
BF16 = jnp.bfloat16
F32 = jnp.float32
VMEM = pl.BlockSpec(memory_space=pltpu.VMEM)
SMEM = pl.BlockSpec(memory_space=pltpu.SMEM)


def route(move):
    pairs = []
    for z in range(Z):
        for y in range(YH):
            for c in range(CORE):
                to_z, to_y, to_c = move(z, y, c)
                source = (z * YH + y) * CORE + c
                pairs.append((source, ((to_z % Z) * YH + to_y) * CORE + to_c))
    return pairs


def shift_z(block, distance):
    return lax.ppermute(block, "loop", route(lambda z, y, c: (z + distance, y, c)))


def swap_core(block):
    return lax.ppermute(block, "loop", route(lambda z, y, c: (z, y, 1 - c)))


def swap_yh(block):
    return lax.ppermute(block, "loop", route(lambda z, y, c: (z, 1 - y, c)))


def inner_rows(left, right):
    return lax.dot_general(left, right, (((1,), (1,)), ((), ())), preferred_element_type=F32)


def inner_cols(left, right):
    return lax.dot_general(left, right, (((0,), (0,)), ((), ())), preferred_element_type=F32)


def call(kernel, out, aliases, *operands):
    return pl.pallas_call(
        kernel,
        out_shape=out,
        in_specs=[SMEM if o.ndim == 1 else VMEM for o in operands],
        out_specs=[VMEM] * len(out),
        input_output_aliases=aliases,
        cost_estimate=pl.CostEstimate(flops=1, bytes_accessed=1, transcendentals=0),
        compiler_params=pltpu.CompilerParams(vmem_limit_bytes=40 << 20),
    )(*operands)


def block_grads(numbers, start, image_emb, match, text):
    wide = text.astype(F32)
    inv = lax.rsqrt(jnp.sum(wide * wide, -1, keepdims=True) + 1e-06)
    emb = (wide * inv).astype(BF16)
    logits = numbers[0] * inner_rows(image_emb, emb) + numbers[1]
    column = lax.broadcasted_iota(jnp.int32, logits.shape, 1) + start
    positive = (match == column.astype(F32)).astype(F32)
    return emb, (jax.nn.sigmoid(logits) - positive).astype(BF16)


def pairs_kernel(count, first, numbers, starts, image_emb, match, *refs):
    texts, refs = refs[:count], refs[count:]
    if not first:
        acc_in, refs = refs[0], refs[1:]
    acc_out, text_out = refs[0], refs[1:]
    image = image_emb[...]
    embs, grads = [], []
    for n in range(count):
        emb, grad = block_grads(numbers, starts[n], image, match[...], texts[n][...])
        embs.append(emb)
        grads.append(grad)
    emb, grad = jnp.concatenate(embs, 0), jnp.concatenate(grads, 1)
    part = jnp.dot(grad, emb, preferred_element_type=F32)
    acc_out[...] = part if first else acc_in[...] + part
    text_part = inner_cols(grad, image)
    rows = texts[0].shape[0]
    for n in range(count):
        text_out[n][...] = text_part[n * rows : (n + 1) * rows].astype(text_out[n].dtype)


def last_kernel(numbers, starts, image_emb, match, low, high, acc_in, unit, acc_out, dot_out, packet, low_out, high_out):
    image = image_emb[...]
    text = jnp.concatenate([low[...], high[...]], 0)
    emb, grad = block_grads(numbers, starts[0], image, match[...], text)
    acc = numbers[0] * (acc_in[...] + jnp.dot(grad, emb, preferred_element_type=F32))
    acc_out[...] = acc
    dot = jnp.sum(unit[...] * acc, -1, keepdims=True)
    dot_out[...] = dot
    rows, width = acc.shape
    half, quarter, block = width // 2, width // 4, rows // 4
    own = pl.multiple_of(starts[1] * half, half)
    other = pl.multiple_of((1 - starts[1]) * half, half)
    packet[:, :half] = acc_out[:, pl.ds(other, half)].astype(BF16)
    top = dot.astype(BF16).astype(F32)
    lane = lax.broadcasted_iota(jnp.int32, (rows, 128), 1)
    digits = jnp.where(lane == 0, top, jnp.where(lane == 1, dot - top, 0.0))
    packet[:, half : half + 128] = digits.astype(BF16)
    for side in range(2):
        lanes = pl.ds(pl.multiple_of(own + side * quarter, quarter), quarter)
        for n, slot in enumerate((1, 3)):
            at = (2 * side + n) * block
            packet[at : at + block, half + 128 :] = acc_out[slot * block : (slot + 1) * block, lanes].astype(BF16)
    text_part = inner_cols(grad, image).astype(BF16)
    middle = low.shape[0]
    low_out[...] = text_part[:middle]
    high_out[...] = text_part[middle:]


def weight_kernel(starts, got, acc, dot, unit, inv, sensor_sorted, weight, row_send, row_keep):
    rows, width = acc.shape
    half, quarter, block = width // 2, width // 4, rows // 4
    own = pl.ds(pl.multiple_of(starts[1] * half, half), half)
    projs = []
    for slot in range(4):
        mine = slice(slot * block, (slot + 1) * block)
        theirs = slice((slot ^ 1) * block, ((slot ^ 1) + 1) * block)
        kept = acc[mine, own] + got[theirs, :half].astype(F32)
        digits = got[theirs, half : half + 128].astype(F32)
        whole_dot = dot[mine, :] + digits[:, 0:1] + digits[:, 1:2]
        projs.append(((kept - unit[mine, own] * whole_dot) * inv[mine, :]).astype(BF16))
        if slot in (0, 2):
            target = (row_keep, row_send)[slot // 2]
            target[:, own] = kept.astype(target.dtype)
            for side in range(2):
                first = pl.multiple_of((1 - starts[1]) * half + side * quarter, quarter)
                lanes = pl.ds(first, quarter)
                at = (2 * side + slot // 2) * block
                extra = got[at : at + block, half + 128 :].astype(F32)
                target[:, lanes] = (acc[mine, lanes] + extra).astype(target.dtype)
    proj = jnp.concatenate(projs, 0)
    chunk_rows, chunk_cols = weight.shape[1:]
    for x in range(4):
        left = sensor_sorted[x * chunk_rows : (x + 1) * chunk_rows, :]
        product = jnp.dot(left, proj, preferred_element_type=F32).astype(BF16)
        for y in range(2):
            weight[2 * x + y] = product[:, y * chunk_cols : (y + 1) * chunk_cols]


def on_device(sensor_feats, text_embeds, proj_weight, matches, log_scale, logit_bias):
    sensor = sensor_feats[0]
    texts = text_embeds[0]
    rows = sensor.shape[0]
    feat, width = proj_weight.shape
    loop_index = lax.axis_index("loop")
    z = loop_index // (YH * CORE)
    core = loop_index % CORE
    logit_scale = jnp.exp(log_scale)
    numbers = jnp.stack([logit_scale, logit_bias])

    slot = {0: texts}
    for k in (1, 2, 3):
        slot[k] = shift_z(slot[k - 1], -1)
        slot[-k] = shift_z(slot[1 - k], 1)

    match = matches.reshape(1, rows)
    digits = jnp.concatenate([match // 64, match % 64], 0).astype(BF16)
    digits = jnp.pad(digits, ((0, 14), (0, feat - rows)))
    packet = jnp.concatenate([sensor, digits], 0)
    packet = jnp.concatenate([packet, swap_yh(packet)], 0)
    packets = jnp.stack([packet.reshape(2, rows + 16, feat), swap_core(packet).reshape(2, rows + 16, feat)], 1)
    sensor_rows = packets[:, :, :rows].reshape(4 * rows, feat)
    digits = packets[:, :, rows : rows + 2, :rows].astype(F32)
    match_rows = (digits[:, :, 0] * 64.0 + digits[:, :, 1]).reshape(4 * rows, 1)

    projected = jnp.dot(sensor_rows, proj_weight, preferred_element_type=F32)
    image_inv = lax.rsqrt(jnp.sum(projected * projected, -1, keepdims=True) + 1e-06)
    image_unit = projected * image_inv
    image_emb = image_unit.astype(BF16)

    per_loop = feat // LOOP
    strip = per_loop // 4
    place = jnp.arange(feat, dtype=jnp.int32)
    rest = place % (feat // 4)
    wanted = (rest // strip) * per_loop + (place // (feat // 4)) * strip + rest % strip
    permutation = (wanted[:, None] == jnp.arange(feat, dtype=jnp.int32)[None, :]).astype(BF16)
    permutation = lax.optimization_barrier(permutation)
    sensor_sorted = inner_rows(permutation, sensor_rows).astype(BF16)

    def starts_of(keys):
        return [(loop_index + k * YH * CORE) % LOOP * rows for k in keys]

    def pairs(keys, dtypes, acc):
        operands = [numbers, jnp.stack(starts_of(keys)), image_emb, match_rows, *(slot[k] for k in keys)]
        out = [jax.ShapeDtypeStruct((4 * rows, width), F32)]
        out += [jax.ShapeDtypeStruct((rows, width), d) for d in dtypes]
        aliases = {}
        if acc is not None:
            aliases = {len(operands): 0}
            operands.append(acc)
        kernel = functools.partial(pairs_kernel, len(keys), acc is None)
        return call(kernel, out, aliases, *operands)

    acc, text_0, text_1, text_m1 = pairs((0, 1, -1), (F32, BF16, BF16), None)
    acc, text_2, text_m2 = pairs((2, -2), (F32, F32), acc)
    half = rows // 2
    end_low, end_high = shift_z(slot[3][:half], -1), shift_z(slot[-3][half:], 1)
    acc, text_3, text_m3 = pairs((3, -3), (BF16, BF16), acc)
    starts = jnp.stack(starts_of((4,)) + [core])
    shapes = [((4 * rows, width), F32), ((4 * rows, 1), F32), ((4 * rows, width // 8 * 7), BF16)]
    shapes += [((half, width), BF16)] * 2
    acc, dot, packet, text_low, text_high = call(
        last_kernel,
        [jax.ShapeDtypeStruct(*s) for s in shapes],
        {6: 0},
        numbers, starts, image_emb, match_rows, end_low, end_high, acc, image_unit,
    )

    shapes = [((DP, feat // 4, width // 4), BF16), ((rows, width), BF16), ((rows, width), F32)]
    weight_part, row_send, row_keep = call(
        weight_kernel,
        [jax.ShapeDtypeStruct(*s) for s in shapes],
        {},
        starts, swap_core(packet), acc, dot, image_unit, image_inv, sensor_sorted,
    )
    weight_part = lax.all_to_all(weight_part, "dp", 0, 0, tiled=True)
    weight_part = jnp.sum(weight_part.astype(F32), 0).astype(BF16)
    weight_part = weight_part.reshape(LOOP, strip, width // 4)
    weight_part = lax.all_to_all(weight_part, "loop", 0, 0, tiled=True)
    weight_part = jnp.sum(weight_part.reshape(Z * YH, CORE, strip, width // 4).astype(F32), 0)
    weight_part = weight_part * (1.0 / DP)
    shares = jnp.broadcast_to(weight_part[None], (DP,) + weight_part.shape)
    shares = lax.all_to_all(shares, "dp", 0, 0, tiled=True)
    shares = shares.reshape(4, 2, CORE, strip, width // 4).transpose(0, 3, 2, 1, 4)
    weight_grad = shares.reshape(per_loop, width)

    text_3, text_m3, text_low, text_high, text_1, text_m1, row_send = lax.optimization_barrier(
        (text_3, text_m3, text_low, text_high, text_1, text_m1, row_send)
    )
    row_got = swap_yh(row_send)
    from_below, from_above = shift_z(text_3, 1), shift_z(text_m3, -1)
    far_below, far_above = shift_z(text_low, 2), shift_z(text_high, -2)
    near_below, near_above = shift_z(text_1, 1), shift_z(text_m1, -1)
    nil = jnp.zeros((half, width), F32)
    up = text_2 + from_below.astype(F32) + jnp.concatenate([far_below.astype(F32), nil], 0)
    down = text_m2 + from_above.astype(F32) + jnp.concatenate([nil, far_above.astype(F32)], 0)
    up, down = shift_z(up.astype(BF16), 2), shift_z(down.astype(BF16), -2)
    text_sum = text_0 + near_below.astype(F32) + near_above.astype(F32)
    text_sum = logit_scale * (text_sum + up.astype(F32) + down.astype(F32))
    text_wide = texts.astype(F32)
    text_inv = lax.rsqrt(jnp.sum(text_wide * text_wide, -1, keepdims=True) + 1e-06)
    text_unit = text_wide * text_inv
    text_grad = (text_sum - text_unit * jnp.sum(text_unit * text_sum, -1, keepdims=True)) * text_inv

    image_grad = row_keep + row_got.astype(F32)
    own_unit = image_unit[:rows]
    own_dot = jnp.sum(own_unit * image_grad, -1, keepdims=True)
    proj_grad = ((image_grad - own_unit * own_dot) * image_inv[:rows]).astype(BF16)
    sensor_grad = inner_rows(proj_grad, proj_weight).astype(BF16)
    return (sensor_grad[None], text_grad[None], weight_grad)


def solution(mesh):
    placed = (P("dp", "loop", None), P("dp", "loop", None), P(), P("dp", "loop"), P(), P())
    return jax.shard_map(
        on_device,
        mesh=mesh,
        in_specs=placed,
        out_specs=(P("dp", "loop", None), P("dp", "loop", None), P("loop", None)),
        check_vma=False,
    )
```

time: 140 us -> 153 us (1.093)
  Pallas kernels: 0 us -> 13.6 us
  between operations: 16 us -> 2.41 us
  starting transfers between devices: 40 us -> 53.4 us
  blocking collectives: 12.3 us -> 0 us
  local copies, waits for them, and re-layouts: 9.75 us -> 21.7 us
  matrix products: 16.5 us -> 8.38 us
  other arithmetic: 17.7 us -> 23.3 us
  waiting for transfers between devices: 26.7 us -> 29 us
    pallas_call x0 -> x5, Pallas kernels: none -> 13.6 us  [call(): pl.pallas_call(kernel, out_shape=out, in_specs=[SMEM if o.ndim == 1 else...]
    unnamed x34 -> x92, local copies, waits for them, and re-layouts: 2.73 us -> 15.6 us
    all_to_all x1 -> x0, blocking collectives: 12.3 us -> none  [on_device(): lax.all_to_all(weight_part.reshape(DP, feat // 4, lanes), 'dp', 0, 0, til...]
    ppermute x8 -> x16, waiting for transfers between devices: 5.79 us -> 15.9 us  [shift_z(): lax.ppermute(block, 'loop', route(lambda z, y, c: (z + distance, y, c)))]
    dot_general x9 -> x0, matrix products: 9.96 us -> none  [the longest x5 6.65 us: inner_cols(): lax.dot_general(left, right, (((0,), (0,)), ((), ())), preferred_element_...]
    ppermute x8 -> x16, starting transfers between devices: 16 us -> 25.5 us  [shift_z(): lax.ppermute(block, 'loop', route(lambda z, y, c: (z + distance, y, c)))]
    ppermute x3 -> x2, waiting for transfers between devices: 7.03 us -> 0.01 us  [swap_yh(): return lax.ppermute(block, 'loop', route(lambda z, y, c: (z, 1 - y, c)))]
    all_to_all x0 -> x1, starting transfers between devices: none -> 4.39 us  [on_device(): weight_part = lax.all_to_all(weight_part, 'dp', 0, 0, tiled=True)]
  transfers between devices with their start and end apart: 17 -> 23, of which waited for: 6 -> 5; matrix products, arithmetic and copies ran while one was open for 19% -> 21% of each run, Pallas kernels for 0% -> 5%
where the time goes in v3:
time: 153 us; the launch traced here: 152 us
  starting transfers between devices  53.4 us (35%)
  waiting for transfers between devices  29 us (19%)
  other arithmetic  23.3 us (15%)
  local copies, waits for them, and re-layouts  21.7 us (14%)
  Pallas kernels  13.6 us (9%)
  matrix products  8.38 us (5%)
  between operations  2.41 us (2%)
    ppermute x16, starting transfers between devices, shift_z(): lax.ppermute(block, 'loop', route(lambda z, y, c: (z + distance, y, c)))  25.5 us
    ppermute x16, waiting for transfers between devices, shift_z(): lax.ppermute(block, 'loop', route(lambda z, y, c: (z + distance, y, c)))  15.9 us
    unnamed x92, local copies, waits for them, and re-layouts  15.6 us
    pallas_call x5, Pallas kernels, call(): pl.pallas_call(kernel, out_shape=out, in_specs=[SMEM if o.ndim == 1 else...  13.6 us
    all_to_all x1, starting transfers between devices, on_device(): weight_part = lax.all_to_all(weight_part, 'loop', 0, 0, tiled=True)  8.98 us
    all_to_all x1, waiting for transfers between devices, on_device(): weight_part = lax.all_to_all(weight_part, 'loop', 0, 0, tiled=True)  8.61 us
    dot_general x2, matrix products, inner_rows(): lax.dot_general(left, right, (((1,), (1,)), ((), ())), preferred_element_...  6.74 us
    ppermute x2, starting transfers between devices, swap_yh(): return lax.ppermute(block, 'loop', route(lambda z, y, c: (z, 1 - y, c)))  5.07 us
  transfers between devices with their start and end apart: 23, of which 5 were waited for; matrix products, arithmetic and copies ran while one was open for 21% of the time, Pallas kernels for 5%

profile of v3, /device:TPU:1, one launch (start us, length us, event | category | flops | bytes accessed | tf_op | source)
XLA Modules:
  0.0 151.8 jit_solution(7931531929576220918)
XLA Ops:
  3.2 3.7 %collective-permute-start = (bf16[144,1152]{1,0:T(8,128)(2,1)}, bf16[144,1152]{1,0:T(8,128)(2,1)}, u32[]{:S(2)}, u32[]{:S(2)}) collective-permute-start(bf16[144,1152]{1,0:T(8,128)(2,1)} %pad_maximum_fusion.1), channel_id=1, source_target_pairs={{0,16},{8,24},{16,0},{24,8},{32,48},{40,56},{48,32},{56,40},{64,80... | collective-permute-start | bytes 995336 | tf_op jit(solution)/shard_map/ppermute | solution.py:39
  8.6 3.9 %collective-permute-start.2 = (bf16[128,1024]{1,0:T(8,128)(2,1)}, bf16[128,1024]{1,0:T(8,128)(2,1)S(1)}, u32[]{:S(2)}, u32[]{:S(2)}) collective-permute-start(bf16[128,1024]{1,0:T(8,128)(2,1)} %bitcast.37), channel_id=1, source_target_pairs={{0,224},{8,232},{16,240},{24,248},{32,0},{40,8},{48,16},{56,24},{6... | collective-permute-start | bytes 786440 | tf_op jit(solution)/shard_map/ppermute | solution.py:31
  12.5 5.9 %collective-permute-done.6.refs_2_ = bf16[128,1024]{1,0:T(8,128)(2,1)S(1)} collective-permute-done((bf16[128,1024]{1,0:T(8,128)(2,1)}, bf16[128,1024]{1,0:T(8,128)(2,1)S(1)}, u32[]{:S(2)}, u32[]{:S(2)}) %collective-permute-start.6) | collective-permute-done | bytes 262176 | tf_op jit(solution)/shard_map/ppermute | solution.py:31
  18.5 2.7 %collective-permute-start.3 = (bf16[128,1024]{1,0:T(8,128)(2,1)S(1)}, bf16[128,1024]{1,0:T(8,128)(2,1)S(1)}, u32[]{:S(2)}, u32[]{:S(2)}) collective-permute-start(bf16[128,1024]{1,0:T(8,128)(2,1)S(1)} %collective-permute-done.2.refs_1_), channel_id=1, source_target_pairs={{0,224},{8,232},{16,240},{24,248},{32,0},{40,8},{48,16},{56,24},{6... | collective-permute-start | bytes 786440 | tf_op jit(solution)/shard_map/ppermute | solution.py:31
  23.1 2.1 %collective-permute-start.1 = (bf16[288,1152]{1,0:T(8,128)(2,1)}, bf16[288,1152]{1,0:T(8,128)(2,1)}, u32[]{:S(2)}, u32[]{:S(2)}) collective-permute-start(bf16[288,1152]{1,0:T(8,128)(2,1)} %pad_maximum_fusion), channel_id=1, source_target_pairs={{0,8},{8,0},{16,24},{24,16},{32,40},{40,32},{48,56},{56,48},{64,72... | collective-permute-start | bytes 1990664 | tf_op jit(solution)/shard_map/ppermute | solution.py:35
  27.4 2.7 %collective-permute-start.4 = (bf16[128,1024]{1,0:T(8,128)(2,1)S(1)}, bf16[128,1024]{1,0:T(8,128)(2,1)S(1)}, u32[]{:S(2)}, u32[]{:S(2)}) collective-permute-start(bf16[128,1024]{1,0:T(8,128)(2,1)S(1)} %collective-permute-done.3.refs_0_), channel_id=1, source_target_pairs={{0,224},{8,232},{16,240},{24,248},{32,0},{40,8},{48,16},{56,24},{6... | collective-permute-start | bytes 786440 | tf_op jit(solution)/shard_map/ppermute | solution.py:31
  30.9 4.5 %collective-permute-done.8.refs_1_ = bf16[128,1024]{1,0:T(8,128)(2,1)S(1)} collective-permute-done((bf16[128,1024]{1,0:T(8,128)(2,1)S(1)}, bf16[128,1024]{1,0:T(8,128)(2,1)S(1)}, u32[]{:S(2)}, u32[]{:S(2)}) %collective-permute-start.8) | collective-permute-done | bytes 262176 | tf_op jit(solution)/shard_map/ppermute | solution.py:31
  36.8 2.7 %collective-permute-start.5 = (bf16[64,1024]{1,0:T(8,128)(2,1)}, bf16[64,1024]{1,0:T(8,128)(2,1)}, u32[]{:S(2)}, u32[]{:S(2)}) collective-permute-start(bf16[64,1024]{1,0:T(8,128)(2,1)} %slice.37), channel_id=1, source_target_pairs={{0,224},{8,232},{16,240},{24,248},{32,0},{40,8},{48,16},{56,24},{6... | collective-permute-start | bytes 393224 | tf_op jit(solution)/shard_map/ppermute | solution.py:31
  50.8 3.0 %shard_map.85 = (f32[512,1024]{1,0:T(8,128)S(1)}, f32[128,1024]{1,0:T(8,128)S(1)}, bf16[128,1024]{1,0:T(8,128)(2,1)S(1)}, bf16[128,1024]{1,0:T(8,128)(2,1)S(1)}) custom-call(f32[2]{0:T(128)S(1)} %pad_maximum_fusion.3.numbers, s32[3]{0:T(128)S(1)} %pad_add_fusion.3.starts, bf16[512,1024]{1,0:T(8,128)(2,1)S(1)} %get-tuple-element.55.image_emb, ...), custom_call_target="tpu_custom_call" | custom-call | flops 1 | bytes 1 | tf_op jit(solution)/shard_map/pallas_call | solution.py:51
  56.7 2.5 %shard_map.86 = (f32[512,1024]{1,0:T(8,128)S(1)}, f32[128,1024]{1,0:T(8,128)S(1)}, f32[128,1024]{1,0:T(8,128)S(1)}) custom-call(f32[2]{0:T(128)S(1)} %pad_maximum_fusion.3.numbers, s32[2]{0:T(128)S(1)} %copy-done.30, bf16[512,1024]{1,0:T(8,128)(2,1)S(1)} %get-tuple-element.55.image_emb, f32[512,1]{1,0:T(8,128)S(1)} %copy-done.6, ...), custom_call_target="tpu_custom_call", output_to_operand_aliasing={{0}: (6, {})} | custom-call | flops 1 | bytes 1 | tf_op jit(solution)/shard_map/pallas_call | solution.py:51
  60.8 2.5 %shard_map.87 = (f32[512,1024]{1,0:T(8,128)S(1)}, bf16[128,1024]{1,0:T(8,128)(2,1)S(1)}, bf16[128,1024]{1,0:T(8,128)(2,1)S(1)}) custom-call(f32[2]{0:T(128)S(1)} %pad_maximum_fusion.3.numbers, s32[2]{0:T(128)S(1)} %pad_add_fusion.1.starts, bf16[512,1024]{1,0:T(8,128)(2,1)S(1)} %get-tuple-element.55.image_emb, ...), custom_call_target="tpu_custom_call", output_to_operand_aliasing={{0}: (6, {})} | custom-call | flops 1 | bytes 1 | tf_op jit(solution)/shard_map/pallas_call | solution.py:51
  64.7 4.1 %shard_map.88 = (f32[512,1024]{1,0:T(8,128)S(1)}, f32[512,1]{1,0:T(8,128)S(1)}, bf16[512,896]{1,0:T(8,128)(2,1)}, bf16[64,1024]{1,0:T(8,128)(2,1)S(1)}, bf16[64,1024]{1,0:T(8,128)(2,1)S(1)}) custom-call(f32[2]{0:T(128)S(1)} %pad_maximum_fusion.3.numbers, s32[2]{0:T(128)S(1)} %pad_add_fusion.starts, ...), custom_call_target="tpu_custom_call", output_to_operand_aliasing={{0}: (6, {})} | custom-call | flops 1 | bytes 1 | tf_op jit(solution)/shard_map/pallas_call | solution.py:51
  70.1 2.8 %collective-permute-start.10 = (bf16[512,896]{1,0:T(8,128)(2,1)}, bf16[512,896]{1,0:T(8,128)(2,1)S(1)}, u32[]{:S(2)}, u32[]{:S(2)}) collective-permute-start(bf16[512,896]{1,0:T(8,128)(2,1)} %get-tuple-element.31), channel_id=1, source_target_pairs={{0,8},{8,0},{16,24},{24,16},{32,40},{40,32},{48,56},{56,48},{64,72... | collective-permute-start | bytes 2752520 | tf_op jit(solution)/shard_map/ppermute | solution.py:35
  75.1 3.9 %convolution_convert_fusion.sensor_sorted = bf16[1152,512]{1,0:T(8,128)(2,1)S(1)} fusion(bf16[1152,1152]{1,0:T(8,128)(2,1)} %fusion, bf16[512,1152]{1,0:T(8,128)(2,1)} %bitcast.40), kind=kOutput, calls=%fused_computation.2 | convolution fusion | flops 1359544320 | bytes 5013504 | tf_op jit(solution)/shard_map/dot_general | solution.py:43
  84.6 4.4 %all-to-all-start = ((bf16[8,288,256]{2,1,0:T(8,128)(2,1)}), bf16[8,288,256]{2,1,0:T(8,128)(2,1)}, u32[]{:S(2)}, u32[]{:S(2)}) async-start(bf16[8,288,256]{2,1,0:T(8,128)(2,1)} %copy-done.9), calls=%async_computation | async-start | bytes 2359296 | tf_op jit(solution)/shard_map/all_to_all | solution.py:226
  93.1 2.3 %collective-permute-start.18 = (bf16[64,1024]{1,0:T(8,128)(2,1)S(1)}, bf16[64,1024]{1,0:T(8,128)(2,1)S(1)}, u32[]{:S(2)}, u32[]{:S(2)}) collective-permute-start(bf16[64,1024]{1,0:T(8,128)(2,1)S(1)} %copy-done.38), channel_id=1, source_target_pairs={{0,192},{8,200},{16,208},{24,216},{32,224},{40,232},{48,240},{56,2... | collective-permute-start | bytes 393224 | tf_op jit(solution)/shard_map/ppermute | solution.py:31
  96.8 5.5 %collective-permute-done.15 = bf16[64,1024]{1,0:T(8,128)(2,1)S(1)} collective-permute-done((bf16[64,1024]{1,0:T(8,128)(2,1)}, bf16[64,1024]{1,0:T(8,128)(2,1)S(1)}, u32[]{:S(2)}, u32[]{:S(2)}) %collective-permute-start.15) | collective-permute-done | bytes 131104 | tf_op jit(solution)/shard_map/ppermute | solution.py:31
  102.2 3.0 %collective-permute-start.12 = (bf16[128,1024]{1,0:T(8,128)(2,1)}, bf16[128,1024]{1,0:T(8,128)(2,1)}, u32[]{:S(2)}, u32[]{:S(2)}) collective-permute-start(bf16[128,1024]{1,0:T(8,128)(2,1)} %copy-done.33), channel_id=1, source_target_pairs={{0,32},{8,40},{16,48},{24,56},{32,64},{40,72},{48,80},{56,88},{64,... | collective-permute-start | bytes 786440 | tf_op jit(solution)/shard_map/ppermute | solution.py:31
  110.2 2.3 %collective-permute-start.19 = (bf16[128,1024]{1,0:T(8,128)(2,1)}, bf16[128,1024]{1,0:T(8,128)(2,1)}, u32[]{:S(2)}, u32[]{:S(2)}) collective-permute-start(bf16[128,1024]{1,0:T(8,128)(2,1)} %add_convert_fusion), channel_id=1, source_target_pairs={{0,192},{8,200},{16,208},{24,216},{32,224},{40,232},{48,240},{56,2... | collective-permute-start | bytes 786440 | tf_op jit(solution)/shard_map/ppermute | solution.py:31
  117.2 9.0 %all-to-all-start.1 = ((bf16[32,9,256]{2,1,0:T(8,128)(2,1)}), bf16[32,9,256]{2,1,0:T(8,128)(2,1)}, u32[]{:S(2)}, u32[]{:S(2)}) async-start(bf16[32,9,256]{2,1,0:T(8,128)(2,1)} %reshape.107), calls=%async_computation.1 | async-start | bytes 524288 | tf_op jit(solution)/shard_map/all_to_all | solution.py:229
  126.2 2.8 %fusion.1 = bf16[1,128,1152]{2,1,0:T(8,128)(2,1)} fusion(bf16[1152,1024]{1,0:T(8,128)(2,1)S(1)} %copy-done, f32[512,1024]{1,0:T(8,128)} %get-tuple-element.56.unit, f32[128,1024]{1,0:T(8,128)S(1)} %get-tuple-element.34, bf16[128,1024]{1,0:T(8,128)(2,1)} %copy-done.41, f32[128]{0:T(128)} %slice.32, f32[128]{0:T(128)} %multiply_reduce_fusion.1), kind=kOutput, calls=%fused_computation.4 | convolution fusion | flops 302923776 | bytes 3965952 | tf_op jit(solution)/shard_map/dot_general | solution.py:43
  130.5 8.6 %all-to-all-done.1 = bf16[32,9,256]{2,1,0:T(8,128)(2,1)} async-done(((bf16[32,9,256]{2,1,0:T(8,128)(2,1)}), bf16[32,9,256]{2,1,0:T(8,128)(2,1)}, u32[]{:S(2)}, u32[]{:S(2)}) %all-to-all-start.1) | async-done | bytes 147488 | tf_op jit(solution)/shard_map/all_to_all | solution.py:229
  140.9 4.5 %all-to-all-start.2 = ((f32[8,2,9,256]{3,1,2,0:T(2,128)}), f32[8,2,9,256]{3,1,2,0:T(2,128)S(1)}, u32[]{:S(2)}, u32[]{:S(2)}) async-start(f32[8,2,9,256]{3,1,2,0:T(2,128)} %broadcast_in_dim.8), calls=%async_computation.2 | async-start | bytes 294912 | tf_op jit(solution)/shard_map/all_to_all | solution.py:233
  146.4 4.5 %all-to-all-done.2 = f32[8,2,9,256]{3,1,2,0:T(2,128)S(1)} async-done(((f32[8,2,9,256]{3,1,2,0:T(2,128)}), f32[8,2,9,256]{3,1,2,0:T(2,128)S(1)}, u32[]{:S(2)}, u32[]{:S(2)}) %all-to-all-start.2) | async-done | bytes 147488 | tf_op jit(solution)/shard_map/all_to_all | solution.py:233
  (158 shorter events, 55.5 us)
Async XLA Ops:
  0.6 41.0 %copy-start = (bf16[1152,1024]{1,0:T(8,128)(2,1)S(1)}, bf16[1152,1024]{1,0:T(8,128)(2,1)}, u32[]{:S(2)}) copy-start(bf16[1152,1024]{1,0:T(8,128)(2,1)} %param.8) | copy-start | bytes 7077892
  3.2 17.9 %collective-permute-start = (bf16[144,1152]{1,0:T(8,128)(2,1)}, bf16[144,1152]{1,0:T(8,128)(2,1)}, u32[]{:S(2)}, u32[]{:S(2)}) collective-permute-start(bf16[144,1152]{1,0:T(8,128)(2,1)} %pad_maximum_fusion.1), channel_id=1, source_target_pairs={{0,16},{8,24},{16,0},{24,8},{32,48},{40,56},{48,32},{56,40},{64,80... | collective-permute-start | bytes 995336 | tf_op jit(solution)/shard_map/ppermute | solution.py:39
  6.9 11.5 %collective-permute-start.6 = (bf16[128,1024]{1,0:T(8,128)(2,1)}, bf16[128,1024]{1,0:T(8,128)(2,1)S(1)}, u32[]{:S(2)}, u32[]{:S(2)}) collective-permute-start(bf16[128,1024]{1,0:T(8,128)(2,1)} %bitcast.36), channel_id=1, source_target_pairs={{0,32},{8,40},{16,48},{24,56},{32,64},{40,72},{48,80},{56,88},{64,... | collective-permute-start | bytes 786440 | tf_op jit(solution)/shard_map/ppermute | solution.py:31
  8.6 9.9 %collective-permute-start.2 = (bf16[128,1024]{1,0:T(8,128)(2,1)}, bf16[128,1024]{1,0:T(8,128)(2,1)S(1)}, u32[]{:S(2)}, u32[]{:S(2)}) collective-permute-start(bf16[128,1024]{1,0:T(8,128)(2,1)} %bitcast.37), channel_id=1, source_target_pairs={{0,224},{8,232},{16,240},{24,248},{32,0},{40,8},{48,16},{56,24},{6... | collective-permute-start | bytes 786440 | tf_op jit(solution)/shard_map/ppermute | solution.py:31
  18.4 8.9 %collective-permute-start.7 = (bf16[128,1024]{1,0:T(8,128)(2,1)S(1)}, bf16[128,1024]{1,0:T(8,128)(2,1)S(1)}, u32[]{:S(2)}, u32[]{:S(2)}) collective-permute-start(bf16[128,1024]{1,0:T(8,128)(2,1)S(1)} %collective-permute-done.6.refs_2_), channel_id=1, source_target_pairs={{0,32},{8,40},{16,48},{24,56},{32,64},{40,72},{48,80},{56,88},{64,... | collective-permute-start | bytes 786440 | tf_op jit(solution)/shard_map/ppermute | solution.py:31
  18.5 8.9 %collective-permute-start.3 = (bf16[128,1024]{1,0:T(8,128)(2,1)S(1)}, bf16[128,1024]{1,0:T(8,128)(2,1)S(1)}, u32[]{:S(2)}, u32[]{:S(2)}) collective-permute-start(bf16[128,1024]{1,0:T(8,128)(2,1)S(1)} %collective-permute-done.2.refs_1_), channel_id=1, source_target_pairs={{0,224},{8,232},{16,240},{24,248},{32,0},{40,8},{48,16},{56,24},{6... | collective-permute-start | bytes 786440 | tf_op jit(solution)/shard_map/ppermute | solution.py:31
  23.1 16.4 %collective-permute-start.1 = (bf16[288,1152]{1,0:T(8,128)(2,1)}, bf16[288,1152]{1,0:T(8,128)(2,1)}, u32[]{:S(2)}, u32[]{:S(2)}) collective-permute-start(bf16[288,1152]{1,0:T(8,128)(2,1)} %pad_maximum_fusion), channel_id=1, source_target_pairs={{0,8},{8,0},{16,24},{24,16},{32,40},{40,32},{48,56},{56,48},{64,72... | collective-permute-start | bytes 1990664 | tf_op jit(solution)/shard_map/ppermute | solution.py:35
  27.3 8.1 %collective-permute-start.8 = (bf16[128,1024]{1,0:T(8,128)(2,1)S(1)}, bf16[128,1024]{1,0:T(8,128)(2,1)S(1)}, u32[]{:S(2)}, u32[]{:S(2)}) collective-permute-start(bf16[128,1024]{1,0:T(8,128)(2,1)S(1)} %collective-permute-done.7.refs_1_), channel_id=1, source_target_pairs={{0,32},{8,40},{16,48},{24,56},{32,64},{40,72},{48,80},{56,88},{64,... | collective-permute-start | bytes 786440 | tf_op jit(solution)/shard_map/ppermute | solution.py:31
  27.4 8.7 %collective-permute-start.4 = (bf16[128,1024]{1,0:T(8,128)(2,1)S(1)}, bf16[128,1024]{1,0:T(8,128)(2,1)S(1)}, u32[]{:S(2)}, u32[]{:S(2)}) collective-permute-start(bf16[128,1024]{1,0:T(8,128)(2,1)S(1)} %collective-permute-done.3.refs_0_), channel_id=1, source_target_pairs={{0,224},{8,232},{16,240},{24,248},{32,0},{40,8},{48,16},{56,24},{6... | collective-permute-start | bytes 786440 | tf_op jit(solution)/shard_map/ppermute | solution.py:31
  36.1 28.6 %collective-permute-start.9 = (bf16[64,1024]{1,0:T(8,128)(2,1)}, bf16[64,1024]{1,0:T(8,128)(2,1)S(1)}, u32[]{:S(2)}, u32[]{:S(2)}) collective-permute-start(bf16[64,1024]{1,0:T(8,128)(2,1)} %slice.38), channel_id=1, source_target_pairs={{0,32},{8,40},{16,48},{24,56},{32,64},{40,72},{48,80},{56,88},{64,... | collective-permute-start | bytes 393224 | tf_op jit(solution)/shard_map/ppermute | solution.py:31
  36.8 27.9 %collective-permute-start.5 = (bf16[64,1024]{1,0:T(8,128)(2,1)}, bf16[64,1024]{1,0:T(8,128)(2,1)}, u32[]{:S(2)}, u32[]{:S(2)}) collective-permute-start(bf16[64,1024]{1,0:T(8,128)(2,1)} %slice.37), channel_id=1, source_target_pairs={{0,224},{8,232},{16,240},{24,248},{32,0},{40,8},{48,16},{56,24},{6... | collective-permute-start | bytes 393224 | tf_op jit(solution)/shard_map/ppermute | solution.py:31
  70.1 8.9 %collective-permute-start.10 = (bf16[512,896]{1,0:T(8,128)(2,1)}, bf16[512,896]{1,0:T(8,128)(2,1)S(1)}, u32[]{:S(2)}, u32[]{:S(2)}) collective-permute-start(bf16[512,896]{1,0:T(8,128)(2,1)} %get-tuple-element.31), channel_id=1, source_target_pairs={{0,8},{8,0},{16,24},{24,16},{32,40},{40,32},{48,56},{56,48},{64,72... | collective-permute-start | bytes 2752520 | tf_op jit(solution)/shard_map/ppermute | solution.py:35
  84.6 30.4 %all-to-all-start = ((bf16[8,288,256]{2,1,0:T(8,128)(2,1)}), bf16[8,288,256]{2,1,0:T(8,128)(2,1)}, u32[]{:S(2)}, u32[]{:S(2)}) async-start(bf16[8,288,256]{2,1,0:T(8,128)(2,1)} %copy-done.9), calls=%async_computation | async-start | bytes 2359296 | tf_op jit(solution)/shard_map/all_to_all | solution.py:226
  89.0 16.3 %collective-permute-start.14 = (bf16[128,1024]{1,0:T(8,128)(2,1)}, bf16[128,1024]{1,0:T(8,128)(2,1)S(1)}, u32[]{:S(2)}, u32[]{:S(2)}) collective-permute-start(bf16[128,1024]{1,0:T(8,128)(2,1)} %copy-done.35), channel_id=1, source_target_pairs={{0,32},{8,40},{16,48},{24,56},{32,64},{40,72},{48,80},{56,88},{64,... | collective-permute-start | bytes 786440 | tf_op jit(solution)/shard_map/ppermute | solution.py:31
  89.2 13.0 %collective-permute-start.15 = (bf16[64,1024]{1,0:T(8,128)(2,1)}, bf16[64,1024]{1,0:T(8,128)(2,1)S(1)}, u32[]{:S(2)}, u32[]{:S(2)}) collective-permute-start(bf16[64,1024]{1,0:T(8,128)(2,1)} %copy-done.39), channel_id=1, source_target_pairs={{0,64},{8,72},{16,80},{24,88},{32,96},{40,104},{48,112},{56,120},{... | collective-permute-start | bytes 393224 | tf_op jit(solution)/shard_map/ppermute | solution.py:31
  90.9 17.5 %collective-permute-start.17 = (bf16[128,1024]{1,0:T(8,128)(2,1)}, bf16[128,1024]{1,0:T(8,128)(2,1)S(1)}, u32[]{:S(2)}, u32[]{:S(2)}) collective-permute-start(bf16[128,1024]{1,0:T(8,128)(2,1)} %copy-done.34), channel_id=1, source_target_pairs={{0,224},{8,232},{16,240},{24,248},{32,0},{40,8},{48,16},{56,24},{6... | collective-permute-start | bytes 786440 | tf_op jit(solution)/shard_map/ppermute | solution.py:31
  93.1 14.0 %collective-permute-start.18 = (bf16[64,1024]{1,0:T(8,128)(2,1)S(1)}, bf16[64,1024]{1,0:T(8,128)(2,1)S(1)}, u32[]{:S(2)}, u32[]{:S(2)}) collective-permute-start(bf16[64,1024]{1,0:T(8,128)(2,1)S(1)} %copy-done.38), channel_id=1, source_target_pairs={{0,192},{8,200},{16,208},{24,216},{32,224},{40,232},{48,240},{56,2... | collective-permute-start | bytes 393224 | tf_op jit(solution)/shard_map/ppermute | solution.py:31
  95.4 17.1 %collective-permute-start.11 = (bf16[128,1024]{1,0:T(8,128)(2,1)}, bf16[128,1024]{1,0:T(8,128)(2,1)S(1)}, u32[]{:S(2)}, u32[]{:S(2)}) collective-permute-start(bf16[128,1024]{1,0:T(8,128)(2,1)} %copy-done.36), channel_id=1, source_target_pairs={{0,16},{8,24},{16,0},{24,8},{32,48},{40,56},{48,32},{56,40},{64,80... | collective-permute-start | bytes 786440 | tf_op jit(solution)/shard_map/ppermute | solution.py:39
  102.2 26.8 %collective-permute-start.12 = (bf16[128,1024]{1,0:T(8,128)(2,1)}, bf16[128,1024]{1,0:T(8,128)(2,1)}, u32[]{:S(2)}, u32[]{:S(2)}) collective-permute-start(bf16[128,1024]{1,0:T(8,128)(2,1)} %copy-done.33), channel_id=1, source_target_pairs={{0,32},{8,40},{16,48},{24,56},{32,64},{40,72},{48,80},{56,88},{64,... | collective-permute-start | bytes 786440 | tf_op jit(solution)/shard_map/ppermute | solution.py:31
  105.2 23.7 %collective-permute-start.13 = (bf16[128,1024]{1,0:T(8,128)(2,1)S(1)}, bf16[128,1024]{1,0:T(8,128)(2,1)}, u32[]{:S(2)}, u32[]{:S(2)}) collective-permute-start(bf16[128,1024]{1,0:T(8,128)(2,1)S(1)} %copy-done.32), channel_id=1, source_target_pairs={{0,224},{8,232},{16,240},{24,248},{32,0},{40,8},{48,16},{56,24},{6... | collective-permute-start | bytes 786440 | tf_op jit(solution)/shard_map/ppermute | solution.py:31
  107.1 21.9 %collective-permute-start.16 = (bf16[128,1024]{1,0:T(8,128)(2,1)}, bf16[128,1024]{1,0:T(8,128)(2,1)}, u32[]{:S(2)}, u32[]{:S(2)}) collective-permute-start(bf16[128,1024]{1,0:T(8,128)(2,1)} %add_convert_fusion.1), channel_id=1, source_target_pairs={{0,64},{8,72},{16,80},{24,88},{32,96},{40,104},{48,112},{56,120},{... | collective-permute-start | bytes 786440 | tf_op jit(solution)/shard_map/ppermute | solution.py:31
  110.2 18.8 %collective-permute-start.19 = (bf16[128,1024]{1,0:T(8,128)(2,1)}, bf16[128,1024]{1,0:T(8,128)(2,1)}, u32[]{:S(2)}, u32[]{:S(2)}) collective-permute-start(bf16[128,1024]{1,0:T(8,128)(2,1)} %add_convert_fusion), channel_id=1, source_target_pairs={{0,192},{8,200},{16,208},{24,216},{32,224},{40,232},{48,240},{56,2... | collective-permute-start | bytes 786440 | tf_op jit(solution)/shard_map/ppermute | solution.py:31
  117.2 22.0 %all-to-all-start.1 = ((bf16[32,9,256]{2,1,0:T(8,128)(2,1)}), bf16[32,9,256]{2,1,0:T(8,128)(2,1)}, u32[]{:S(2)}, u32[]{:S(2)}) async-start(bf16[32,9,256]{2,1,0:T(8,128)(2,1)} %reshape.107), calls=%async_computation.1 | async-start | bytes 524288 | tf_op jit(solution)/shard_map/all_to_all | solution.py:229
  140.9 10.1 %all-to-all-start.2 = ((f32[8,2,9,256]{3,1,2,0:T(2,128)}), f32[8,2,9,256]{3,1,2,0:T(2,128)S(1)}, u32[]{:S(2)}, u32[]{:S(2)}) async-start(f32[8,2,9,256]{3,1,2,0:T(2,128)} %broadcast_in_dim.8), calls=%async_computation.2 | async-start | bytes 294912 | tf_op jit(solution)/shard_map/all_to_all | solution.py:233
  (45 other events, 189.1 us)

commit v4 on v3

--- a/solution.py
+++ b/solution.py
@@ -28,7 +28,7 @@
 
 
 def shift_z(block, distance):
-    return lax.ppermute(block, "loop", route(lambda z, y, c: (z + distance, y, c)))
+    return lax.ppermute(block, "loop", route(lambda z, y, c: (z + (1 - 2 * c) * distance, y, c)))
 
 
 def swap_core(block):
@@ -55,7 +55,7 @@
         out_specs=[VMEM] * len(out),
         input_output_aliases=aliases,
         cost_estimate=pl.CostEstimate(flops=1, bytes_accessed=1, transcendentals=0),
-        compiler_params=pltpu.CompilerParams(vmem_limit_bytes=40 << 20),
+        compiler_params=pltpu.CompilerParams(vmem_limit_bytes=20 << 20),
     )(*operands)
 
 
@@ -89,10 +89,24 @@
         text_out[n][...] = text_part[n * rows : (n + 1) * rows].astype(text_out[n].dtype)
 
 
-def last_kernel(numbers, starts, image_emb, match, low, high, acc_in, unit, acc_out, dot_out, packet, low_out, high_out):
-    image = image_emb[...]
-    text = jnp.concatenate([low[...], high[...]], 0)
-    emb, grad = block_grads(numbers, starts[0], image, match[...], text)
+def project_kernel(own, core, yh, both, proj_weight, *refs):
+    matches, (unit, emb, inv_out, match_out) = refs[:4], refs[4:]
+    rows = own.shape[0]
+    for n, sensor in enumerate((own, core, yh, both)):
+        here = slice(n * rows, (n + 1) * rows)
+        projected = jnp.dot(sensor[...], proj_weight[...], preferred_element_type=F32)
+        inv = lax.rsqrt(jnp.sum(projected * projected, -1, keepdims=True) + 1e-06)
+        scaled = projected * inv
+        unit[here, :] = scaled
+        emb[here, :] = scaled.astype(BF16)
+        inv_out[here, :] = inv
+        match = jnp.broadcast_to(matches[n][...].astype(F32), (rows, rows))
+        match_out[here, :] = match.T[:, 0:1]
+
+
+def last_kernel(numbers, starts, image_emb, match, text, acc_in, unit, acc_out, dot_out, packet, grad_out):
+    emb, grad = block_grads(numbers, starts[0], image_emb[...], match[...], text[...])
+    grad_out[...] = grad
     acc = numbers[0] * (acc_in[...] + jnp.dot(grad, emb, preferred_element_type=F32))
     acc_out[...] = acc
     dot = jnp.sum(unit[...] * acc, -1, keepdims=True)
@@ -111,13 +125,13 @@
         for n, slot in enumerate((1, 3)):
             at = (2 * side + n) * block
             packet[at : at + block, half + 128 :] = acc_out[slot * block : (slot + 1) * block, lanes].astype(BF16)
-    text_part = inner_cols(grad, image).astype(BF16)
-    middle = low.shape[0]
-    low_out[...] = text_part[:middle]
-    high_out[...] = text_part[middle:]
-
-
-def weight_kernel(starts, got, acc, dot, unit, inv, sensor_sorted, weight, row_send, row_keep):
+
+
+def last_text_kernel(grad, image_emb, out):
+    out[...] = inner_cols(grad[...], image_emb[...]).astype(out.dtype)
+
+
+def weight_kernel(starts, got, acc, dot, unit, inv, own_rows, core_rows, yh_rows, both_rows, weight, row_send, row_keep):
     rows, width = acc.shape
     half, quarter, block = width // 2, width // 4, rows // 4
     own = pl.ds(pl.multiple_of(starts[1] * half, half), half)
@@ -139,12 +153,44 @@
                 extra = got[at : at + block, half + 128 :].astype(F32)
                 target[:, lanes] = (acc[mine, lanes] + extra).astype(target.dtype)
     proj = jnp.concatenate(projs, 0)
-    chunk_rows, chunk_cols = weight.shape[1:]
-    for x in range(4):
-        left = sensor_sorted[x * chunk_rows : (x + 1) * chunk_rows, :]
-        product = jnp.dot(left, proj, preferred_element_type=F32).astype(BF16)
-        for y in range(2):
-            weight[2 * x + y] = product[:, y * chunk_cols : (y + 1) * chunk_cols]
+    sensor = jnp.concatenate([own_rows[...], core_rows[...], yh_rows[...], both_rows[...]], 0)
+    chunk = weight.shape[1]
+    for n in range(half // 128):
+        product = inner_cols(proj[:, n * 128 : (n + 1) * 128], sensor).astype(BF16)
+        for m in range(128 // chunk):
+            weight[n * (128 // chunk) + m] = product[m * chunk : (m + 1) * chunk]
+
+
+def chunk_kernel(parts, out):
+    total = parts[0].astype(F32)
+    for n in range(1, parts.shape[0]):
+        total = total + parts[n].astype(F32)
+    turned = total.T
+    count, rows, lanes = out.shape
+    for n in range(count):
+        at = 2 * rows * n
+        out[n] = jnp.concatenate([turned[at : at + rows], turned[at + rows : at + 2 * rows]], 1).astype(BF16)
+
+
+def share_kernel(parts, out):
+    for core in range(CORE):
+        total = parts[core].astype(F32)
+        for n in range(1, Z * YH):
+            total = total + parts[n * CORE + core].astype(F32)
+        total = total * (1.0 / DP)
+        for n in range(DP):
+            out[n, core] = total
+
+
+def layout_kernel(shares, out):
+    rows, lanes = shares.shape[2:]
+    cols = lanes // 2
+    for core in range(CORE):
+        for pair in range(DP // 2):
+            left, right = shares[2 * pair, core], shares[2 * pair + 1, core]
+            at = core * DP * cols + pair * lanes
+            out[:rows, at : at + lanes] = jnp.concatenate([left[:, :cols], right[:, :cols]], 1)
+            out[rows:, at : at + lanes] = jnp.concatenate([left[:, cols:], right[:, cols:]], 1)
 
 
 def on_device(sensor_feats, text_embeds, proj_weight, matches, log_scale, logit_bias):
@@ -162,33 +208,22 @@
     for k in (1, 2, 3):
         slot[k] = shift_z(slot[k - 1], -1)
         slot[-k] = shift_z(slot[1 - k], 1)
-
+    slot[4] = shift_z(slot[-3], 1)
+
+    sensor_yh = swap_yh(sensor)
+    sensors = [sensor, swap_core(sensor), sensor_yh, swap_core(sensor_yh)]
     match = matches.reshape(1, rows)
-    digits = jnp.concatenate([match // 64, match % 64], 0).astype(BF16)
-    digits = jnp.pad(digits, ((0, 14), (0, feat - rows)))
-    packet = jnp.concatenate([sensor, digits], 0)
-    packet = jnp.concatenate([packet, swap_yh(packet)], 0)
-    packets = jnp.stack([packet.reshape(2, rows + 16, feat), swap_core(packet).reshape(2, rows + 16, feat)], 1)
-    sensor_rows = packets[:, :, :rows].reshape(4 * rows, feat)
-    digits = packets[:, :, rows : rows + 2, :rows].astype(F32)
-    match_rows = (digits[:, :, 0] * 64.0 + digits[:, :, 1]).reshape(4 * rows, 1)
-
-    projected = jnp.dot(sensor_rows, proj_weight, preferred_element_type=F32)
-    image_inv = lax.rsqrt(jnp.sum(projected * projected, -1, keepdims=True) + 1e-06)
-    image_unit = projected * image_inv
-    image_emb = image_unit.astype(BF16)
-
-    per_loop = feat // LOOP
-    strip = per_loop // 4
-    place = jnp.arange(feat, dtype=jnp.int32)
-    rest = place % (feat // 4)
-    wanted = (rest // strip) * per_loop + (place // (feat // 4)) * strip + rest % strip
-    permutation = (wanted[:, None] == jnp.arange(feat, dtype=jnp.int32)[None, :]).astype(BF16)
-    permutation = lax.optimization_barrier(permutation)
-    sensor_sorted = inner_rows(permutation, sensor_rows).astype(BF16)
+    match_yh = swap_yh(match)
+    match_both = swap_core(jnp.concatenate([match, match_yh], 0))
+    match = [match, match_both[:1], match_yh, match_both[1:]]
+    shapes = [((4 * rows, width), F32), ((4 * rows, width), BF16), ((4 * rows, 1), F32), ((4 * rows, 1), F32)]
+    image_unit, image_emb, image_inv, match_rows = call(
+        project_kernel, [jax.ShapeDtypeStruct(*s) for s in shapes], {}, *sensors, proj_weight, *match
+    )
 
     def starts_of(keys):
-        return [(loop_index + k * YH * CORE) % LOOP * rows for k in keys]
+        step = (1 - 2 * core) * YH * CORE
+        return [(loop_index + k * step + LOOP) % LOOP * rows for k in keys]
 
     def pairs(keys, dtypes, acc):
         operands = [numbers, jnp.stack(starts_of(keys)), image_emb, match_rows, *(slot[k] for k in keys)]
@@ -201,49 +236,43 @@
         kernel = functools.partial(pairs_kernel, len(keys), acc is None)
         return call(kernel, out, aliases, *operands)
 
-    acc, text_0, text_1, text_m1 = pairs((0, 1, -1), (F32, BF16, BF16), None)
-    acc, text_2, text_m2 = pairs((2, -2), (F32, F32), acc)
-    half = rows // 2
-    end_low, end_high = shift_z(slot[3][:half], -1), shift_z(slot[-3][half:], 1)
+    acc, text_0, text_1, text_m1, text_2, text_m2 = pairs((0, 1, -1, 2, -2), (F32, BF16, BF16, F32, F32), None)
     acc, text_3, text_m3 = pairs((3, -3), (BF16, BF16), acc)
     starts = jnp.stack(starts_of((4,)) + [core])
-    shapes = [((4 * rows, width), F32), ((4 * rows, 1), F32), ((4 * rows, width // 8 * 7), BF16)]
-    shapes += [((half, width), BF16)] * 2
-    acc, dot, packet, text_low, text_high = call(
+    shapes = [((4 * rows, width), F32), ((4 * rows, 1), F32), ((4 * rows, width // 8 * 7), BF16), ((4 * rows, rows), BF16)]
+    acc, dot, packet, last_grad = call(
         last_kernel,
         [jax.ShapeDtypeStruct(*s) for s in shapes],
-        {6: 0},
-        numbers, starts, image_emb, match_rows, end_low, end_high, acc, image_unit,
-    )
-
-    shapes = [((DP, feat // 4, width // 4), BF16), ((rows, width), BF16), ((rows, width), F32)]
+        {5: 0},
+        numbers, starts, image_emb, match_rows, slot[4], acc, image_unit,
+    )
+    (text_4,) = call(last_text_kernel, [jax.ShapeDtypeStruct((rows, width), BF16)], {}, last_grad, image_emb)
+
+    shapes = [((DP, width // 16, feat), BF16), ((rows, width), BF16), ((rows, width), F32)]
     weight_part, row_send, row_keep = call(
         weight_kernel,
         [jax.ShapeDtypeStruct(*s) for s in shapes],
         {},
-        starts, swap_core(packet), acc, dot, image_unit, image_inv, sensor_sorted,
+        starts, swap_core(packet), acc, dot, image_unit, image_inv, *sensors,
     )
     weight_part = lax.all_to_all(weight_part, "dp", 0, 0, tiled=True)
-    weight_part = jnp.sum(weight_part.astype(F32), 0).astype(BF16)
-    weight_part = weight_part.reshape(LOOP, strip, width // 4)
+    per_loop = feat // LOOP
+    block = (per_loop // 2, width // 8)
+    (weight_part,) = call(chunk_kernel, [jax.ShapeDtypeStruct((LOOP,) + block, BF16)], {}, weight_part)
+    text_2, text_m2, weight_part = lax.optimization_barrier((text_2, text_m2, weight_part))
     weight_part = lax.all_to_all(weight_part, "loop", 0, 0, tiled=True)
-    weight_part = jnp.sum(weight_part.reshape(Z * YH, CORE, strip, width // 4).astype(F32), 0)
-    weight_part = weight_part * (1.0 / DP)
-    shares = jnp.broadcast_to(weight_part[None], (DP,) + weight_part.shape)
+    (shares,) = call(share_kernel, [jax.ShapeDtypeStruct((DP, CORE) + block, F32)], {}, weight_part)
     shares = lax.all_to_all(shares, "dp", 0, 0, tiled=True)
-    shares = shares.reshape(4, 2, CORE, strip, width // 4).transpose(0, 3, 2, 1, 4)
-    weight_grad = shares.reshape(per_loop, width)
-
-    text_3, text_m3, text_low, text_high, text_1, text_m1, row_send = lax.optimization_barrier(
-        (text_3, text_m3, text_low, text_high, text_1, text_m1, row_send)
+    (weight_grad,) = call(layout_kernel, [jax.ShapeDtypeStruct((per_loop, width), F32)], {}, shares)
+
+    text_3, text_m3, text_4, text_1, text_m1, row_send = lax.optimization_barrier(
+        (text_3, text_m3, text_4, text_1, text_m1, row_send)
     )
     row_got = swap_yh(row_send)
-    from_below, from_above = shift_z(text_3, 1), shift_z(text_m3, -1)
-    far_below, far_above = shift_z(text_low, 2), shift_z(text_high, -2)
+    from_below, from_above, far = shift_z(text_3, 1), shift_z(text_m3, -1), shift_z(text_4, 2)
     near_below, near_above = shift_z(text_1, 1), shift_z(text_m1, -1)
-    nil = jnp.zeros((half, width), F32)
-    up = text_2 + from_below.astype(F32) + jnp.concatenate([far_below.astype(F32), nil], 0)
-    down = text_m2 + from_above.astype(F32) + jnp.concatenate([nil, far_above.astype(F32)], 0)
+    up = text_2 + from_below.astype(F32) + far.astype(F32)
+    down = text_m2 + from_above.astype(F32)
     up, down = shift_z(up.astype(BF16), 2), shift_z(down.astype(BF16), -2)
     text_sum = text_0 + near_below.astype(F32) + near_above.astype(F32)
     text_sum = logit_scale * (text_sum + up.astype(F32) + down.astype(F32))

time: 153 us -> 134 us (0.88)
  other arithmetic: 23.3 us -> 7.47 us
  Pallas kernels: 13.6 us -> 18.7 us
  matrix products: 8.38 us -> 3.38 us
  local copies, waits for them, and re-layouts: 21.7 us -> 18.6 us
  starting transfers between devices: 53.4 us -> 51.1 us
  waiting for transfers between devices: 29 us -> 31.1 us
    ppermute x2 -> x3, waiting for transfers between devices: 0.01 us -> 11 us  [swap_yh(): return lax.ppermute(block, 'loop', route(lambda z, y, c: (z, 1 - y, c)))]
    ppermute x16 -> x14, waiting for transfers between devices: 15.9 us -> 8.73 us  [shift_z(): lax.ppermute(block, 'loop', route(lambda z, y, c: (z + (1 - 2 * c) * dist...]
    pallas_call x5 -> x9, Pallas kernels: 13.6 us -> 18.7 us  [call(): pl.pallas_call(kernel, out_shape=out, in_specs=[SMEM if o.ndim == 1 else...]
    ppermute x2 -> x4, starting transfers between devices: 4.88 us -> 0.35 us  [swap_core(): return lax.ppermute(block, 'loop', route(lambda z, y, c: (z, y, 1 - c)))]
    all_to_all x1, waiting for transfers between devices: 8.61 us -> 4.3 us  [on_device(): weight_part = lax.all_to_all(weight_part, 'loop', 0, 0, tiled=True)]
    convert_element_type x3 -> x0, other arithmetic: 4.28 us -> none  [the longest x1 1.99 us: on_device(): (wanted[:, None] == jnp.arange(feat, dtype=jnp.int32)[None, :]).astype(BF16)]
    dot_general x2 -> x1, matrix products: 6.74 us -> 3.38 us  [inner_rows(): lax.dot_general(left, right, (((1,), (1,)), ((), ())), preferred_element_...]
    ppermute x2 -> x4, waiting for transfers between devices: 0.01 us -> 3.29 us  [swap_core(): return lax.ppermute(block, 'loop', route(lambda z, y, c: (z, y, 1 - c)))]
  transfers between devices with their start and end apart: 23 -> 24, of which waited for: 5 -> 9; matrix products, arithmetic and copies ran while one was open for 21% -> 9% of each run, Pallas kernels for 5% -> 10%
where the time goes in v4:
time: 134 us; the launch traced here: 133 us
  starting transfers between devices  51.1 us (38%)
  waiting for transfers between devices  31.1 us (23%)
  Pallas kernels  18.7 us (14%)
  local copies, waits for them, and re-layouts  18.6 us (14%)
  other arithmetic  7.47 us (6%)
  matrix products  3.38 us (3%)
  between operations  2.28 us (2%)
    ppermute x14, starting transfers between devices, shift_z(): lax.ppermute(block, 'loop', route(lambda z, y, c: (z + (1 - 2 * c) * dist...  26.4 us
    pallas_call x9, Pallas kernels, call(): pl.pallas_call(kernel, out_shape=out, in_specs=[SMEM if o.ndim == 1 else...  18.7 us
    unnamed x70, local copies, waits for them, and re-layouts  16.8 us
    ppermute x3, waiting for transfers between devices, swap_yh(): return lax.ppermute(block, 'loop', route(lambda z, y, c: (z, 1 - y, c)))  11 us
    ppermute x14, waiting for transfers between devices, shift_z(): lax.ppermute(block, 'loop', route(lambda z, y, c: (z + (1 - 2 * c) * dist...  8.73 us
    all_to_all x1, starting transfers between devices, on_device(): weight_part = lax.all_to_all(weight_part, 'loop', 0, 0, tiled=True)  8.52 us
    ppermute x3, starting transfers between devices, swap_yh(): return lax.ppermute(block, 'loop', route(lambda z, y, c: (z, 1 - y, c)))  5.59 us
    all_to_all x1, starting transfers between devices, on_device(): shares = lax.all_to_all(shares, 'dp', 0, 0, tiled=True)  5.14 us
  transfers between devices with their start and end apart: 24, of which 9 were waited for; matrix products, arithmetic and copies ran while one was open for 9% of the time, Pallas kernels for 10%

profile of v4, /device:TPU:1, one launch (start us, length us, event | category | flops | bytes accessed | tf_op | source)
XLA Modules:
  0.0 132.6 jit_solution(5450425209752357807)
XLA Ops:
  0.6 6.5 %collective-permute-start.5 = (bf16[128,1024]{1,0:T(8,128)(2,1)}, bf16[128,1024]{1,0:T(8,128)(2,1)S(1)}, u32[]{:S(2)}, u32[]{:S(2)}) collective-permute-start(bf16[128,1024]{1,0:T(8,128)(2,1)} %bitcast.22), channel_id=1, source_target_pairs={{0,32},{8,232},{16,48},{24,248},{32,64},{40,8},{48,80},{56,24},{64... | collective-permute-start | bytes 786440 | tf_op jit(solution)/shard_map/ppermute | solution.py:31
  7.1 5.2 %collective-permute-done.5.refs_2_ = bf16[128,1024]{1,0:T(8,128)(2,1)S(1)} collective-permute-done((bf16[128,1024]{1,0:T(8,128)(2,1)}, bf16[128,1024]{1,0:T(8,128)(2,1)S(1)}, u32[]{:S(2)}, u32[]{:S(2)}) %collective-permute-start.5) | collective-permute-done | bytes 262176 | tf_op jit(solution)/shard_map/ppermute | solution.py:31
  12.3 3.3 %collective-permute-start.6 = (bf16[128,1024]{1,0:T(8,128)(2,1)S(1)}, bf16[128,1024]{1,0:T(8,128)(2,1)S(1)}, u32[]{:S(2)}, u32[]{:S(2)}) collective-permute-start(bf16[128,1024]{1,0:T(8,128)(2,1)S(1)} %collective-permute-done.5.refs_2_), channel_id=1, source_target_pairs={{0,32},{8,232},{16,48},{24,248},{32,64},{40,8},{48,80},{56,24},{64... | collective-permute-start | bytes 786440 | tf_op jit(solution)/shard_map/ppermute | solution.py:31
  16.3 2.9 %collective-permute-start.1 = (bf16[128,1152]{1,0:T(8,128)(2,1)}, bf16[128,1152]{1,0:T(8,128)(2,1)S(1)}, u32[]{:S(2)}, u32[]{:S(2)}) collective-permute-start(bf16[128,1152]{1,0:T(8,128)(2,1)} %bitcast.25), channel_id=1, source_target_pairs={{0,16},{8,24},{16,0},{24,8},{32,48},{40,56},{48,32},{56,40},{64,80... | collective-permute-start | bytes 884744 | tf_op jit(solution)/shard_map/ppermute | solution.py:39
  21.4 2.7 %collective-permute-start.7 = (bf16[128,1024]{1,0:T(8,128)(2,1)S(1)}, bf16[128,1024]{1,0:T(8,128)(2,1)}, u32[]{:S(2)}, u32[]{:S(2)}) collective-permute-start(bf16[128,1024]{1,0:T(8,128)(2,1)S(1)} %collective-permute-done.6.refs_4_), channel_id=1, source_target_pairs={{0,32},{8,232},{16,48},{24,248},{32,64},{40,8},{48,80},{56,24},{64... | collective-permute-start | bytes 786440 | tf_op jit(solution)/shard_map/ppermute | solution.py:31
  27.3 2.2 %collective-permute-done.7.refs_1_ = bf16[128,1024]{1,0:T(8,128)(2,1)} collective-permute-done((bf16[128,1024]{1,0:T(8,128)(2,1)S(1)}, bf16[128,1024]{1,0:T(8,128)(2,1)}, u32[]{:S(2)}, u32[]{:S(2)}) %collective-permute-start.7) | collective-permute-done | bytes 262176 | tf_op jit(solution)/shard_map/ppermute | solution.py:31
  29.4 2.8 %collective-permute-start.8 = (bf16[128,1024]{1,0:T(8,128)(2,1)}, bf16[128,1024]{1,0:T(8,128)(2,1)}, u32[]{:S(2)}, u32[]{:S(2)}) collective-permute-start(bf16[128,1024]{1,0:T(8,128)(2,1)} %collective-permute-done.7.refs_1_), channel_id=1, source_target_pairs={{0,32},{8,232},{16,48},{24,248},{32,64},{40,8},{48,80},{56,24},{64... | collective-permute-start | bytes 786440 | tf_op jit(solution)/shard_map/ppermute | solution.py:31
  43.4 4.8 %shard_map.86 = (f32[512,1024]{1,0:T(8,128)S(1)}, f32[128,1024]{1,0:T(8,128)S(1)}, bf16[128,1024]{1,0:T(8,128)(2,1)S(1)}, bf16[128,1024]{1,0:T(8,128)(2,1)S(1)},...) custom-call(f32[2]{0:T(128)S(1)} %pad_maximum_fusion.numbers, s32[5]{0:T(128)S(1)} %stack.59.starts, ...), custom_call_target="tpu_custom_call" | custom-call | flops 1 | bytes 1 | tf_op jit(solution)/shard_map/pallas_call | solution.py:51
  50.0 3.0 %shard_map.87 = (f32[512,1024]{1,0:T(8,128)S(1)}, bf16[128,1024]{1,0:T(8,128)(2,1)S(1)}, bf16[128,1024]{1,0:T(8,128)(2,1)S(1)}) custom-call(f32[2]{0:T(128)S(1)} %pad_maximum_fusion.numbers, s32[2]{0:T(128)S(1)} %pad_add_fusion.2.starts, bf16[512,1024]{1,0:T(8,128)(2,1)S(1)} %get-tuple-element.32.image_emb, ...), custom_call_target="tpu_custom_call", output_to_operand_aliasing={{0}: (6, {})} | custom-call | flops 1 | bytes 1 | tf_op jit(solution)/shard_map/pallas_call | solution.py:51
  54.5 3.2 %shard_map.88 = (f32[512,1024]{1,0:T(8,128)S(1)}, f32[512,1]{1,0:T(8,128)S(1)}, bf16[512,896]{1,0:T(8,128)(2,1)S(1)}, bf16[512,128]{1,0:T(8,128)(2,1)S(1)}) custom-call(f32[2]{0:T(128)S(1)} %pad_maximum_fusion.numbers, s32[2]{0:T(128)S(1)} %pad_add_fusion.1.starts, ...), custom_call_target="tpu_custom_call", output_to_operand_aliasing={{0}: (5, {})} | custom-call | flops 1 | bytes 1 | tf_op jit(solution)/shard_map/pallas_call | solution.py:51
  58.0 2.3 %collective-permute-done.12.got = bf16[512,896]{1,0:T(8,128)(2,1)S(1)} collective-permute-done((bf16[512,896]{1,0:T(8,128)(2,1)S(1)}, bf16[512,896]{1,0:T(8,128)(2,1)S(1)}, u32[]{:S(2)}, u32[]{:S(2)}) %collective-permute-start.12) | collective-permute-done | bytes 917536 | tf_op jit(solution)/shard_map/ppermute | solution.py:35
  64.6 5.0 %all-to-all-start = ((bf16[8,64,1152]{2,1,0:T(8,128)(2,1)}), bf16[8,64,1152]{2,1,0:T(8,128)(2,1)}, u32[]{:S(2)}, u32[]{:S(2)}) async-start(bf16[8,64,1152]{2,1,0:T(8,128)(2,1)} %copy-done.5), calls=%async_computation | async-start | bytes 2359296 | tf_op jit(solution)/shard_map/all_to_all | solution.py:258
  70.9 2.6 %collective-permute-start.13 = (bf16[128,1024]{1,0:T(8,128)(2,1)}, bf16[128,1024]{1,0:T(8,128)(2,1)S(1)}, u32[]{:S(2)}, u32[]{:S(2)}) collective-permute-start(bf16[128,1024]{1,0:T(8,128)(2,1)} %copy-done.33), channel_id=1, source_target_pairs={{0,16},{8,24},{16,0},{24,8},{32,48},{40,56},{48,32},{56,40},{64,80... | collective-permute-start | bytes 786440 | tf_op jit(solution)/shard_map/ppermute | solution.py:39
  73.5 2.4 %collective-permute-start.16 = (bf16[128,1024]{1,0:T(8,128)(2,1)}, bf16[128,1024]{1,0:T(8,128)(2,1)}, u32[]{:S(2)}, u32[]{:S(2)}) collective-permute-start(bf16[128,1024]{1,0:T(8,128)(2,1)} %copy-done.32), channel_id=1, source_target_pairs={{0,32},{8,232},{16,48},{24,248},{32,64},{40,8},{48,80},{56,24},{64... | collective-permute-start | bytes 786440 | tf_op jit(solution)/shard_map/ppermute | solution.py:31
  78.6 1.9 %collective-permute-start.14 = (bf16[128,1024]{1,0:T(8,128)(2,1)}, bf16[128,1024]{1,0:T(8,128)(2,1)}, u32[]{:S(2)}, u32[]{:S(2)}) collective-permute-start(bf16[128,1024]{1,0:T(8,128)(2,1)} %copy-done.30), channel_id=1, source_target_pairs={{0,32},{8,232},{16,48},{24,248},{32,64},{40,8},{48,80},{56,24},{64... | collective-permute-start | bytes 786440 | tf_op jit(solution)/shard_map/ppermute | solution.py:31
  80.5 10.9 %collective-permute-done.13 = bf16[128,1024]{1,0:T(8,128)(2,1)S(1)} collective-permute-done((bf16[128,1024]{1,0:T(8,128)(2,1)}, bf16[128,1024]{1,0:T(8,128)(2,1)S(1)}, u32[]{:S(2)}, u32[]{:S(2)}) %collective-permute-start.13) | collective-permute-done | bytes 262176 | tf_op jit(solution)/shard_map/ppermute | solution.py:39
  92.3 2.4 %shard_map.91 = bf16[32,18,128]{2,1,0:T(8,128)(2,1)} custom-call(bf16[8,64,1152]{2,1,0:T(8,128)(2,1)} %all-to-all-done.parts), custom_call_target="tpu_custom_call" | custom-call | flops 1 | bytes 1 | tf_op jit(solution)/shard_map/pallas_call | solution.py:51
  96.5 2.7 %collective-permute-start.18 = (bf16[128,1024]{1,0:T(8,128)(2,1)}, bf16[128,1024]{1,0:T(8,128)(2,1)S(1)}, u32[]{:S(2)}, u32[]{:S(2)}) collective-permute-start(bf16[128,1024]{1,0:T(8,128)(2,1)} %add_convert_fusion.1), channel_id=1, source_target_pairs={{0,64},{8,200},{16,80},{24,216},{32,96},{40,232},{48,112},{56,248}... | collective-permute-start | bytes 786440 | tf_op jit(solution)/shard_map/ppermute | solution.py:31
  99.2 8.5 %all-to-all-start.1 = ((bf16[32,18,128]{2,1,0:T(8,128)(2,1)}), bf16[32,18,128]{2,1,0:T(8,128)(2,1)S(1)}, u32[]{:S(2)}, u32[]{:S(2)}) async-start(bf16[32,18,128]{2,1,0:T(8,128)(2,1)} %shard_map.91), calls=%async_computation.1 | async-start | bytes 393216 | tf_op jit(solution)/shard_map/all_to_all | solution.py:263
  109.6 2.3 %collective-permute-start.20 = (bf16[128,1024]{1,0:T(8,128)(2,1)}, bf16[128,1024]{1,0:T(8,128)(2,1)}, u32[]{:S(2)}, u32[]{:S(2)}) collective-permute-start(bf16[128,1024]{1,0:T(8,128)(2,1)} %add_convert_fusion), channel_id=1, source_target_pairs={{0,192},{8,72},{16,208},{24,88},{32,224},{40,104},{48,240},{56,120... | collective-permute-start | bytes 786440 | tf_op jit(solution)/shard_map/ppermute | solution.py:31
  111.9 3.4 %fusion = bf16[1,128,1152]{2,1,0:T(8,128)(2,1)} fusion(bf16[1152,1024]{1,0:T(8,128)(2,1)} %proj_weight.1, f32[512,1024]{1,0:T(8,128)S(1)} %get-tuple-element.36.unit, f32[128,1024]{1,0:T(8,128)S(1)} %copy-done.4, bf16[128,1024]{1,0:T(8,128)(2,1)} %copy-done.34, f32[128]{0:T(128)S(1)} %slice_reduce_fusion, f32[128]{0:T(128)S(1)} %multiply_reduce_fusion), kind=kOutput, calls=%fused_computation.1 | convolution fusion | flops 302923776 | bytes 3965952 | tf_op jit(solution)/shard_map/dot_general | solution.py:43
  115.3 4.3 %all-to-all-done.1.parts = bf16[32,18,128]{2,1,0:T(8,128)(2,1)S(1)} async-done(((bf16[32,18,128]{2,1,0:T(8,128)(2,1)}), bf16[32,18,128]{2,1,0:T(8,128)(2,1)S(1)}, u32[]{:S(2)}, u32[]{:S(2)}) %all-to-all-start.1) | async-done | bytes 147488 | tf_op jit(solution)/shard_map/all_to_all | solution.py:263
  120.4 5.1 %all-to-all-start.2 = ((f32[8,2,18,128]{3,1,2,0:T(2,128)}), f32[8,2,18,128]{3,1,2,0:T(2,128)S(1)}, u32[]{:S(2)}, u32[]{:S(2)}) async-start(f32[8,2,18,128]{3,1,2,0:T(2,128)} %copy.11), calls=%async_computation.2 | async-start | bytes 294912 | tf_op jit(solution)/shard_map/all_to_all | solution.py:265
  127.1 3.7 %all-to-all-done.2 = f32[8,2,18,128]{3,1,2,0:T(2,128)S(1)} async-done(((f32[8,2,18,128]{3,1,2,0:T(2,128)}), f32[8,2,18,128]{3,1,2,0:T(2,128)S(1)}, u32[]{:S(2)}, u32[]{:S(2)}) %all-to-all-start.2) | async-done | bytes 147488 | tf_op jit(solution)/shard_map/all_to_all | solution.py:265
  (120 shorter events, 36.3 us)
Async XLA Ops:
  0.6 11.7 %collective-permute-start.5 = (bf16[128,1024]{1,0:T(8,128)(2,1)}, bf16[128,1024]{1,0:T(8,128)(2,1)S(1)}, u32[]{:S(2)}, u32[]{:S(2)}) collective-permute-start(bf16[128,1024]{1,0:T(8,128)(2,1)} %bitcast.22), channel_id=1, source_target_pairs={{0,32},{8,232},{16,48},{24,248},{32,64},{40,8},{48,80},{56,24},{64... | collective-permute-start | bytes 786440 | tf_op jit(solution)/shard_map/ppermute | solution.py:31
  7.1 13.5 %collective-permute-start.9 = (bf16[128,1024]{1,0:T(8,128)(2,1)}, bf16[128,1024]{1,0:T(8,128)(2,1)S(1)}, u32[]{:S(2)}, u32[]{:S(2)}) collective-permute-start(bf16[128,1024]{1,0:T(8,128)(2,1)} %bitcast.23), channel_id=1, source_target_pairs={{0,224},{8,40},{16,240},{24,56},{32,0},{40,72},{48,16},{56,88},{64... | collective-permute-start | bytes 786440 | tf_op jit(solution)/shard_map/ppermute | solution.py:31
  12.3 9.1 %collective-permute-start.6 = (bf16[128,1024]{1,0:T(8,128)(2,1)S(1)}, bf16[128,1024]{1,0:T(8,128)(2,1)S(1)}, u32[]{:S(2)}, u32[]{:S(2)}) collective-permute-start(bf16[128,1024]{1,0:T(8,128)(2,1)S(1)} %collective-permute-done.5.refs_2_), channel_id=1, source_target_pairs={{0,32},{8,232},{16,48},{24,248},{32,64},{40,8},{48,80},{56,24},{64... | collective-permute-start | bytes 786440 | tf_op jit(solution)/shard_map/ppermute | solution.py:31
  16.3 8.9 %collective-permute-start.1 = (bf16[128,1152]{1,0:T(8,128)(2,1)}, bf16[128,1152]{1,0:T(8,128)(2,1)S(1)}, u32[]{:S(2)}, u32[]{:S(2)}) collective-permute-start(bf16[128,1152]{1,0:T(8,128)(2,1)} %bitcast.25), channel_id=1, source_target_pairs={{0,16},{8,24},{16,0},{24,8},{32,48},{40,56},{48,32},{56,40},{64,80... | collective-permute-start | bytes 884744 | tf_op jit(solution)/shard_map/ppermute | solution.py:39
  19.2 14.8 %collective-permute-start = (bf16[128,1152]{1,0:T(8,128)(2,1)}, bf16[128,1152]{1,0:T(8,128)(2,1)S(1)}, u32[]{:S(2)}, u32[]{:S(2)}) collective-permute-start(bf16[128,1152]{1,0:T(8,128)(2,1)} %bitcast.26), channel_id=1, source_target_pairs={{0,8},{8,0},{16,24},{24,16},{32,40},{40,32},{48,56},{56,48},{64,72... | collective-permute-start | bytes 884744 | tf_op jit(solution)/shard_map/ppermute | solution.py:35
  19.2 13.0 %collective-permute-start.3 = (s32[1,128]{1,0:T(1,128)}, s32[1,128]{1,0:T(1,128)S(1)}, u32[]{:S(2)}, u32[]{:S(2)}) collective-permute-start(s32[1,128]{1,0:T(1,128)} %refs_0_.1), channel_id=1, source_target_pairs={{0,16},{8,24},{16,0},{24,8},{32,48},{40,56},{48,32},{56,40},{64,80... | collective-permute-start | bytes 1544 | tf_op jit(solution)/shard_map/ppermute | solution.py:39
  20.6 6.6 %collective-permute-start.10 = (bf16[128,1024]{1,0:T(8,128)(2,1)S(1)}, bf16[128,1024]{1,0:T(8,128)(2,1)}, u32[]{:S(2)}, u32[]{:S(2)}) collective-permute-start(bf16[128,1024]{1,0:T(8,128)(2,1)S(1)} %collective-permute-done.9.refs_1_), channel_id=1, source_target_pairs={{0,224},{8,40},{16,240},{24,56},{32,0},{40,72},{48,16},{56,88},{64... | collective-permute-start | bytes 786440 | tf_op jit(solution)/shard_map/ppermute | solution.py:31
  21.4 8.0 %collective-permute-start.7 = (bf16[128,1024]{1,0:T(8,128)(2,1)S(1)}, bf16[128,1024]{1,0:T(8,128)(2,1)}, u32[]{:S(2)}, u32[]{:S(2)}) collective-permute-start(bf16[128,1024]{1,0:T(8,128)(2,1)S(1)} %collective-permute-done.6.refs_4_), channel_id=1, source_target_pairs={{0,32},{8,232},{16,48},{24,248},{32,64},{40,8},{48,80},{56,24},{64... | collective-permute-start | bytes 786440 | tf_op jit(solution)/shard_map/ppermute | solution.py:31
  25.2 9.6 %collective-permute-start.2 = (bf16[128,1152]{1,0:T(8,128)(2,1)S(1)}, bf16[128,1152]{1,0:T(8,128)(2,1)S(1)}, u32[]{:S(2)}, u32[]{:S(2)}) collective-permute-start(bf16[128,1152]{1,0:T(8,128)(2,1)S(1)} %collective-permute-done.1.yh.yh_rows), channel_id=1, source_target_pairs={{0,8},{8,0},{16,24},{24,16},{32,40},{40,32},{48,56},{56,48},{64,72... | collective-permute-start | bytes 884744 | tf_op jit(solution)/shard_map/ppermute | solution.py:35
  27.3 21.8 %collective-permute-start.11 = (bf16[128,1024]{1,0:T(8,128)(2,1)}, bf16[128,1024]{1,0:T(8,128)(2,1)}, u32[]{:S(2)}, u32[]{:S(2)}) collective-permute-start(bf16[128,1024]{1,0:T(8,128)(2,1)} %collective-permute-done.10.refs_3_), channel_id=1, source_target_pairs={{0,224},{8,40},{16,240},{24,56},{32,0},{40,72},{48,16},{56,88},{64... | collective-permute-start | bytes 786440 | tf_op jit(solution)/shard_map/ppermute | solution.py:31
  29.4 25.0 %collective-permute-start.8 = (bf16[128,1024]{1,0:T(8,128)(2,1)}, bf16[128,1024]{1,0:T(8,128)(2,1)}, u32[]{:S(2)}, u32[]{:S(2)}) collective-permute-start(bf16[128,1024]{1,0:T(8,128)(2,1)} %collective-permute-done.7.refs_1_), channel_id=1, source_target_pairs={{0,32},{8,232},{16,48},{24,248},{32,64},{40,8},{48,80},{56,24},{64... | collective-permute-start | bytes 786440 | tf_op jit(solution)/shard_map/ppermute | solution.py:31
  32.9 1.1 collective-permute-start.4
  57.7 2.6 %collective-permute-start.12 = (bf16[512,896]{1,0:T(8,128)(2,1)S(1)}, bf16[512,896]{1,0:T(8,128)(2,1)S(1)}, u32[]{:S(2)}, u32[]{:S(2)}) collective-permute-start(bf16[512,896]{1,0:T(8,128)(2,1)S(1)} %get-tuple-element.37), channel_id=1, source_target_pairs={{0,8},{8,0},{16,24},{24,16},{32,40},{40,32},{48,56},{56,48},{64,72... | collective-permute-start | bytes 2752520 | tf_op jit(solution)/shard_map/ppermute | solution.py:35
  64.6 27.6 %all-to-all-start = ((bf16[8,64,1152]{2,1,0:T(8,128)(2,1)}), bf16[8,64,1152]{2,1,0:T(8,128)(2,1)}, u32[]{:S(2)}, u32[]{:S(2)}) async-start(bf16[8,64,1152]{2,1,0:T(8,128)(2,1)} %copy-done.5), calls=%async_computation | async-start | bytes 2359296 | tf_op jit(solution)/shard_map/all_to_all | solution.py:258
  70.9 20.6 %collective-permute-start.13 = (bf16[128,1024]{1,0:T(8,128)(2,1)}, bf16[128,1024]{1,0:T(8,128)(2,1)S(1)}, u32[]{:S(2)}, u32[]{:S(2)}) collective-permute-start(bf16[128,1024]{1,0:T(8,128)(2,1)} %copy-done.33), channel_id=1, source_target_pairs={{0,16},{8,24},{16,0},{24,8},{32,48},{40,56},{48,32},{56,40},{64,80... | collective-permute-start | bytes 786440 | tf_op jit(solution)/shard_map/ppermute | solution.py:39
  73.5 21.2 %collective-permute-start.16 = (bf16[128,1024]{1,0:T(8,128)(2,1)}, bf16[128,1024]{1,0:T(8,128)(2,1)}, u32[]{:S(2)}, u32[]{:S(2)}) collective-permute-start(bf16[128,1024]{1,0:T(8,128)(2,1)} %copy-done.32), channel_id=1, source_target_pairs={{0,32},{8,232},{16,48},{24,248},{32,64},{40,8},{48,80},{56,24},{64... | collective-permute-start | bytes 786440 | tf_op jit(solution)/shard_map/ppermute | solution.py:31
  75.9 18.8 %collective-permute-start.17 = (bf16[128,1024]{1,0:T(8,128)(2,1)}, bf16[128,1024]{1,0:T(8,128)(2,1)}, u32[]{:S(2)}, u32[]{:S(2)}) collective-permute-start(bf16[128,1024]{1,0:T(8,128)(2,1)} %shard_map.90), channel_id=1, source_target_pairs={{0,64},{8,200},{16,80},{24,216},{32,96},{40,232},{48,112},{56,248}... | collective-permute-start | bytes 786440 | tf_op jit(solution)/shard_map/ppermute | solution.py:31
  77.1 30.6 %collective-permute-start.19 = (bf16[128,1024]{1,0:T(8,128)(2,1)}, bf16[128,1024]{1,0:T(8,128)(2,1)}, u32[]{:S(2)}, u32[]{:S(2)}) collective-permute-start(bf16[128,1024]{1,0:T(8,128)(2,1)} %copy-done.31), channel_id=1, source_target_pairs={{0,224},{8,40},{16,240},{24,56},{32,0},{40,72},{48,16},{56,88},{64... | collective-permute-start | bytes 786440 | tf_op jit(solution)/shard_map/ppermute | solution.py:31
  78.6 46.9 %collective-permute-start.14 = (bf16[128,1024]{1,0:T(8,128)(2,1)}, bf16[128,1024]{1,0:T(8,128)(2,1)}, u32[]{:S(2)}, u32[]{:S(2)}) collective-permute-start(bf16[128,1024]{1,0:T(8,128)(2,1)} %copy-done.30), channel_id=1, source_target_pairs={{0,32},{8,232},{16,48},{24,248},{32,64},{40,8},{48,80},{56,24},{64... | collective-permute-start | bytes 786440 | tf_op jit(solution)/shard_map/ppermute | solution.py:31
  91.4 34.1 %collective-permute-start.15 = (bf16[128,1024]{1,0:T(8,128)(2,1)}, bf16[128,1024]{1,0:T(8,128)(2,1)}, u32[]{:S(2)}, u32[]{:S(2)}) collective-permute-start(bf16[128,1024]{1,0:T(8,128)(2,1)} %copy-done.29), channel_id=1, source_target_pairs={{0,224},{8,40},{16,240},{24,56},{32,0},{40,72},{48,16},{56,88},{64... | collective-permute-start | bytes 786440 | tf_op jit(solution)/shard_map/ppermute | solution.py:31
  96.5 29.0 %collective-permute-start.18 = (bf16[128,1024]{1,0:T(8,128)(2,1)}, bf16[128,1024]{1,0:T(8,128)(2,1)S(1)}, u32[]{:S(2)}, u32[]{:S(2)}) collective-permute-start(bf16[128,1024]{1,0:T(8,128)(2,1)} %add_convert_fusion.1), channel_id=1, source_target_pairs={{0,64},{8,200},{16,80},{24,216},{32,96},{40,232},{48,112},{56,248}... | collective-permute-start | bytes 786440 | tf_op jit(solution)/shard_map/ppermute | solution.py:31
  99.2 20.4 %all-to-all-start.1 = ((bf16[32,18,128]{2,1,0:T(8,128)(2,1)}), bf16[32,18,128]{2,1,0:T(8,128)(2,1)S(1)}, u32[]{:S(2)}, u32[]{:S(2)}) async-start(bf16[32,18,128]{2,1,0:T(8,128)(2,1)} %shard_map.91), calls=%async_computation.1 | async-start | bytes 393216 | tf_op jit(solution)/shard_map/all_to_all | solution.py:263
  109.6 15.9 %collective-permute-start.20 = (bf16[128,1024]{1,0:T(8,128)(2,1)}, bf16[128,1024]{1,0:T(8,128)(2,1)}, u32[]{:S(2)}, u32[]{:S(2)}) collective-permute-start(bf16[128,1024]{1,0:T(8,128)(2,1)} %add_convert_fusion), channel_id=1, source_target_pairs={{0,192},{8,72},{16,208},{24,88},{32,224},{40,104},{48,240},{56,120... | collective-permute-start | bytes 786440 | tf_op jit(solution)/shard_map/ppermute | solution.py:31
  120.4 10.5 %all-to-all-start.2 = ((f32[8,2,18,128]{3,1,2,0:T(2,128)}), f32[8,2,18,128]{3,1,2,0:T(2,128)S(1)}, u32[]{:S(2)}, u32[]{:S(2)}) async-start(f32[8,2,18,128]{3,1,2,0:T(2,128)} %copy.11), calls=%async_computation.2 | async-start | bytes 294912 | tf_op jit(solution)/shard_map/all_to_all | solution.py:265
  (35 other events, 182.6 us)

commit v5 on v4

--- a/solution.py
+++ b/solution.py
@@ -13,6 +13,7 @@
 BF16 = jnp.bfloat16
 F32 = jnp.float32
 VMEM = pl.BlockSpec(memory_space=pltpu.VMEM)
+HBM = pl.BlockSpec(memory_space=pltpu.HBM)
 SMEM = pl.BlockSpec(memory_space=pltpu.SMEM)
 
 
@@ -47,12 +48,45 @@
     return lax.dot_general(left, right, (((0,), (0,)), ((), ())), preferred_element_type=F32)
 
 
-def call(kernel, out, aliases, *operands):
+def call(kernel, out, aliases, *operands, far=(), late=(), far_out=()):
+    far, far_out, total = list(far), list(far_out), len(operands)
+
+    def body(*refs):
+        ins, outs, scratch = refs[:total], refs[total : total + len(out)], refs[total + len(out) :]
+        held, held_out = scratch[: len(far)], scratch[len(far) : len(far) + len(far_out)]
+        sems = scratch[len(far) + len(far_out)]
+        loads = [pltpu.make_async_copy(ins[n], held[m], sems.at[m]) for m, n in enumerate(far)]
+        for load in loads:
+            load.start()
+        for m, n in enumerate(far):
+            if n not in late:
+                loads[m].wait()
+
+        def ready():
+            for m, n in enumerate(far):
+                if n in late:
+                    loads[m].wait()
+
+        ins = [held[far.index(n)] if n in far else ref for n, ref in enumerate(ins)]
+        local = [held_out[far_out.index(n)] if n in far_out else ref for n, ref in enumerate(outs)]
+        kernel(ready, *ins, *local)
+        stores = [pltpu.make_async_copy(held_out[m], outs[n], sems.at[len(far) + m]) for m, n in enumerate(far_out)]
+        for store in stores:
+            store.start()
+        for store in stores:
+            store.wait()
+
+    in_specs = [SMEM if o.ndim == 1 else HBM if n in far else VMEM for n, o in enumerate(operands)]
+    scratch = [pltpu.VMEM(operands[n].shape, operands[n].dtype) for n in far]
+    scratch += [pltpu.VMEM(out[n].shape, out[n].dtype) for n in far_out]
+    scratch.append(pltpu.SemaphoreType.DMA((max(1, len(far) + len(far_out)),)))
+    operands = [pltpu.with_memory_space_constraint(o, pltpu.HBM) if n in far else o for n, o in enumerate(operands)]
     return pl.pallas_call(
-        kernel,
-        out_shape=out,
-        in_specs=[SMEM if o.ndim == 1 else VMEM for o in operands],
-        out_specs=[VMEM] * len(out),
+        body,
+        out_shape=[pltpu.HBM(o.shape, o.dtype) if n in far_out else o for n, o in enumerate(out)],
+        in_specs=in_specs,
+        out_specs=[HBM if n in far_out else VMEM for n in range(len(out))],
+        scratch_shapes=scratch,
         input_output_aliases=aliases,
         cost_estimate=pl.CostEstimate(flops=1, bytes_accessed=1, transcendentals=0),
         compiler_params=pltpu.CompilerParams(vmem_limit_bytes=20 << 20),
@@ -69,7 +103,7 @@
     return emb, (jax.nn.sigmoid(logits) - positive).astype(BF16)
 
 
-def pairs_kernel(count, first, numbers, starts, image_emb, match, *refs):
+def pairs_kernel(count, first, ready, numbers, starts, image_emb, match, *refs):
     texts, refs = refs[:count], refs[count:]
     if not first:
         acc_in, refs = refs[0], refs[1:]
@@ -89,7 +123,7 @@
         text_out[n][...] = text_part[n * rows : (n + 1) * rows].astype(text_out[n].dtype)
 
 
-def project_kernel(own, core, yh, both, proj_weight, *refs):
+def project_kernel(ready, own, core, yh, both, proj_weight, *refs):
     matches, (unit, emb, inv_out, match_out) = refs[:4], refs[4:]
     rows = own.shape[0]
     for n, sensor in enumerate((own, core, yh, both)):
@@ -104,11 +138,12 @@
         match_out[here, :] = match.T[:, 0:1]
 
 
-def last_kernel(numbers, starts, image_emb, match, text, acc_in, unit, acc_out, dot_out, packet, grad_out):
+def last_kernel(ready, numbers, starts, image_emb, match, text, acc_in, unit, acc_out, dot_out, packet, grad_out):
     emb, grad = block_grads(numbers, starts[0], image_emb[...], match[...], text[...])
     grad_out[...] = grad
     acc = numbers[0] * (acc_in[...] + jnp.dot(grad, emb, preferred_element_type=F32))
     acc_out[...] = acc
+    ready()
     dot = jnp.sum(unit[...] * acc, -1, keepdims=True)
     dot_out[...] = dot
     rows, width = acc.shape
@@ -127,11 +162,11 @@
             packet[at : at + block, half + 128 :] = acc_out[slot * block : (slot + 1) * block, lanes].astype(BF16)
 
 
-def last_text_kernel(grad, image_emb, out):
+def last_text_kernel(ready, grad, image_emb, out):
     out[...] = inner_cols(grad[...], image_emb[...]).astype(out.dtype)
 
 
-def weight_kernel(starts, got, acc, dot, unit, inv, own_rows, core_rows, yh_rows, both_rows, weight, row_send, row_keep):
+def weight_kernel(ready, starts, got, acc, dot, unit, inv, own_rows, core_rows, yh_rows, both_rows, weight, row_send, row_keep):
     rows, width = acc.shape
     half, quarter, block = width // 2, width // 4, rows // 4
     own = pl.ds(pl.multiple_of(starts[1] * half, half), half)
@@ -153,6 +188,7 @@
                 extra = got[at : at + block, half + 128 :].astype(F32)
                 target[:, lanes] = (acc[mine, lanes] + extra).astype(target.dtype)
     proj = jnp.concatenate(projs, 0)
+    ready()
     sensor = jnp.concatenate([own_rows[...], core_rows[...], yh_rows[...], both_rows[...]], 0)
     chunk = weight.shape[1]
     for n in range(half // 128):
@@ -161,7 +197,7 @@
             weight[n * (128 // chunk) + m] = product[m * chunk : (m + 1) * chunk]
 
 
-def chunk_kernel(parts, out):
+def chunk_kernel(ready, parts, out):
     total = parts[0].astype(F32)
     for n in range(1, parts.shape[0]):
         total = total + parts[n].astype(F32)
@@ -172,22 +208,24 @@
         out[n] = jnp.concatenate([turned[at : at + rows], turned[at + rows : at + 2 * rows]], 1).astype(BF16)
 
 
-def share_kernel(parts, out):
+def share_kernel(ready, parts, out):
+    rows = parts.shape[1]
     for core in range(CORE):
         total = parts[core].astype(F32)
         for n in range(1, Z * YH):
             total = total + parts[n * CORE + core].astype(F32)
         total = total * (1.0 / DP)
         for n in range(DP):
-            out[n, core] = total
-
-
-def layout_kernel(shares, out):
-    rows, lanes = shares.shape[2:]
+            out[n, core * rows : (core + 1) * rows] = total
+
+
+def layout_kernel(ready, shares, out):
+    rows, lanes = shares.shape[1] // 2, shares.shape[2]
     cols = lanes // 2
     for core in range(CORE):
+        here = slice(core * rows, (core + 1) * rows)
         for pair in range(DP // 2):
-            left, right = shares[2 * pair, core], shares[2 * pair + 1, core]
+            left, right = shares[2 * pair, here], shares[2 * pair + 1, here]
             at = core * DP * cols + pair * lanes
             out[:rows, at : at + lanes] = jnp.concatenate([left[:, :cols], right[:, :cols]], 1)
             out[rows:, at : at + lanes] = jnp.concatenate([left[:, cols:], right[:, cols:]], 1)
@@ -208,7 +246,6 @@
     for k in (1, 2, 3):
         slot[k] = shift_z(slot[k - 1], -1)
         slot[-k] = shift_z(slot[1 - k], 1)
-    slot[4] = shift_z(slot[-3], 1)
 
     sensor_yh = swap_yh(sensor)
     sensors = [sensor, swap_core(sensor), sensor_yh, swap_core(sensor_yh)]
@@ -218,7 +255,7 @@
     match = [match, match_both[:1], match_yh, match_both[1:]]
     shapes = [((4 * rows, width), F32), ((4 * rows, width), BF16), ((4 * rows, 1), F32), ((4 * rows, 1), F32)]
     image_unit, image_emb, image_inv, match_rows = call(
-        project_kernel, [jax.ShapeDtypeStruct(*s) for s in shapes], {}, *sensors, proj_weight, *match
+        project_kernel, [jax.ShapeDtypeStruct(*s) for s in shapes], {}, *sensors, proj_weight, *match, far=range(5), far_out=(0,)
     )
 
     def starts_of(keys):
@@ -234,9 +271,12 @@
             aliases = {len(operands): 0}
             operands.append(acc)
         kernel = functools.partial(pairs_kernel, len(keys), acc is None)
-        return call(kernel, out, aliases, *operands)
+        far = range(4, 4 + len(keys))
+        return call(kernel, out, aliases, *operands, far=far, far_out=range(1, len(out)))
 
     acc, text_0, text_1, text_m1, text_2, text_m2 = pairs((0, 1, -1, 2, -2), (F32, BF16, BF16, F32, F32), None)
+    last_text, acc = lax.optimization_barrier((slot[-3], acc))
+    last_text = shift_z(last_text, 1)
     acc, text_3, text_m3 = pairs((3, -3), (BF16, BF16), acc)
     starts = jnp.stack(starts_of((4,)) + [core])
     shapes = [((4 * rows, width), F32), ((4 * rows, 1), F32), ((4 * rows, width // 8 * 7), BF16), ((4 * rows, rows), BF16)]
@@ -244,9 +284,13 @@
         last_kernel,
         [jax.ShapeDtypeStruct(*s) for s in shapes],
         {5: 0},
-        numbers, starts, image_emb, match_rows, slot[4], acc, image_unit,
-    )
-    (text_4,) = call(last_text_kernel, [jax.ShapeDtypeStruct((rows, width), BF16)], {}, last_grad, image_emb)
+        numbers, starts, image_emb, match_rows, last_text, acc, image_unit,
+        far=(4, 6),
+        late=(6,),
+    )
+    (text_4,) = call(
+        last_text_kernel, [jax.ShapeDtypeStruct((rows, width), BF16)], {}, last_grad, image_emb, far_out=(0,)
+    )
 
     shapes = [((DP, width // 16, feat), BF16), ((rows, width), BF16), ((rows, width), F32)]
     weight_part, row_send, row_keep = call(
@@ -254,19 +298,24 @@
         [jax.ShapeDtypeStruct(*s) for s in shapes],
         {},
         starts, swap_core(packet), acc, dot, image_unit, image_inv, *sensors,
+        far=(4, *range(6, 10)),
+        late=range(6, 10),
+        far_out=range(3),
     )
     weight_part = lax.all_to_all(weight_part, "dp", 0, 0, tiled=True)
     per_loop = feat // LOOP
     block = (per_loop // 2, width // 8)
-    (weight_part,) = call(chunk_kernel, [jax.ShapeDtypeStruct((LOOP,) + block, BF16)], {}, weight_part)
-    text_2, text_m2, weight_part = lax.optimization_barrier((text_2, text_m2, weight_part))
+    (weight_part,) = call(
+        chunk_kernel, [jax.ShapeDtypeStruct((LOOP,) + block, BF16)], {}, weight_part, far_out=(0,)
+    )
+    text_2, text_m2, row_send, _ = lax.optimization_barrier((text_2, text_m2, row_send, weight_part))
     weight_part = lax.all_to_all(weight_part, "loop", 0, 0, tiled=True)
-    (shares,) = call(share_kernel, [jax.ShapeDtypeStruct((DP, CORE) + block, F32)], {}, weight_part)
-    shares = lax.all_to_all(shares, "dp", 0, 0, tiled=True)
-    (weight_grad,) = call(layout_kernel, [jax.ShapeDtypeStruct((per_loop, width), F32)], {}, shares)
-
-    text_3, text_m3, text_4, text_1, text_m1, row_send = lax.optimization_barrier(
-        (text_3, text_m3, text_4, text_1, text_m1, row_send)
+    (shares,) = call(
+        share_kernel, [jax.ShapeDtypeStruct((DP, per_loop, width // 8), F32)], {}, weight_part, far_out=(0,)
+    )
+
+    text_3, text_m3, text_4, text_1, text_m1, _ = lax.optimization_barrier(
+        (text_3, text_m3, text_4, text_1, text_m1, row_keep)
     )
     row_got = swap_yh(row_send)
     from_below, from_above, far = shift_z(text_3, 1), shift_z(text_m3, -1), shift_z(text_4, 2)
@@ -274,6 +323,11 @@
     up = text_2 + from_below.astype(F32) + far.astype(F32)
     down = text_m2 + from_above.astype(F32)
     up, down = shift_z(up.astype(BF16), 2), shift_z(down.astype(BF16), -2)
+    up, down, row_got, _ = lax.optimization_barrier((up, down, row_got, shares))
+    shares = lax.all_to_all(shares, "dp", 0, 0, tiled=True)
+    (weight_grad,) = call(
+        layout_kernel, [jax.ShapeDtypeStruct((per_loop, width), F32)], {}, shares, far_out=(0,)
+    )
     text_sum = text_0 + near_below.astype(F32) + near_above.astype(F32)
     text_sum = logit_scale * (text_sum + up.astype(F32) + down.astype(F32))
     text_wide = texts.astype(F32)

time: 134 us -> 127 us (0.948)
  local copies, waits for them, and re-layouts: 18.6 us -> 3.19 us
  waiting for transfers between devices: 31.1 us -> 20.2 us
  Pallas kernels: 18.7 us -> 28.6 us
  starting transfers between devices: 51.1 us -> 61 us
    unnamed x70 -> x24, local copies, waits for them, and re-layouts: 16.8 us -> 2.16 us
    ppermute x3, waiting for transfers between devices: 11 us -> 0.01 us  [swap_yh(): return lax.ppermute(block, 'loop', route(lambda z, y, c: (z, 1 - y, c)))]
    all_to_all x1, waiting for transfers between devices: 0.01 us -> 11 us  [on_device(): weight_part = lax.all_to_all(weight_part, 'dp', 0, 0, tiled=True)]
    pallas_call x9, Pallas kernels: 18.7 us -> 28.6 us  [call(): pl.pallas_call(body, out_shape=[pltpu.HBM(o.shape, o.dtype) if n in far_o...]
    ppermute x4, starting transfers between devices: 0.35 us -> 7.51 us  [swap_core(): return lax.ppermute(block, 'loop', route(lambda z, y, c: (z, y, 1 - c)))]
    all_to_all x1, waiting for transfers between devices: 4.3 us -> 0.01 us  [on_device(): weight_part = lax.all_to_all(weight_part, 'loop', 0, 0, tiled=True)]
    ppermute x3, starting transfers between devices: 5.59 us -> 9.89 us  [swap_yh(): return lax.ppermute(block, 'loop', route(lambda z, y, c: (z, 1 - y, c)))]
    all_to_all x1, waiting for transfers between devices: 3.71 us -> 0.01 us  [on_device(): shares = lax.all_to_all(shares, 'dp', 0, 0, tiled=True)]
  transfers between devices with their start and end apart: 24 -> 24, of which waited for: 9 -> 9; matrix products, arithmetic and copies ran while one was open for 9% -> 9% of each run, Pallas kernels for 10% -> 15%
where the time goes in v5:
time: 127 us; the launch traced here: 126 us
  starting transfers between devices  61 us (48%)
  Pallas kernels  28.6 us (23%)
  waiting for transfers between devices  20.2 us (16%)
  other arithmetic  7.55 us (6%)
  matrix products  3.36 us (3%)
  local copies, waits for them, and re-layouts  3.19 us (3%)
  between operations  2.4 us (2%)
    pallas_call x9, Pallas kernels, call(): pl.pallas_call(body, out_shape=[pltpu.HBM(o.shape, o.dtype) if n in far_o...  28.6 us
    ppermute x14, starting transfers between devices, shift_z(): lax.ppermute(block, 'loop', route(lambda z, y, c: (z + (1 - 2 * c) * dist...  24.9 us
    all_to_all x1, starting transfers between devices, on_device(): weight_part = lax.all_to_all(weight_part, 'loop', 0, 0, tiled=True)  11.2 us
    all_to_all x1, waiting for transfers between devices, on_device(): weight_part = lax.all_to_all(weight_part, 'dp', 0, 0, tiled=True)  11 us
    ppermute x3, starting transfers between devices, swap_yh(): return lax.ppermute(block, 'loop', route(lambda z, y, c: (z, 1 - y, c)))  9.89 us
    ppermute x4, starting transfers between devices, swap_core(): return lax.ppermute(block, 'loop', route(lambda z, y, c: (z, y, 1 - c)))  7.51 us
    ppermute x14, waiting for transfers between devices, shift_z(): lax.ppermute(block, 'loop', route(lambda z, y, c: (z + (1 - 2 * c) * dist...  6.01 us
    all_to_all x1, starting transfers between devices, on_device(): weight_part = lax.all_to_all(weight_part, 'dp', 0, 0, tiled=True)  4.17 us
  transfers between devices with their start and end apart: 24, of which 9 were waited for; matrix products, arithmetic and copies ran while one was open for 9% of the time, Pallas kernels for 15%

profile of v5, /device:TPU:1, one launch (start us, length us, event | category | flops | bytes accessed | tf_op | source)
XLA Modules:
  0.0 126.3 jit_solution(11563754901133909873)
XLA Ops:
  0.6 6.5 %collective-permute-start.5 = (bf16[128,1024]{1,0:T(8,128)(2,1)}, bf16[128,1024]{1,0:T(8,128)(2,1)S(1)}, u32[]{:S(2)}, u32[]{:S(2)}) collective-permute-start(bf16[128,1024]{1,0:T(8,128)(2,1)} %bitcast.22), channel_id=1, source_target_pairs={{0,32},{8,232},{16,48},{24,248},{32,64},{40,8},{48,80},{56,24},{64... | collective-permute-start | bytes 786440 | tf_op jit(solution)/shard_map/ppermute | solution.py:32
  7.1 2.9 %collective-permute-start.1 = (bf16[128,1152]{1,0:T(8,128)(2,1)}, bf16[128,1152]{1,0:T(8,128)(2,1)S(1)}, u32[]{:S(2)}, u32[]{:S(2)}) collective-permute-start(bf16[128,1152]{1,0:T(8,128)(2,1)} %bitcast.25), channel_id=1, source_target_pairs={{0,16},{8,24},{16,0},{24,8},{32,48},{40,56},{48,32},{56,40},{64,80... | collective-permute-start | bytes 884744 | tf_op jit(solution)/shard_map/ppermute | solution.py:40
  10.7 3.3 %collective-permute-start.6 = (bf16[128,1024]{1,0:T(8,128)(2,1)S(1)}, bf16[128,1024]{1,0:T(8,128)(2,1)}, u32[]{:S(2)}, u32[]{:S(2)}) collective-permute-start(bf16[128,1024]{1,0:T(8,128)(2,1)S(1)} %collective-permute-done.5.refs_6_), channel_id=1, source_target_pairs={{0,32},{8,232},{16,48},{24,248},{32,64},{40,8},{48,80},{56,24},{64... | collective-permute-start | bytes 786440 | tf_op jit(solution)/shard_map/ppermute | solution.py:32
  14.1 4.1 %collective-permute-start.3 = (s32[1,128]{1,0:T(1,128)}, s32[1,128]{1,0:T(1,128)S(1)}, u32[]{:S(2)}, u32[]{:S(2)}) collective-permute-start(s32[1,128]{1,0:T(1,128)} %refs_5_.1), channel_id=1, source_target_pairs={{0,16},{8,24},{16,0},{24,8},{32,48},{40,56},{48,32},{56,40},{64,80... | collective-permute-start | bytes 1544 | tf_op jit(solution)/shard_map/ppermute | solution.py:40
  19.6 2.2 %collective-permute-start.2 = (bf16[128,1152]{1,0:T(8,128)(2,1)S(1)}, bf16[128,1152]{1,0:T(8,128)(2,1)S(1)}, u32[]{:S(2)}, u32[]{:S(2)}) collective-permute-start(bf16[128,1152]{1,0:T(8,128)(2,1)S(1)} %collective-permute-done.1.refs_2_.refs_8_), channel_id=1, source_target_pairs={{0,8},{8,0},{16,24},{24,16},{32,40},{40,32},{48,56},{56,48},{64,72... | collective-permute-start | bytes 884744 | tf_op jit(solution)/shard_map/ppermute | solution.py:36
  28.1 5.1 %shard_map.85 = (f32[512,1024]{1,0:T(8,128)}, bf16[512,1024]{1,0:T(8,128)(2,1)S(1)}, f32[512,1]{1,0:T(8,128)S(1)}, f32[512,1]{1,0:T(8,128)S(1)}) custom-call(bf16[128,1152]{1,0:T(8,128)(2,1)} %bitcast.27, bf16[128,1152]{1,0:T(8,128)(2,1)} %copy-done.7, bf16[128,1152]{1,0:T(8,128)(2,1)} %copy-done.6, bf16[128,1152]{1,0:T(8,128)(2,1)} %copy-done.8, ...), custom_call_target="tpu_custom_call" | custom-call | flops 1 | bytes 1 | tf_op jit(solution)/shard_map/pallas_call | solution.py:84
  33.9 6.8 %shard_map.86 = (f32[512,1024]{1,0:T(8,128)S(1)}, f32[128,1024]{1,0:T(8,128)}, bf16[128,1024]{1,0:T(8,128)(2,1)}, bf16[128,1024]{1,0:T(8,128)(2,1)}, f32[128,1024]{1,0:T(8,128)}, /*index=5*/f32[128,1024]{1,0:T(8,128)}) custom-call(f32[2]{0:T(128)S(1)} %pad_maximum_fusion.refs_0_, s32[5]{0:T(128)S(1)} %stack.56.refs_1_, ...), custom_call_target="tpu_custom_call" | custom-call | flops 1 | bytes 1 | tf_op jit(solution)/shard_map/pallas_call | solution.py:84
  40.8 2.3 %collective-permute-start.10 = (bf16[128,1024]{1,0:T(8,128)(2,1)}, bf16[128,1024]{1,0:T(8,128)(2,1)}, u32[]{:S(2)}, u32[]{:S(2)}) collective-permute-start(bf16[128,1024]{1,0:T(8,128)(2,1)} %collective-permute-done.7.refs_5_), channel_id=1, source_target_pairs={{0,32},{8,232},{16,48},{24,248},{32,64},{40,8},{48,80},{56,24},{64... | collective-permute-start | bytes 786440 | tf_op jit(solution)/shard_map/ppermute | solution.py:32
  43.2 4.3 %shard_map.87 = (f32[512,1024]{1,0:T(8,128)S(1)}, bf16[128,1024]{1,0:T(8,128)(2,1)}, bf16[128,1024]{1,0:T(8,128)(2,1)}) custom-call(f32[2]{0:T(128)S(1)} %pad_maximum_fusion.refs_0_, s32[2]{0:T(128)S(1)} %pad_add_fusion.2.refs_1_, bf16[512,1024]{1,0:T(8,128)(2,1)S(1)} %get-tuple-element.36.refs_2_.refs_1_, ...), custom_call_target="tpu_custom_call", output_to_operand_aliasing={{0}: (6, {})} | custom-call | flops 1 | bytes 1 | tf_op jit(solution)/shard_map/pallas_call | solution.py:84
  47.5 3.9 %shard_map.88 = (f32[512,1024]{1,0:T(8,128)S(1)}, f32[512,1]{1,0:T(8,128)S(1)}, bf16[512,896]{1,0:T(8,128)(2,1)S(1)}, bf16[512,128]{1,0:T(8,128)(2,1)S(1)}) custom-call(f32[2]{0:T(128)S(1)} %pad_maximum_fusion.refs_0_, s32[2]{0:T(128)S(1)} %pad_add_fusion.1.refs_1_.refs_0_, ...), custom_call_target="tpu_custom_call", output_to_operand_aliasing={{0}: (5, {})} | custom-call | flops 1 | bytes 1 | tf_op jit(solution)/shard_map/pallas_call | solution.py:84
  51.5 5.3 %collective-permute-start.12 = (bf16[512,896]{1,0:T(8,128)(2,1)S(1)}, bf16[512,896]{1,0:T(8,128)(2,1)S(1)}, u32[]{:S(2)}, u32[]{:S(2)}) collective-permute-start(bf16[512,896]{1,0:T(8,128)(2,1)S(1)} %get-tuple-element.43), channel_id=1, source_target_pairs={{0,8},{8,0},{16,24},{24,16},{32,40},{40,32},{48,56},{56,48},{64,72... | collective-permute-start | bytes 2752520 | tf_op jit(solution)/shard_map/ppermute | solution.py:36
  56.7 2.1 %collective-permute-done.12.refs_1_ = bf16[512,896]{1,0:T(8,128)(2,1)S(1)} collective-permute-done((bf16[512,896]{1,0:T(8,128)(2,1)S(1)}, bf16[512,896]{1,0:T(8,128)(2,1)S(1)}, u32[]{:S(2)}, u32[]{:S(2)}) %collective-permute-start.12) | collective-permute-done | bytes 917536 | tf_op jit(solution)/shard_map/ppermute | solution.py:36
  58.8 4.9 %shard_map.89 = (bf16[8,64,1152]{2,1,0:T(8,128)(2,1)}, bf16[128,1024]{1,0:T(8,128)(2,1)}, f32[128,1024]{1,0:T(8,128)}) custom-call(s32[2]{0:T(128)S(1)} %pad_add_fusion.1.refs_1_.refs_0_, bf16[512,896]{1,0:T(8,128)(2,1)S(1)} %collective-permute-done.12.refs_1_, f32[512,1024]{1,0:T(8,128)S(1)} %get-tuple-element.44.refs_2_, ...), custom_call_target="tpu_custom_call" | custom-call | flops 1 | bytes 1 | tf_op jit(solution)/shard_map/pallas_call | solution.py:84
  63.7 4.2 %all-to-all-start = ((bf16[8,64,1152]{2,1,0:T(8,128)(2,1)}), bf16[8,64,1152]{2,1,0:T(8,128)(2,1)S(1)}, u32[]{:S(2)}, u32[]{:S(2)}) async-start(bf16[8,64,1152]{2,1,0:T(8,128)(2,1)} %get-tuple-element.51), calls=%async_computation | async-start | bytes 2359296 | tf_op jit(solution)/shard_map/all_to_all | solution.py:305
  69.1 2.7 %collective-permute-start.13 = (bf16[128,1024]{1,0:T(8,128)(2,1)}, bf16[128,1024]{1,0:T(8,128)(2,1)S(1)}, u32[]{:S(2)}, u32[]{:S(2)}) collective-permute-start(bf16[128,1024]{1,0:T(8,128)(2,1)} %get-tuple-element.58), channel_id=1, source_target_pairs={{0,32},{8,232},{16,48},{24,248},{32,64},{40,8},{48,80},{56,24},{64... | collective-permute-start | bytes 786440 | tf_op jit(solution)/shard_map/ppermute | solution.py:32
  71.7 2.8 %collective-permute-start.14 = (bf16[128,1024]{1,0:T(8,128)(2,1)}, bf16[128,1024]{1,0:T(8,128)(2,1)}, u32[]{:S(2)}, u32[]{:S(2)}) collective-permute-start(bf16[128,1024]{1,0:T(8,128)(2,1)} %shard_map.91), channel_id=1, source_target_pairs={{0,64},{8,200},{16,80},{24,216},{32,96},{40,232},{48,112},{56,248}... | collective-permute-start | bytes 786440 | tf_op jit(solution)/shard_map/ppermute | solution.py:32
  74.6 11.0 %all-to-all-done.refs_0_ = bf16[8,64,1152]{2,1,0:T(8,128)(2,1)S(1)} async-done(((bf16[8,64,1152]{2,1,0:T(8,128)(2,1)}), bf16[8,64,1152]{2,1,0:T(8,128)(2,1)S(1)}, u32[]{:S(2)}, u32[]{:S(2)}) %all-to-all-start) | async-done | bytes 1179680 | tf_op jit(solution)/shard_map/all_to_all | solution.py:305
  86.7 11.2 %all-to-all-start.1 = ((bf16[32,18,128]{2,1,0:T(8,128)(2,1)}), bf16[32,18,128]{2,1,0:T(8,128)(2,1)S(1)}, u32[]{:S(2)}, u32[]{:S(2)}) async-start(bf16[32,18,128]{2,1,0:T(8,128)(2,1)} %shard_map.90), calls=%async_computation.1 | async-start | bytes 393216 | tf_op jit(solution)/shard_map/all_to_all | solution.py:312
  99.8 2.3 %collective-permute-start.17 = (bf16[128,1024]{1,0:T(8,128)(2,1)}, bf16[128,1024]{1,0:T(8,128)(2,1)}, u32[]{:S(2)}, u32[]{:S(2)}) collective-permute-start(bf16[128,1024]{1,0:T(8,128)(2,1)} %add_convert_fusion), channel_id=1, source_target_pairs={{0,192},{8,72},{16,208},{24,88},{32,224},{40,104},{48,240},{56,120... | collective-permute-start | bytes 786440 | tf_op jit(solution)/shard_map/ppermute | solution.py:32
  102.1 1.9 %add_convert_fusion.1 = bf16[128,1024]{1,0:T(8,128)(2,1)} fusion(bf16[128,1024]{1,0:T(8,128)(2,1)} %collective-permute-done.14, f32[128,1024]{1,0:T(8,128)} %get-tuple-element.52, bf16[128,1024]{1,0:T(8,128)(2,1)S(1)} %collective-permute-done.13), kind=kLoop, calls=%fused_computation.16 | loop fusion | flops 655360 | bytes 1310720 | tf_op jit(solution)/shard_map/convert_element_type | solution.py:325
  105.3 2.9 %collective-permute-start.18 = (bf16[128,1024]{1,0:T(8,128)(2,1)}, bf16[128,1024]{1,0:T(8,128)(2,1)S(1)}, u32[]{:S(2)}, u32[]{:S(2)}) collective-permute-start(bf16[128,1024]{1,0:T(8,128)(2,1)} %get-tuple-element.62), channel_id=1, source_target_pairs={{0,16},{8,24},{16,0},{24,8},{32,48},{40,56},{48,32},{56,40},{64,80... | collective-permute-start | bytes 786440 | tf_op jit(solution)/shard_map/ppermute | solution.py:40
  111.4 3.4 %all-to-all-start.2 = ((f32[8,36,128]{2,1,0:T(8,128)}), f32[8,36,128]{2,1,0:T(8,128)S(1)}, u32[]{:S(2)}, u32[]{:S(2)}) async-start(f32[8,36,128]{2,1,0:T(8,128)} %shard_map.92), calls=%async_computation.2 | async-start | bytes 327680 | tf_op jit(solution)/shard_map/all_to_all | solution.py:327
  115.6 2.2 %collective-permute-done.15 = bf16[128,1024]{1,0:T(8,128)(2,1)} collective-permute-done((bf16[128,1024]{1,0:T(8,128)(2,1)}, bf16[128,1024]{1,0:T(8,128)(2,1)}, u32[]{:S(2)}, u32[]{:S(2)}) %collective-permute-start.15) | collective-permute-done | bytes 262176 | tf_op jit(solution)/shard_map/ppermute | solution.py:32
  118.0 3.4 %fusion = bf16[1,128,1152]{2,1,0:T(8,128)(2,1)} fusion(bf16[1152,1024]{1,0:T(8,128)(2,1)} %refs_4_.1, f32[512,1024]{1,0:T(8,128)S(1)} %copy-done.3, f32[128,1024]{1,0:T(8,128)S(1)} %copy-done.5, bf16[128,1024]{1,0:T(8,128)(2,1)S(1)} %collective-permute-done.18, f32[128]{0:T(128)S(1)} %slice_reduce_fusion, f32[128]{0:T(128)S(1)} %multiply_reduce_fusion), kind=kOutput, calls=%fused_computation.1 | convolution fusion | flops 302923776 | bytes 3965952 | tf_op jit(solution)/shard_map/dot_general | solution.py:44
  (72 shorter events, 22.4 us)
Async XLA Ops:
  0.6 10.1 %collective-permute-start.5 = (bf16[128,1024]{1,0:T(8,128)(2,1)}, bf16[128,1024]{1,0:T(8,128)(2,1)S(1)}, u32[]{:S(2)}, u32[]{:S(2)}) collective-permute-start(bf16[128,1024]{1,0:T(8,128)(2,1)} %bitcast.22), channel_id=1, source_target_pairs={{0,32},{8,232},{16,48},{24,248},{32,64},{40,8},{48,80},{56,24},{64... | collective-permute-start | bytes 786440 | tf_op jit(solution)/shard_map/ppermute | solution.py:32
  7.1 12.5 %collective-permute-start.1 = (bf16[128,1152]{1,0:T(8,128)(2,1)}, bf16[128,1152]{1,0:T(8,128)(2,1)S(1)}, u32[]{:S(2)}, u32[]{:S(2)}) collective-permute-start(bf16[128,1152]{1,0:T(8,128)(2,1)} %bitcast.25), channel_id=1, source_target_pairs={{0,16},{8,24},{16,0},{24,8},{32,48},{40,56},{48,32},{56,40},{64,80... | collective-permute-start | bytes 884744 | tf_op jit(solution)/shard_map/ppermute | solution.py:40
  10.0 9.5 %collective-permute-start.8 = (bf16[128,1024]{1,0:T(8,128)(2,1)}, bf16[128,1024]{1,0:T(8,128)(2,1)S(1)}, u32[]{:S(2)}, u32[]{:S(2)}) collective-permute-start(bf16[128,1024]{1,0:T(8,128)(2,1)} %bitcast.23), channel_id=1, source_target_pairs={{0,224},{8,40},{16,240},{24,56},{32,0},{40,72},{48,16},{56,88},{64... | collective-permute-start | bytes 786440 | tf_op jit(solution)/shard_map/ppermute | solution.py:32
  10.7 11.1 %collective-permute-start.6 = (bf16[128,1024]{1,0:T(8,128)(2,1)S(1)}, bf16[128,1024]{1,0:T(8,128)(2,1)}, u32[]{:S(2)}, u32[]{:S(2)}) collective-permute-start(bf16[128,1024]{1,0:T(8,128)(2,1)S(1)} %collective-permute-done.5.refs_6_), channel_id=1, source_target_pairs={{0,32},{8,232},{16,48},{24,248},{32,64},{40,8},{48,80},{56,24},{64... | collective-permute-start | bytes 786440 | tf_op jit(solution)/shard_map/ppermute | solution.py:32
  14.1 12.5 %collective-permute-start = (bf16[128,1152]{1,0:T(8,128)(2,1)}, bf16[128,1152]{1,0:T(8,128)(2,1)S(1)}, u32[]{:S(2)}, u32[]{:S(2)}) collective-permute-start(bf16[128,1152]{1,0:T(8,128)(2,1)} %bitcast.26), channel_id=1, source_target_pairs={{0,8},{8,0},{16,24},{24,16},{32,40},{40,32},{48,56},{56,48},{64,72... | collective-permute-start | bytes 884744 | tf_op jit(solution)/shard_map/ppermute | solution.py:36
  14.1 9.5 %collective-permute-start.3 = (s32[1,128]{1,0:T(1,128)}, s32[1,128]{1,0:T(1,128)S(1)}, u32[]{:S(2)}, u32[]{:S(2)}) collective-permute-start(s32[1,128]{1,0:T(1,128)} %refs_5_.1), channel_id=1, source_target_pairs={{0,16},{8,24},{16,0},{24,8},{32,48},{40,56},{48,32},{56,40},{64,80... | collective-permute-start | bytes 1544 | tf_op jit(solution)/shard_map/ppermute | solution.py:40
  19.6 6.6 %collective-permute-start.9 = (bf16[128,1024]{1,0:T(8,128)(2,1)S(1)}, bf16[128,1024]{1,0:T(8,128)(2,1)}, u32[]{:S(2)}, u32[]{:S(2)}) collective-permute-start(bf16[128,1024]{1,0:T(8,128)(2,1)S(1)} %collective-permute-done.8.refs_5_), channel_id=1, source_target_pairs={{0,224},{8,40},{16,240},{24,56},{32,0},{40,72},{48,16},{56,88},{64... | collective-permute-start | bytes 786440 | tf_op jit(solution)/shard_map/ppermute | solution.py:32
  19.6 7.0 %collective-permute-start.2 = (bf16[128,1152]{1,0:T(8,128)(2,1)S(1)}, bf16[128,1152]{1,0:T(8,128)(2,1)S(1)}, u32[]{:S(2)}, u32[]{:S(2)}) collective-permute-start(bf16[128,1152]{1,0:T(8,128)(2,1)S(1)} %collective-permute-done.1.refs_2_.refs_8_), channel_id=1, source_target_pairs={{0,8},{8,0},{16,24},{24,16},{32,40},{40,32},{48,56},{56,48},{64,72... | collective-permute-start | bytes 884744 | tf_op jit(solution)/shard_map/ppermute | solution.py:36
  21.9 18.9 %collective-permute-start.7 = (bf16[128,1024]{1,0:T(8,128)(2,1)}, bf16[128,1024]{1,0:T(8,128)(2,1)}, u32[]{:S(2)}, u32[]{:S(2)}) collective-permute-start(bf16[128,1024]{1,0:T(8,128)(2,1)} %collective-permute-done.6.refs_8_), channel_id=1, source_target_pairs={{0,32},{8,232},{16,48},{24,248},{32,64},{40,8},{48,80},{56,24},{64... | collective-permute-start | bytes 786440 | tf_op jit(solution)/shard_map/ppermute | solution.py:32
  24.2 1.1 collective-permute-start.4
  26.1 17.1 %collective-permute-start.11 = (bf16[128,1024]{1,0:T(8,128)(2,1)}, bf16[128,1024]{1,0:T(8,128)(2,1)}, u32[]{:S(2)}, u32[]{:S(2)}) collective-permute-start(bf16[128,1024]{1,0:T(8,128)(2,1)} %collective-permute-done.9.refs_7_), channel_id=1, source_target_pairs={{0,224},{8,40},{16,240},{24,56},{32,0},{40,72},{48,16},{56,88},{64... | collective-permute-start | bytes 786440 | tf_op jit(solution)/shard_map/ppermute | solution.py:32
  40.8 6.8 %collective-permute-start.10 = (bf16[128,1024]{1,0:T(8,128)(2,1)}, bf16[128,1024]{1,0:T(8,128)(2,1)}, u32[]{:S(2)}, u32[]{:S(2)}) collective-permute-start(bf16[128,1024]{1,0:T(8,128)(2,1)} %collective-permute-done.7.refs_5_), channel_id=1, source_target_pairs={{0,32},{8,232},{16,48},{24,248},{32,64},{40,8},{48,80},{56,24},{64... | collective-permute-start | bytes 786440 | tf_op jit(solution)/shard_map/ppermute | solution.py:32
  51.5 7.4 %collective-permute-start.12 = (bf16[512,896]{1,0:T(8,128)(2,1)S(1)}, bf16[512,896]{1,0:T(8,128)(2,1)S(1)}, u32[]{:S(2)}, u32[]{:S(2)}) collective-permute-start(bf16[512,896]{1,0:T(8,128)(2,1)S(1)} %get-tuple-element.43), channel_id=1, source_target_pairs={{0,8},{8,0},{16,24},{24,16},{32,40},{40,32},{48,56},{56,48},{64,72... | collective-permute-start | bytes 2752520 | tf_op jit(solution)/shard_map/ppermute | solution.py:36
  63.7 21.9 %all-to-all-start = ((bf16[8,64,1152]{2,1,0:T(8,128)(2,1)}), bf16[8,64,1152]{2,1,0:T(8,128)(2,1)S(1)}, u32[]{:S(2)}, u32[]{:S(2)}) async-start(bf16[8,64,1152]{2,1,0:T(8,128)(2,1)} %get-tuple-element.51), calls=%async_computation | async-start | bytes 2359296 | tf_op jit(solution)/shard_map/all_to_all | solution.py:305
  69.0 28.9 %collective-permute-start.16 = (bf16[128,1024]{1,0:T(8,128)(2,1)}, bf16[128,1024]{1,0:T(8,128)(2,1)}, u32[]{:S(2)}, u32[]{:S(2)}) collective-permute-start(bf16[128,1024]{1,0:T(8,128)(2,1)} %get-tuple-element.61), channel_id=1, source_target_pairs={{0,224},{8,40},{16,240},{24,56},{32,0},{40,72},{48,16},{56,88},{64... | collective-permute-start | bytes 786440 | tf_op jit(solution)/shard_map/ppermute | solution.py:32
  69.1 33.0 %collective-permute-start.13 = (bf16[128,1024]{1,0:T(8,128)(2,1)}, bf16[128,1024]{1,0:T(8,128)(2,1)S(1)}, u32[]{:S(2)}, u32[]{:S(2)}) collective-permute-start(bf16[128,1024]{1,0:T(8,128)(2,1)} %get-tuple-element.58), channel_id=1, source_target_pairs={{0,32},{8,232},{16,48},{24,248},{32,64},{40,8},{48,80},{56,24},{64... | collective-permute-start | bytes 786440 | tf_op jit(solution)/shard_map/ppermute | solution.py:32
  71.7 30.3 %collective-permute-start.14 = (bf16[128,1024]{1,0:T(8,128)(2,1)}, bf16[128,1024]{1,0:T(8,128)(2,1)}, u32[]{:S(2)}, u32[]{:S(2)}) collective-permute-start(bf16[128,1024]{1,0:T(8,128)(2,1)} %shard_map.91), channel_id=1, source_target_pairs={{0,64},{8,200},{16,80},{24,216},{32,96},{40,232},{48,112},{56,248}... | collective-permute-start | bytes 786440 | tf_op jit(solution)/shard_map/ppermute | solution.py:32
  86.7 24.0 %all-to-all-start.1 = ((bf16[32,18,128]{2,1,0:T(8,128)(2,1)}), bf16[32,18,128]{2,1,0:T(8,128)(2,1)S(1)}, u32[]{:S(2)}, u32[]{:S(2)}) async-start(bf16[32,18,128]{2,1,0:T(8,128)(2,1)} %shard_map.90), calls=%async_computation.1 | async-start | bytes 393216 | tf_op jit(solution)/shard_map/all_to_all | solution.py:312
  99.8 15.8 %collective-permute-start.17 = (bf16[128,1024]{1,0:T(8,128)(2,1)}, bf16[128,1024]{1,0:T(8,128)(2,1)}, u32[]{:S(2)}, u32[]{:S(2)}) collective-permute-start(bf16[128,1024]{1,0:T(8,128)(2,1)} %add_convert_fusion), channel_id=1, source_target_pairs={{0,192},{8,72},{16,208},{24,88},{32,224},{40,104},{48,240},{56,120... | collective-permute-start | bytes 786440 | tf_op jit(solution)/shard_map/ppermute | solution.py:32
  104.0 13.8 %collective-permute-start.15 = (bf16[128,1024]{1,0:T(8,128)(2,1)}, bf16[128,1024]{1,0:T(8,128)(2,1)}, u32[]{:S(2)}, u32[]{:S(2)}) collective-permute-start(bf16[128,1024]{1,0:T(8,128)(2,1)} %add_convert_fusion.1), channel_id=1, source_target_pairs={{0,64},{8,200},{16,80},{24,216},{32,96},{40,232},{48,112},{56,248}... | collective-permute-start | bytes 786440 | tf_op jit(solution)/shard_map/ppermute | solution.py:32
  105.3 12.5 %collective-permute-start.18 = (bf16[128,1024]{1,0:T(8,128)(2,1)}, bf16[128,1024]{1,0:T(8,128)(2,1)S(1)}, u32[]{:S(2)}, u32[]{:S(2)}) collective-permute-start(bf16[128,1024]{1,0:T(8,128)(2,1)} %get-tuple-element.62), channel_id=1, source_target_pairs={{0,16},{8,24},{16,0},{24,8},{32,48},{40,56},{48,32},{56,40},{64,80... | collective-permute-start | bytes 786440 | tf_op jit(solution)/shard_map/ppermute | solution.py:40
  109.1 12.7 %collective-permute-start.19 = (bf16[128,1024]{1,0:T(8,128)(2,1)}, bf16[128,1024]{1,0:T(8,128)(2,1)}, u32[]{:S(2)}, u32[]{:S(2)}) collective-permute-start(bf16[128,1024]{1,0:T(8,128)(2,1)} %get-tuple-element.65), channel_id=1, source_target_pairs={{0,32},{8,232},{16,48},{24,248},{32,64},{40,8},{48,80},{56,24},{64... | collective-permute-start | bytes 786440 | tf_op jit(solution)/shard_map/ppermute | solution.py:32
  110.5 12.3 %collective-permute-start.20 = (bf16[128,1024]{1,0:T(8,128)(2,1)}, bf16[128,1024]{1,0:T(8,128)(2,1)}, u32[]{:S(2)}, u32[]{:S(2)}) collective-permute-start(bf16[128,1024]{1,0:T(8,128)(2,1)} %get-tuple-element.66), channel_id=1, source_target_pairs={{0,224},{8,40},{16,240},{24,56},{32,0},{40,72},{48,16},{56,88},{64... | collective-permute-start | bytes 786440 | tf_op jit(solution)/shard_map/ppermute | solution.py:32
  111.4 14.0 %all-to-all-start.2 = ((f32[8,36,128]{2,1,0:T(8,128)}), f32[8,36,128]{2,1,0:T(8,128)S(1)}, u32[]{:S(2)}, u32[]{:S(2)}) async-start(f32[8,36,128]{2,1,0:T(8,128)} %shard_map.92), calls=%async_computation.2 | async-start | bytes 327680 | tf_op jit(solution)/shard_map/all_to_all | solution.py:327
  (12 other events, 122.0 us)

commit v6 on v5

--- a/solution.py
+++ b/solution.py
@@ -48,38 +48,42 @@
     return lax.dot_general(left, right, (((0,), (0,)), ((), ())), preferred_element_type=F32)
 
 
-def call(kernel, out, aliases, *operands, far=(), late=(), far_out=()):
+class Moves:
+    def __init__(self, sems, loads, held, outs):
+        self.sems, self.loads, self.held, self.outs, self.sent = sems, loads, held, outs, []
+
+    def need(self, n):
+        self.loads[n].wait()
+
+    def send(self, n, part=None):
+        source, target = self.held[n], self.outs[n]
+        if part is not None:
+            source, target = source.at[part], target.at[part]
+        copy = pltpu.make_async_copy(source, target, self.sems.at[len(self.loads) + len(self.sent)])
+        copy.start()
+        self.sent.append(copy)
+
+
+def call(kernel, out, aliases, *operands, far=(), far_out=(), sends=None):
     far, far_out, total = list(far), list(far_out), len(operands)
+    sends = len(far_out) if sends is None else sends
 
     def body(*refs):
         ins, outs, scratch = refs[:total], refs[total : total + len(out)], refs[total + len(out) :]
-        held, held_out = scratch[: len(far)], scratch[len(far) : len(far) + len(far_out)]
-        sems = scratch[len(far) + len(far_out)]
-        loads = [pltpu.make_async_copy(ins[n], held[m], sems.at[m]) for m, n in enumerate(far)]
-        for load in loads:
+        held = dict(zip(far, scratch[: len(far)]))
+        held_out = dict(zip(far_out, scratch[len(far) : -1]))
+        loads = {n: pltpu.make_async_copy(ins[n], held[n], scratch[-1].at[m]) for m, n in enumerate(far)}
+        for load in loads.values():
             load.start()
-        for m, n in enumerate(far):
-            if n not in late:
-                loads[m].wait()
-
-        def ready():
-            for m, n in enumerate(far):
-                if n in late:
-                    loads[m].wait()
-
-        ins = [held[far.index(n)] if n in far else ref for n, ref in enumerate(ins)]
-        local = [held_out[far_out.index(n)] if n in far_out else ref for n, ref in enumerate(outs)]
-        kernel(ready, *ins, *local)
-        stores = [pltpu.make_async_copy(held_out[m], outs[n], sems.at[len(far) + m]) for m, n in enumerate(far_out)]
-        for store in stores:
-            store.start()
-        for store in stores:
-            store.wait()
+        moves = Moves(scratch[-1], loads, held_out, outs)
+        kernel(moves, *(held.get(n, ref) for n, ref in enumerate(ins)), *(held_out.get(n, ref) for n, ref in enumerate(outs)))
+        for copy in moves.sent:
+            copy.wait()
 
     in_specs = [SMEM if o.ndim == 1 else HBM if n in far else VMEM for n, o in enumerate(operands)]
     scratch = [pltpu.VMEM(operands[n].shape, operands[n].dtype) for n in far]
     scratch += [pltpu.VMEM(out[n].shape, out[n].dtype) for n in far_out]
-    scratch.append(pltpu.SemaphoreType.DMA((max(1, len(far) + len(far_out)),)))
+    scratch.append(pltpu.SemaphoreType.DMA((max(1, len(far) + sends),)))
     operands = [pltpu.with_memory_space_constraint(o, pltpu.HBM) if n in far else o for n, o in enumerate(operands)]
     return pl.pallas_call(
         body,
@@ -103,7 +107,7 @@
     return emb, (jax.nn.sigmoid(logits) - positive).astype(BF16)
 
 
-def pairs_kernel(count, first, ready, numbers, starts, image_emb, match, *refs):
+def pairs_kernel(count, first, moves, numbers, starts, image_emb, match, *refs):
     texts, refs = refs[:count], refs[count:]
     if not first:
         acc_in, refs = refs[0], refs[1:]
@@ -111,40 +115,37 @@
     image = image_emb[...]
     embs, grads = [], []
     for n in range(count):
+        moves.need(4 + n)
         emb, grad = block_grads(numbers, starts[n], image, match[...], texts[n][...])
         embs.append(emb)
         grads.append(grad)
-    emb, grad = jnp.concatenate(embs, 0), jnp.concatenate(grads, 1)
-    part = jnp.dot(grad, emb, preferred_element_type=F32)
+        text_out[n][...] = inner_cols(grad, image).astype(text_out[n].dtype)
+        moves.send(1 + n)
+    part = jnp.dot(jnp.concatenate(grads, 1), jnp.concatenate(embs, 0), preferred_element_type=F32)
     acc_out[...] = part if first else acc_in[...] + part
-    text_part = inner_cols(grad, image)
-    rows = texts[0].shape[0]
-    for n in range(count):
-        text_out[n][...] = text_part[n * rows : (n + 1) * rows].astype(text_out[n].dtype)
-
-
-def project_kernel(ready, own, core, yh, both, proj_weight, *refs):
-    matches, (unit, emb, inv_out, match_out) = refs[:4], refs[4:]
+
+
+def project_kernel(moves, own, core, yh, both, proj_weight, *refs):
+    matches, (emb, inv_out, match_out) = refs[:4], refs[4:]
     rows = own.shape[0]
+    moves.need(4)
     for n, sensor in enumerate((own, core, yh, both)):
         here = slice(n * rows, (n + 1) * rows)
+        moves.need(n)
         projected = jnp.dot(sensor[...], proj_weight[...], preferred_element_type=F32)
         inv = lax.rsqrt(jnp.sum(projected * projected, -1, keepdims=True) + 1e-06)
-        scaled = projected * inv
-        unit[here, :] = scaled
-        emb[here, :] = scaled.astype(BF16)
+        emb[here, :] = (projected * inv).astype(BF16)
         inv_out[here, :] = inv
         match = jnp.broadcast_to(matches[n][...].astype(F32), (rows, rows))
         match_out[here, :] = match.T[:, 0:1]
 
 
-def last_kernel(ready, numbers, starts, image_emb, match, text, acc_in, unit, acc_out, dot_out, packet, grad_out):
+def last_kernel(moves, numbers, starts, image_emb, match, text, acc_in, acc_out, dot_out, packet, grad_out):
     emb, grad = block_grads(numbers, starts[0], image_emb[...], match[...], text[...])
     grad_out[...] = grad
     acc = numbers[0] * (acc_in[...] + jnp.dot(grad, emb, preferred_element_type=F32))
     acc_out[...] = acc
-    ready()
-    dot = jnp.sum(unit[...] * acc, -1, keepdims=True)
+    dot = jnp.sum(image_emb[...].astype(F32) * acc, -1, keepdims=True)
     dot_out[...] = dot
     rows, width = acc.shape
     half, quarter, block = width // 2, width // 4, rows // 4
@@ -162,11 +163,12 @@
             packet[at : at + block, half + 128 :] = acc_out[slot * block : (slot + 1) * block, lanes].astype(BF16)
 
 
-def last_text_kernel(ready, grad, image_emb, out):
+def last_text_kernel(moves, grad, image_emb, out):
     out[...] = inner_cols(grad[...], image_emb[...]).astype(out.dtype)
-
-
-def weight_kernel(ready, starts, got, acc, dot, unit, inv, own_rows, core_rows, yh_rows, both_rows, weight, row_send, row_keep):
+    moves.send(0)
+
+
+def weight_kernel(moves, starts, got, acc, dot, image_emb, inv, own_rows, core_rows, yh_rows, both_rows, weight, row_send, row_keep):
     rows, width = acc.shape
     half, quarter, block = width // 2, width // 4, rows // 4
     own = pl.ds(pl.multiple_of(starts[1] * half, half), half)
@@ -177,7 +179,8 @@
         kept = acc[mine, own] + got[theirs, :half].astype(F32)
         digits = got[theirs, half : half + 128].astype(F32)
         whole_dot = dot[mine, :] + digits[:, 0:1] + digits[:, 1:2]
-        projs.append(((kept - unit[mine, own] * whole_dot) * inv[mine, :]).astype(BF16))
+        unit = image_emb[mine, own].astype(F32)
+        projs.append(((kept - unit * whole_dot) * inv[mine, :]).astype(BF16))
         if slot in (0, 2):
             target = (row_keep, row_send)[slot // 2]
             target[:, own] = kept.astype(target.dtype)
@@ -187,17 +190,21 @@
                 at = (2 * side + slot // 2) * block
                 extra = got[at : at + block, half + 128 :].astype(F32)
                 target[:, lanes] = (acc[mine, lanes] + extra).astype(target.dtype)
+            moves.send(2 - slot // 2)
     proj = jnp.concatenate(projs, 0)
-    ready()
+    for n in range(6, 10):
+        moves.need(n)
     sensor = jnp.concatenate([own_rows[...], core_rows[...], yh_rows[...], both_rows[...]], 0)
     chunk = weight.shape[1]
     for n in range(half // 128):
         product = inner_cols(proj[:, n * 128 : (n + 1) * 128], sensor).astype(BF16)
         for m in range(128 // chunk):
-            weight[n * (128 // chunk) + m] = product[m * chunk : (m + 1) * chunk]
-
-
-def chunk_kernel(ready, parts, out):
+            at = n * (128 // chunk) + m
+            weight[at] = product[m * chunk : (m + 1) * chunk]
+            moves.send(0, at)
+
+
+def chunk_kernel(moves, parts, out):
     total = parts[0].astype(F32)
     for n in range(1, parts.shape[0]):
         total = total + parts[n].astype(F32)
@@ -206,9 +213,10 @@
     for n in range(count):
         at = 2 * rows * n
         out[n] = jnp.concatenate([turned[at : at + rows], turned[at + rows : at + 2 * rows]], 1).astype(BF16)
-
-
-def share_kernel(ready, parts, out):
+    moves.send(0)
+
+
+def share_kernel(moves, parts, out):
     rows = parts.shape[1]
     for core in range(CORE):
         total = parts[core].astype(F32)
@@ -217,9 +225,10 @@
         total = total * (1.0 / DP)
         for n in range(DP):
             out[n, core * rows : (core + 1) * rows] = total
-
-
-def layout_kernel(ready, shares, out):
+    moves.send(0)
+
+
+def layout_kernel(moves, shares, out):
     rows, lanes = shares.shape[1] // 2, shares.shape[2]
     cols = lanes // 2
     for core in range(CORE):
@@ -229,6 +238,7 @@
             at = core * DP * cols + pair * lanes
             out[:rows, at : at + lanes] = jnp.concatenate([left[:, :cols], right[:, :cols]], 1)
             out[rows:, at : at + lanes] = jnp.concatenate([left[:, cols:], right[:, cols:]], 1)
+    moves.send(0)
 
 
 def on_device(sensor_feats, text_embeds, proj_weight, matches, log_scale, logit_bias):
@@ -243,20 +253,23 @@
     numbers = jnp.stack([logit_scale, logit_bias])
 
     slot = {0: texts}
-    for k in (1, 2, 3):
+    for k in (1, 2):
         slot[k] = shift_z(slot[k - 1], -1)
         slot[-k] = shift_z(slot[1 - k], 1)
 
     sensor_yh = swap_yh(sensor)
-    sensors = [sensor, swap_core(sensor), sensor_yh, swap_core(sensor_yh)]
     match = matches.reshape(1, rows)
-    match_yh = swap_yh(match)
+    sensor_later, match_later, _ = lax.optimization_barrier((sensor, match, sensor_yh))
+    sensors = [sensor, swap_core(sensor_later), sensor_yh, swap_core(sensor_yh)]
+    match_yh = swap_yh(match_later)
     match_both = swap_core(jnp.concatenate([match, match_yh], 0))
     match = [match, match_both[:1], match_yh, match_both[1:]]
-    shapes = [((4 * rows, width), F32), ((4 * rows, width), BF16), ((4 * rows, 1), F32), ((4 * rows, 1), F32)]
-    image_unit, image_emb, image_inv, match_rows = call(
-        project_kernel, [jax.ShapeDtypeStruct(*s) for s in shapes], {}, *sensors, proj_weight, *match, far=range(5), far_out=(0,)
-    )
+    shapes = [((4 * rows, width), BF16), ((4 * rows, 1), F32), ((4 * rows, 1), F32)]
+    image_emb, image_inv, match_rows = call(
+        project_kernel, [jax.ShapeDtypeStruct(*s) for s in shapes], {}, *sensors, proj_weight, *match, far=range(5)
+    )
+    up, down, _ = lax.optimization_barrier((slot[2], slot[-2], image_emb))
+    slot[3], slot[-3] = shift_z(up, -1), shift_z(down, 1)
 
     def starts_of(keys):
         step = (1 - 2 * core) * YH * CORE
@@ -274,8 +287,8 @@
         far = range(4, 4 + len(keys))
         return call(kernel, out, aliases, *operands, far=far, far_out=range(1, len(out)))
 
-    acc, text_0, text_1, text_m1, text_2, text_m2 = pairs((0, 1, -1, 2, -2), (F32, BF16, BF16, F32, F32), None)
-    last_text, acc = lax.optimization_barrier((slot[-3], acc))
+    acc, text_0, text_1, text_m1, text_2, text_m2 = pairs((0, 1, -1, 2, -2), (F32, BF16, BF16, BF16, BF16), None)
+    last_text, _ = lax.optimization_barrier((slot[-3], acc))
     last_text = shift_z(last_text, 1)
     acc, text_3, text_m3 = pairs((3, -3), (BF16, BF16), acc)
     starts = jnp.stack(starts_of((4,)) + [core])
@@ -284,9 +297,7 @@
         last_kernel,
         [jax.ShapeDtypeStruct(*s) for s in shapes],
         {5: 0},
-        numbers, starts, image_emb, match_rows, last_text, acc, image_unit,
-        far=(4, 6),
-        late=(6,),
+        numbers, starts, image_emb, match_rows, last_text, acc,
     )
     (text_4,) = call(
         last_text_kernel, [jax.ShapeDtypeStruct((rows, width), BF16)], {}, last_grad, image_emb, far_out=(0,)
@@ -297,19 +308,18 @@
         weight_kernel,
         [jax.ShapeDtypeStruct(*s) for s in shapes],
         {},
-        starts, swap_core(packet), acc, dot, image_unit, image_inv, *sensors,
-        far=(4, *range(6, 10)),
-        late=range(6, 10),
+        starts, swap_core(packet), acc, dot, image_emb, image_inv, *sensors,
+        far=range(6, 10),
         far_out=range(3),
+        sends=2 + DP,
     )
     weight_part = lax.all_to_all(weight_part, "dp", 0, 0, tiled=True)
     per_loop = feat // LOOP
     block = (per_loop // 2, width // 8)
-    (weight_part,) = call(
+    (weight_chunks,) = call(
         chunk_kernel, [jax.ShapeDtypeStruct((LOOP,) + block, BF16)], {}, weight_part, far_out=(0,)
     )
-    text_2, text_m2, row_send, _ = lax.optimization_barrier((text_2, text_m2, row_send, weight_part))
-    weight_part = lax.all_to_all(weight_part, "loop", 0, 0, tiled=True)
+    weight_part = lax.all_to_all(weight_chunks, "loop", 0, 0, tiled=True)
     (shares,) = call(
         share_kernel, [jax.ShapeDtypeStruct((DP, per_loop, width // 8), F32)], {}, weight_part, far_out=(0,)
     )
@@ -320,8 +330,11 @@
     row_got = swap_yh(row_send)
     from_below, from_above, far = shift_z(text_3, 1), shift_z(text_m3, -1), shift_z(text_4, 2)
     near_below, near_above = shift_z(text_1, 1), shift_z(text_m1, -1)
-    up = text_2 + from_below.astype(F32) + far.astype(F32)
-    down = text_m2 + from_above.astype(F32)
+    from_below, from_above, far, near_below, near_above, row_got, _ = lax.optimization_barrier(
+        (from_below, from_above, far, near_below, near_above, row_got, weight_chunks)
+    )
+    up = text_2.astype(F32) + from_below.astype(F32) + far.astype(F32)
+    down = text_m2.astype(F32) + from_above.astype(F32)
     up, down = shift_z(up.astype(BF16), 2), shift_z(down.astype(BF16), -2)
     up, down, row_got, _ = lax.optimization_barrier((up, down, row_got, shares))
     shares = lax.all_to_all(shares, "dp", 0, 0, tiled=True)
@@ -336,7 +349,7 @@
     text_grad = (text_sum - text_unit * jnp.sum(text_unit * text_sum, -1, keepdims=True)) * text_inv
 
     image_grad = row_keep + row_got.astype(F32)
-    own_unit = image_unit[:rows]
+    own_unit = image_emb[:rows].astype(F32)
     own_dot = jnp.sum(own_unit * image_grad, -1, keepdims=True)
     proj_grad = ((image_grad - own_unit * own_dot) * image_inv[:rows]).astype(BF16)
     sensor_grad = inner_rows(proj_grad, proj_weight).astype(BF16)

time: 127 us -> 120 us (0.945)
  starting transfers between devices: 61 us -> 55.6 us
    all_to_all x1, waiting for transfers between devices: 11 us -> 6.8 us  [on_device(): weight_part = lax.all_to_all(weight_part, 'dp', 0, 0, tiled=True)]
    all_to_all x1, waiting for transfers between devices: 0.01 us -> 4.14 us  [on_device(): weight_part = lax.all_to_all(weight_chunks, 'loop', 0, 0, tiled=True)]
    ppermute x4, starting transfers between devices: 7.51 us -> 3.72 us  [swap_core(): return lax.ppermute(block, 'loop', route(lambda z, y, c: (z, y, 1 - c)))]
    all_to_all x1, starting transfers between devices: 11.2 us -> 8.72 us  [on_device(): weight_part = lax.all_to_all(weight_chunks, 'loop', 0, 0, tiled=True)]
    unnamed x24 -> x26, local copies, waits for them, and re-layouts: 2.16 us -> 2.9 us
  transfers between devices with their start and end apart: 24 -> 24, of which waited for: 9 -> 8; matrix products, arithmetic and copies ran while one was open for 9% -> 9% of each run, Pallas kernels for 15% -> 17%
where the time goes in v6:
time: 120 us
  starting transfers between devices  55.6 us (46%)
  Pallas kernels  28.7 us (24%)
  waiting for transfers between devices  19.3 us (16%)
  other arithmetic  6.52 us (5%)
  local copies, waits for them, and re-layouts  3.93 us (3%)
  matrix products  3.34 us (3%)
  between operations  2.42 us (2%)
    pallas_call x9, Pallas kernels, call(): pl.pallas_call(body, out_shape=[pltpu.HBM(o.shape, o.dtype) if n in far_o...  28.7 us
    ppermute x14, starting transfers between devices, shift_z(): lax.ppermute(block, 'loop', route(lambda z, y, c: (z + (1 - 2 * c) * dist...  25.9 us
    ppermute x3, starting transfers between devices, swap_yh(): return lax.ppermute(block, 'loop', route(lambda z, y, c: (z, 1 - y, c)))  9.56 us
    all_to_all x1, starting transfers between devices, on_device(): weight_part = lax.all_to_all(weight_chunks, 'loop', 0, 0, tiled=True)  8.72 us
    all_to_all x1, waiting for transfers between devices, on_device(): weight_part = lax.all_to_all(weight_part, 'dp', 0, 0, tiled=True)  6.8 us
    ppermute x14, waiting for transfers between devices, shift_z(): lax.ppermute(block, 'loop', route(lambda z, y, c: (z + (1 - 2 * c) * dist...  4.98 us
    all_to_all x1, starting transfers between devices, on_device(): weight_part = lax.all_to_all(weight_part, 'dp', 0, 0, tiled=True)  4.3 us
    all_to_all x1, waiting for transfers between devices, on_device(): weight_part = lax.all_to_all(weight_chunks, 'loop', 0, 0, tiled=True)  4.14 us
  transfers between devices with their start and end apart: 24, of which 8 were waited for; matrix products, arithmetic and copies ran while one was open for 9% of the time, Pallas kernels for 17%

profile of v6, /device:TPU:1, one launch (start us, length us, event | category | flops | bytes accessed | tf_op | source)
XLA Modules:
  0.0 119.8 jit_solution(6493838017888115913)
XLA Ops:
  0.6 3.8 %collective-permute-start = (bf16[128,1152]{1,0:T(8,128)(2,1)}, bf16[128,1152]{1,0:T(8,128)(2,1)S(1)}, u32[]{:S(2)}, u32[]{:S(2)}) collective-permute-start(bf16[128,1152]{1,0:T(8,128)(2,1)} %bitcast.25), channel_id=1, source_target_pairs={{0,16},{8,24},{16,0},{24,8},{32,48},{40,56},{48,32},{56,40},{64,80... | collective-permute-start | bytes 884744 | tf_op jit(solution)/shard_map/ppermute | solution.py:40
  6.1 3.9 %collective-permute-start.7 = (bf16[128,1024]{1,0:T(8,128)(2,1)}, bf16[128,1024]{1,0:T(8,128)(2,1)S(1)}, u32[]{:S(2)}, u32[]{:S(2)}) collective-permute-start(bf16[128,1024]{1,0:T(8,128)(2,1)} %bitcast.23), channel_id=1, source_target_pairs={{0,32},{8,232},{16,48},{24,248},{32,64},{40,8},{48,80},{56,24},{64... | collective-permute-start | bytes 786440 | tf_op jit(solution)/shard_map/ppermute | solution.py:32
  10.5 3.6 %collective-permute-start.3 = (s32[1,128]{1,0:T(1,128)}, s32[1,128]{1,0:T(1,128)S(1)}, u32[]{:S(2)}, u32[]{:S(2)}) collective-permute-start(s32[1,128]{1,0:T(1,128)} %refs_5_.1), channel_id=1, source_target_pairs={{0,16},{8,24},{16,0},{24,8},{32,48},{40,56},{48,32},{56,40},{64,80... | collective-permute-start | bytes 1544 | tf_op jit(solution)/shard_map/ppermute | solution.py:40
  15.7 4.0 %collective-permute-start.8 = (bf16[128,1024]{1,0:T(8,128)(2,1)S(1)}, bf16[128,1024]{1,0:T(8,128)(2,1)}, u32[]{:S(2)}, u32[]{:S(2)}) collective-permute-start(bf16[128,1024]{1,0:T(8,128)(2,1)S(1)} %collective-permute-done.7.refs_6_), channel_id=1, source_target_pairs={{0,32},{8,232},{16,48},{24,248},{32,64},{40,8},{48,80},{56,24},{64... | collective-permute-start | bytes 786440 | tf_op jit(solution)/shard_map/ppermute | solution.py:32
  19.7 2.1 %collective-permute-start.1 = (bf16[128,1152]{1,0:T(8,128)(2,1)}, bf16[128,1152]{1,0:T(8,128)(2,1)S(1)}, u32[]{:S(2)}, u32[]{:S(2)}) collective-permute-start(bf16[128,1152]{1,0:T(8,128)(2,1)} %bitcast.26), channel_id=1, source_target_pairs={{0,8},{8,0},{16,24},{24,16},{32,40},{40,32},{48,56},{56,48},{64,72... | collective-permute-start | bytes 884744 | tf_op jit(solution)/shard_map/ppermute | solution.py:36
  25.3 4.7 %shard_map.85 = (bf16[512,1024]{1,0:T(8,128)(2,1)S(1)}, f32[512,1]{1,0:T(8,128)S(1)}, f32[512,1]{1,0:T(8,128)S(1)}) custom-call(bf16[128,1152]{1,0:T(8,128)(2,1)} %bitcast.27, bf16[128,1152]{1,0:T(8,128)(2,1)} %copy-done.6, bf16[128,1152]{1,0:T(8,128)(2,1)} %copy-done.5, bf16[128,1152]{1,0:T(8,128)(2,1)} %copy-done.7, bf16[1152,1024]{1,0:T(8,128)(2,1)} %refs_4_.1, ...), custom_call_target="tpu_custom_call" | custom-call | flops 1 | bytes 1 | tf_op jit(solution)/shard_map/pallas_call | solution.py:88
  30.7 2.9 %collective-permute-start.9 = (bf16[128,1024]{1,0:T(8,128)(2,1)}, bf16[128,1024]{1,0:T(8,128)(2,1)}, u32[]{:S(2)}, u32[]{:S(2)}) collective-permute-start(bf16[128,1024]{1,0:T(8,128)(2,1)} %collective-permute-done.8.refs_8_), channel_id=1, source_target_pairs={{0,32},{8,232},{16,48},{24,248},{32,64},{40,8},{48,80},{56,24},{64... | collective-permute-start | bytes 786440 | tf_op jit(solution)/shard_map/ppermute | solution.py:32
  35.4 8.3 %shard_map.86 = (f32[512,1024]{1,0:T(8,128)S(1)}, f32[128,1024]{1,0:T(8,128)}, bf16[128,1024]{1,0:T(8,128)(2,1)}, bf16[128,1024]{1,0:T(8,128)(2,1)}, bf16[128,10...) custom-call(f32[2]{0:T(128)S(1)} %pad_maximum_fusion.refs_0_, s32[5]{0:T(128)S(1)} %stack.56.refs_1_, ...), custom_call_target="tpu_custom_call" | custom-call | flops 1 | bytes 1 | tf_op jit(solution)/shard_map/pallas_call | solution.py:88
  43.7 2.7 %collective-permute-start.10 = (bf16[128,1024]{1,0:T(8,128)(2,1)}, bf16[128,1024]{1,0:T(8,128)(2,1)}, u32[]{:S(2)}, u32[]{:S(2)}) collective-permute-start(bf16[128,1024]{1,0:T(8,128)(2,1)} %collective-permute-done.9.refs_5_), channel_id=1, source_target_pairs={{0,32},{8,232},{16,48},{24,248},{32,64},{40,8},{48,80},{56,24},{64... | collective-permute-start | bytes 786440 | tf_op jit(solution)/shard_map/ppermute | solution.py:32
  46.6 4.7 %shard_map.87 = (f32[512,1024]{1,0:T(8,128)S(1)}, bf16[128,1024]{1,0:T(8,128)(2,1)}, bf16[128,1024]{1,0:T(8,128)(2,1)}) custom-call(f32[2]{0:T(128)S(1)} %pad_maximum_fusion.refs_0_, s32[2]{0:T(128)S(1)} %pad_add_fusion.2.refs_1_, bf16[512,1024]{1,0:T(8,128)(2,1)S(1)} %get-tuple-element.43.refs_2_.refs_4_.refs_1_, ...), custom_call_target="tpu_custom_call", output_to_operand_aliasing={{0}: (6, {})} | custom-call | flops 1 | bytes 1 | tf_op jit(solution)/shard_map/pallas_call | solution.py:88
  51.3 3.3 %shard_map.88 = (f32[512,1024]{1,0:T(8,128)S(1)}, f32[512,1]{1,0:T(8,128)S(1)}, bf16[512,896]{1,0:T(8,128)(2,1)S(1)}, bf16[512,128]{1,0:T(8,128)(2,1)S(1)}) custom-call(f32[2]{0:T(128)S(1)} %pad_maximum_fusion.refs_0_, s32[2]{0:T(128)S(1)} %pad_add_fusion.1.refs_1_.refs_0_, ...), custom_call_target="tpu_custom_call", output_to_operand_aliasing={{0}: (5, {})} | custom-call | flops 1 | bytes 1 | tf_op jit(solution)/shard_map/pallas_call | solution.py:88
  55.8 2.1 %collective-permute-done.12.refs_1_ = bf16[512,896]{1,0:T(8,128)(2,1)S(1)} collective-permute-done((bf16[512,896]{1,0:T(8,128)(2,1)S(1)}, bf16[512,896]{1,0:T(8,128)(2,1)S(1)}, u32[]{:S(2)}, u32[]{:S(2)}) %collective-permute-start.12) | collective-permute-done | bytes 917536 | tf_op jit(solution)/shard_map/ppermute | solution.py:36
  57.9 4.1 %shard_map.89 = (bf16[8,64,1152]{2,1,0:T(8,128)(2,1)}, bf16[128,1024]{1,0:T(8,128)(2,1)}, f32[128,1024]{1,0:T(8,128)}) custom-call(s32[2]{0:T(128)S(1)} %pad_add_fusion.1.refs_1_.refs_0_, bf16[512,896]{1,0:T(8,128)(2,1)S(1)} %collective-permute-done.12.refs_1_, f32[512,1024]{1,0:T(8,128)S(1)} %get-tuple-element.51.refs_2_, ...), custom_call_target="tpu_custom_call" | custom-call | flops 1 | bytes 1 | tf_op jit(solution)/shard_map/pallas_call | solution.py:88
  62.0 4.3 %all-to-all-start = ((bf16[8,64,1152]{2,1,0:T(8,128)(2,1)}), bf16[8,64,1152]{2,1,0:T(8,128)(2,1)S(1)}, u32[]{:S(2)}, u32[]{:S(2)}) async-start(bf16[8,64,1152]{2,1,0:T(8,128)(2,1)} %get-tuple-element.67), calls=%async_computation | async-start | bytes 2359296 | tf_op jit(solution)/shard_map/all_to_all | solution.py:316
  72.5 1.8 %collective-permute-done.13 = bf16[128,1024]{1,0:T(8,128)(2,1)S(1)} collective-permute-done((bf16[128,1024]{1,0:T(8,128)(2,1)S(1)}, bf16[128,1024]{1,0:T(8,128)(2,1)S(1)}, u32[]{:S(2)}, u32[]{:S(2)}) %collective-permute-start.13) | collective-permute-done | bytes 262176 | tf_op jit(solution)/shard_map/ppermute | solution.py:32
  75.1 2.1 %collective-permute-start.18 = (bf16[128,1024]{1,0:T(8,128)(2,1)}, bf16[128,1024]{1,0:T(8,128)(2,1)S(1)}, u32[]{:S(2)}, u32[]{:S(2)}) collective-permute-start(bf16[128,1024]{1,0:T(8,128)(2,1)} %get-tuple-element.66), channel_id=1, source_target_pairs={{0,16},{8,24},{16,0},{24,8},{32,48},{40,56},{48,32},{56,40},{64,80... | collective-permute-start | bytes 786440 | tf_op jit(solution)/shard_map/ppermute | solution.py:40
  77.4 6.8 %all-to-all-done.refs_0_ = bf16[8,64,1152]{2,1,0:T(8,128)(2,1)S(1)} async-done(((bf16[8,64,1152]{2,1,0:T(8,128)(2,1)}), bf16[8,64,1152]{2,1,0:T(8,128)(2,1)S(1)}, u32[]{:S(2)}, u32[]{:S(2)}) %all-to-all-start) | async-done | bytes 1179680 | tf_op jit(solution)/shard_map/all_to_all | solution.py:316
  85.2 8.7 %all-to-all-start.1 = ((bf16[32,18,128]{2,1,0:T(8,128)(2,1)}), bf16[32,18,128]{2,1,0:T(8,128)(2,1)S(1)}, u32[]{:S(2)}, u32[]{:S(2)}) async-start(bf16[32,18,128]{2,1,0:T(8,128)(2,1)} %shard_map.91), calls=%async_computation.1 | async-start | bytes 393216 | tf_op jit(solution)/shard_map/all_to_all | solution.py:322
  95.1 2.4 %collective-permute-start.20 = (bf16[128,1024]{1,0:T(8,128)(2,1)S(1)}, bf16[128,1024]{1,0:T(8,128)(2,1)S(1)}, u32[]{:S(2)}, u32[]{:S(2)}) collective-permute-start(bf16[128,1024]{1,0:T(8,128)(2,1)S(1)} %add_convert_fusion), channel_id=1, source_target_pairs={{0,192},{8,72},{16,208},{24,88},{32,224},{40,104},{48,240},{56,120... | collective-permute-start | bytes 786440 | tf_op jit(solution)/shard_map/ppermute | solution.py:32
  97.4 1.9 %add_convert_fusion.1 = bf16[128,1024]{1,0:T(8,128)(2,1)} fusion(bf16[128,1024]{1,0:T(8,128)(2,1)} %collective-permute-done.15, bf16[128,1024]{1,0:T(8,128)(2,1)} %copy-done.11, bf16[128,1024]{1,0:T(8,128)(2,1)} %get-tuple-element.55), kind=kLoop, calls=%fused_computation.20 | loop fusion | flops 786432 | bytes 1048576 | tf_op jit(solution)/shard_map/convert_element_type | solution.py:338
  101.6 4.1 %all-to-all-done.1.refs_0_ = bf16[32,18,128]{2,1,0:T(8,128)(2,1)S(1)} async-done(((bf16[32,18,128]{2,1,0:T(8,128)(2,1)}), bf16[32,18,128]{2,1,0:T(8,128)(2,1)S(1)}, u32[]{:S(2)}, u32[]{:S(2)}) %all-to-all-start.1) | async-done | bytes 147488 | tf_op jit(solution)/shard_map/all_to_all | solution.py:322
  106.5 3.4 %all-to-all-start.2 = ((f32[8,36,128]{2,1,0:T(8,128)}), f32[8,36,128]{2,1,0:T(8,128)S(1)}, u32[]{:S(2)}, u32[]{:S(2)}) async-start(f32[8,36,128]{2,1,0:T(8,128)} %shard_map.92), calls=%async_computation.2 | async-start | bytes 327680 | tf_op jit(solution)/shard_map/all_to_all | solution.py:340
  110.5 2.5 %collective-permute-done.19 = bf16[128,1024]{1,0:T(8,128)(2,1)S(1)} collective-permute-done((bf16[128,1024]{1,0:T(8,128)(2,1)}, bf16[128,1024]{1,0:T(8,128)(2,1)S(1)}, u32[]{:S(2)}, u32[]{:S(2)}) %collective-permute-start.19) | collective-permute-done | bytes 262176 | tf_op jit(solution)/shard_map/ppermute | solution.py:32
  113.2 3.3 %fusion = bf16[1,128,1152]{2,1,0:T(8,128)(2,1)} fusion(bf16[1152,1024]{1,0:T(8,128)(2,1)} %refs_4_.1, f32[128,1024]{1,0:T(8,128)S(1)} %copy-done.4, bf16[128,1024]{1,0:T(8,128)(2,1)S(1)} %collective-permute-done.18, f32[128]{0:T(128)S(1)} %slice_reduce_fusion, f32[128]{0:T(128)S(1)} %fusion.7, bf16[512,1024]{1,0:T(8,128)(2,1)S(1)} %get-tuple-element.43.refs_2_.refs_4_.refs_1_), kind=kOutput, calls=%fused_computation.1 | convolution fusion | flops 303054848 | bytes 3703808 | tf_op jit(solution)/shard_map/dot_general | solution.py:44
  (74 shorter events, 25.5 us)
Async XLA Ops:
  0.6 9.8 %collective-permute-start = (bf16[128,1152]{1,0:T(8,128)(2,1)}, bf16[128,1152]{1,0:T(8,128)(2,1)S(1)}, u32[]{:S(2)}, u32[]{:S(2)}) collective-permute-start(bf16[128,1152]{1,0:T(8,128)(2,1)} %bitcast.25), channel_id=1, source_target_pairs={{0,16},{8,24},{16,0},{24,8},{32,48},{40,56},{48,32},{56,40},{64,80... | collective-permute-start | bytes 884744 | tf_op jit(solution)/shard_map/ppermute | solution.py:40
  4.5 9.6 %collective-permute-start.5 = (bf16[128,1024]{1,0:T(8,128)(2,1)}, bf16[128,1024]{1,0:T(8,128)(2,1)S(1)}, u32[]{:S(2)}, u32[]{:S(2)}) collective-permute-start(bf16[128,1024]{1,0:T(8,128)(2,1)} %bitcast.22), channel_id=1, source_target_pairs={{0,224},{8,40},{16,240},{24,56},{32,0},{40,72},{48,16},{56,88},{64... | collective-permute-start | bytes 786440 | tf_op jit(solution)/shard_map/ppermute | solution.py:32
  6.1 9.6 %collective-permute-start.7 = (bf16[128,1024]{1,0:T(8,128)(2,1)}, bf16[128,1024]{1,0:T(8,128)(2,1)S(1)}, u32[]{:S(2)}, u32[]{:S(2)}) collective-permute-start(bf16[128,1024]{1,0:T(8,128)(2,1)} %bitcast.23), channel_id=1, source_target_pairs={{0,32},{8,232},{16,48},{24,248},{32,64},{40,8},{48,80},{56,24},{64... | collective-permute-start | bytes 786440 | tf_op jit(solution)/shard_map/ppermute | solution.py:32
  10.5 11.5 %collective-permute-start.3 = (s32[1,128]{1,0:T(1,128)}, s32[1,128]{1,0:T(1,128)S(1)}, u32[]{:S(2)}, u32[]{:S(2)}) collective-permute-start(s32[1,128]{1,0:T(1,128)} %refs_5_.1), channel_id=1, source_target_pairs={{0,16},{8,24},{16,0},{24,8},{32,48},{40,56},{48,32},{56,40},{64,80... | collective-permute-start | bytes 1544 | tf_op jit(solution)/shard_map/ppermute | solution.py:40
  14.1 16.7 %collective-permute-start.6 = (bf16[128,1024]{1,0:T(8,128)(2,1)S(1)}, bf16[128,1024]{1,0:T(8,128)(2,1)}, u32[]{:S(2)}, u32[]{:S(2)}) collective-permute-start(bf16[128,1024]{1,0:T(8,128)(2,1)S(1)} %collective-permute-done.5.refs_5_), channel_id=1, source_target_pairs={{0,224},{8,40},{16,240},{24,56},{32,0},{40,72},{48,16},{56,88},{64... | collective-permute-start | bytes 786440 | tf_op jit(solution)/shard_map/ppermute | solution.py:32
  15.7 15.0 %collective-permute-start.8 = (bf16[128,1024]{1,0:T(8,128)(2,1)S(1)}, bf16[128,1024]{1,0:T(8,128)(2,1)}, u32[]{:S(2)}, u32[]{:S(2)}) collective-permute-start(bf16[128,1024]{1,0:T(8,128)(2,1)S(1)} %collective-permute-done.7.refs_6_), channel_id=1, source_target_pairs={{0,32},{8,232},{16,48},{24,248},{32,64},{40,8},{48,80},{56,24},{64... | collective-permute-start | bytes 786440 | tf_op jit(solution)/shard_map/ppermute | solution.py:32
  19.7 4.1 %collective-permute-start.1 = (bf16[128,1152]{1,0:T(8,128)(2,1)}, bf16[128,1152]{1,0:T(8,128)(2,1)S(1)}, u32[]{:S(2)}, u32[]{:S(2)}) collective-permute-start(bf16[128,1152]{1,0:T(8,128)(2,1)} %bitcast.26), channel_id=1, source_target_pairs={{0,8},{8,0},{16,24},{24,16},{32,40},{40,32},{48,56},{56,48},{64,72... | collective-permute-start | bytes 884744 | tf_op jit(solution)/shard_map/ppermute | solution.py:36
  21.8 2.0 %collective-permute-start.2 = (bf16[128,1152]{1,0:T(8,128)(2,1)S(1)}, bf16[128,1152]{1,0:T(8,128)(2,1)S(1)}, u32[]{:S(2)}, u32[]{:S(2)}) collective-permute-start(bf16[128,1152]{1,0:T(8,128)(2,1)S(1)} %collective-permute-done.refs_2_.refs_8_), channel_id=1, source_target_pairs={{0,8},{8,0},{16,24},{24,16},{32,40},{40,32},{48,56},{56,48},{64,72... | collective-permute-start | bytes 884744 | tf_op jit(solution)/shard_map/ppermute | solution.py:36
  22.6 1.2 %collective-permute-start.4 = (s32[2,128]{1,0:T(2,128)S(1)}, s32[2,128]{1,0:T(2,128)S(1)}, u32[]{:S(2)}, u32[]{:S(2)}) collective-permute-start(s32[2,128]{1,0:T(2,128)S(1)} %pad_add_fusion), channel_id=1, source_target_pairs={{0,8},{8,0},{16,24},{24,16},{32,40},{40,32},{48,56},{56,48},{64,72... | collective-permute-start | bytes 3080 | tf_op jit(solution)/shard_map/ppermute | solution.py:36
  30.7 13.0 %collective-permute-start.9 = (bf16[128,1024]{1,0:T(8,128)(2,1)}, bf16[128,1024]{1,0:T(8,128)(2,1)}, u32[]{:S(2)}, u32[]{:S(2)}) collective-permute-start(bf16[128,1024]{1,0:T(8,128)(2,1)} %collective-permute-done.8.refs_8_), channel_id=1, source_target_pairs={{0,32},{8,232},{16,48},{24,248},{32,64},{40,8},{48,80},{56,24},{64... | collective-permute-start | bytes 786440 | tf_op jit(solution)/shard_map/ppermute | solution.py:32
  35.2 11.4 %collective-permute-start.11 = (bf16[128,1024]{1,0:T(8,128)(2,1)}, bf16[128,1024]{1,0:T(8,128)(2,1)}, u32[]{:S(2)}, u32[]{:S(2)}) collective-permute-start(bf16[128,1024]{1,0:T(8,128)(2,1)} %collective-permute-done.6.refs_7_), channel_id=1, source_target_pairs={{0,224},{8,40},{16,240},{24,56},{32,0},{40,72},{48,16},{56,88},{64... | collective-permute-start | bytes 786440 | tf_op jit(solution)/shard_map/ppermute | solution.py:32
  43.7 7.6 %collective-permute-start.10 = (bf16[128,1024]{1,0:T(8,128)(2,1)}, bf16[128,1024]{1,0:T(8,128)(2,1)}, u32[]{:S(2)}, u32[]{:S(2)}) collective-permute-start(bf16[128,1024]{1,0:T(8,128)(2,1)} %collective-permute-done.9.refs_5_), channel_id=1, source_target_pairs={{0,32},{8,232},{16,48},{24,248},{32,64},{40,8},{48,80},{56,24},{64... | collective-permute-start | bytes 786440 | tf_op jit(solution)/shard_map/ppermute | solution.py:32
  54.7 3.2 %collective-permute-start.12 = (bf16[512,896]{1,0:T(8,128)(2,1)S(1)}, bf16[512,896]{1,0:T(8,128)(2,1)S(1)}, u32[]{:S(2)}, u32[]{:S(2)}) collective-permute-start(bf16[512,896]{1,0:T(8,128)(2,1)S(1)} %get-tuple-element.50), channel_id=1, source_target_pairs={{0,8},{8,0},{16,24},{24,16},{32,40},{40,32},{48,56},{56,48},{64,72... | collective-permute-start | bytes 2752520 | tf_op jit(solution)/shard_map/ppermute | solution.py:36
  62.0 22.1 %all-to-all-start = ((bf16[8,64,1152]{2,1,0:T(8,128)(2,1)}), bf16[8,64,1152]{2,1,0:T(8,128)(2,1)S(1)}, u32[]{:S(2)}, u32[]{:S(2)}) async-start(bf16[8,64,1152]{2,1,0:T(8,128)(2,1)} %get-tuple-element.67), calls=%async_computation | async-start | bytes 2359296 | tf_op jit(solution)/shard_map/all_to_all | solution.py:316
  67.4 7.0 %collective-permute-start.13 = (bf16[128,1024]{1,0:T(8,128)(2,1)S(1)}, bf16[128,1024]{1,0:T(8,128)(2,1)S(1)}, u32[]{:S(2)}, u32[]{:S(2)}) collective-permute-start(bf16[128,1024]{1,0:T(8,128)(2,1)S(1)} %copy-done.12), channel_id=1, source_target_pairs={{0,32},{8,232},{16,48},{24,248},{32,64},{40,8},{48,80},{56,24},{64... | collective-permute-start | bytes 786440 | tf_op jit(solution)/shard_map/ppermute | solution.py:32
  68.7 25.3 %collective-permute-start.14 = (bf16[128,1024]{1,0:T(8,128)(2,1)}, bf16[128,1024]{1,0:T(8,128)(2,1)}, u32[]{:S(2)}, u32[]{:S(2)}) collective-permute-start(bf16[128,1024]{1,0:T(8,128)(2,1)} %get-tuple-element.62), channel_id=1, source_target_pairs={{0,224},{8,40},{16,240},{24,56},{32,0},{40,72},{48,16},{56,88},{64... | collective-permute-start | bytes 786440 | tf_op jit(solution)/shard_map/ppermute | solution.py:32
  68.9 25.0 %collective-permute-start.15 = (bf16[128,1024]{1,0:T(8,128)(2,1)}, bf16[128,1024]{1,0:T(8,128)(2,1)}, u32[]{:S(2)}, u32[]{:S(2)}) collective-permute-start(bf16[128,1024]{1,0:T(8,128)(2,1)} %shard_map.90), channel_id=1, source_target_pairs={{0,64},{8,200},{16,80},{24,216},{32,96},{40,232},{48,112},{56,248}... | collective-permute-start | bytes 786440 | tf_op jit(solution)/shard_map/ppermute | solution.py:32
  70.2 23.8 %collective-permute-start.16 = (bf16[128,1024]{1,0:T(8,128)(2,1)}, bf16[128,1024]{1,0:T(8,128)(2,1)S(1)}, u32[]{:S(2)}, u32[]{:S(2)}) collective-permute-start(bf16[128,1024]{1,0:T(8,128)(2,1)} %get-tuple-element.64), channel_id=1, source_target_pairs={{0,32},{8,232},{16,48},{24,248},{32,64},{40,8},{48,80},{56,24},{64... | collective-permute-start | bytes 786440 | tf_op jit(solution)/shard_map/ppermute | solution.py:32
  71.4 22.6 %collective-permute-start.17 = (bf16[128,1024]{1,0:T(8,128)(2,1)}, bf16[128,1024]{1,0:T(8,128)(2,1)}, u32[]{:S(2)}, u32[]{:S(2)}) collective-permute-start(bf16[128,1024]{1,0:T(8,128)(2,1)} %get-tuple-element.65), channel_id=1, source_target_pairs={{0,224},{8,40},{16,240},{24,56},{32,0},{40,72},{48,16},{56,88},{64... | collective-permute-start | bytes 786440 | tf_op jit(solution)/shard_map/ppermute | solution.py:32
  75.1 18.9 %collective-permute-start.18 = (bf16[128,1024]{1,0:T(8,128)(2,1)}, bf16[128,1024]{1,0:T(8,128)(2,1)S(1)}, u32[]{:S(2)}, u32[]{:S(2)}) collective-permute-start(bf16[128,1024]{1,0:T(8,128)(2,1)} %get-tuple-element.66), channel_id=1, source_target_pairs={{0,16},{8,24},{16,0},{24,8},{32,48},{40,56},{48,32},{56,40},{64,80... | collective-permute-start | bytes 786440 | tf_op jit(solution)/shard_map/ppermute | solution.py:40
  85.2 20.6 %all-to-all-start.1 = ((bf16[32,18,128]{2,1,0:T(8,128)(2,1)}), bf16[32,18,128]{2,1,0:T(8,128)(2,1)S(1)}, u32[]{:S(2)}, u32[]{:S(2)}) async-start(bf16[32,18,128]{2,1,0:T(8,128)(2,1)} %shard_map.91), calls=%async_computation.1 | async-start | bytes 393216 | tf_op jit(solution)/shard_map/all_to_all | solution.py:322
  95.1 15.5 %collective-permute-start.20 = (bf16[128,1024]{1,0:T(8,128)(2,1)S(1)}, bf16[128,1024]{1,0:T(8,128)(2,1)S(1)}, u32[]{:S(2)}, u32[]{:S(2)}) collective-permute-start(bf16[128,1024]{1,0:T(8,128)(2,1)S(1)} %add_convert_fusion), channel_id=1, source_target_pairs={{0,192},{8,72},{16,208},{24,88},{32,224},{40,104},{48,240},{56,120... | collective-permute-start | bytes 786440 | tf_op jit(solution)/shard_map/ppermute | solution.py:32
  99.4 13.6 %collective-permute-start.19 = (bf16[128,1024]{1,0:T(8,128)(2,1)}, bf16[128,1024]{1,0:T(8,128)(2,1)S(1)}, u32[]{:S(2)}, u32[]{:S(2)}) collective-permute-start(bf16[128,1024]{1,0:T(8,128)(2,1)} %add_convert_fusion.1), channel_id=1, source_target_pairs={{0,64},{8,200},{16,80},{24,216},{32,96},{40,232},{48,112},{56,248}... | collective-permute-start | bytes 786440 | tf_op jit(solution)/shard_map/ppermute | solution.py:32
  106.5 12.3 %all-to-all-start.2 = ((f32[8,36,128]{2,1,0:T(8,128)}), f32[8,36,128]{2,1,0:T(8,128)S(1)}, u32[]{:S(2)}, u32[]{:S(2)}) async-start(f32[8,36,128]{2,1,0:T(8,128)} %shard_map.92), calls=%async_computation.2 | async-start | bytes 327680 | tf_op jit(solution)/shard_map/all_to_all | solution.py:340
  (13 other events, 114.1 us)

commit v7 on v6

--- a/solution.py
+++ b/solution.py
@@ -10,6 +10,7 @@
 Z, YH, CORE = 8, 2, 2
 LOOP = Z * YH * CORE
 DP = 8
+CUT = 640
 BF16 = jnp.bfloat16
 F32 = jnp.float32
 VMEM = pl.BlockSpec(memory_space=pltpu.VMEM)
@@ -49,8 +50,9 @@
 
 
 class Moves:
-    def __init__(self, sems, loads, held, outs):
-        self.sems, self.loads, self.held, self.outs, self.sent = sems, loads, held, outs, []
+    def __init__(self, base, sems, loads, held, outs, pack):
+        self.base = base
+        self.sems, self.loads, self.held, self.outs, self.pack, self.sent = sems, loads, held, outs, pack, []
 
     def need(self, n):
         self.loads[n].wait()
@@ -59,32 +61,45 @@
         source, target = self.held[n], self.outs[n]
         if part is not None:
             source, target = source.at[part], target.at[part]
-        copy = pltpu.make_async_copy(source, target, self.sems.at[len(self.loads) + len(self.sent)])
+        copy = pltpu.make_async_copy(source, target, self.sems.at[self.base + len(self.sent)])
         copy.start()
         self.sent.append(copy)
 
 
-def call(kernel, out, aliases, *operands, far=(), far_out=(), sends=None):
-    far, far_out, total = list(far), list(far_out), len(operands)
+def call(kernel, out, aliases, *operands, far=(), packed=(), far_out=(), sends=None, cuts=()):
+    cuts = dict(cuts)
+    far, packed, far_out, total = list(far), list(packed), list(far_out), len(operands)
     sends = len(far_out) if sends is None else sends
 
     def body(*refs):
         ins, outs, scratch = refs[:total], refs[total : total + len(out)], refs[total + len(out) :]
         held = dict(zip(far, scratch[: len(far)]))
-        held_out = dict(zip(far_out, scratch[len(far) : -1]))
-        loads = {n: pltpu.make_async_copy(ins[n], held[n], scratch[-1].at[m]) for m, n in enumerate(far)}
+        held_out = dict(zip(far_out, scratch[len(far) : len(far) + len(far_out)]))
+        for m, n in enumerate(packed):
+            height = operands[n].shape[0]
+            held[n] = scratch[-2].at[pl.ds(m * height, height)]
+        whole = [(m, n) for m, n in enumerate(in_hbm) if n not in cuts]
+        loads = {n: pltpu.make_async_copy(ins[n], held[n], scratch[-1].at[m]) for m, n in whole}
+        for n, cut in cuts.items():
+            for m, part in enumerate((pl.ds(0, cut), pl.ds(cut, operands[n].shape[0] - cut))):
+                sem = scratch[-1].at[len(in_hbm) + sends] if m else scratch[-1].at[far.index(n)]
+                loads[n, m] = pltpu.make_async_copy(ins[n].at[part], held[n].at[part], sem)
         for load in loads.values():
             load.start()
-        moves = Moves(scratch[-1], loads, held_out, outs)
+        moves = Moves(len(in_hbm), scratch[-1], loads, held_out, outs, scratch[-2] if packed else None)
         kernel(moves, *(held.get(n, ref) for n, ref in enumerate(ins)), *(held_out.get(n, ref) for n, ref in enumerate(outs)))
         for copy in moves.sent:
             copy.wait()
 
-    in_specs = [SMEM if o.ndim == 1 else HBM if n in far else VMEM for n, o in enumerate(operands)]
+    in_hbm = far + packed
+    in_specs = [SMEM if o.ndim == 1 else HBM if n in in_hbm else VMEM for n, o in enumerate(operands)]
     scratch = [pltpu.VMEM(operands[n].shape, operands[n].dtype) for n in far]
     scratch += [pltpu.VMEM(out[n].shape, out[n].dtype) for n in far_out]
-    scratch.append(pltpu.SemaphoreType.DMA((max(1, len(far) + sends),)))
-    operands = [pltpu.with_memory_space_constraint(o, pltpu.HBM) if n in far else o for n, o in enumerate(operands)]
+    if packed:
+        height, width = operands[packed[0]].shape
+        scratch.append(pltpu.VMEM((len(packed) * height, width), operands[packed[0]].dtype))
+    scratch.append(pltpu.SemaphoreType.DMA((len(in_hbm) + sends + 1,)))
+    operands = [pltpu.with_memory_space_constraint(o, pltpu.HBM) if n in in_hbm else o for n, o in enumerate(operands)]
     return pl.pallas_call(
         body,
         out_shape=[pltpu.HBM(o.shape, o.dtype) if n in far_out else o for n, o in enumerate(out)],
@@ -97,14 +112,17 @@
     )(*operands)
 
 
-def block_grads(numbers, start, image_emb, match, text):
+def block_grads(numbers, columns, image_emb, match, text):
     wide = text.astype(F32)
     inv = lax.rsqrt(jnp.sum(wide * wide, -1, keepdims=True) + 1e-06)
     emb = (wide * inv).astype(BF16)
     logits = numbers[0] * inner_rows(image_emb, emb) + numbers[1]
-    column = lax.broadcasted_iota(jnp.int32, logits.shape, 1) + start
-    positive = (match == column.astype(F32)).astype(F32)
+    positive = (match == columns).astype(F32)
     return emb, (jax.nn.sigmoid(logits) - positive).astype(BF16)
+
+
+def columns_of(start, rows):
+    return (lax.broadcasted_iota(jnp.int32, (1, rows), 1) + start).astype(F32)
 
 
 def pairs_kernel(count, first, moves, numbers, starts, image_emb, match, *refs):
@@ -113,35 +131,40 @@
         acc_in, refs = refs[0], refs[1:]
     acc_out, text_out = refs[0], refs[1:]
     image = image_emb[...]
-    embs, grads = [], []
+    rows = texts[0].shape[0]
+    columns = jnp.concatenate([columns_of(starts[n], rows) for n in range(count)], 1)
     for n in range(count):
         moves.need(4 + n)
-        emb, grad = block_grads(numbers, starts[n], image, match[...], texts[n][...])
-        embs.append(emb)
-        grads.append(grad)
-        text_out[n][...] = inner_cols(grad, image).astype(text_out[n].dtype)
+    emb, grad = block_grads(numbers, columns, image, match[...], moves.pack[...])
+    text_part = inner_cols(grad, image)
+    for n in range(count):
+        text_out[n][...] = text_part[n * rows : (n + 1) * rows].astype(text_out[n].dtype)
         moves.send(1 + n)
-    part = jnp.dot(jnp.concatenate(grads, 1), jnp.concatenate(embs, 0), preferred_element_type=F32)
+    part = jnp.dot(grad, emb, preferred_element_type=F32)
     acc_out[...] = part if first else acc_in[...] + part
 
 
-def project_kernel(moves, own, core, yh, both, proj_weight, *refs):
+def project_kernel(moves, proj_weight, own, core, yh, both, *refs):
     matches, (emb, inv_out, match_out) = refs[:4], refs[4:]
-    rows = own.shape[0]
-    moves.need(4)
-    for n, sensor in enumerate((own, core, yh, both)):
-        here = slice(n * rows, (n + 1) * rows)
-        moves.need(n)
-        projected = jnp.dot(sensor[...], proj_weight[...], preferred_element_type=F32)
-        inv = lax.rsqrt(jnp.sum(projected * projected, -1, keepdims=True) + 1e-06)
-        emb[here, :] = (projected * inv).astype(BF16)
-        inv_out[here, :] = inv
+    rows, cut = own.shape[0], CUT
+    for n in range(4):
+        moves.need(1 + n)
+    sensor = moves.pack[...]
+    moves.need((0, 0))
+    projected = jnp.dot(sensor[:, :cut], proj_weight[:cut], preferred_element_type=F32)
+    moves.need((0, 1))
+    projected = projected + jnp.dot(sensor[:, cut:], proj_weight[cut:], preferred_element_type=F32)
+    inv = lax.rsqrt(jnp.sum(projected * projected, -1, keepdims=True) + 1e-06)
+    emb[...] = (projected * inv).astype(BF16)
+    inv_out[...] = inv
+    for n in range(4):
         match = jnp.broadcast_to(matches[n][...].astype(F32), (rows, rows))
-        match_out[here, :] = match.T[:, 0:1]
+        match_out[n * rows : (n + 1) * rows, :] = match.T[:, 0:1]
 
 
 def last_kernel(moves, numbers, starts, image_emb, match, text, acc_in, acc_out, dot_out, packet, grad_out):
-    emb, grad = block_grads(numbers, starts[0], image_emb[...], match[...], text[...])
+    columns = columns_of(starts[0], text.shape[0])
+    emb, grad = block_grads(numbers, columns, image_emb[...], match[...], text[...])
     grad_out[...] = grad
     acc = numbers[0] * (acc_in[...] + jnp.dot(grad, emb, preferred_element_type=F32))
     acc_out[...] = acc
@@ -194,12 +217,12 @@
     proj = jnp.concatenate(projs, 0)
     for n in range(6, 10):
         moves.need(n)
-    sensor = jnp.concatenate([own_rows[...], core_rows[...], yh_rows[...], both_rows[...]], 0)
+    sensor = moves.pack[...]
     chunk = weight.shape[1]
-    for n in range(half // 128):
-        product = inner_cols(proj[:, n * 128 : (n + 1) * 128], sensor).astype(BF16)
-        for m in range(128 // chunk):
-            at = n * (128 // chunk) + m
+    for side in range(2):
+        product = inner_cols(proj[:, side * quarter : (side + 1) * quarter], sensor).astype(BF16)
+        for m in range(quarter // chunk):
+            at = side * (quarter // chunk) + m
             weight[at] = product[m * chunk : (m + 1) * chunk]
             moves.send(0, at)
 
@@ -253,20 +276,26 @@
     numbers = jnp.stack([logit_scale, logit_bias])
 
     slot = {0: texts}
-    for k in (1, 2):
-        slot[k] = shift_z(slot[k - 1], -1)
-        slot[-k] = shift_z(slot[1 - k], 1)
+    slot[1], slot[-1] = shift_z(texts, -1), shift_z(texts, 1)
 
     sensor_yh = swap_yh(sensor)
     match = matches.reshape(1, rows)
-    sensor_later, match_later, _ = lax.optimization_barrier((sensor, match, sensor_yh))
+    match_yh = swap_yh(match)
+    up, down, _, _ = lax.optimization_barrier((slot[1], slot[-1], sensor_yh, match_yh))
+    slot[2], slot[-2] = shift_z(up, -1), shift_z(down, 1)
+    sensor_later, _ = lax.optimization_barrier((sensor, sensor_yh))
     sensors = [sensor, swap_core(sensor_later), sensor_yh, swap_core(sensor_yh)]
-    match_yh = swap_yh(match_later)
     match_both = swap_core(jnp.concatenate([match, match_yh], 0))
     match = [match, match_both[:1], match_yh, match_both[1:]]
     shapes = [((4 * rows, width), BF16), ((4 * rows, 1), F32), ((4 * rows, 1), F32)]
     image_emb, image_inv, match_rows = call(
-        project_kernel, [jax.ShapeDtypeStruct(*s) for s in shapes], {}, *sensors, proj_weight, *match, far=range(5)
+        project_kernel,
+        [jax.ShapeDtypeStruct(*s) for s in shapes],
+        {},
+        proj_weight, *sensors, *match,
+        far=(0,),
+        packed=range(1, 5),
+        cuts={0: CUT},
     )
     up, down, _ = lax.optimization_barrier((slot[2], slot[-2], image_emb))
     slot[3], slot[-3] = shift_z(up, -1), shift_z(down, 1)
@@ -284,8 +313,7 @@
             aliases = {len(operands): 0}
             operands.append(acc)
         kernel = functools.partial(pairs_kernel, len(keys), acc is None)
-        far = range(4, 4 + len(keys))
-        return call(kernel, out, aliases, *operands, far=far, far_out=range(1, len(out)))
+        return call(kernel, out, aliases, *operands, packed=range(4, 4 + len(keys)), far_out=range(1, len(out)))
 
     acc, text_0, text_1, text_m1, text_2, text_m2 = pairs((0, 1, -1, 2, -2), (F32, BF16, BF16, BF16, BF16), None)
     last_text, _ = lax.optimization_barrier((slot[-3], acc))
@@ -309,7 +337,7 @@
         [jax.ShapeDtypeStruct(*s) for s in shapes],
         {},
         starts, swap_core(packet), acc, dot, image_emb, image_inv, *sensors,
-        far=range(6, 10),
+        packed=range(6, 10),
         far_out=range(3),
         sends=2 + DP,
     )

time: 120 us -> 115 us (0.958)
  starting transfers between devices: 55.6 us -> 50.6 us
  Pallas kernels: 28.7 us -> 24.3 us
  waiting for transfers between devices: 19.3 us -> 23.1 us
    ppermute x3, starting transfers between devices: 9.56 us -> 5.07 us  [swap_yh(): return lax.ppermute(block, 'loop', route(lambda z, y, c: (z, 1 - y, c)))]
    pallas_call x9, Pallas kernels: 28.7 us -> 24.3 us  [call(): pl.pallas_call(body, out_shape=[pltpu.HBM(o.shape, o.dtype) if n in far_o...]
    ppermute x4, starting transfers between devices: 3.72 us -> 7.01 us  [swap_core(): return lax.ppermute(block, 'loop', route(lambda z, y, c: (z, y, 1 - c)))]
    ppermute x14, starting transfers between devices: 25.9 us -> 22.9 us  [shift_z(): lax.ppermute(block, 'loop', route(lambda z, y, c: (z + (1 - 2 * c) * dist...]
    ppermute x14, waiting for transfers between devices: 4.98 us -> 7 us  [shift_z(): lax.ppermute(block, 'loop', route(lambda z, y, c: (z + (1 - 2 * c) * dist...]
    ppermute x3, waiting for transfers between devices: 0.42 us -> 1.66 us  [swap_yh(): return lax.ppermute(block, 'loop', route(lambda z, y, c: (z, 1 - y, c)))]
  transfers between devices with their start and end apart: 24 -> 24, of which waited for: 8 -> 10; matrix products, arithmetic and copies ran while one was open for 9% -> 10% of each run, Pallas kernels for 17% -> 14%
where the time goes in v7:
time: 115 us; the launch traced here: 114 us
  starting transfers between devices  50.6 us (44%)
  Pallas kernels  24.3 us (21%)
  waiting for transfers between devices  23.1 us (20%)
  other arithmetic  6.52 us (6%)
  local copies, waits for them, and re-layouts  3.93 us (3%)
  matrix products  3.34 us (3%)
  between operations  2.4 us (2%)
    pallas_call x9, Pallas kernels, call(): pl.pallas_call(body, out_shape=[pltpu.HBM(o.shape, o.dtype) if n in far_o...  24.3 us
    ppermute x14, starting transfers between devices, shift_z(): lax.ppermute(block, 'loop', route(lambda z, y, c: (z + (1 - 2 * c) * dist...  22.9 us
    all_to_all x1, starting transfers between devices, on_device(): weight_part = lax.all_to_all(weight_chunks, 'loop', 0, 0, tiled=True)  7.91 us
    all_to_all x1, waiting for transfers between devices, on_device(): weight_part = lax.all_to_all(weight_part, 'dp', 0, 0, tiled=True)  7.08 us
    ppermute x4, starting transfers between devices, swap_core(): return lax.ppermute(block, 'loop', route(lambda z, y, c: (z, y, 1 - c)))  7.01 us
    ppermute x14, waiting for transfers between devices, shift_z(): lax.ppermute(block, 'loop', route(lambda z, y, c: (z + (1 - 2 * c) * dist...  7 us
    ppermute x3, starting transfers between devices, swap_yh(): return lax.ppermute(block, 'loop', route(lambda z, y, c: (z, 1 - y, c)))  5.07 us
    all_to_all x1, starting transfers between devices, on_device(): weight_part = lax.all_to_all(weight_part, 'dp', 0, 0, tiled=True)  4.27 us
  transfers between devices with their start and end apart: 24, of which 10 were waited for; matrix products, arithmetic and copies ran while one was open for 10% of the time, Pallas kernels for 14%

profile of v7, /device:TPU:1, one launch (start us, length us, event | category | flops | bytes accessed | tf_op | source)
XLA Modules:
  0.0 114.1 jit_solution(16914595022207122576)
XLA Ops:
  0.6 3.8 %collective-permute-start = (bf16[128,1152]{1,0:T(8,128)(2,1)}, bf16[128,1152]{1,0:T(8,128)(2,1)S(1)}, u32[]{:S(2)}, u32[]{:S(2)}) collective-permute-start(bf16[128,1152]{1,0:T(8,128)(2,1)} %bitcast.25), channel_id=1, source_target_pairs={{0,16},{8,24},{16,0},{24,8},{32,48},{40,56},{48,32},{56,40},{64,80... | collective-permute-start | bytes 884744 | tf_op jit(solution)/shard_map/ppermute | solution.py:41
  6.1 3.9 %collective-permute-start.6 = (bf16[128,1024]{1,0:T(8,128)(2,1)}, bf16[128,1024]{1,0:T(8,128)(2,1)S(1)}, u32[]{:S(2)}, u32[]{:S(2)}) collective-permute-start(bf16[128,1024]{1,0:T(8,128)(2,1)} %bitcast.23), channel_id=1, source_target_pairs={{0,32},{8,232},{16,48},{24,248},{32,64},{40,8},{48,80},{56,24},{64... | collective-permute-start | bytes 786440 | tf_op jit(solution)/shard_map/ppermute | solution.py:33
  10.5 2.2 %collective-permute-start.1 = (bf16[128,1152]{1,0:T(8,128)(2,1)}, bf16[128,1152]{1,0:T(8,128)(2,1)S(1)}, u32[]{:S(2)}, u32[]{:S(2)}) collective-permute-start(bf16[128,1152]{1,0:T(8,128)(2,1)} %bitcast.26), channel_id=1, source_target_pairs={{0,8},{8,0},{16,24},{24,16},{32,40},{40,32},{48,56},{56,48},{64,72... | collective-permute-start | bytes 884744 | tf_op jit(solution)/shard_map/ppermute | solution.py:37
  16.1 2.4 %collective-permute-start.8 = (bf16[128,1024]{1,0:T(8,128)(2,1)S(1)}, bf16[128,1024]{1,0:T(8,128)(2,1)}, u32[]{:S(2)}, u32[]{:S(2)}) collective-permute-start(bf16[128,1024]{1,0:T(8,128)(2,1)S(1)} %collective-permute-done.6.refs_6_), channel_id=1, source_target_pairs={{0,32},{8,232},{16,48},{24,248},{32,64},{40,8},{48,80},{56,24},{64... | collective-permute-start | bytes 786440 | tf_op jit(solution)/shard_map/ppermute | solution.py:33
  18.5 2.6 %collective-permute-start.2 = (bf16[128,1152]{1,0:T(8,128)(2,1)S(1)}, bf16[128,1152]{1,0:T(8,128)(2,1)S(1)}, u32[]{:S(2)}, u32[]{:S(2)}) collective-permute-start(bf16[128,1152]{1,0:T(8,128)(2,1)S(1)} %collective-permute-done.refs_3_.refs_8_), channel_id=1, source_target_pairs={{0,8},{8,0},{16,24},{24,16},{32,40},{40,32},{48,56},{56,48},{64,72... | collective-permute-start | bytes 884744 | tf_op jit(solution)/shard_map/ppermute | solution.py:37
  24.4 3.7 %shard_map.85 = (bf16[512,1024]{1,0:T(8,128)(2,1)S(1)}, f32[512,1]{1,0:T(8,128)S(1)}, f32[512,1]{1,0:T(8,128)S(1)}) custom-call(bf16[1152,1024]{1,0:T(8,128)(2,1)} %refs_0_.1, bf16[128,1152]{1,0:T(8,128)(2,1)} %bitcast.27, bf16[128,1152]{1,0:T(8,128)(2,1)} %copy-done.6, bf16[128,1152]{1,0:T(8,128)(2,1)} %copy-done.5, bf16[128,1152]{1,0:T(8,128)(2,1)} %copy-done.7, ...), custom_call_target="tpu_custom_call" | custom-call | flops 1 | bytes 1 | tf_op jit(solution)/shard_map/pallas_call | solution.py:103
  28.8 2.5 %collective-permute-start.9 = (bf16[128,1024]{1,0:T(8,128)(2,1)}, bf16[128,1024]{1,0:T(8,128)(2,1)}, u32[]{:S(2)}, u32[]{:S(2)}) collective-permute-start(bf16[128,1024]{1,0:T(8,128)(2,1)} %collective-permute-done.8.refs_8_), channel_id=1, source_target_pairs={{0,32},{8,232},{16,48},{24,248},{32,64},{40,8},{48,80},{56,24},{64... | collective-permute-start | bytes 786440 | tf_op jit(solution)/shard_map/ppermute | solution.py:33
  32.8 5.4 %shard_map.86 = (f32[512,1024]{1,0:T(8,128)S(1)}, f32[128,1024]{1,0:T(8,128)}, bf16[128,1024]{1,0:T(8,128)(2,1)}, bf16[128,1024]{1,0:T(8,128)(2,1)}, bf16[128,10...) custom-call(f32[2]{0:T(128)S(1)} %pad_maximum_fusion.refs_0_, s32[5]{0:T(128)S(1)} %stack.56.refs_1_, ...), custom_call_target="tpu_custom_call" | custom-call | flops 1 | bytes 1 | tf_op jit(solution)/shard_map/pallas_call | solution.py:103
  38.3 2.9 %collective-permute-start.10 = (bf16[128,1024]{1,0:T(8,128)(2,1)}, bf16[128,1024]{1,0:T(8,128)(2,1)}, u32[]{:S(2)}, u32[]{:S(2)}) collective-permute-start(bf16[128,1024]{1,0:T(8,128)(2,1)} %collective-permute-done.9.refs_5_), channel_id=1, source_target_pairs={{0,32},{8,232},{16,48},{24,248},{32,64},{40,8},{48,80},{56,24},{64... | collective-permute-start | bytes 786440 | tf_op jit(solution)/shard_map/ppermute | solution.py:33
  41.4 3.9 %shard_map.87 = (f32[512,1024]{1,0:T(8,128)S(1)}, bf16[128,1024]{1,0:T(8,128)(2,1)}, bf16[128,1024]{1,0:T(8,128)(2,1)}) custom-call(f32[2]{0:T(128)S(1)} %pad_maximum_fusion.refs_0_, s32[2]{0:T(128)S(1)} %pad_add_fusion.2.refs_1_, bf16[512,1024]{1,0:T(8,128)(2,1)S(1)} %get-tuple-element.43.refs_2_.refs_4_.refs_1_, ...), custom_call_target="tpu_custom_call", output_to_operand_aliasing={{0}: (6, {})} | custom-call | flops 1 | bytes 1 | tf_op jit(solution)/shard_map/pallas_call | solution.py:103
  45.3 3.4 %shard_map.88 = (f32[512,1024]{1,0:T(8,128)S(1)}, f32[512,1]{1,0:T(8,128)S(1)}, bf16[512,896]{1,0:T(8,128)(2,1)S(1)}, bf16[512,128]{1,0:T(8,128)(2,1)S(1)}) custom-call(f32[2]{0:T(128)S(1)} %pad_maximum_fusion.refs_0_, s32[2]{0:T(128)S(1)} %pad_add_fusion.1.refs_1_.refs_0_, ...), custom_call_target="tpu_custom_call", output_to_operand_aliasing={{0}: (5, {})} | custom-call | flops 1 | bytes 1 | tf_op jit(solution)/shard_map/pallas_call | solution.py:103
  48.7 2.2 %collective-permute-start.12 = (bf16[512,896]{1,0:T(8,128)(2,1)S(1)}, bf16[512,896]{1,0:T(8,128)(2,1)S(1)}, u32[]{:S(2)}, u32[]{:S(2)}) collective-permute-start(bf16[512,896]{1,0:T(8,128)(2,1)S(1)} %get-tuple-element.52), channel_id=1, source_target_pairs={{0,8},{8,0},{16,24},{24,16},{32,40},{40,32},{48,56},{56,48},{64,72... | collective-permute-start | bytes 2752520 | tf_op jit(solution)/shard_map/ppermute | solution.py:37
  50.9 2.1 %collective-permute-done.12.refs_1_ = bf16[512,896]{1,0:T(8,128)(2,1)S(1)} collective-permute-done((bf16[512,896]{1,0:T(8,128)(2,1)S(1)}, bf16[512,896]{1,0:T(8,128)(2,1)S(1)}, u32[]{:S(2)}, u32[]{:S(2)}) %collective-permute-start.12) | collective-permute-done | bytes 917536 | tf_op jit(solution)/shard_map/ppermute | solution.py:37
  53.0 4.2 %shard_map.89 = (bf16[8,64,1152]{2,1,0:T(8,128)(2,1)}, bf16[128,1024]{1,0:T(8,128)(2,1)}, f32[128,1024]{1,0:T(8,128)}) custom-call(s32[2]{0:T(128)S(1)} %pad_add_fusion.1.refs_1_.refs_0_, bf16[512,896]{1,0:T(8,128)(2,1)S(1)} %collective-permute-done.12.refs_1_, f32[512,1024]{1,0:T(8,128)S(1)} %get-tuple-element.53.refs_2_, ...), custom_call_target="tpu_custom_call" | custom-call | flops 1 | bytes 1 | tf_op jit(solution)/shard_map/pallas_call | solution.py:103
  57.2 4.3 %all-to-all-start = ((bf16[8,64,1152]{2,1,0:T(8,128)(2,1)}), bf16[8,64,1152]{2,1,0:T(8,128)(2,1)S(1)}, u32[]{:S(2)}, u32[]{:S(2)}) async-start(bf16[8,64,1152]{2,1,0:T(8,128)(2,1)} %get-tuple-element.69), calls=%async_computation | async-start | bytes 2359296 | tf_op jit(solution)/shard_map/all_to_all | solution.py:344
  67.4 2.9 %collective-permute-done.13 = bf16[128,1024]{1,0:T(8,128)(2,1)S(1)} collective-permute-done((bf16[128,1024]{1,0:T(8,128)(2,1)S(1)}, bf16[128,1024]{1,0:T(8,128)(2,1)S(1)}, u32[]{:S(2)}, u32[]{:S(2)}) %collective-permute-start.13) | collective-permute-done | bytes 262176 | tf_op jit(solution)/shard_map/ppermute | solution.py:33
  72.2 7.1 %all-to-all-done.refs_0_ = bf16[8,64,1152]{2,1,0:T(8,128)(2,1)S(1)} async-done(((bf16[8,64,1152]{2,1,0:T(8,128)(2,1)}), bf16[8,64,1152]{2,1,0:T(8,128)(2,1)S(1)}, u32[]{:S(2)}, u32[]{:S(2)}) %all-to-all-start) | async-done | bytes 1179680 | tf_op jit(solution)/shard_map/all_to_all | solution.py:344
  80.4 7.9 %all-to-all-start.1 = ((bf16[32,18,128]{2,1,0:T(8,128)(2,1)}), bf16[32,18,128]{2,1,0:T(8,128)(2,1)S(1)}, u32[]{:S(2)}, u32[]{:S(2)}) async-start(bf16[32,18,128]{2,1,0:T(8,128)(2,1)} %shard_map.91), calls=%async_computation.1 | async-start | bytes 393216 | tf_op jit(solution)/shard_map/all_to_all | solution.py:350
  89.4 2.4 %collective-permute-start.20 = (bf16[128,1024]{1,0:T(8,128)(2,1)S(1)}, bf16[128,1024]{1,0:T(8,128)(2,1)S(1)}, u32[]{:S(2)}, u32[]{:S(2)}) collective-permute-start(bf16[128,1024]{1,0:T(8,128)(2,1)S(1)} %add_convert_fusion), channel_id=1, source_target_pairs={{0,192},{8,72},{16,208},{24,88},{32,224},{40,104},{48,240},{56,120... | collective-permute-start | bytes 786440 | tf_op jit(solution)/shard_map/ppermute | solution.py:33
  91.8 1.9 %add_convert_fusion.1 = bf16[128,1024]{1,0:T(8,128)(2,1)} fusion(bf16[128,1024]{1,0:T(8,128)(2,1)} %collective-permute-done.15, bf16[128,1024]{1,0:T(8,128)(2,1)} %copy-done.11, bf16[128,1024]{1,0:T(8,128)(2,1)} %get-tuple-element.57), kind=kLoop, calls=%fused_computation.20 | loop fusion | flops 786432 | bytes 1048576 | tf_op jit(solution)/shard_map/convert_element_type | solution.py:366
  96.0 4.1 %all-to-all-done.1.refs_0_ = bf16[32,18,128]{2,1,0:T(8,128)(2,1)S(1)} async-done(((bf16[32,18,128]{2,1,0:T(8,128)(2,1)}), bf16[32,18,128]{2,1,0:T(8,128)(2,1)S(1)}, u32[]{:S(2)}, u32[]{:S(2)}) %all-to-all-start.1) | async-done | bytes 147488 | tf_op jit(solution)/shard_map/all_to_all | solution.py:350
  100.9 3.4 %all-to-all-start.2 = ((f32[8,36,128]{2,1,0:T(8,128)}), f32[8,36,128]{2,1,0:T(8,128)S(1)}, u32[]{:S(2)}, u32[]{:S(2)}) async-start(f32[8,36,128]{2,1,0:T(8,128)} %shard_map.92), calls=%async_computation.2 | async-start | bytes 327680 | tf_op jit(solution)/shard_map/all_to_all | solution.py:368
  104.9 2.5 %collective-permute-done.19 = bf16[128,1024]{1,0:T(8,128)(2,1)S(1)} collective-permute-done((bf16[128,1024]{1,0:T(8,128)(2,1)}, bf16[128,1024]{1,0:T(8,128)(2,1)S(1)}, u32[]{:S(2)}, u32[]{:S(2)}) %collective-permute-start.19) | collective-permute-done | bytes 262176 | tf_op jit(solution)/shard_map/ppermute | solution.py:33
  107.5 3.3 %fusion = bf16[1,128,1152]{2,1,0:T(8,128)(2,1)} fusion(bf16[1152,1024]{1,0:T(8,128)(2,1)} %refs_0_.1, f32[128,1024]{1,0:T(8,128)S(1)} %copy-done.4, bf16[128,1024]{1,0:T(8,128)(2,1)S(1)} %collective-permute-done.18, f32[128]{0:T(128)S(1)} %slice_reduce_fusion, f32[128]{0:T(128)S(1)} %fusion.7, bf16[512,1024]{1,0:T(8,128)(2,1)S(1)} %get-tuple-element.43.refs_2_.refs_4_.refs_1_), kind=kOutput, calls=%fused_computation.1 | convolution fusion | flops 303054848 | bytes 3703808 | tf_op jit(solution)/shard_map/dot_general | solution.py:45
  (74 shorter events, 26.6 us)
Async XLA Ops:
  0.6 9.8 %collective-permute-start = (bf16[128,1152]{1,0:T(8,128)(2,1)}, bf16[128,1152]{1,0:T(8,128)(2,1)S(1)}, u32[]{:S(2)}, u32[]{:S(2)}) collective-permute-start(bf16[128,1152]{1,0:T(8,128)(2,1)} %bitcast.25), channel_id=1, source_target_pairs={{0,16},{8,24},{16,0},{24,8},{32,48},{40,56},{48,32},{56,40},{64,80... | collective-permute-start | bytes 884744 | tf_op jit(solution)/shard_map/ppermute | solution.py:41
  4.5 9.6 %collective-permute-start.5 = (bf16[128,1024]{1,0:T(8,128)(2,1)}, bf16[128,1024]{1,0:T(8,128)(2,1)S(1)}, u32[]{:S(2)}, u32[]{:S(2)}) collective-permute-start(bf16[128,1024]{1,0:T(8,128)(2,1)} %bitcast.22), channel_id=1, source_target_pairs={{0,224},{8,40},{16,240},{24,56},{32,0},{40,72},{48,16},{56,88},{64... | collective-permute-start | bytes 786440 | tf_op jit(solution)/shard_map/ppermute | solution.py:33
  6.1 8.9 %collective-permute-start.6 = (bf16[128,1024]{1,0:T(8,128)(2,1)}, bf16[128,1024]{1,0:T(8,128)(2,1)S(1)}, u32[]{:S(2)}, u32[]{:S(2)}) collective-permute-start(bf16[128,1024]{1,0:T(8,128)(2,1)} %bitcast.23), channel_id=1, source_target_pairs={{0,32},{8,232},{16,48},{24,248},{32,64},{40,8},{48,80},{56,24},{64... | collective-permute-start | bytes 786440 | tf_op jit(solution)/shard_map/ppermute | solution.py:33
  10.0 4.0 %collective-permute-start.3 = (s32[1,128]{1,0:T(1,128)}, s32[1,128]{1,0:T(1,128)S(1)}, u32[]{:S(2)}, u32[]{:S(2)}) collective-permute-start(s32[1,128]{1,0:T(1,128)} %refs_5_.1), channel_id=1, source_target_pairs={{0,16},{8,24},{16,0},{24,8},{32,48},{40,56},{48,32},{56,40},{64,80... | collective-permute-start | bytes 1544 | tf_op jit(solution)/shard_map/ppermute | solution.py:41
  10.5 12.4 %collective-permute-start.1 = (bf16[128,1152]{1,0:T(8,128)(2,1)}, bf16[128,1152]{1,0:T(8,128)(2,1)S(1)}, u32[]{:S(2)}, u32[]{:S(2)}) collective-permute-start(bf16[128,1152]{1,0:T(8,128)(2,1)} %bitcast.26), channel_id=1, source_target_pairs={{0,8},{8,0},{16,24},{24,16},{32,40},{40,32},{48,56},{56,48},{64,72... | collective-permute-start | bytes 884744 | tf_op jit(solution)/shard_map/ppermute | solution.py:37
  15.0 13.8 %collective-permute-start.7 = (bf16[128,1024]{1,0:T(8,128)(2,1)S(1)}, bf16[128,1024]{1,0:T(8,128)(2,1)}, u32[]{:S(2)}, u32[]{:S(2)}) collective-permute-start(bf16[128,1024]{1,0:T(8,128)(2,1)S(1)} %collective-permute-done.5.refs_5_), channel_id=1, source_target_pairs={{0,224},{8,40},{16,240},{24,56},{32,0},{40,72},{48,16},{56,88},{64... | collective-permute-start | bytes 786440 | tf_op jit(solution)/shard_map/ppermute | solution.py:33
  16.1 12.8 %collective-permute-start.8 = (bf16[128,1024]{1,0:T(8,128)(2,1)S(1)}, bf16[128,1024]{1,0:T(8,128)(2,1)}, u32[]{:S(2)}, u32[]{:S(2)}) collective-permute-start(bf16[128,1024]{1,0:T(8,128)(2,1)S(1)} %collective-permute-done.6.refs_6_), channel_id=1, source_target_pairs={{0,32},{8,232},{16,48},{24,248},{32,64},{40,8},{48,80},{56,24},{64... | collective-permute-start | bytes 786440 | tf_op jit(solution)/shard_map/ppermute | solution.py:33
  18.5 4.4 %collective-permute-start.2 = (bf16[128,1152]{1,0:T(8,128)(2,1)S(1)}, bf16[128,1152]{1,0:T(8,128)(2,1)S(1)}, u32[]{:S(2)}, u32[]{:S(2)}) collective-permute-start(bf16[128,1152]{1,0:T(8,128)(2,1)S(1)} %collective-permute-done.refs_3_.refs_8_), channel_id=1, source_target_pairs={{0,8},{8,0},{16,24},{24,16},{32,40},{40,32},{48,56},{56,48},{64,72... | collective-permute-start | bytes 884744 | tf_op jit(solution)/shard_map/ppermute | solution.py:37
  21.8 1.1 collective-permute-start.4
  28.8 9.4 %collective-permute-start.9 = (bf16[128,1024]{1,0:T(8,128)(2,1)}, bf16[128,1024]{1,0:T(8,128)(2,1)}, u32[]{:S(2)}, u32[]{:S(2)}) collective-permute-start(bf16[128,1024]{1,0:T(8,128)(2,1)} %collective-permute-done.8.refs_8_), channel_id=1, source_target_pairs={{0,32},{8,232},{16,48},{24,248},{32,64},{40,8},{48,80},{56,24},{64... | collective-permute-start | bytes 786440 | tf_op jit(solution)/shard_map/ppermute | solution.py:33
  32.8 8.5 %collective-permute-start.11 = (bf16[128,1024]{1,0:T(8,128)(2,1)}, bf16[128,1024]{1,0:T(8,128)(2,1)}, u32[]{:S(2)}, u32[]{:S(2)}) collective-permute-start(bf16[128,1024]{1,0:T(8,128)(2,1)} %collective-permute-done.7.refs_7_), channel_id=1, source_target_pairs={{0,224},{8,40},{16,240},{24,56},{32,0},{40,72},{48,16},{56,88},{64... | collective-permute-start | bytes 786440 | tf_op jit(solution)/shard_map/ppermute | solution.py:33
  38.3 7.0 %collective-permute-start.10 = (bf16[128,1024]{1,0:T(8,128)(2,1)}, bf16[128,1024]{1,0:T(8,128)(2,1)}, u32[]{:S(2)}, u32[]{:S(2)}) collective-permute-start(bf16[128,1024]{1,0:T(8,128)(2,1)} %collective-permute-done.9.refs_5_), channel_id=1, source_target_pairs={{0,32},{8,232},{16,48},{24,248},{32,64},{40,8},{48,80},{56,24},{64... | collective-permute-start | bytes 786440 | tf_op jit(solution)/shard_map/ppermute | solution.py:33
  48.7 4.3 %collective-permute-start.12 = (bf16[512,896]{1,0:T(8,128)(2,1)S(1)}, bf16[512,896]{1,0:T(8,128)(2,1)S(1)}, u32[]{:S(2)}, u32[]{:S(2)}) collective-permute-start(bf16[512,896]{1,0:T(8,128)(2,1)S(1)} %get-tuple-element.52), channel_id=1, source_target_pairs={{0,8},{8,0},{16,24},{24,16},{32,40},{40,32},{48,56},{56,48},{64,72... | collective-permute-start | bytes 2752520 | tf_op jit(solution)/shard_map/ppermute | solution.py:37
  57.2 22.1 %all-to-all-start = ((bf16[8,64,1152]{2,1,0:T(8,128)(2,1)}), bf16[8,64,1152]{2,1,0:T(8,128)(2,1)S(1)}, u32[]{:S(2)}, u32[]{:S(2)}) async-start(bf16[8,64,1152]{2,1,0:T(8,128)(2,1)} %get-tuple-element.69), calls=%async_computation | async-start | bytes 2359296 | tf_op jit(solution)/shard_map/all_to_all | solution.py:344
  62.6 7.8 %collective-permute-start.13 = (bf16[128,1024]{1,0:T(8,128)(2,1)S(1)}, bf16[128,1024]{1,0:T(8,128)(2,1)S(1)}, u32[]{:S(2)}, u32[]{:S(2)}) collective-permute-start(bf16[128,1024]{1,0:T(8,128)(2,1)S(1)} %copy-done.12), channel_id=1, source_target_pairs={{0,32},{8,232},{16,48},{24,248},{32,64},{40,8},{48,80},{56,24},{64... | collective-permute-start | bytes 786440 | tf_op jit(solution)/shard_map/ppermute | solution.py:33
  63.5 24.8 %collective-permute-start.14 = (bf16[128,1024]{1,0:T(8,128)(2,1)}, bf16[128,1024]{1,0:T(8,128)(2,1)}, u32[]{:S(2)}, u32[]{:S(2)}) collective-permute-start(bf16[128,1024]{1,0:T(8,128)(2,1)} %get-tuple-element.64), channel_id=1, source_target_pairs={{0,224},{8,40},{16,240},{24,56},{32,0},{40,72},{48,16},{56,88},{64... | collective-permute-start | bytes 786440 | tf_op jit(solution)/shard_map/ppermute | solution.py:33
  64.1 24.2 %collective-permute-start.15 = (bf16[128,1024]{1,0:T(8,128)(2,1)}, bf16[128,1024]{1,0:T(8,128)(2,1)}, u32[]{:S(2)}, u32[]{:S(2)}) collective-permute-start(bf16[128,1024]{1,0:T(8,128)(2,1)} %shard_map.90), channel_id=1, source_target_pairs={{0,64},{8,200},{16,80},{24,216},{32,96},{40,232},{48,112},{56,248}... | collective-permute-start | bytes 786440 | tf_op jit(solution)/shard_map/ppermute | solution.py:33
  64.8 23.5 %collective-permute-start.16 = (bf16[128,1024]{1,0:T(8,128)(2,1)}, bf16[128,1024]{1,0:T(8,128)(2,1)S(1)}, u32[]{:S(2)}, u32[]{:S(2)}) collective-permute-start(bf16[128,1024]{1,0:T(8,128)(2,1)} %get-tuple-element.66), channel_id=1, source_target_pairs={{0,32},{8,232},{16,48},{24,248},{32,64},{40,8},{48,80},{56,24},{64... | collective-permute-start | bytes 786440 | tf_op jit(solution)/shard_map/ppermute | solution.py:33
  66.2 22.1 %collective-permute-start.17 = (bf16[128,1024]{1,0:T(8,128)(2,1)}, bf16[128,1024]{1,0:T(8,128)(2,1)}, u32[]{:S(2)}, u32[]{:S(2)}) collective-permute-start(bf16[128,1024]{1,0:T(8,128)(2,1)} %get-tuple-element.67), channel_id=1, source_target_pairs={{0,224},{8,40},{16,240},{24,56},{32,0},{40,72},{48,16},{56,88},{64... | collective-permute-start | bytes 786440 | tf_op jit(solution)/shard_map/ppermute | solution.py:33
  71.0 17.3 %collective-permute-start.18 = (bf16[128,1024]{1,0:T(8,128)(2,1)}, bf16[128,1024]{1,0:T(8,128)(2,1)S(1)}, u32[]{:S(2)}, u32[]{:S(2)}) collective-permute-start(bf16[128,1024]{1,0:T(8,128)(2,1)} %get-tuple-element.68), channel_id=1, source_target_pairs={{0,16},{8,24},{16,0},{24,8},{32,48},{40,56},{48,32},{56,40},{64,80... | collective-permute-start | bytes 786440 | tf_op jit(solution)/shard_map/ppermute | solution.py:41
  80.4 19.8 %all-to-all-start.1 = ((bf16[32,18,128]{2,1,0:T(8,128)(2,1)}), bf16[32,18,128]{2,1,0:T(8,128)(2,1)S(1)}, u32[]{:S(2)}, u32[]{:S(2)}) async-start(bf16[32,18,128]{2,1,0:T(8,128)(2,1)} %shard_map.91), calls=%async_computation.1 | async-start | bytes 393216 | tf_op jit(solution)/shard_map/all_to_all | solution.py:350
  89.4 15.5 %collective-permute-start.20 = (bf16[128,1024]{1,0:T(8,128)(2,1)S(1)}, bf16[128,1024]{1,0:T(8,128)(2,1)S(1)}, u32[]{:S(2)}, u32[]{:S(2)}) collective-permute-start(bf16[128,1024]{1,0:T(8,128)(2,1)S(1)} %add_convert_fusion), channel_id=1, source_target_pairs={{0,192},{8,72},{16,208},{24,88},{32,224},{40,104},{48,240},{56,120... | collective-permute-start | bytes 786440 | tf_op jit(solution)/shard_map/ppermute | solution.py:33
  93.7 13.6 %collective-permute-start.19 = (bf16[128,1024]{1,0:T(8,128)(2,1)}, bf16[128,1024]{1,0:T(8,128)(2,1)S(1)}, u32[]{:S(2)}, u32[]{:S(2)}) collective-permute-start(bf16[128,1024]{1,0:T(8,128)(2,1)} %add_convert_fusion.1), channel_id=1, source_target_pairs={{0,64},{8,200},{16,80},{24,216},{32,96},{40,232},{48,112},{56,248}... | collective-permute-start | bytes 786440 | tf_op jit(solution)/shard_map/ppermute | solution.py:33
  100.9 12.3 %all-to-all-start.2 = ((f32[8,36,128]{2,1,0:T(8,128)}), f32[8,36,128]{2,1,0:T(8,128)S(1)}, u32[]{:S(2)}, u32[]{:S(2)}) async-start(f32[8,36,128]{2,1,0:T(8,128)} %shard_map.92), calls=%async_computation.2 | async-start | bytes 327680 | tf_op jit(solution)/shard_map/all_to_all | solution.py:368
  (13 other events, 110.4 us)

commit v8 on v7

--- a/solution.py
+++ b/solution.py
@@ -121,18 +121,21 @@
     return emb, (jax.nn.sigmoid(logits) - positive).astype(BF16)
 
 
-def columns_of(start, rows):
+def columns_of(place, key, rows):
+    owner = place[0] + (key + Z) * (YH * CORE) - 2 * key * place[2] * (YH * CORE)
+    start = owner % LOOP * rows
     return (lax.broadcasted_iota(jnp.int32, (1, rows), 1) + start).astype(F32)
 
 
-def pairs_kernel(count, first, moves, numbers, starts, image_emb, match, *refs):
+def pairs_kernel(keys, first, moves, numbers, place, image_emb, match, *refs):
+    count = len(keys)
     texts, refs = refs[:count], refs[count:]
     if not first:
         acc_in, refs = refs[0], refs[1:]
     acc_out, text_out = refs[0], refs[1:]
     image = image_emb[...]
     rows = texts[0].shape[0]
-    columns = jnp.concatenate([columns_of(starts[n], rows) for n in range(count)], 1)
+    columns = jnp.concatenate([columns_of(place, key, rows) for key in keys], 1)
     for n in range(count):
         moves.need(4 + n)
     emb, grad = block_grads(numbers, columns, image, match[...], moves.pack[...])
@@ -157,13 +160,15 @@
     inv = lax.rsqrt(jnp.sum(projected * projected, -1, keepdims=True) + 1e-06)
     emb[...] = (projected * inv).astype(BF16)
     inv_out[...] = inv
+    moves.send(1)
+    moves.need(5)
     for n in range(4):
         match = jnp.broadcast_to(matches[n][...].astype(F32), (rows, rows))
         match_out[n * rows : (n + 1) * rows, :] = match.T[:, 0:1]
 
 
-def last_kernel(moves, numbers, starts, image_emb, match, text, acc_in, acc_out, dot_out, packet, grad_out):
-    columns = columns_of(starts[0], text.shape[0])
+def last_kernel(moves, numbers, place, image_emb, match, text, acc_in, acc_out, dot_out, packet, grad_out):
+    columns = columns_of(place, 4, text.shape[0])
     emb, grad = block_grads(numbers, columns, image_emb[...], match[...], text[...])
     grad_out[...] = grad
     acc = numbers[0] * (acc_in[...] + jnp.dot(grad, emb, preferred_element_type=F32))
@@ -172,8 +177,8 @@
     dot_out[...] = dot
     rows, width = acc.shape
     half, quarter, block = width // 2, width // 4, rows // 4
-    own = pl.multiple_of(starts[1] * half, half)
-    other = pl.multiple_of((1 - starts[1]) * half, half)
+    own = pl.multiple_of(place[2] * half, half)
+    other = pl.multiple_of((1 - place[2]) * half, half)
     packet[:, :half] = acc_out[:, pl.ds(other, half)].astype(BF16)
     top = dot.astype(BF16).astype(F32)
     lane = lax.broadcasted_iota(jnp.int32, (rows, 128), 1)
@@ -191,76 +196,99 @@
     moves.send(0)
 
 
-def weight_kernel(moves, starts, got, acc, dot, image_emb, inv, own_rows, core_rows, yh_rows, both_rows, weight, row_send, row_keep):
+def half_kernel(moves, place, got, acc, dot, kept, dot_out, packet, row_send, row_keep):
     rows, width = acc.shape
     half, quarter, block = width // 2, width // 4, rows // 4
-    own = pl.ds(pl.multiple_of(starts[1] * half, half), half)
-    projs = []
+    own_half = pl.multiple_of(place[2] * half, half)
+    packet[rows:, :] = jnp.zeros((packet.shape[0] - rows, quarter), BF16)
+    digit_rows = []
     for slot in range(4):
         mine = slice(slot * block, (slot + 1) * block)
         theirs = slice((slot ^ 1) * block, ((slot ^ 1) + 1) * block)
-        kept = acc[mine, own] + got[theirs, :half].astype(F32)
         digits = got[theirs, half : half + 128].astype(F32)
         whole_dot = dot[mine, :] + digits[:, 0:1] + digits[:, 1:2]
-        unit = image_emb[mine, own].astype(F32)
-        projs.append(((kept - unit * whole_dot) * inv[mine, :]).astype(BF16))
-        if slot in (0, 2):
-            target = (row_keep, row_send)[slot // 2]
-            target[:, own] = kept.astype(target.dtype)
-            for side in range(2):
-                first = pl.multiple_of((1 - starts[1]) * half + side * quarter, quarter)
+        dot_out[mine, :] = whole_dot
+        flat = jnp.broadcast_to(whole_dot, (block, 128)).T[0:1, :]
+        top = flat.astype(BF16).astype(F32)
+        digit_rows.append(jnp.concatenate([top, flat - top], 1))
+        for side in range(2):
+            lanes = pl.ds(pl.multiple_of(own_half + side * quarter, quarter), quarter)
+            total = acc[mine, lanes] + got[theirs, side * quarter : (side + 1) * quarter].astype(F32)
+
+            @pl.when(place[1] == side)
+            def _():
+                kept[mine, :] = total
+
+            @pl.when(place[1] != side)
+            def _():
+                packet[mine, :] = total.astype(BF16)
+
+            if slot in (0, 2):
+                target = (row_keep, row_send)[slot // 2]
+                target[:, lanes] = total.astype(target.dtype)
+                first = pl.multiple_of((1 - place[2]) * half + side * quarter, quarter)
                 lanes = pl.ds(first, quarter)
                 at = (2 * side + slot // 2) * block
                 extra = got[at : at + block, half + 128 :].astype(F32)
                 target[:, lanes] = (acc[mine, lanes] + extra).astype(target.dtype)
-            moves.send(2 - slot // 2)
+        if slot in (0, 2):
+            moves.send(4 - slot // 2)
+    fill = jnp.zeros((packet.shape[0] - rows - 4, quarter), F32)
+    packet[rows:, :] = jnp.concatenate(digit_rows + [fill], 0).astype(BF16)
+
+
+def weight_kernel(moves, place, got, kept, dot, image_emb, inv, own_rows, core_rows, yh_rows, both_rows, weight):
+    rows, quarter = kept.shape
+    block = rows // 4
+    lanes = pl.ds(pl.multiple_of((place[2] * 2 + place[1]) * quarter, quarter), quarter)
+    digits = got[rows:, :].astype(F32)
+    moves.need(5)
+    projs = []
+    for slot in range(4):
+        mine = slice(slot * block, (slot + 1) * block)
+        theirs = slice((slot ^ 2) * block, ((slot ^ 2) + 1) * block)
+        line = digits[slot ^ 2 : (slot ^ 2) + 1, :]
+        other_dot = jnp.broadcast_to(line[:, :128] + line[:, 128:], (block, 128)).T[:, 0:1]
+        whole = kept[mine, :] + got[theirs, :].astype(F32)
+        unit = image_emb[mine, lanes].astype(F32)
+        projs.append(((whole - unit * (dot[mine, :] + other_dot)) * inv[mine, :]).astype(BF16))
     proj = jnp.concatenate(projs, 0)
     for n in range(6, 10):
         moves.need(n)
-    sensor = moves.pack[...]
-    chunk = weight.shape[1]
-    for side in range(2):
-        product = inner_cols(proj[:, side * quarter : (side + 1) * quarter], sensor).astype(BF16)
-        for m in range(quarter // chunk):
-            at = side * (quarter // chunk) + m
-            weight[at] = product[m * chunk : (m + 1) * chunk]
-            moves.send(0, at)
-
-
-def chunk_kernel(moves, parts, out):
+    product = inner_cols(moves.pack[...], proj)
+    count, height, wide = weight.shape
+    tall = height // 2
+    for n in range(count):
+        piece = product[n * tall : (n + 1) * tall]
+        weight[n] = jnp.concatenate([piece[:, :wide], piece[:, wide:]], 0).astype(BF16)
+    moves.send(0)
+
+
+def group_kernel(moves, parts, out):
+    count, rows, _ = parts.shape
+    quarters = count // Z
+    for quarter in range(quarters):
+        total = parts[quarter].astype(F32)
+        for n in range(1, Z):
+            total = total + parts[n * quarters + quarter].astype(F32)
+        total = total.astype(BF16)
+        for n in range(DP):
+            out[n, quarter * rows : (quarter + 1) * rows] = total
+    moves.send(0)
+
+
+def layout_kernel(moves, parts, out):
     total = parts[0].astype(F32)
-    for n in range(1, parts.shape[0]):
+    for n in range(1, DP):
         total = total + parts[n].astype(F32)
-    turned = total.T
-    count, rows, lanes = out.shape
-    for n in range(count):
-        at = 2 * rows * n
-        out[n] = jnp.concatenate([turned[at : at + rows], turned[at + rows : at + 2 * rows]], 1).astype(BF16)
-    moves.send(0)
-
-
-def share_kernel(moves, parts, out):
-    rows = parts.shape[1]
-    for core in range(CORE):
-        total = parts[core].astype(F32)
-        for n in range(1, Z * YH):
-            total = total + parts[n * CORE + core].astype(F32)
-        total = total * (1.0 / DP)
-        for n in range(DP):
-            out[n, core * rows : (core + 1) * rows] = total
-    moves.send(0)
-
-
-def layout_kernel(moves, shares, out):
-    rows, lanes = shares.shape[1] // 2, shares.shape[2]
-    cols = lanes // 2
-    for core in range(CORE):
-        here = slice(core * rows, (core + 1) * rows)
-        for pair in range(DP // 2):
-            left, right = shares[2 * pair, here], shares[2 * pair + 1, here]
-            at = core * DP * cols + pair * lanes
-            out[:rows, at : at + lanes] = jnp.concatenate([left[:, :cols], right[:, :cols]], 1)
-            out[rows:, at : at + lanes] = jnp.concatenate([left[:, cols:], right[:, cols:]], 1)
+    total = total * (1.0 / DP)
+    tall, wide = out.shape[0], parts.shape[2]
+    for y in range(YH):
+        for core in range(CORE):
+            for side in range(2):
+                at = (y * CORE + core) * 2 + side
+                to = ((core * YH + y) * 2 + side) * wide
+                out[:, to : to + wide] = total[at * tall : (at + 1) * tall]
     moves.send(0)
 
 
@@ -270,8 +298,7 @@
     rows = sensor.shape[0]
     feat, width = proj_weight.shape
     loop_index = lax.axis_index("loop")
-    z = loop_index // (YH * CORE)
-    core = loop_index % CORE
+    place = jnp.stack([loop_index, loop_index // CORE % YH, loop_index % CORE])
     logit_scale = jnp.exp(log_scale)
     numbers = jnp.stack([logit_scale, logit_bias])
 
@@ -285,82 +312,82 @@
     slot[2], slot[-2] = shift_z(up, -1), shift_z(down, 1)
     sensor_later, _ = lax.optimization_barrier((sensor, sensor_yh))
     sensors = [sensor, swap_core(sensor_later), sensor_yh, swap_core(sensor_yh)]
-    match_both = swap_core(jnp.concatenate([match, match_yh], 0))
-    match = [match, match_both[:1], match_yh, match_both[1:]]
+    match = [match, swap_core(match), match_yh, swap_core(match_yh)]
     shapes = [((4 * rows, width), BF16), ((4 * rows, 1), F32), ((4 * rows, 1), F32)]
     image_emb, image_inv, match_rows = call(
         project_kernel,
         [jax.ShapeDtypeStruct(*s) for s in shapes],
         {},
         proj_weight, *sensors, *match,
-        far=(0,),
+        far=(0, 5),
         packed=range(1, 5),
+        far_out=(1,),
         cuts={0: CUT},
     )
     up, down, _ = lax.optimization_barrier((slot[2], slot[-2], image_emb))
     slot[3], slot[-3] = shift_z(up, -1), shift_z(down, 1)
 
-    def starts_of(keys):
-        step = (1 - 2 * core) * YH * CORE
-        return [(loop_index + k * step + LOOP) % LOOP * rows for k in keys]
-
     def pairs(keys, dtypes, acc):
-        operands = [numbers, jnp.stack(starts_of(keys)), image_emb, match_rows, *(slot[k] for k in keys)]
+        operands = [numbers, place, image_emb, match_rows, *(slot[k] for k in keys)]
         out = [jax.ShapeDtypeStruct((4 * rows, width), F32)]
         out += [jax.ShapeDtypeStruct((rows, width), d) for d in dtypes]
         aliases = {}
         if acc is not None:
             aliases = {len(operands): 0}
             operands.append(acc)
-        kernel = functools.partial(pairs_kernel, len(keys), acc is None)
+        kernel = functools.partial(pairs_kernel, keys, acc is None)
         return call(kernel, out, aliases, *operands, packed=range(4, 4 + len(keys)), far_out=range(1, len(out)))
 
     acc, text_0, text_1, text_m1, text_2, text_m2 = pairs((0, 1, -1, 2, -2), (F32, BF16, BF16, BF16, BF16), None)
     last_text, _ = lax.optimization_barrier((slot[-3], acc))
     last_text = shift_z(last_text, 1)
     acc, text_3, text_m3 = pairs((3, -3), (BF16, BF16), acc)
-    starts = jnp.stack(starts_of((4,)) + [core])
     shapes = [((4 * rows, width), F32), ((4 * rows, 1), F32), ((4 * rows, width // 8 * 7), BF16), ((4 * rows, rows), BF16)]
     acc, dot, packet, last_grad = call(
         last_kernel,
         [jax.ShapeDtypeStruct(*s) for s in shapes],
         {5: 0},
-        numbers, starts, image_emb, match_rows, last_text, acc,
+        numbers, place, image_emb, match_rows, last_text, acc,
     )
     (text_4,) = call(
         last_text_kernel, [jax.ShapeDtypeStruct((rows, width), BF16)], {}, last_grad, image_emb, far_out=(0,)
     )
 
-    shapes = [((DP, width // 16, feat), BF16), ((rows, width), BF16), ((rows, width), F32)]
-    weight_part, row_send, row_keep = call(
-        weight_kernel,
+    shapes = [((4 * rows, width // 4), F32), ((4 * rows, 1), F32), ((4 * rows + 16, width // 4), BF16)]
+    shapes += [((rows, width), BF16), ((rows, width), F32)]
+    kept, dot, packet, row_send, row_keep = call(
+        half_kernel,
         [jax.ShapeDtypeStruct(*s) for s in shapes],
         {},
-        starts, swap_core(packet), acc, dot, image_emb, image_inv, *sensors,
+        place, swap_core(packet), acc, dot,
+        far_out=(3, 4),
+    )
+    text_3, text_m3, text_4, _ = lax.optimization_barrier((text_3, text_m3, text_4, kept))
+    from_below, from_above = shift_z(text_3, 1), shift_z(text_m3, -1)
+    packet, text_4, from_below, from_above = lax.optimization_barrier((swap_yh(packet), text_4, from_below, from_above))
+    per_loop = feat // LOOP
+    block = (2 * per_loop, width // 8)
+    (weight_part,) = call(
+        weight_kernel,
+        [jax.ShapeDtypeStruct((LOOP,) + block, BF16)],
+        {},
+        place, packet, kept, dot, image_emb, image_inv, *sensors,
+        far=(5,),
         packed=range(6, 10),
-        far_out=range(3),
-        sends=2 + DP,
-    )
-    weight_part = lax.all_to_all(weight_part, "dp", 0, 0, tiled=True)
-    per_loop = feat // LOOP
-    block = (per_loop // 2, width // 8)
-    (weight_chunks,) = call(
-        chunk_kernel, [jax.ShapeDtypeStruct((LOOP,) + block, BF16)], {}, weight_part, far_out=(0,)
-    )
-    weight_part = lax.all_to_all(weight_chunks, "loop", 0, 0, tiled=True)
+        far_out=(0,),
+    )
+    group_part = lax.all_to_all(weight_part, "loop", 0, 0, tiled=True)
     (shares,) = call(
-        share_kernel, [jax.ShapeDtypeStruct((DP, per_loop, width // 8), F32)], {}, weight_part, far_out=(0,)
-    )
-
-    text_3, text_m3, text_4, text_1, text_m1, _ = lax.optimization_barrier(
-        (text_3, text_m3, text_4, text_1, text_m1, row_keep)
+        group_kernel, [jax.ShapeDtypeStruct((DP, YH * CORE * block[0], block[1]), BF16)], {}, group_part, far_out=(0,)
+    )
+
+    text_4, text_1, text_m1, _ = lax.optimization_barrier((text_4, text_1, text_m1, packet))
+    far = shift_z(text_4, 2)
+    near_below, near_above = shift_z(text_1, 1), shift_z(text_m1, -1)
+    from_below, from_above, far, near_below, near_above, row_send, _ = lax.optimization_barrier(
+        (from_below, from_above, far, near_below, near_above, row_send, weight_part)
     )
     row_got = swap_yh(row_send)
-    from_below, from_above, far = shift_z(text_3, 1), shift_z(text_m3, -1), shift_z(text_4, 2)
-    near_below, near_above = shift_z(text_1, 1), shift_z(text_m1, -1)
-    from_below, from_above, far, near_below, near_above, row_got, _ = lax.optimization_barrier(
-        (from_below, from_above, far, near_below, near_above, row_got, weight_chunks)
-    )
     up = text_2.astype(F32) + from_below.astype(F32) + far.astype(F32)
     down = text_m2.astype(F32) + from_above.astype(F32)
     up, down = shift_z(up.astype(BF16), 2), shift_z(down.astype(BF16), -2)

time: 115 us -> 133 us (1.16)
  waiting for transfers between devices: 23.1 us -> 39.8 us
  starting transfers between devices: 50.6 us -> 54.6 us
  matrix products: 3.34 us -> 1.66 us
    ppermute x14, waiting for transfers between devices: 7 us -> 31.3 us  [shift_z(): lax.ppermute(block, 'loop', route(lambda z, y, c: (z + (1 - 2 * c) * dist...]
    all_to_all x2 -> x1, waiting for transfers between devices: 11.2 us -> 0.01 us  [on_device(): group_part = lax.all_to_all(weight_part, 'loop', 0, 0, tiled=True)]
    all_to_all x2 -> x1, starting transfers between devices: 12.2 us -> 4.27 us  [on_device(): group_part = lax.all_to_all(weight_part, 'loop', 0, 0, tiled=True)]
    ppermute x3 -> x4, starting transfers between devices: 5.07 us -> 12.5 us  [swap_yh(): return lax.ppermute(block, 'loop', route(lambda z, y, c: (z, 1 - y, c)))]
    ppermute x14, starting transfers between devices: 22.9 us -> 27.7 us  [shift_z(): lax.ppermute(block, 'loop', route(lambda z, y, c: (z + (1 - 2 * c) * dist...]
    all_to_all x1, waiting for transfers between devices: 0.01 us -> 3.09 us  [on_device(): shares = lax.all_to_all(shares, 'dp', 0, 0, tiled=True)]
    dot_general x1, matrix products: 3.34 us -> 1.66 us  [inner_rows(): lax.dot_general(left, right, (((1,), (1,)), ((), ())), preferred_element_...]
    ppermute x4 -> x5, starting transfers between devices: 7.01 us -> 5.33 us  [swap_core(): return lax.ppermute(block, 'loop', route(lambda z, y, c: (z, y, 1 - c)))]
  transfers between devices with their start and end apart: 24 -> 25, of which waited for: 10 -> 11; matrix products, arithmetic and copies ran while one was open for 10% -> 6% of each run, Pallas kernels for 14% -> 12%
where the time goes in v8:
time: 133 us; the launch traced here: 132 us
  starting transfers between devices  54.6 us (41%)
  waiting for transfers between devices  39.8 us (30%)
  Pallas kernels  24.8 us (19%)
  other arithmetic  5.6 us (4%)
  local copies, waits for them, and re-layouts  3.14 us (2%)
  between operations  2.43 us (2%)
  matrix products  1.66 us (1%)
    ppermute x14, waiting for transfers between devices, shift_z(): lax.ppermute(block, 'loop', route(lambda z, y, c: (z + (1 - 2 * c) * dist...  31.3 us
    ppermute x14, starting transfers between devices, shift_z(): lax.ppermute(block, 'loop', route(lambda z, y, c: (z + (1 - 2 * c) * dist...  27.7 us
    pallas_call x9, Pallas kernels, call(): pl.pallas_call(body, out_shape=[pltpu.HBM(o.shape, o.dtype) if n in far_o...  24.8 us
    ppermute x4, starting transfers between devices, swap_yh(): return lax.ppermute(block, 'loop', route(lambda z, y, c: (z, 1 - y, c)))  12.5 us
    ppermute x5, starting transfers between devices, swap_core(): return lax.ppermute(block, 'loop', route(lambda z, y, c: (z, y, 1 - c)))  5.33 us
    all_to_all x1, starting transfers between devices, on_device(): shares = lax.all_to_all(shares, 'dp', 0, 0, tiled=True)  4.81 us
    all_to_all x1, starting transfers between devices, on_device(): group_part = lax.all_to_all(weight_part, 'loop', 0, 0, tiled=True)  4.27 us
    ppermute x5, waiting for transfers between devices, swap_core(): return lax.ppermute(block, 'loop', route(lambda z, y, c: (z, y, 1 - c)))  3.88 us
  transfers between devices with their start and end apart: 25, of which 11 were waited for; matrix products, arithmetic and copies ran while one was open for 6% of the time, Pallas kernels for 12%

profile of v8, /device:TPU:1, one launch (start us, length us, event | category | flops | bytes accessed | tf_op | source)
XLA Modules:
  0.0 132.0 jit_solution(13040151681953037747)
XLA Ops:
  0.6 3.8 %collective-permute-start = (bf16[128,1152]{1,0:T(8,128)(2,1)}, bf16[128,1152]{1,0:T(8,128)(2,1)S(1)}, u32[]{:S(2)}, u32[]{:S(2)}) collective-permute-start(bf16[128,1152]{1,0:T(8,128)(2,1)} %bitcast.19), channel_id=1, source_target_pairs={{0,16},{8,24},{16,0},{24,8},{32,48},{40,56},{48,32},{56,40},{64,80... | collective-permute-start | bytes 884744 | tf_op jit(solution)/shard_map/ppermute | solution.py:41
  6.1 3.9 %collective-permute-start.7 = (bf16[128,1024]{1,0:T(8,128)(2,1)}, bf16[128,1024]{1,0:T(8,128)(2,1)S(1)}, u32[]{:S(2)}, u32[]{:S(2)}) collective-permute-start(bf16[128,1024]{1,0:T(8,128)(2,1)} %bitcast.17), channel_id=1, source_target_pairs={{0,32},{8,232},{16,48},{24,248},{32,64},{40,8},{48,80},{56,24},{64... | collective-permute-start | bytes 786440 | tf_op jit(solution)/shard_map/ppermute | solution.py:33
  10.5 2.2 %collective-permute-start.1 = (bf16[128,1152]{1,0:T(8,128)(2,1)}, bf16[128,1152]{1,0:T(8,128)(2,1)S(1)}, u32[]{:S(2)}, u32[]{:S(2)}) collective-permute-start(bf16[128,1152]{1,0:T(8,128)(2,1)} %bitcast.20), channel_id=1, source_target_pairs={{0,8},{8,0},{16,24},{24,16},{32,40},{40,32},{48,56},{56,48},{64,72... | collective-permute-start | bytes 884744 | tf_op jit(solution)/shard_map/ppermute | solution.py:37
  12.6 3.0 %collective-permute-start.4 = (s32[1,128]{1,0:T(1,128)}, s32[1,128]{1,0:T(1,128)S(1)}, u32[]{:S(2)}, u32[]{:S(2)}) collective-permute-start(s32[1,128]{1,0:T(1,128)} %refs_5_.1), channel_id=1, source_target_pairs={{0,16},{8,24},{16,0},{24,8},{32,48},{40,56},{48,32},{56,40},{64,80... | collective-permute-start | bytes 1544 | tf_op jit(solution)/shard_map/ppermute | solution.py:41
  18.5 4.0 %collective-permute-start.9 = (bf16[128,1024]{1,0:T(8,128)(2,1)S(1)}, bf16[128,1024]{1,0:T(8,128)(2,1)S(1)}, u32[]{:S(2)}, u32[]{:S(2)}) collective-permute-start(bf16[128,1024]{1,0:T(8,128)(2,1)S(1)} %collective-permute-done.7.refs_6_), channel_id=1, source_target_pairs={{0,32},{8,232},{16,48},{24,248},{32,64},{40,8},{48,80},{56,24},{64... | collective-permute-start | bytes 786440 | tf_op jit(solution)/shard_map/ppermute | solution.py:33
  27.9 4.4 %shard_map.85 = (bf16[512,1024]{1,0:T(8,128)(2,1)S(1)}, f32[512,1]{1,0:T(8,128)}, f32[512,1]{1,0:T(8,128)S(1)}) custom-call(bf16[1152,1024]{1,0:T(8,128)(2,1)} %refs_0_.1, bf16[128,1152]{1,0:T(8,128)(2,1)} %bitcast.21, bf16[128,1152]{1,0:T(8,128)(2,1)} %copy-done.4, bf16[128,1152]{1,0:T(8,128)(2,1)} %copy-done.3, bf16[128,1152]{1,0:T(8,128)(2,1)} %copy-done.5, ...), custom_call_target="tpu_custom_call" | custom-call | flops 1 | bytes 1 | tf_op jit(solution)/shard_map/pallas_call | solution.py:103
  32.3 3.0 %collective-permute-start.10 = (bf16[128,1024]{1,0:T(8,128)(2,1)S(1)}, bf16[128,1024]{1,0:T(8,128)(2,1)S(1)}, u32[]{:S(2)}, u32[]{:S(2)}) collective-permute-start(bf16[128,1024]{1,0:T(8,128)(2,1)S(1)} %collective-permute-done.9.refs_8_), channel_id=1, source_target_pairs={{0,32},{8,232},{16,48},{24,248},{32,64},{40,8},{48,80},{56,24},{64... | collective-permute-start | bytes 786440 | tf_op jit(solution)/shard_map/ppermute | solution.py:33
  37.1 5.4 %shard_map.86 = (f32[512,1024]{1,0:T(8,128)S(1)}, f32[128,1024]{1,0:T(8,128)}, bf16[128,1024]{1,0:T(8,128)(2,1)}, bf16[128,1024]{1,0:T(8,128)(2,1)}, bf16[128,10...) custom-call(f32[2]{0:T(128)S(1)} %pad_maximum_fusion.refs_0_, s32[3]{0:T(128)S(1)} %pad_add_fusion.refs_1_.refs_0_, ...), custom_call_target="tpu_custom_call" | custom-call | flops 1 | bytes 1 | tf_op jit(solution)/shard_map/pallas_call | solution.py:103
  42.6 2.7 %collective-permute-start.11 = (bf16[128,1024]{1,0:T(8,128)(2,1)S(1)}, bf16[128,1024]{1,0:T(8,128)(2,1)S(1)}, u32[]{:S(2)}, u32[]{:S(2)}) collective-permute-start(bf16[128,1024]{1,0:T(8,128)(2,1)S(1)} %collective-permute-done.10.refs_5_), channel_id=1, source_target_pairs={{0,32},{8,232},{16,48},{24,248},{32,64},{40,8},{48,80},{56,24},{64... | collective-permute-start | bytes 786440 | tf_op jit(solution)/shard_map/ppermute | solution.py:33
  46.0 3.9 %shard_map.87 = (f32[512,1024]{1,0:T(8,128)S(1)}, bf16[128,1024]{1,0:T(8,128)(2,1)}, bf16[128,1024]{1,0:T(8,128)(2,1)}) custom-call(f32[2]{0:T(128)S(1)} %pad_maximum_fusion.refs_0_, s32[3]{0:T(128)S(1)} %pad_add_fusion.refs_1_.refs_0_, bf16[512,1024]{1,0:T(8,128)(2,1)S(1)} %get-tuple-element.50.refs_2_.refs_1_.refs_4_, ...), custom_call_target="tpu_custom_call", output_to_operand_aliasing={{0}: (6, {})} | custom-call | flops 1 | bytes 1 | tf_op jit(solution)/shard_map/pallas_call | solution.py:103
  49.9 2.9 %shard_map.88 = (f32[512,1024]{1,0:T(8,128)S(1)}, f32[512,1]{1,0:T(8,128)S(1)}, bf16[512,896]{1,0:T(8,128)(2,1)S(1)}, bf16[512,128]{1,0:T(8,128)(2,1)S(1)}) custom-call(f32[2]{0:T(128)S(1)} %pad_maximum_fusion.refs_0_, s32[3]{0:T(128)S(1)} %pad_add_fusion.refs_1_.refs_0_, ...), custom_call_target="tpu_custom_call", output_to_operand_aliasing={{0}: (5, {})} | custom-call | flops 1 | bytes 1 | tf_op jit(solution)/shard_map/pallas_call | solution.py:103
  53.8 2.1 %collective-permute-done.13.refs_1_ = bf16[512,896]{1,0:T(8,128)(2,1)S(1)} collective-permute-done((bf16[512,896]{1,0:T(8,128)(2,1)S(1)}, bf16[512,896]{1,0:T(8,128)(2,1)S(1)}, u32[]{:S(2)}, u32[]{:S(2)}) %collective-permute-start.13) | collective-permute-done | bytes 917536 | tf_op jit(solution)/shard_map/ppermute | solution.py:37
  55.9 2.1 %shard_map.89 = (f32[512,256]{1,0:T(8,128)S(1)}, f32[512,1]{1,0:T(8,128)S(1)}, bf16[528,256]{1,0:T(8,128)(2,1)S(1)}, bf16[128,1024]{1,0:T(8,128)(2,1)}, f32[128,1024]{1,0:T(8,128)}) custom-call(s32[3]{0:T(128)S(1)} %pad_add_fusion.refs_1_.refs_0_, bf16[512,896]{1,0:T(8,128)(2,1)S(1)} %collective-permute-done.13.refs_1_, ...), custom_call_target="tpu_custom_call" | custom-call | flops 1 | bytes 1 | tf_op jit(solution)/shard_map/pallas_call | solution.py:103
  58.1 3.0 %collective-permute-start.14 = (bf16[528,256]{1,0:T(8,128)(2,1)S(1)}, bf16[528,256]{1,0:T(8,128)(2,1)S(1)}, u32[]{:S(2)}, u32[]{:S(2)}) collective-permute-start(bf16[528,256]{1,0:T(8,128)(2,1)S(1)} %get-tuple-element.64), channel_id=1, source_target_pairs={{0,16},{8,24},{16,0},{24,8},{32,48},{40,56},{48,32},{56,40},{64,80... | collective-permute-start | bytes 811016 | tf_op jit(solution)/shard_map/ppermute | solution.py:41
  63.7 5.6 %collective-permute-done.15 = bf16[128,1024]{1,0:T(8,128)(2,1)S(1)} collective-permute-done((bf16[128,1024]{1,0:T(8,128)(2,1)S(1)}, bf16[128,1024]{1,0:T(8,128)(2,1)S(1)}, u32[]{:S(2)}, u32[]{:S(2)}) %collective-permute-start.15) | collective-permute-done | bytes 262176 | tf_op jit(solution)/shard_map/ppermute | solution.py:33
  69.3 3.4 %collective-permute-done.16 = bf16[128,1024]{1,0:T(8,128)(2,1)S(1)} collective-permute-done((bf16[128,1024]{1,0:T(8,128)(2,1)S(1)}, bf16[128,1024]{1,0:T(8,128)(2,1)S(1)}, u32[]{:S(2)}, u32[]{:S(2)}) %collective-permute-start.16) | collective-permute-done | bytes 262176 | tf_op jit(solution)/shard_map/ppermute | solution.py:33
  72.7 3.3 %shard_map.91 = bf16[32,72,128]{2,1,0:T(8,128)(2,1)} custom-call(s32[3]{0:T(128)S(1)} %pad_add_fusion.refs_1_.refs_0_, bf16[528,256]{1,0:T(8,128)(2,1)S(1)} %collective-permute-done.14.refs_1_, f32[512,256]{1,0:T(8,128)S(1)} %get-tuple-element.68.refs_2_, f32[512,1]{1,0:T(8,128)S(1)} %get-tuple-element.82.refs_3_, ...), custom_call_target="tpu_custom_call" | custom-call | flops 1 | bytes 1 | tf_op jit(solution)/shard_map/pallas_call | solution.py:103
  76.0 4.3 %all-to-all-start = ((bf16[32,72,128]{2,1,0:T(8,128)(2,1)}), bf16[32,72,128]{2,1,0:T(8,128)(2,1)S(1)}, u32[]{:S(2)}, u32[]{:S(2)}) async-start(bf16[32,72,128]{2,1,0:T(8,128)(2,1)} %shard_map.91), calls=%async_computation | async-start | bytes 1179648 | tf_op jit(solution)/shard_map/all_to_all | solution.py:379
  80.3 3.8 %collective-permute-start.17 = (bf16[128,1024]{1,0:T(8,128)(2,1)}, bf16[128,1024]{1,0:T(8,128)(2,1)S(1)}, u32[]{:S(2)}, u32[]{:S(2)}) collective-permute-start(bf16[128,1024]{1,0:T(8,128)(2,1)} %shard_map.90), channel_id=1, source_target_pairs={{0,64},{8,200},{16,80},{24,216},{32,96},{40,232},{48,112},{56,248}... | collective-permute-start | bytes 786440 | tf_op jit(solution)/shard_map/ppermute | solution.py:33
  85.8 18.8 %collective-permute-done.17 = bf16[128,1024]{1,0:T(8,128)(2,1)S(1)} collective-permute-done((bf16[128,1024]{1,0:T(8,128)(2,1)}, bf16[128,1024]{1,0:T(8,128)(2,1)S(1)}, u32[]{:S(2)}, u32[]{:S(2)}) %collective-permute-start.17) | collective-permute-done | bytes 262176 | tf_op jit(solution)/shard_map/ppermute | solution.py:33
  104.5 2.4 %collective-permute-done.18 = bf16[128,1024]{1,0:T(8,128)(2,1)S(1)} collective-permute-done((bf16[128,1024]{1,0:T(8,128)(2,1)}, bf16[128,1024]{1,0:T(8,128)(2,1)S(1)}, u32[]{:S(2)}, u32[]{:S(2)}) %collective-permute-start.18) | collective-permute-done | bytes 262176 | tf_op jit(solution)/shard_map/ppermute | solution.py:33
  113.1 2.7 %collective-permute-start.22 = (bf16[128,1024]{1,0:T(8,128)(2,1)}, bf16[128,1024]{1,0:T(8,128)(2,1)S(1)}, u32[]{:S(2)}, u32[]{:S(2)}) collective-permute-start(bf16[128,1024]{1,0:T(8,128)(2,1)} %get-tuple-element.88), channel_id=1, source_target_pairs={{0,16},{8,24},{16,0},{24,8},{32,48},{40,56},{48,32},{56,40},{64,80... | collective-permute-start | bytes 786440 | tf_op jit(solution)/shard_map/ppermute | solution.py:41
  117.6 4.8 %all-to-all-start.1 = ((bf16[8,288,128]{2,1,0:T(8,128)(2,1)}), bf16[8,288,128]{2,1,0:T(8,128)(2,1)S(1)}, u32[]{:S(2)}, u32[]{:S(2)}) async-start(bf16[8,288,128]{2,1,0:T(8,128)(2,1)} %shard_map.92), calls=%async_computation.1 | async-start | bytes 1179648 | tf_op jit(solution)/shard_map/all_to_all | solution.py:395
  128.0 3.1 %all-to-all-done.1.refs_0_ = bf16[8,288,128]{2,1,0:T(8,128)(2,1)S(1)} async-done(((bf16[8,288,128]{2,1,0:T(8,128)(2,1)}), bf16[8,288,128]{2,1,0:T(8,128)(2,1)S(1)}, u32[]{:S(2)}, u32[]{:S(2)}) %all-to-all-start.1) | async-done | bytes 589856 | tf_op jit(solution)/shard_map/all_to_all | solution.py:395
  (82 shorter events, 30.8 us)
Async XLA Ops:
  0.6 9.8 %collective-permute-start = (bf16[128,1152]{1,0:T(8,128)(2,1)}, bf16[128,1152]{1,0:T(8,128)(2,1)S(1)}, u32[]{:S(2)}, u32[]{:S(2)}) collective-permute-start(bf16[128,1152]{1,0:T(8,128)(2,1)} %bitcast.19), channel_id=1, source_target_pairs={{0,16},{8,24},{16,0},{24,8},{32,48},{40,56},{48,32},{56,40},{64,80... | collective-permute-start | bytes 884744 | tf_op jit(solution)/shard_map/ppermute | solution.py:41
  4.5 12.2 %collective-permute-start.6 = (bf16[128,1024]{1,0:T(8,128)(2,1)}, bf16[128,1024]{1,0:T(8,128)(2,1)S(1)}, u32[]{:S(2)}, u32[]{:S(2)}) collective-permute-start(bf16[128,1024]{1,0:T(8,128)(2,1)} %bitcast.16), channel_id=1, source_target_pairs={{0,224},{8,40},{16,240},{24,56},{32,0},{40,72},{48,16},{56,88},{64... | collective-permute-start | bytes 786440 | tf_op jit(solution)/shard_map/ppermute | solution.py:33
  6.1 10.6 %collective-permute-start.7 = (bf16[128,1024]{1,0:T(8,128)(2,1)}, bf16[128,1024]{1,0:T(8,128)(2,1)S(1)}, u32[]{:S(2)}, u32[]{:S(2)}) collective-permute-start(bf16[128,1024]{1,0:T(8,128)(2,1)} %bitcast.17), channel_id=1, source_target_pairs={{0,32},{8,232},{16,48},{24,248},{32,64},{40,8},{48,80},{56,24},{64... | collective-permute-start | bytes 786440 | tf_op jit(solution)/shard_map/ppermute | solution.py:33
  10.5 16.0 %collective-permute-start.1 = (bf16[128,1152]{1,0:T(8,128)(2,1)}, bf16[128,1152]{1,0:T(8,128)(2,1)S(1)}, u32[]{:S(2)}, u32[]{:S(2)}) collective-permute-start(bf16[128,1152]{1,0:T(8,128)(2,1)} %bitcast.20), channel_id=1, source_target_pairs={{0,8},{8,0},{16,24},{24,16},{32,40},{40,32},{48,56},{56,48},{64,72... | collective-permute-start | bytes 884744 | tf_op jit(solution)/shard_map/ppermute | solution.py:37
  12.6 13.8 %collective-permute-start.2 = (bf16[128,1152]{1,0:T(8,128)(2,1)S(1)}, bf16[128,1152]{1,0:T(8,128)(2,1)S(1)}, u32[]{:S(2)}, u32[]{:S(2)}) collective-permute-start(bf16[128,1152]{1,0:T(8,128)(2,1)S(1)} %collective-permute-done.refs_3_.refs_8_), channel_id=1, source_target_pairs={{0,8},{8,0},{16,24},{24,16},{32,40},{40,32},{48,56},{56,48},{64,72... | collective-permute-start | bytes 884744 | tf_op jit(solution)/shard_map/ppermute | solution.py:37
  12.6 4.0 %collective-permute-start.4 = (s32[1,128]{1,0:T(1,128)}, s32[1,128]{1,0:T(1,128)S(1)}, u32[]{:S(2)}, u32[]{:S(2)}) collective-permute-start(s32[1,128]{1,0:T(1,128)} %refs_5_.1), channel_id=1, source_target_pairs={{0,16},{8,24},{16,0},{24,8},{32,48},{40,56},{48,32},{56,40},{64,80... | collective-permute-start | bytes 1544 | tf_op jit(solution)/shard_map/ppermute | solution.py:41
  16.7 15.6 %collective-permute-start.8 = (bf16[128,1024]{1,0:T(8,128)(2,1)S(1)}, bf16[128,1024]{1,0:T(8,128)(2,1)S(1)}, u32[]{:S(2)}, u32[]{:S(2)}) collective-permute-start(bf16[128,1024]{1,0:T(8,128)(2,1)S(1)} %collective-permute-done.6.refs_5_), channel_id=1, source_target_pairs={{0,224},{8,40},{16,240},{24,56},{32,0},{40,72},{48,16},{56,88},{64... | collective-permute-start | bytes 786440 | tf_op jit(solution)/shard_map/ppermute | solution.py:33
  18.5 13.9 %collective-permute-start.9 = (bf16[128,1024]{1,0:T(8,128)(2,1)S(1)}, bf16[128,1024]{1,0:T(8,128)(2,1)S(1)}, u32[]{:S(2)}, u32[]{:S(2)}) collective-permute-start(bf16[128,1024]{1,0:T(8,128)(2,1)S(1)} %collective-permute-done.7.refs_6_), channel_id=1, source_target_pairs={{0,32},{8,232},{16,48},{24,248},{32,64},{40,8},{48,80},{56,24},{64... | collective-permute-start | bytes 786440 | tf_op jit(solution)/shard_map/ppermute | solution.py:33
  22.5 2.8 %collective-permute-start.3 = (s32[1,128]{1,0:T(1,128)}, s32[1,128]{1,0:T(1,128)S(1)}, u32[]{:S(2)}, u32[]{:S(2)}) collective-permute-start(s32[1,128]{1,0:T(1,128)} %refs_5_.1), channel_id=1, source_target_pairs={{0,8},{8,0},{16,24},{24,16},{32,40},{40,32},{48,56},{56,48},{64,72... | collective-permute-start | bytes 1544 | tf_op jit(solution)/shard_map/ppermute | solution.py:37
  32.3 10.2 %collective-permute-start.10 = (bf16[128,1024]{1,0:T(8,128)(2,1)S(1)}, bf16[128,1024]{1,0:T(8,128)(2,1)S(1)}, u32[]{:S(2)}, u32[]{:S(2)}) collective-permute-start(bf16[128,1024]{1,0:T(8,128)(2,1)S(1)} %collective-permute-done.9.refs_8_), channel_id=1, source_target_pairs={{0,32},{8,232},{16,48},{24,248},{32,64},{40,8},{48,80},{56,24},{64... | collective-permute-start | bytes 786440 | tf_op jit(solution)/shard_map/ppermute | solution.py:33
  36.9 8.4 %collective-permute-start.12 = (bf16[128,1024]{1,0:T(8,128)(2,1)S(1)}, bf16[128,1024]{1,0:T(8,128)(2,1)S(1)}, u32[]{:S(2)}, u32[]{:S(2)}) collective-permute-start(bf16[128,1024]{1,0:T(8,128)(2,1)S(1)} %collective-permute-done.8.refs_7_), channel_id=1, source_target_pairs={{0,224},{8,40},{16,240},{24,56},{32,0},{40,72},{48,16},{56,88},{64... | collective-permute-start | bytes 786440 | tf_op jit(solution)/shard_map/ppermute | solution.py:33
  42.6 7.4 %collective-permute-start.11 = (bf16[128,1024]{1,0:T(8,128)(2,1)S(1)}, bf16[128,1024]{1,0:T(8,128)(2,1)S(1)}, u32[]{:S(2)}, u32[]{:S(2)}) collective-permute-start(bf16[128,1024]{1,0:T(8,128)(2,1)S(1)} %collective-permute-done.10.refs_5_), channel_id=1, source_target_pairs={{0,32},{8,232},{16,48},{24,248},{32,64},{40,8},{48,80},{56,24},{64... | collective-permute-start | bytes 786440 | tf_op jit(solution)/shard_map/ppermute | solution.py:33
  52.8 3.1 %collective-permute-start.13 = (bf16[512,896]{1,0:T(8,128)(2,1)S(1)}, bf16[512,896]{1,0:T(8,128)(2,1)S(1)}, u32[]{:S(2)}, u32[]{:S(2)}) collective-permute-start(bf16[512,896]{1,0:T(8,128)(2,1)S(1)} %get-tuple-element.59), channel_id=1, source_target_pairs={{0,8},{8,0},{16,24},{24,16},{32,40},{40,32},{48,56},{56,48},{64,72... | collective-permute-start | bytes 2752520 | tf_op jit(solution)/shard_map/ppermute | solution.py:37
  58.1 14.7 %collective-permute-start.14 = (bf16[528,256]{1,0:T(8,128)(2,1)S(1)}, bf16[528,256]{1,0:T(8,128)(2,1)S(1)}, u32[]{:S(2)}, u32[]{:S(2)}) collective-permute-start(bf16[528,256]{1,0:T(8,128)(2,1)S(1)} %get-tuple-element.64), channel_id=1, source_target_pairs={{0,16},{8,24},{16,0},{24,8},{32,48},{40,56},{48,32},{56,40},{64,80... | collective-permute-start | bytes 811016 | tf_op jit(solution)/shard_map/ppermute | solution.py:41
  62.1 7.2 %collective-permute-start.15 = (bf16[128,1024]{1,0:T(8,128)(2,1)S(1)}, bf16[128,1024]{1,0:T(8,128)(2,1)S(1)}, u32[]{:S(2)}, u32[]{:S(2)}) collective-permute-start(bf16[128,1024]{1,0:T(8,128)(2,1)S(1)} %copy-done.17), channel_id=1, source_target_pairs={{0,32},{8,232},{16,48},{24,248},{32,64},{40,8},{48,80},{56,24},{64... | collective-permute-start | bytes 786440 | tf_op jit(solution)/shard_map/ppermute | solution.py:33
  63.5 9.3 %collective-permute-start.16 = (bf16[128,1024]{1,0:T(8,128)(2,1)S(1)}, bf16[128,1024]{1,0:T(8,128)(2,1)S(1)}, u32[]{:S(2)}, u32[]{:S(2)}) collective-permute-start(bf16[128,1024]{1,0:T(8,128)(2,1)S(1)} %copy-done.16), channel_id=1, source_target_pairs={{0,224},{8,40},{16,240},{24,56},{32,0},{40,72},{48,16},{56,88},{64... | collective-permute-start | bytes 786440 | tf_op jit(solution)/shard_map/ppermute | solution.py:33
  76.0 40.7 %all-to-all-start = ((bf16[32,72,128]{2,1,0:T(8,128)(2,1)}), bf16[32,72,128]{2,1,0:T(8,128)(2,1)S(1)}, u32[]{:S(2)}, u32[]{:S(2)}) async-start(bf16[32,72,128]{2,1,0:T(8,128)(2,1)} %shard_map.91), calls=%async_computation | async-start | bytes 1179648 | tf_op jit(solution)/shard_map/all_to_all | solution.py:379
  80.3 24.2 %collective-permute-start.17 = (bf16[128,1024]{1,0:T(8,128)(2,1)}, bf16[128,1024]{1,0:T(8,128)(2,1)S(1)}, u32[]{:S(2)}, u32[]{:S(2)}) collective-permute-start(bf16[128,1024]{1,0:T(8,128)(2,1)} %shard_map.90), channel_id=1, source_target_pairs={{0,64},{8,200},{16,80},{24,216},{32,96},{40,232},{48,112},{56,248}... | collective-permute-start | bytes 786440 | tf_op jit(solution)/shard_map/ppermute | solution.py:33
  84.1 22.8 %collective-permute-start.18 = (bf16[128,1024]{1,0:T(8,128)(2,1)}, bf16[128,1024]{1,0:T(8,128)(2,1)S(1)}, u32[]{:S(2)}, u32[]{:S(2)}) collective-permute-start(bf16[128,1024]{1,0:T(8,128)(2,1)} %get-tuple-element.79), channel_id=1, source_target_pairs={{0,32},{8,232},{16,48},{24,248},{32,64},{40,8},{48,80},{56,24},{64... | collective-permute-start | bytes 786440 | tf_op jit(solution)/shard_map/ppermute | solution.py:33
  85.3 21.6 %collective-permute-start.19 = (bf16[128,1024]{1,0:T(8,128)(2,1)}, bf16[128,1024]{1,0:T(8,128)(2,1)}, u32[]{:S(2)}, u32[]{:S(2)}) collective-permute-start(bf16[128,1024]{1,0:T(8,128)(2,1)} %get-tuple-element.80), channel_id=1, source_target_pairs={{0,224},{8,40},{16,240},{24,56},{32,0},{40,72},{48,16},{56,88},{64... | collective-permute-start | bytes 786440 | tf_op jit(solution)/shard_map/ppermute | solution.py:33
  107.7 14.8 %collective-permute-start.21 = (bf16[128,1024]{1,0:T(8,128)(2,1)}, bf16[128,1024]{1,0:T(8,128)(2,1)}, u32[]{:S(2)}, u32[]{:S(2)}) collective-permute-start(bf16[128,1024]{1,0:T(8,128)(2,1)} %add_convert_fusion), channel_id=1, source_target_pairs={{0,192},{8,72},{16,208},{24,88},{32,224},{40,104},{48,240},{56,120... | collective-permute-start | bytes 786440 | tf_op jit(solution)/shard_map/ppermute | solution.py:33
  111.3 12.3 %collective-permute-start.20 = (bf16[128,1024]{1,0:T(8,128)(2,1)}, bf16[128,1024]{1,0:T(8,128)(2,1)}, u32[]{:S(2)}, u32[]{:S(2)}) collective-permute-start(bf16[128,1024]{1,0:T(8,128)(2,1)} %add_convert_fusion.1), channel_id=1, source_target_pairs={{0,64},{8,200},{16,80},{24,216},{32,96},{40,232},{48,112},{56,248}... | collective-permute-start | bytes 786440 | tf_op jit(solution)/shard_map/ppermute | solution.py:33
  113.1 10.5 %collective-permute-start.22 = (bf16[128,1024]{1,0:T(8,128)(2,1)}, bf16[128,1024]{1,0:T(8,128)(2,1)S(1)}, u32[]{:S(2)}, u32[]{:S(2)}) collective-permute-start(bf16[128,1024]{1,0:T(8,128)(2,1)} %get-tuple-element.88), channel_id=1, source_target_pairs={{0,16},{8,24},{16,0},{24,8},{32,48},{40,56},{48,32},{56,40},{64,80... | collective-permute-start | bytes 786440 | tf_op jit(solution)/shard_map/ppermute | solution.py:41
  117.6 13.4 %all-to-all-start.1 = ((bf16[8,288,128]{2,1,0:T(8,128)(2,1)}), bf16[8,288,128]{2,1,0:T(8,128)(2,1)S(1)}, u32[]{:S(2)}, u32[]{:S(2)}) async-start(bf16[8,288,128]{2,1,0:T(8,128)(2,1)} %shard_map.92), calls=%async_computation.1 | async-start | bytes 1179648 | tf_op jit(solution)/shard_map/all_to_all | solution.py:395
  (19 other events, 238.6 us)

commit v9 on v7

--- a/solution.py
+++ b/solution.py
@@ -121,18 +121,21 @@
     return emb, (jax.nn.sigmoid(logits) - positive).astype(BF16)
 
 
-def columns_of(start, rows):
+def columns_of(place, key, rows):
+    step = (1 - 2 * (place[0] & 1)) * (YH * CORE)
+    start = (place[0] + key * step + LOOP) % LOOP * rows
     return (lax.broadcasted_iota(jnp.int32, (1, rows), 1) + start).astype(F32)
 
 
-def pairs_kernel(count, first, moves, numbers, starts, image_emb, match, *refs):
+def pairs_kernel(keys, first, moves, numbers, place, image_emb, match, *refs):
+    count = len(keys)
     texts, refs = refs[:count], refs[count:]
     if not first:
         acc_in, refs = refs[0], refs[1:]
     acc_out, text_out = refs[0], refs[1:]
     image = image_emb[...]
     rows = texts[0].shape[0]
-    columns = jnp.concatenate([columns_of(starts[n], rows) for n in range(count)], 1)
+    columns = jnp.concatenate([columns_of(place, key, rows) for key in keys], 1)
     for n in range(count):
         moves.need(4 + n)
     emb, grad = block_grads(numbers, columns, image, match[...], moves.pack[...])
@@ -157,13 +160,15 @@
     inv = lax.rsqrt(jnp.sum(projected * projected, -1, keepdims=True) + 1e-06)
     emb[...] = (projected * inv).astype(BF16)
     inv_out[...] = inv
+    moves.send(1)
+    moves.need(5)
     for n in range(4):
         match = jnp.broadcast_to(matches[n][...].astype(F32), (rows, rows))
         match_out[n * rows : (n + 1) * rows, :] = match.T[:, 0:1]
 
 
-def last_kernel(moves, numbers, starts, image_emb, match, text, acc_in, acc_out, dot_out, packet, grad_out):
-    columns = columns_of(starts[0], text.shape[0])
+def last_kernel(moves, numbers, place, image_emb, match, text, acc_in, acc_out, dot_out, packet, extra, grad_out):
+    columns = columns_of(place, 4, text.shape[0])
     emb, grad = block_grads(numbers, columns, image_emb[...], match[...], text[...])
     grad_out[...] = grad
     acc = numbers[0] * (acc_in[...] + jnp.dot(grad, emb, preferred_element_type=F32))
@@ -171,19 +176,22 @@
     dot = jnp.sum(image_emb[...].astype(F32) * acc, -1, keepdims=True)
     dot_out[...] = dot
     rows, width = acc.shape
-    half, quarter, block = width // 2, width // 4, rows // 4
-    own = pl.multiple_of(starts[1] * half, half)
-    other = pl.multiple_of((1 - starts[1]) * half, half)
-    packet[:, :half] = acc_out[:, pl.ds(other, half)].astype(BF16)
-    top = dot.astype(BF16).astype(F32)
-    lane = lax.broadcasted_iota(jnp.int32, (rows, 128), 1)
-    digits = jnp.where(lane == 0, top, jnp.where(lane == 1, dot - top, 0.0))
-    packet[:, half : half + 128] = digits.astype(BF16)
-    for side in range(2):
-        lanes = pl.ds(pl.multiple_of(own + side * quarter, quarter), quarter)
-        for n, slot in enumerate((1, 3)):
-            at = (2 * side + n) * block
-            packet[at : at + block, half + 128 :] = acc_out[slot * block : (slot + 1) * block, lanes].astype(BF16)
+    half, block = width // 2, rows // 4
+    core = place[0] & 1
+    own = pl.ds(pl.multiple_of(core * half, half), half)
+    other = pl.ds(pl.multiple_of((1 - core) * half, half), half)
+    for n, slot in enumerate((1, 3)):
+        extra[n * block : (n + 1) * block, :] = acc_out[slot * block : (slot + 1) * block, own].astype(BF16)
+    moves.send(3)
+    packet[:rows, :] = acc_out[:, other].astype(BF16)
+    lines = []
+    for slot in range(4):
+        mine = slice(slot * block, (slot + 1) * block)
+        flat = jnp.broadcast_to(dot[mine], (block, 128)).T[0:1, :]
+        top = flat.astype(BF16).astype(F32)
+        lines.append(jnp.concatenate([top, flat - top, jnp.zeros((1, half - 256), F32)], 1))
+    lines.append(jnp.zeros((packet.shape[0] - rows - 4, half), F32))
+    packet[rows:, :] = jnp.concatenate(lines, 0).astype(BF16)
 
 
 def last_text_kernel(moves, grad, image_emb, out):
@@ -191,33 +199,23 @@
     moves.send(0)
 
 
-def weight_kernel(moves, starts, got, acc, dot, image_emb, inv, own_rows, core_rows, yh_rows, both_rows, weight, row_send, row_keep):
+def weight_kernel(moves, place, got, acc, dot, image_emb, inv, own_rows, core_rows, yh_rows, both_rows, weight):
     rows, width = acc.shape
     half, quarter, block = width // 2, width // 4, rows // 4
-    own = pl.ds(pl.multiple_of(starts[1] * half, half), half)
+    own = pl.ds(pl.multiple_of((place[0] & 1) * half, half), half)
+    digits = got[rows:, :256].astype(F32)
+    moves.need(5)
     projs = []
     for slot in range(4):
         mine = slice(slot * block, (slot + 1) * block)
         theirs = slice((slot ^ 1) * block, ((slot ^ 1) + 1) * block)
-        kept = acc[mine, own] + got[theirs, :half].astype(F32)
-        digits = got[theirs, half : half + 128].astype(F32)
-        whole_dot = dot[mine, :] + digits[:, 0:1] + digits[:, 1:2]
+        kept = acc[mine, own] + got[theirs, :].astype(F32)
+        line = digits[slot ^ 1 : (slot ^ 1) + 1, :]
+        other_dot = jnp.broadcast_to(line[:, :128] + line[:, 128:], (block, 128)).T[:, 0:1]
         unit = image_emb[mine, own].astype(F32)
-        projs.append(((kept - unit * whole_dot) * inv[mine, :]).astype(BF16))
-        if slot in (0, 2):
-            target = (row_keep, row_send)[slot // 2]
-            target[:, own] = kept.astype(target.dtype)
-            for side in range(2):
-                first = pl.multiple_of((1 - starts[1]) * half + side * quarter, quarter)
-                lanes = pl.ds(first, quarter)
-                at = (2 * side + slot // 2) * block
-                extra = got[at : at + block, half + 128 :].astype(F32)
-                target[:, lanes] = (acc[mine, lanes] + extra).astype(target.dtype)
-            moves.send(2 - slot // 2)
+        projs.append(((kept - unit * (dot[mine, :] + other_dot)) * inv[mine, :]).astype(BF16))
     proj = jnp.concatenate(projs, 0)
-    for n in range(6, 10):
-        moves.need(n)
-    sensor = moves.pack[...]
+    sensor = jnp.concatenate([own_rows[...], core_rows[...], yh_rows[...], both_rows[...]], 0)
     chunk = weight.shape[1]
     for side in range(2):
         product = inner_cols(proj[:, side * quarter : (side + 1) * quarter], sensor).astype(BF16)
@@ -225,6 +223,23 @@
             at = side * (quarter // chunk) + m
             weight[at] = product[m * chunk : (m + 1) * chunk]
             moves.send(0, at)
+
+
+def row_kernel(moves, place, got, extra, acc, row_send, row_keep):
+    rows, width = acc.shape
+    half, block = width // 2, rows // 4
+    core = place[0] & 1
+    own = pl.ds(pl.multiple_of(core * half, half), half)
+    other = pl.ds(pl.multiple_of((1 - core) * half, half), half)
+    moves.need(1)
+    for n, target in enumerate((row_keep, row_send)):
+        slot = 2 * n
+        mine = slice(slot * block, (slot + 1) * block)
+        theirs = slice((slot + 1) * block, (slot + 2) * block)
+        target[:, own] = (acc[mine, own] + got[theirs, :].astype(F32)).astype(target.dtype)
+        rest = extra[n * block : (n + 1) * block, :].astype(F32)
+        target[:, other] = (acc[mine, other] + rest).astype(target.dtype)
+        moves.send(1 - n)
 
 
 def chunk_kernel(moves, parts, out):
@@ -270,8 +285,7 @@
     rows = sensor.shape[0]
     feat, width = proj_weight.shape
     loop_index = lax.axis_index("loop")
-    z = loop_index // (YH * CORE)
-    core = loop_index % CORE
+    place = loop_index.reshape(1)
     logit_scale = jnp.exp(log_scale)
     numbers = jnp.stack([logit_scale, logit_bias])
 
@@ -285,63 +299,73 @@
     slot[2], slot[-2] = shift_z(up, -1), shift_z(down, 1)
     sensor_later, _ = lax.optimization_barrier((sensor, sensor_yh))
     sensors = [sensor, swap_core(sensor_later), sensor_yh, swap_core(sensor_yh)]
-    match_both = swap_core(jnp.concatenate([match, match_yh], 0))
-    match = [match, match_both[:1], match_yh, match_both[1:]]
+    match = [match, swap_core(match), match_yh, swap_core(match_yh)]
     shapes = [((4 * rows, width), BF16), ((4 * rows, 1), F32), ((4 * rows, 1), F32)]
     image_emb, image_inv, match_rows = call(
         project_kernel,
         [jax.ShapeDtypeStruct(*s) for s in shapes],
         {},
         proj_weight, *sensors, *match,
-        far=(0,),
+        far=(0, 5),
         packed=range(1, 5),
+        far_out=(1,),
         cuts={0: CUT},
     )
     up, down, _ = lax.optimization_barrier((slot[2], slot[-2], image_emb))
     slot[3], slot[-3] = shift_z(up, -1), shift_z(down, 1)
 
-    def starts_of(keys):
-        step = (1 - 2 * core) * YH * CORE
-        return [(loop_index + k * step + LOOP) % LOOP * rows for k in keys]
-
     def pairs(keys, dtypes, acc):
-        operands = [numbers, jnp.stack(starts_of(keys)), image_emb, match_rows, *(slot[k] for k in keys)]
+        operands = [numbers, place, image_emb, match_rows, *(slot[k] for k in keys)]
         out = [jax.ShapeDtypeStruct((4 * rows, width), F32)]
         out += [jax.ShapeDtypeStruct((rows, width), d) for d in dtypes]
         aliases = {}
         if acc is not None:
             aliases = {len(operands): 0}
             operands.append(acc)
-        kernel = functools.partial(pairs_kernel, len(keys), acc is None)
+        kernel = functools.partial(pairs_kernel, keys, acc is None)
         return call(kernel, out, aliases, *operands, packed=range(4, 4 + len(keys)), far_out=range(1, len(out)))
 
     acc, text_0, text_1, text_m1, text_2, text_m2 = pairs((0, 1, -1, 2, -2), (F32, BF16, BF16, BF16, BF16), None)
     last_text, _ = lax.optimization_barrier((slot[-3], acc))
     last_text = shift_z(last_text, 1)
     acc, text_3, text_m3 = pairs((3, -3), (BF16, BF16), acc)
-    starts = jnp.stack(starts_of((4,)) + [core])
-    shapes = [((4 * rows, width), F32), ((4 * rows, 1), F32), ((4 * rows, width // 8 * 7), BF16), ((4 * rows, rows), BF16)]
-    acc, dot, packet, last_grad = call(
+    shapes = [((4 * rows, width), F32), ((4 * rows, 1), F32), ((4 * rows + 16, width // 2), BF16)]
+    shapes += [((2 * rows, width // 2), BF16), ((4 * rows, rows), BF16)]
+    acc, dot, packet, extra, last_grad = call(
         last_kernel,
         [jax.ShapeDtypeStruct(*s) for s in shapes],
         {5: 0},
-        numbers, starts, image_emb, match_rows, last_text, acc,
+        numbers, place, image_emb, match_rows, last_text, acc,
+        far_out=(3,),
+    )
+
+    got = swap_core(packet)
+    (weight_part,) = call(
+        weight_kernel,
+        [jax.ShapeDtypeStruct((DP, width // 16, feat), BF16)],
+        {},
+        place, got, acc, dot, image_emb, image_inv, *sensors,
+        far=(5,),
+        far_out=(0,),
+        sends=DP,
+    )
+    last_grad, extra, text_1, text_m1, text_3, text_m3, _ = lax.optimization_barrier(
+        (last_grad, extra, text_1, text_m1, text_3, text_m3, weight_part)
     )
     (text_4,) = call(
         last_text_kernel, [jax.ShapeDtypeStruct((rows, width), BF16)], {}, last_grad, image_emb, far_out=(0,)
     )
-
-    shapes = [((DP, width // 16, feat), BF16), ((rows, width), BF16), ((rows, width), F32)]
-    weight_part, row_send, row_keep = call(
-        weight_kernel,
+    shapes = [((rows, width), BF16), ((rows, width), F32)]
+    row_send, row_keep = call(
+        row_kernel,
         [jax.ShapeDtypeStruct(*s) for s in shapes],
         {},
-        starts, swap_core(packet), acc, dot, image_emb, image_inv, *sensors,
-        packed=range(6, 10),
-        far_out=range(3),
-        sends=2 + DP,
+        place, got, swap_core(extra), acc,
+        far=(1,),
+        far_out=(0, 1),
     )
     weight_part = lax.all_to_all(weight_part, "dp", 0, 0, tiled=True)
+
     per_loop = feat // LOOP
     block = (per_loop // 2, width // 8)
     (weight_chunks,) = call(
@@ -352,15 +376,12 @@
         share_kernel, [jax.ShapeDtypeStruct((DP, per_loop, width // 8), F32)], {}, weight_part, far_out=(0,)
     )
 
-    text_3, text_m3, text_4, text_1, text_m1, _ = lax.optimization_barrier(
-        (text_3, text_m3, text_4, text_1, text_m1, row_keep)
-    )
-    row_got = swap_yh(row_send)
     from_below, from_above, far = shift_z(text_3, 1), shift_z(text_m3, -1), shift_z(text_4, 2)
     near_below, near_above = shift_z(text_1, 1), shift_z(text_m1, -1)
-    from_below, from_above, far, near_below, near_above, row_got, _ = lax.optimization_barrier(
-        (from_below, from_above, far, near_below, near_above, row_got, weight_chunks)
-    )
+    from_below, from_above, far, near_below, near_above, row_send, _ = lax.optimization_barrier(
+        (from_below, from_above, far, near_below, near_above, row_send, weight_chunks)
+    )
+    row_got = swap_yh(row_send)
     up = text_2.astype(F32) + from_below.astype(F32) + far.astype(F32)
     down = text_m2.astype(F32) + from_above.astype(F32)
     up, down = shift_z(up.astype(BF16), 2), shift_z(down.astype(BF16), -2)

time: 115 us -> 120 us (1.043)
  starting transfers between devices: 50.6 us -> 57.7 us
  waiting for transfers between devices: 23.1 us -> 19 us
  Pallas kernels: 24.3 us -> 27.4 us
    ppermute x3, starting transfers between devices: 5.07 us -> 9.68 us  [swap_yh(): return lax.ppermute(block, 'loop', route(lambda z, y, c: (z, 1 - y, c)))]
    ppermute x14, waiting for transfers between devices: 7 us -> 3.14 us  [shift_z(): lax.ppermute(block, 'loop', route(lambda z, y, c: (z + (1 - 2 * c) * dist...]
    pallas_call x9 -> x10, Pallas kernels: 24.3 us -> 27.4 us  [call(): pl.pallas_call(body, out_shape=[pltpu.HBM(o.shape, o.dtype) if n in far_o...]
    all_to_all x1, waiting for transfers between devices: 4.14 us -> 1.95 us  [on_device(): weight_part = lax.all_to_all(weight_chunks, 'loop', 0, 0, tiled=True)]
    ppermute x14, starting transfers between devices: 22.9 us -> 25 us  [shift_z(): lax.ppermute(block, 'loop', route(lambda z, y, c: (z + (1 - 2 * c) * dist...]
    all_to_all x1, waiting for transfers between devices: 7.08 us -> 9.04 us  [on_device(): weight_part = lax.all_to_all(weight_part, 'dp', 0, 0, tiled=True)]
    ppermute x4 -> x6, starting transfers between devices: 7.01 us -> 6.07 us  [swap_core(): return lax.ppermute(block, 'loop', route(lambda z, y, c: (z, y, 1 - c)))]
    ppermute x4 -> x6, waiting for transfers between devices: 3.24 us -> 3.34 us  [swap_core(): return lax.ppermute(block, 'loop', route(lambda z, y, c: (z, y, 1 - c)))]
  transfers between devices with their start and end apart: 24 -> 26, of which waited for: 10 -> 9; matrix products, arithmetic and copies ran while one was open for 10% -> 9% of each run, Pallas kernels for 14% -> 17%
where the time goes in v9:
time: 120 us
  starting transfers between devices  57.7 us (48%)
  Pallas kernels  27.4 us (23%)
  waiting for transfers between devices  19 us (16%)
  other arithmetic  5.95 us (5%)
  local copies, waits for them, and re-layouts  3.9 us (3%)
  matrix products  3.36 us (3%)
  between operations  2.48 us (2%)
    pallas_call x10, Pallas kernels, call(): pl.pallas_call(body, out_shape=[pltpu.HBM(o.shape, o.dtype) if n in far_o...  27.4 us
    ppermute x14, starting transfers between devices, shift_z(): lax.ppermute(block, 'loop', route(lambda z, y, c: (z + (1 - 2 * c) * dist...  25 us
    ppermute x3, starting transfers between devices, swap_yh(): return lax.ppermute(block, 'loop', route(lambda z, y, c: (z, 1 - y, c)))  9.68 us
    all_to_all x1, waiting for transfers between devices, on_device(): weight_part = lax.all_to_all(weight_part, 'dp', 0, 0, tiled=True)  9.04 us
    all_to_all x1, starting transfers between devices, on_device(): weight_part = lax.all_to_all(weight_chunks, 'loop', 0, 0, tiled=True)  8.56 us
    ppermute x6, starting transfers between devices, swap_core(): return lax.ppermute(block, 'loop', route(lambda z, y, c: (z, y, 1 - c)))  6.07 us
    all_to_all x1, starting transfers between devices, on_device(): weight_part = lax.all_to_all(weight_part, 'dp', 0, 0, tiled=True)  5.04 us
    all_to_all x1, starting transfers between devices, on_device(): shares = lax.all_to_all(shares, 'dp', 0, 0, tiled=True)  3.39 us
  transfers between devices with their start and end apart: 26, of which 9 were waited for; matrix products, arithmetic and copies ran while one was open for 9% of the time, Pallas kernels for 17%

profile of v9, /device:TPU:1, one launch (start us, length us, event | category | flops | bytes accessed | tf_op | source)
XLA Modules:
  0.0 119.8 jit_solution(2809057445156901504)
XLA Ops:
  0.6 3.8 %collective-permute-start = (bf16[128,1152]{1,0:T(8,128)(2,1)}, bf16[128,1152]{1,0:T(8,128)(2,1)S(1)}, u32[]{:S(2)}, u32[]{:S(2)}) collective-permute-start(bf16[128,1152]{1,0:T(8,128)(2,1)} %bitcast.14), channel_id=1, source_target_pairs={{0,16},{8,24},{16,0},{24,8},{32,48},{40,56},{48,32},{56,40},{64,80... | collective-permute-start | bytes 884744 | tf_op jit(solution)/shard_map/ppermute | solution.py:41
  6.1 3.9 %collective-permute-start.7 = (bf16[128,1024]{1,0:T(8,128)(2,1)}, bf16[128,1024]{1,0:T(8,128)(2,1)S(1)}, u32[]{:S(2)}, u32[]{:S(2)}) collective-permute-start(bf16[128,1024]{1,0:T(8,128)(2,1)} %bitcast.19), channel_id=1, source_target_pairs={{0,32},{8,232},{16,48},{24,248},{32,64},{40,8},{48,80},{56,24},{64... | collective-permute-start | bytes 786440 | tf_op jit(solution)/shard_map/ppermute | solution.py:33
  10.5 2.2 %collective-permute-start.1 = (bf16[128,1152]{1,0:T(8,128)(2,1)}, bf16[128,1152]{1,0:T(8,128)(2,1)S(1)}, u32[]{:S(2)}, u32[]{:S(2)}) collective-permute-start(bf16[128,1152]{1,0:T(8,128)(2,1)} %bitcast.15), channel_id=1, source_target_pairs={{0,8},{8,0},{16,24},{24,16},{32,40},{40,32},{48,56},{56,48},{64,72... | collective-permute-start | bytes 884744 | tf_op jit(solution)/shard_map/ppermute | solution.py:37
  12.6 3.0 %collective-permute-start.4 = (s32[1,128]{1,0:T(1,128)}, s32[1,128]{1,0:T(1,128)S(1)}, u32[]{:S(2)}, u32[]{:S(2)}) collective-permute-start(s32[1,128]{1,0:T(1,128)} %refs_5_.1), channel_id=1, source_target_pairs={{0,16},{8,24},{16,0},{24,8},{32,48},{40,56},{48,32},{56,40},{64,80... | collective-permute-start | bytes 1544 | tf_op jit(solution)/shard_map/ppermute | solution.py:41
  16.7 1.8 %collective-permute-start.8 = (bf16[128,1024]{1,0:T(8,128)(2,1)S(1)}, bf16[128,1024]{1,0:T(8,128)(2,1)}, u32[]{:S(2)}, u32[]{:S(2)}) collective-permute-start(bf16[128,1024]{1,0:T(8,128)(2,1)S(1)} %collective-permute-done.6.refs_5_), channel_id=1, source_target_pairs={{0,224},{8,40},{16,240},{24,56},{32,0},{40,72},{48,16},{56,88},{64... | collective-permute-start | bytes 786440 | tf_op jit(solution)/shard_map/ppermute | solution.py:33
  18.5 4.0 %collective-permute-start.9 = (bf16[128,1024]{1,0:T(8,128)(2,1)S(1)}, bf16[128,1024]{1,0:T(8,128)(2,1)}, u32[]{:S(2)}, u32[]{:S(2)}) collective-permute-start(bf16[128,1024]{1,0:T(8,128)(2,1)S(1)} %collective-permute-done.7.refs_6_), channel_id=1, source_target_pairs={{0,32},{8,232},{16,48},{24,248},{32,64},{40,8},{48,80},{56,24},{64... | collective-permute-start | bytes 786440 | tf_op jit(solution)/shard_map/ppermute | solution.py:33
  22.5 1.8 %collective-permute-start.3 = (s32[1,128]{1,0:T(1,128)}, s32[1,128]{1,0:T(1,128)S(1)}, u32[]{:S(2)}, u32[]{:S(2)}) collective-permute-start(s32[1,128]{1,0:T(1,128)} %refs_5_.1), channel_id=1, source_target_pairs={{0,8},{8,0},{16,24},{24,16},{32,40},{40,32},{48,56},{56,48},{64,72... | collective-permute-start | bytes 1544 | tf_op jit(solution)/shard_map/ppermute | solution.py:37
  27.8 4.4 %shard_map.85 = (bf16[512,1024]{1,0:T(8,128)(2,1)S(1)}, f32[512,1]{1,0:T(8,128)}, f32[512,1]{1,0:T(8,128)S(1)}) custom-call(bf16[1152,1024]{1,0:T(8,128)(2,1)} %refs_0_.1, bf16[128,1152]{1,0:T(8,128)(2,1)} %bitcast.16, bf16[128,1152]{1,0:T(8,128)(2,1)} %copy-done.4, bf16[128,1152]{1,0:T(8,128)(2,1)} %copy-done.2, bf16[128,1152]{1,0:T(8,128)(2,1)} %copy-done.6, ...), custom_call_target="tpu_custom_call" | custom-call | flops 1 | bytes 1 | tf_op jit(solution)/shard_map/pallas_call | solution.py:103
  32.3 3.0 %collective-permute-start.10 = (bf16[128,1024]{1,0:T(8,128)(2,1)}, bf16[128,1024]{1,0:T(8,128)(2,1)}, u32[]{:S(2)}, u32[]{:S(2)}) collective-permute-start(bf16[128,1024]{1,0:T(8,128)(2,1)} %collective-permute-done.9.refs_8_), channel_id=1, source_target_pairs={{0,32},{8,232},{16,48},{24,248},{32,64},{40,8},{48,80},{56,24},{64... | collective-permute-start | bytes 786440 | tf_op jit(solution)/shard_map/ppermute | solution.py:33
  37.0 5.4 %shard_map.86 = (f32[512,1024]{1,0:T(8,128)S(1)}, f32[128,1024]{1,0:T(8,128)}, bf16[128,1024]{1,0:T(8,128)(2,1)}, bf16[128,1024]{1,0:T(8,128)(2,1)}, bf16[128,10...) custom-call(f32[2]{0:T(128)S(1)} %pad_maximum_fusion.refs_0_, s32[1]{0:T(128)} %bitcast.refs_1_.refs_0_, ...), custom_call_target="tpu_custom_call" | custom-call | flops 1 | bytes 1 | tf_op jit(solution)/shard_map/pallas_call | solution.py:103
  42.4 2.7 %collective-permute-start.11 = (bf16[128,1024]{1,0:T(8,128)(2,1)}, bf16[128,1024]{1,0:T(8,128)(2,1)S(1)}, u32[]{:S(2)}, u32[]{:S(2)}) collective-permute-start(bf16[128,1024]{1,0:T(8,128)(2,1)} %collective-permute-done.10.refs_5_), channel_id=1, source_target_pairs={{0,32},{8,232},{16,48},{24,248},{32,64},{40,8},{48,80},{56,24},{64... | collective-permute-start | bytes 786440 | tf_op jit(solution)/shard_map/ppermute | solution.py:33
  45.8 4.0 %shard_map.87 = (f32[512,1024]{1,0:T(8,128)S(1)}, bf16[128,1024]{1,0:T(8,128)(2,1)}, bf16[128,1024]{1,0:T(8,128)(2,1)}) custom-call(f32[2]{0:T(128)S(1)} %pad_maximum_fusion.refs_0_, s32[1]{0:T(128)} %bitcast.refs_1_.refs_0_, bf16[512,1024]{1,0:T(8,128)(2,1)S(1)} %get-tuple-element.44.refs_2_.refs_4_.refs_1_, ...), custom_call_target="tpu_custom_call", output_to_operand_aliasing={{0}: (6, {})} | custom-call | flops 1 | bytes 1 | tf_op jit(solution)/shard_map/pallas_call | solution.py:103
  49.8 3.7 %shard_map.88 = (f32[512,1024]{1,0:T(8,128)S(1)}, f32[512,1]{1,0:T(8,128)S(1)}, bf16[528,512]{1,0:T(8,128)(2,1)S(1)}, bf16[256,512]{1,0:T(8,128)(2,1)}, bf16[512,128]{1,0:T(8,128)(2,1)S(1)}) custom-call(f32[2]{0:T(128)S(1)} %pad_maximum_fusion.refs_0_, s32[1]{0:T(128)} %bitcast.refs_1_.refs_0_, ...), custom_call_target="tpu_custom_call", output_to_operand_aliasing={{0}: (5, {})} | custom-call | flops 1 | bytes 1 | tf_op jit(solution)/shard_map/pallas_call | solution.py:103
  56.1 3.1 %shard_map.89 = bf16[8,64,1152]{2,1,0:T(8,128)(2,1)} custom-call(s32[1]{0:T(128)} %bitcast.refs_1_.refs_0_, bf16[528,512]{1,0:T(8,128)(2,1)S(1)} %collective-permute-done.13.refs_1_, f32[512,1024]{1,0:T(8,128)S(1)} %get-tuple-element.60.refs_2_.refs_3_, f32[512,1]{1,0:T(8,128)S(1)} %get-tuple-element.61.refs_3_, ...), custom_call_target="tpu_custom_call" | custom-call | flops 1 | bytes 1 | tf_op jit(solution)/shard_map/pallas_call | solution.py:103
  60.1 5.0 %all-to-all-start = ((bf16[8,64,1152]{2,1,0:T(8,128)(2,1)}), bf16[8,64,1152]{2,1,0:T(8,128)(2,1)}, u32[]{:S(2)}, u32[]{:S(2)}) async-start(bf16[8,64,1152]{2,1,0:T(8,128)(2,1)} %shard_map.89), calls=%async_computation | async-start | bytes 2359296 | tf_op jit(solution)/shard_map/all_to_all | solution.py:367
  71.9 2.0 %shard_map.90 = (bf16[128,1024]{1,0:T(8,128)(2,1)}, f32[128,1024]{1,0:T(8,128)}) custom-call(s32[1]{0:T(128)} %bitcast.refs_1_.refs_0_, bf16[528,512]{1,0:T(8,128)(2,1)} %copy-done, bf16[256,512]{1,0:T(8,128)(2,1)S(1)} %collective-permute-done.14.refs_2_, f32[512,1024]{1,0:T(8,128)S(1)} %get-tuple-element.60.refs_2_.refs_3_), custom_call_target="tpu_custom_call" | custom-call | flops 1 | bytes 1 | tf_op jit(solution)/shard_map/pallas_call | solution.py:103
  73.9 9.0 %all-to-all-done.refs_0_ = bf16[8,64,1152]{2,1,0:T(8,128)(2,1)} async-done(((bf16[8,64,1152]{2,1,0:T(8,128)(2,1)}), bf16[8,64,1152]{2,1,0:T(8,128)(2,1)}, u32[]{:S(2)}, u32[]{:S(2)}) %all-to-all-start) | async-done | bytes 1179680 | tf_op jit(solution)/shard_map/all_to_all | solution.py:367
  82.9 2.3 %shard_map.92 = bf16[32,18,128]{2,1,0:T(8,128)(2,1)} custom-call(bf16[8,64,1152]{2,1,0:T(8,128)(2,1)} %all-to-all-done.refs_0_), custom_call_target="tpu_custom_call" | custom-call | flops 1 | bytes 1 | tf_op jit(solution)/shard_map/pallas_call | solution.py:103
  85.3 8.6 %all-to-all-start.1 = ((bf16[32,18,128]{2,1,0:T(8,128)(2,1)}), bf16[32,18,128]{2,1,0:T(8,128)(2,1)S(1)}, u32[]{:S(2)}, u32[]{:S(2)}) async-start(bf16[32,18,128]{2,1,0:T(8,128)(2,1)} %shard_map.92), calls=%async_computation.1 | async-start | bytes 393216 | tf_op jit(solution)/shard_map/all_to_all | solution.py:374
  95.0 2.4 %collective-permute-start.21 = (bf16[128,1024]{1,0:T(8,128)(2,1)S(1)}, bf16[128,1024]{1,0:T(8,128)(2,1)S(1)}, u32[]{:S(2)}, u32[]{:S(2)}) collective-permute-start(bf16[128,1024]{1,0:T(8,128)(2,1)S(1)} %add_convert_fusion), channel_id=1, source_target_pairs={{0,192},{8,72},{16,208},{24,88},{32,224},{40,104},{48,240},{56,120... | collective-permute-start | bytes 786440 | tf_op jit(solution)/shard_map/ppermute | solution.py:33
  99.9 2.9 %collective-permute-start.22 = (bf16[128,1024]{1,0:T(8,128)(2,1)S(1)}, bf16[128,1024]{1,0:T(8,128)(2,1)S(1)}, u32[]{:S(2)}, u32[]{:S(2)}) collective-permute-start(bf16[128,1024]{1,0:T(8,128)(2,1)S(1)} %copy-done.15), channel_id=1, source_target_pairs={{0,16},{8,24},{16,0},{24,8},{32,48},{40,56},{48,32},{56,40},{64,80... | collective-permute-start | bytes 786440 | tf_op jit(solution)/shard_map/ppermute | solution.py:41
  103.7 2.0 %all-to-all-done.1.refs_0_ = bf16[32,18,128]{2,1,0:T(8,128)(2,1)S(1)} async-done(((bf16[32,18,128]{2,1,0:T(8,128)(2,1)}), bf16[32,18,128]{2,1,0:T(8,128)(2,1)S(1)}, u32[]{:S(2)}, u32[]{:S(2)}) %all-to-all-start.1) | async-done | bytes 147488 | tf_op jit(solution)/shard_map/all_to_all | solution.py:374
  106.4 3.4 %all-to-all-start.2 = ((f32[8,36,128]{2,1,0:T(8,128)}), f32[8,36,128]{2,1,0:T(8,128)S(1)}, u32[]{:S(2)}, u32[]{:S(2)}) async-start(f32[8,36,128]{2,1,0:T(8,128)} %shard_map.93), calls=%async_computation.2 | async-start | bytes 327680 | tf_op jit(solution)/shard_map/all_to_all | solution.py:389
  113.1 3.4 %fusion = bf16[1,128,1152]{2,1,0:T(8,128)(2,1)} fusion(bf16[1152,1024]{1,0:T(8,128)(2,1)} %refs_0_.1, f32[128,1024]{1,0:T(8,128)S(1)} %copy-done.9, bf16[128,1024]{1,0:T(8,128)(2,1)S(1)} %collective-permute-done.22, f32[128]{0:T(128)S(1)} %slice_reduce_fusion, f32[128]{0:T(128)S(1)} %fusion.7, bf16[512,1024]{1,0:T(8,128)(2,1)S(1)} %get-tuple-element.44.refs_2_.refs_4_.refs_1_), kind=kOutput, calls=%fused_computation.1 | convolution fusion | flops 303054848 | bytes 3703808 | tf_op jit(solution)/shard_map/dot_general | solution.py:45
  (80 shorter events, 29.6 us)
Async XLA Ops:
  0.6 9.8 %collective-permute-start = (bf16[128,1152]{1,0:T(8,128)(2,1)}, bf16[128,1152]{1,0:T(8,128)(2,1)S(1)}, u32[]{:S(2)}, u32[]{:S(2)}) collective-permute-start(bf16[128,1152]{1,0:T(8,128)(2,1)} %bitcast.14), channel_id=1, source_target_pairs={{0,16},{8,24},{16,0},{24,8},{32,48},{40,56},{48,32},{56,40},{64,80... | collective-permute-start | bytes 884744 | tf_op jit(solution)/shard_map/ppermute | solution.py:41
  4.5 12.2 %collective-permute-start.6 = (bf16[128,1024]{1,0:T(8,128)(2,1)}, bf16[128,1024]{1,0:T(8,128)(2,1)S(1)}, u32[]{:S(2)}, u32[]{:S(2)}) collective-permute-start(bf16[128,1024]{1,0:T(8,128)(2,1)} %bitcast.18), channel_id=1, source_target_pairs={{0,224},{8,40},{16,240},{24,56},{32,0},{40,72},{48,16},{56,88},{64... | collective-permute-start | bytes 786440 | tf_op jit(solution)/shard_map/ppermute | solution.py:33
  6.1 10.6 %collective-permute-start.7 = (bf16[128,1024]{1,0:T(8,128)(2,1)}, bf16[128,1024]{1,0:T(8,128)(2,1)S(1)}, u32[]{:S(2)}, u32[]{:S(2)}) collective-permute-start(bf16[128,1024]{1,0:T(8,128)(2,1)} %bitcast.19), channel_id=1, source_target_pairs={{0,32},{8,232},{16,48},{24,248},{32,64},{40,8},{48,80},{56,24},{64... | collective-permute-start | bytes 786440 | tf_op jit(solution)/shard_map/ppermute | solution.py:33
  10.5 16.0 %collective-permute-start.1 = (bf16[128,1152]{1,0:T(8,128)(2,1)}, bf16[128,1152]{1,0:T(8,128)(2,1)S(1)}, u32[]{:S(2)}, u32[]{:S(2)}) collective-permute-start(bf16[128,1152]{1,0:T(8,128)(2,1)} %bitcast.15), channel_id=1, source_target_pairs={{0,8},{8,0},{16,24},{24,16},{32,40},{40,32},{48,56},{56,48},{64,72... | collective-permute-start | bytes 884744 | tf_op jit(solution)/shard_map/ppermute | solution.py:37
  12.6 13.8 %collective-permute-start.2 = (bf16[128,1152]{1,0:T(8,128)(2,1)S(1)}, bf16[128,1152]{1,0:T(8,128)(2,1)S(1)}, u32[]{:S(2)}, u32[]{:S(2)}) collective-permute-start(bf16[128,1152]{1,0:T(8,128)(2,1)S(1)} %collective-permute-done.refs_3_.refs_8_), channel_id=1, source_target_pairs={{0,8},{8,0},{16,24},{24,16},{32,40},{40,32},{48,56},{56,48},{64,72... | collective-permute-start | bytes 884744 | tf_op jit(solution)/shard_map/ppermute | solution.py:37
  12.6 4.0 %collective-permute-start.4 = (s32[1,128]{1,0:T(1,128)}, s32[1,128]{1,0:T(1,128)S(1)}, u32[]{:S(2)}, u32[]{:S(2)}) collective-permute-start(s32[1,128]{1,0:T(1,128)} %refs_5_.1), channel_id=1, source_target_pairs={{0,16},{8,24},{16,0},{24,8},{32,48},{40,56},{48,32},{56,40},{64,80... | collective-permute-start | bytes 1544 | tf_op jit(solution)/shard_map/ppermute | solution.py:41
  16.7 15.6 %collective-permute-start.8 = (bf16[128,1024]{1,0:T(8,128)(2,1)S(1)}, bf16[128,1024]{1,0:T(8,128)(2,1)}, u32[]{:S(2)}, u32[]{:S(2)}) collective-permute-start(bf16[128,1024]{1,0:T(8,128)(2,1)S(1)} %collective-permute-done.6.refs_5_), channel_id=1, source_target_pairs={{0,224},{8,40},{16,240},{24,56},{32,0},{40,72},{48,16},{56,88},{64... | collective-permute-start | bytes 786440 | tf_op jit(solution)/shard_map/ppermute | solution.py:33
  18.5 13.8 %collective-permute-start.9 = (bf16[128,1024]{1,0:T(8,128)(2,1)S(1)}, bf16[128,1024]{1,0:T(8,128)(2,1)}, u32[]{:S(2)}, u32[]{:S(2)}) collective-permute-start(bf16[128,1024]{1,0:T(8,128)(2,1)S(1)} %collective-permute-done.7.refs_6_), channel_id=1, source_target_pairs={{0,32},{8,232},{16,48},{24,248},{32,64},{40,8},{48,80},{56,24},{64... | collective-permute-start | bytes 786440 | tf_op jit(solution)/shard_map/ppermute | solution.py:33
  22.5 2.8 %collective-permute-start.3 = (s32[1,128]{1,0:T(1,128)}, s32[1,128]{1,0:T(1,128)S(1)}, u32[]{:S(2)}, u32[]{:S(2)}) collective-permute-start(s32[1,128]{1,0:T(1,128)} %refs_5_.1), channel_id=1, source_target_pairs={{0,8},{8,0},{16,24},{24,16},{32,40},{40,32},{48,56},{56,48},{64,72... | collective-permute-start | bytes 1544 | tf_op jit(solution)/shard_map/ppermute | solution.py:37
  32.3 10.1 %collective-permute-start.10 = (bf16[128,1024]{1,0:T(8,128)(2,1)}, bf16[128,1024]{1,0:T(8,128)(2,1)}, u32[]{:S(2)}, u32[]{:S(2)}) collective-permute-start(bf16[128,1024]{1,0:T(8,128)(2,1)} %collective-permute-done.9.refs_8_), channel_id=1, source_target_pairs={{0,32},{8,232},{16,48},{24,248},{32,64},{40,8},{48,80},{56,24},{64... | collective-permute-start | bytes 786440 | tf_op jit(solution)/shard_map/ppermute | solution.py:33
  36.7 8.4 %collective-permute-start.12 = (bf16[128,1024]{1,0:T(8,128)(2,1)}, bf16[128,1024]{1,0:T(8,128)(2,1)S(1)}, u32[]{:S(2)}, u32[]{:S(2)}) collective-permute-start(bf16[128,1024]{1,0:T(8,128)(2,1)} %collective-permute-done.8.refs_7_), channel_id=1, source_target_pairs={{0,224},{8,40},{16,240},{24,56},{32,0},{40,72},{48,16},{56,88},{64... | collective-permute-start | bytes 786440 | tf_op jit(solution)/shard_map/ppermute | solution.py:33
  42.4 7.4 %collective-permute-start.11 = (bf16[128,1024]{1,0:T(8,128)(2,1)}, bf16[128,1024]{1,0:T(8,128)(2,1)S(1)}, u32[]{:S(2)}, u32[]{:S(2)}) collective-permute-start(bf16[128,1024]{1,0:T(8,128)(2,1)} %collective-permute-done.10.refs_5_), channel_id=1, source_target_pairs={{0,32},{8,232},{16,48},{24,248},{32,64},{40,8},{48,80},{56,24},{64... | collective-permute-start | bytes 786440 | tf_op jit(solution)/shard_map/ppermute | solution.py:33
  60.1 22.9 %all-to-all-start = ((bf16[8,64,1152]{2,1,0:T(8,128)(2,1)}), bf16[8,64,1152]{2,1,0:T(8,128)(2,1)}, u32[]{:S(2)}, u32[]{:S(2)}) async-start(bf16[8,64,1152]{2,1,0:T(8,128)(2,1)} %shard_map.89), calls=%async_computation | async-start | bytes 2359296 | tf_op jit(solution)/shard_map/all_to_all | solution.py:367
  65.1 5.7 %collective-permute-start.14 = (bf16[256,512]{1,0:T(8,128)(2,1)}, bf16[256,512]{1,0:T(8,128)(2,1)S(1)}, u32[]{:S(2)}, u32[]{:S(2)}) collective-permute-start(bf16[256,512]{1,0:T(8,128)(2,1)} %get-tuple-element.63), channel_id=1, source_target_pairs={{0,8},{8,0},{16,24},{24,16},{32,40},{40,32},{48,56},{56,48},{64,72... | collective-permute-start | bytes 786440 | tf_op jit(solution)/shard_map/ppermute | solution.py:37
  66.8 27.0 %collective-permute-start.17 = (bf16[128,1024]{1,0:T(8,128)(2,1)}, bf16[128,1024]{1,0:T(8,128)(2,1)}, u32[]{:S(2)}, u32[]{:S(2)}) collective-permute-start(bf16[128,1024]{1,0:T(8,128)(2,1)} %shard_map.91), channel_id=1, source_target_pairs={{0,64},{8,200},{16,80},{24,216},{32,96},{40,232},{48,112},{56,248}... | collective-permute-start | bytes 786440 | tf_op jit(solution)/shard_map/ppermute | solution.py:33
  67.0 26.8 %collective-permute-start.15 = (bf16[128,1024]{1,0:T(8,128)(2,1)}, bf16[128,1024]{1,0:T(8,128)(2,1)}, u32[]{:S(2)}, u32[]{:S(2)}) collective-permute-start(bf16[128,1024]{1,0:T(8,128)(2,1)} %get-tuple-element.66), channel_id=1, source_target_pairs={{0,32},{8,232},{16,48},{24,248},{32,64},{40,8},{48,80},{56,24},{64... | collective-permute-start | bytes 786440 | tf_op jit(solution)/shard_map/ppermute | solution.py:33
  68.1 25.7 %collective-permute-start.16 = (bf16[128,1024]{1,0:T(8,128)(2,1)}, bf16[128,1024]{1,0:T(8,128)(2,1)}, u32[]{:S(2)}, u32[]{:S(2)}) collective-permute-start(bf16[128,1024]{1,0:T(8,128)(2,1)} %get-tuple-element.67), channel_id=1, source_target_pairs={{0,224},{8,40},{16,240},{24,56},{32,0},{40,72},{48,16},{56,88},{64... | collective-permute-start | bytes 786440 | tf_op jit(solution)/shard_map/ppermute | solution.py:33
  69.2 24.7 %collective-permute-start.18 = (bf16[128,1024]{1,0:T(8,128)(2,1)}, bf16[128,1024]{1,0:T(8,128)(2,1)}, u32[]{:S(2)}, u32[]{:S(2)}) collective-permute-start(bf16[128,1024]{1,0:T(8,128)(2,1)} %get-tuple-element.69), channel_id=1, source_target_pairs={{0,32},{8,232},{16,48},{24,248},{32,64},{40,8},{48,80},{56,24},{64... | collective-permute-start | bytes 786440 | tf_op jit(solution)/shard_map/ppermute | solution.py:33
  70.8 23.1 %collective-permute-start.19 = (bf16[128,1024]{1,0:T(8,128)(2,1)}, bf16[128,1024]{1,0:T(8,128)(2,1)}, u32[]{:S(2)}, u32[]{:S(2)}) collective-permute-start(bf16[128,1024]{1,0:T(8,128)(2,1)} %get-tuple-element.70), channel_id=1, source_target_pairs={{0,224},{8,40},{16,240},{24,56},{32,0},{40,72},{48,16},{56,88},{64... | collective-permute-start | bytes 786440 | tf_op jit(solution)/shard_map/ppermute | solution.py:33
  85.3 20.4 %all-to-all-start.1 = ((bf16[32,18,128]{2,1,0:T(8,128)(2,1)}), bf16[32,18,128]{2,1,0:T(8,128)(2,1)S(1)}, u32[]{:S(2)}, u32[]{:S(2)}) async-start(bf16[32,18,128]{2,1,0:T(8,128)(2,1)} %shard_map.92), calls=%async_computation.1 | async-start | bytes 393216 | tf_op jit(solution)/shard_map/all_to_all | solution.py:374
  95.0 16.4 %collective-permute-start.21 = (bf16[128,1024]{1,0:T(8,128)(2,1)S(1)}, bf16[128,1024]{1,0:T(8,128)(2,1)S(1)}, u32[]{:S(2)}, u32[]{:S(2)}) collective-permute-start(bf16[128,1024]{1,0:T(8,128)(2,1)S(1)} %add_convert_fusion), channel_id=1, source_target_pairs={{0,192},{8,72},{16,208},{24,88},{32,224},{40,104},{48,240},{56,120... | collective-permute-start | bytes 786440 | tf_op jit(solution)/shard_map/ppermute | solution.py:33
  98.5 14.4 %collective-permute-start.20 = (bf16[128,1024]{1,0:T(8,128)(2,1)S(1)}, bf16[128,1024]{1,0:T(8,128)(2,1)S(1)}, u32[]{:S(2)}, u32[]{:S(2)}) collective-permute-start(bf16[128,1024]{1,0:T(8,128)(2,1)S(1)} %add_convert_fusion.1), channel_id=1, source_target_pairs={{0,64},{8,200},{16,80},{24,216},{32,96},{40,232},{48,112},{56,248}... | collective-permute-start | bytes 786440 | tf_op jit(solution)/shard_map/ppermute | solution.py:33
  99.9 13.0 %collective-permute-start.22 = (bf16[128,1024]{1,0:T(8,128)(2,1)S(1)}, bf16[128,1024]{1,0:T(8,128)(2,1)S(1)}, u32[]{:S(2)}, u32[]{:S(2)}) collective-permute-start(bf16[128,1024]{1,0:T(8,128)(2,1)S(1)} %copy-done.15), channel_id=1, source_target_pairs={{0,16},{8,24},{16,0},{24,8},{32,48},{40,56},{48,32},{56,40},{64,80... | collective-permute-start | bytes 786440 | tf_op jit(solution)/shard_map/ppermute | solution.py:41
  106.4 12.4 %all-to-all-start.2 = ((f32[8,36,128]{2,1,0:T(8,128)}), f32[8,36,128]{2,1,0:T(8,128)S(1)}, u32[]{:S(2)}, u32[]{:S(2)}) async-start(f32[8,36,128]{2,1,0:T(8,128)} %shard_map.93), calls=%async_computation.2 | async-start | bytes 327680 | tf_op jit(solution)/shard_map/all_to_all | solution.py:389
  (18 other events, 183.8 us)

commit v10 on v9

--- a/solution.py
+++ b/solution.py
@@ -112,11 +112,15 @@
     )(*operands)
 
 
+def scale_of(numbers):
+    return jnp.exp(jnp.full((1, 128), numbers[0], F32))[:, 0:1]
+
+
 def block_grads(numbers, columns, image_emb, match, text):
     wide = text.astype(F32)
     inv = lax.rsqrt(jnp.sum(wide * wide, -1, keepdims=True) + 1e-06)
     emb = (wide * inv).astype(BF16)
-    logits = numbers[0] * inner_rows(image_emb, emb) + numbers[1]
+    logits = scale_of(numbers) * inner_rows(image_emb, emb) + numbers[1]
     positive = (match == columns).astype(F32)
     return emb, (jax.nn.sigmoid(logits) - positive).astype(BF16)
 
@@ -171,7 +175,7 @@
     columns = columns_of(place, 4, text.shape[0])
     emb, grad = block_grads(numbers, columns, image_emb[...], match[...], text[...])
     grad_out[...] = grad
-    acc = numbers[0] * (acc_in[...] + jnp.dot(grad, emb, preferred_element_type=F32))
+    acc = scale_of(numbers) * (acc_in[...] + jnp.dot(grad, emb, preferred_element_type=F32))
     acc_out[...] = acc
     dot = jnp.sum(image_emb[...].astype(F32) * acc, -1, keepdims=True)
     dot_out[...] = dot
@@ -199,7 +203,7 @@
     moves.send(0)
 
 
-def weight_kernel(moves, place, got, acc, dot, image_emb, inv, own_rows, core_rows, yh_rows, both_rows, weight):
+def weight_kernel(moves, place, got, acc, dot, image_emb, inv, own_rows, core_rows, yh_rows, both_rows, weight, row_half):
     rows, width = acc.shape
     half, quarter, block = width // 2, width // 4, rows // 4
     own = pl.ds(pl.multiple_of((place[0] & 1) * half, half), half)
@@ -210,6 +214,10 @@
         mine = slice(slot * block, (slot + 1) * block)
         theirs = slice((slot ^ 1) * block, ((slot ^ 1) + 1) * block)
         kept = acc[mine, own] + got[theirs, :].astype(F32)
+        if slot in (0, 2):
+            row_half[slot // 2 * block : (slot // 2 + 1) * block, :] = kept
+            if slot == 2:
+                moves.send(1)
         line = digits[slot ^ 1 : (slot ^ 1) + 1, :]
         other_dot = jnp.broadcast_to(line[:, :128] + line[:, 128:], (block, 128)).T[:, 0:1]
         unit = image_emb[mine, own].astype(F32)
@@ -225,7 +233,7 @@
             moves.send(0, at)
 
 
-def row_kernel(moves, place, got, extra, acc, row_send, row_keep):
+def row_kernel(moves, place, row_half, extra, acc, row_send, row_keep):
     rows, width = acc.shape
     half, block = width // 2, rows // 4
     core = place[0] & 1
@@ -233,12 +241,10 @@
     other = pl.ds(pl.multiple_of((1 - core) * half, half), half)
     moves.need(1)
     for n, target in enumerate((row_keep, row_send)):
-        slot = 2 * n
-        mine = slice(slot * block, (slot + 1) * block)
-        theirs = slice((slot + 1) * block, (slot + 2) * block)
-        target[:, own] = (acc[mine, own] + got[theirs, :].astype(F32)).astype(target.dtype)
-        rest = extra[n * block : (n + 1) * block, :].astype(F32)
-        target[:, other] = (acc[mine, other] + rest).astype(target.dtype)
+        here = slice(n * block, (n + 1) * block)
+        target[:, own] = row_half[here, :].astype(target.dtype)
+        rest = extra[here, :].astype(F32)
+        target[:, other] = (acc[2 * n * block : (2 * n + 1) * block, other] + rest).astype(target.dtype)
         moves.send(1 - n)
 
 
@@ -287,7 +293,7 @@
     loop_index = lax.axis_index("loop")
     place = loop_index.reshape(1)
     logit_scale = jnp.exp(log_scale)
-    numbers = jnp.stack([logit_scale, logit_bias])
+    numbers = jnp.stack([log_scale, logit_bias])
 
     slot = {0: texts}
     slot[1], slot[-1] = shift_z(texts, -1), shift_z(texts, 1)
@@ -299,7 +305,8 @@
     slot[2], slot[-2] = shift_z(up, -1), shift_z(down, 1)
     sensor_later, _ = lax.optimization_barrier((sensor, sensor_yh))
     sensors = [sensor, swap_core(sensor_later), sensor_yh, swap_core(sensor_yh)]
-    match = [match, swap_core(match), match_yh, swap_core(match_yh)]
+    match_both = swap_core(jnp.concatenate([match, match_yh], 0))
+    match = [match, match_both[:1], match_yh, match_both[1:]]
     shapes = [((4 * rows, width), BF16), ((4 * rows, 1), F32), ((4 * rows, 1), F32)]
     image_emb, image_inv, match_rows = call(
         project_kernel,
@@ -312,7 +319,7 @@
         cuts={0: CUT},
     )
     up, down, _ = lax.optimization_barrier((slot[2], slot[-2], image_emb))
-    slot[3], slot[-3] = shift_z(up, -1), shift_z(down, 1)
+    slot[3], slot[-3], slot[4] = shift_z(up, -1), shift_z(down, 1), shift_z(down, 2)
 
     def pairs(keys, dtypes, acc):
         operands = [numbers, place, image_emb, match_rows, *(slot[k] for k in keys)]
@@ -326,8 +333,6 @@
         return call(kernel, out, aliases, *operands, packed=range(4, 4 + len(keys)), far_out=range(1, len(out)))
 
     acc, text_0, text_1, text_m1, text_2, text_m2 = pairs((0, 1, -1, 2, -2), (F32, BF16, BF16, BF16, BF16), None)
-    last_text, _ = lax.optimization_barrier((slot[-3], acc))
-    last_text = shift_z(last_text, 1)
     acc, text_3, text_m3 = pairs((3, -3), (BF16, BF16), acc)
     shapes = [((4 * rows, width), F32), ((4 * rows, 1), F32), ((4 * rows + 16, width // 2), BF16)]
     shapes += [((2 * rows, width // 2), BF16), ((4 * rows, rows), BF16)]
@@ -335,19 +340,19 @@
         last_kernel,
         [jax.ShapeDtypeStruct(*s) for s in shapes],
         {5: 0},
-        numbers, place, image_emb, match_rows, last_text, acc,
+        numbers, place, image_emb, match_rows, slot[4], acc,
         far_out=(3,),
     )
 
     got = swap_core(packet)
-    (weight_part,) = call(
+    weight_part, row_half = call(
         weight_kernel,
-        [jax.ShapeDtypeStruct((DP, width // 16, feat), BF16)],
+        [jax.ShapeDtypeStruct((DP, width // 16, feat), BF16), jax.ShapeDtypeStruct((2 * rows, width // 2), F32)],
         {},
         place, got, acc, dot, image_emb, image_inv, *sensors,
         far=(5,),
-        far_out=(0,),
-        sends=DP,
+        far_out=(0, 1),
+        sends=DP + 1,
     )
     last_grad, extra, text_1, text_m1, text_3, text_m3, _ = lax.optimization_barrier(
         (last_grad, extra, text_1, text_m1, text_3, text_m3, weight_part)
@@ -360,7 +365,7 @@
         row_kernel,
         [jax.ShapeDtypeStruct(*s) for s in shapes],
         {},
-        place, got, swap_core(extra), acc,
+        place, row_half, swap_core(extra), acc,
         far=(1,),
         far_out=(0, 1),
     )

time: 120 us -> 113 us (0.942)
  starting transfers between devices: 57.7 us -> 46.5 us
  waiting for transfers between devices: 19 us -> 24 us
  local copies, waits for them, and re-layouts: 3.9 us -> 1.77 us
    ppermute x14, waiting for transfers between devices: 3.14 us -> 8.04 us  [shift_z(): lax.ppermute(block, 'loop', route(lambda z, y, c: (z + (1 - 2 * c) * dist...]
    ppermute x14, starting transfers between devices: 25 us -> 20.9 us  [shift_z(): lax.ppermute(block, 'loop', route(lambda z, y, c: (z + (1 - 2 * c) * dist...]
    ppermute x3, starting transfers between devices: 9.68 us -> 6.9 us  [swap_yh(): return lax.ppermute(block, 'loop', route(lambda z, y, c: (z, 1 - y, c)))]
    all_to_all x1, starting transfers between devices: 8.56 us -> 5.83 us  [on_device(): weight_part = lax.all_to_all(weight_chunks, 'loop', 0, 0, tiled=True)]
    unnamed x32 -> x28, local copies, waits for them, and re-layouts: 2.95 us -> 0.83 us
    ppermute x6 -> x5, starting transfers between devices: 6.07 us -> 5.22 us  [swap_core(): return lax.ppermute(block, 'loop', route(lambda z, y, c: (z, y, 1 - c)))]
    ppermute x6 -> x5, waiting for transfers between devices: 3.34 us -> 3.06 us  [swap_core(): return lax.ppermute(block, 'loop', route(lambda z, y, c: (z, y, 1 - c)))]
  transfers between devices with their start and end apart: 26 -> 25, of which waited for: 9 -> 10; matrix products, arithmetic and copies ran while one was open for 9% -> 10% of each run, Pallas kernels for 17% -> 18%
where the time goes in v10:
time: 113 us
  starting transfers between devices  46.5 us (41%)
  Pallas kernels  27.9 us (25%)
  waiting for transfers between devices  24 us (21%)
  other arithmetic  6.62 us (6%)
  matrix products  3.35 us (3%)
  between operations  2.51 us (2%)
  local copies, waits for them, and re-layouts  1.77 us (2%)
    pallas_call x10, Pallas kernels, call(): pl.pallas_call(body, out_shape=[pltpu.HBM(o.shape, o.dtype) if n in far_o...  27.9 us
    ppermute x14, starting transfers between devices, shift_z(): lax.ppermute(block, 'loop', route(lambda z, y, c: (z + (1 - 2 * c) * dist...  20.9 us
    all_to_all x1, waiting for transfers between devices, on_device(): weight_part = lax.all_to_all(weight_part, 'dp', 0, 0, tiled=True)  9.33 us
    ppermute x14, waiting for transfers between devices, shift_z(): lax.ppermute(block, 'loop', route(lambda z, y, c: (z + (1 - 2 * c) * dist...  8.04 us
    ppermute x3, starting transfers between devices, swap_yh(): return lax.ppermute(block, 'loop', route(lambda z, y, c: (z, 1 - y, c)))  6.9 us
    all_to_all x1, starting transfers between devices, on_device(): weight_part = lax.all_to_all(weight_chunks, 'loop', 0, 0, tiled=True)  5.83 us
    ppermute x5, starting transfers between devices, swap_core(): return lax.ppermute(block, 'loop', route(lambda z, y, c: (z, y, 1 - c)))  5.22 us
    all_to_all x1, starting transfers between devices, on_device(): weight_part = lax.all_to_all(weight_part, 'dp', 0, 0, tiled=True)  4.25 us
  transfers between devices with their start and end apart: 25, of which 10 were waited for; matrix products, arithmetic and copies ran while one was open for 10% of the time, Pallas kernels for 18%

profile of v10, /device:TPU:1, one launch (start us, length us, event | category | flops | bytes accessed | tf_op | source)
XLA Modules:
  0.0 112.7 jit_solution(4562994302249339215)
XLA Ops:
  0.6 3.8 %collective-permute-start = (bf16[128,1152]{1,0:T(8,128)(2,1)}, bf16[128,1152]{1,0:T(8,128)(2,1)S(1)}, u32[]{:S(2)}, u32[]{:S(2)}) collective-permute-start(bf16[128,1152]{1,0:T(8,128)(2,1)} %bitcast.15), channel_id=1, source_target_pairs={{0,16},{8,24},{16,0},{24,8},{32,48},{40,56},{48,32},{56,40},{64,80... | collective-permute-start | bytes 884744 | tf_op jit(solution)/shard_map/ppermute | solution.py:41
  4.5 1.6 %collective-permute-start.5 = (bf16[128,1024]{1,0:T(8,128)(2,1)}, bf16[128,1024]{1,0:T(8,128)(2,1)S(1)}, u32[]{:S(2)}, u32[]{:S(2)}) collective-permute-start(bf16[128,1024]{1,0:T(8,128)(2,1)} %bitcast.19), channel_id=1, source_target_pairs={{0,224},{8,40},{16,240},{24,56},{32,0},{40,72},{48,16},{56,88},{64... | collective-permute-start | bytes 786440 | tf_op jit(solution)/shard_map/ppermute | solution.py:33
  6.1 3.9 %collective-permute-start.6 = (bf16[128,1024]{1,0:T(8,128)(2,1)}, bf16[128,1024]{1,0:T(8,128)(2,1)S(1)}, u32[]{:S(2)}, u32[]{:S(2)}) collective-permute-start(bf16[128,1024]{1,0:T(8,128)(2,1)} %bitcast.20), channel_id=1, source_target_pairs={{0,32},{8,232},{16,48},{24,248},{32,64},{40,8},{48,80},{56,24},{64... | collective-permute-start | bytes 786440 | tf_op jit(solution)/shard_map/ppermute | solution.py:33
  10.5 2.2 %collective-permute-start.1 = (bf16[128,1152]{1,0:T(8,128)(2,1)}, bf16[128,1152]{1,0:T(8,128)(2,1)S(1)}, u32[]{:S(2)}, u32[]{:S(2)}) collective-permute-start(bf16[128,1152]{1,0:T(8,128)(2,1)} %bitcast.16), channel_id=1, source_target_pairs={{0,8},{8,0},{16,24},{24,16},{32,40},{40,32},{48,56},{56,48},{64,72... | collective-permute-start | bytes 884744 | tf_op jit(solution)/shard_map/ppermute | solution.py:37
  16.1 2.4 %collective-permute-start.8 = (bf16[128,1024]{1,0:T(8,128)(2,1)S(1)}, bf16[128,1024]{1,0:T(8,128)(2,1)}, u32[]{:S(2)}, u32[]{:S(2)}) collective-permute-start(bf16[128,1024]{1,0:T(8,128)(2,1)S(1)} %collective-permute-done.6.refs_6_), channel_id=1, source_target_pairs={{0,32},{8,232},{16,48},{24,248},{32,64},{40,8},{48,80},{56,24},{64... | collective-permute-start | bytes 786440 | tf_op jit(solution)/shard_map/ppermute | solution.py:33
  18.5 2.6 %collective-permute-start.2 = (bf16[128,1152]{1,0:T(8,128)(2,1)S(1)}, bf16[128,1152]{1,0:T(8,128)(2,1)S(1)}, u32[]{:S(2)}, u32[]{:S(2)}) collective-permute-start(bf16[128,1152]{1,0:T(8,128)(2,1)S(1)} %collective-permute-done.refs_3_.refs_8_), channel_id=1, source_target_pairs={{0,8},{8,0},{16,24},{24,16},{32,40},{40,32},{48,56},{56,48},{64,72... | collective-permute-start | bytes 884744 | tf_op jit(solution)/shard_map/ppermute | solution.py:37
  23.7 4.4 %shard_map.85 = (bf16[512,1024]{1,0:T(8,128)(2,1)S(1)}, f32[512,1]{1,0:T(8,128)}, f32[512,1]{1,0:T(8,128)S(1)}) custom-call(bf16[1152,1024]{1,0:T(8,128)(2,1)} %refs_0_.1, bf16[128,1152]{1,0:T(8,128)(2,1)} %bitcast.17, bf16[128,1152]{1,0:T(8,128)(2,1)} %copy-done.3, bf16[128,1152]{1,0:T(8,128)(2,1)} %copy-done.1, bf16[128,1152]{1,0:T(8,128)(2,1)} %copy-done.5, ...), custom_call_target="tpu_custom_call" | custom-call | flops 1 | bytes 1 | tf_op jit(solution)/shard_map/pallas_call | solution.py:103
  28.2 2.5 %collective-permute-start.11 = (bf16[128,1024]{1,0:T(8,128)(2,1)}, bf16[128,1024]{1,0:T(8,128)(2,1)}, u32[]{:S(2)}, u32[]{:S(2)}) collective-permute-start(bf16[128,1024]{1,0:T(8,128)(2,1)} %collective-permute-done.8.refs_8_), channel_id=1, source_target_pairs={{0,32},{8,232},{16,48},{24,248},{32,64},{40,8},{48,80},{56,24},{64... | collective-permute-start | bytes 786440 | tf_op jit(solution)/shard_map/ppermute | solution.py:33
  33.3 5.4 %shard_map.86 = (f32[512,1024]{1,0:T(8,128)S(1)}, f32[128,1024]{1,0:T(8,128)}, bf16[128,1024]{1,0:T(8,128)(2,1)}, bf16[128,1024]{1,0:T(8,128)(2,1)}, bf16[128,10...) custom-call(f32[2]{0:T(128)S(1)} %pad_maximum_fusion.refs_0_, s32[1]{0:T(128)} %bitcast.refs_1_.refs_0_, ...), custom_call_target="tpu_custom_call" | custom-call | flops 1 | bytes 1 | tf_op jit(solution)/shard_map/pallas_call | solution.py:103
  38.7 4.0 %collective-permute-done.10.refs_4_ = bf16[128,1024]{1,0:T(8,128)(2,1)} collective-permute-done((bf16[128,1024]{1,0:T(8,128)(2,1)}, bf16[128,1024]{1,0:T(8,128)(2,1)}, u32[]{:S(2)}, u32[]{:S(2)}) %collective-permute-start.10) | collective-permute-done | bytes 262176 | tf_op jit(solution)/shard_map/ppermute | solution.py:33
  42.7 3.9 %shard_map.87 = (f32[512,1024]{1,0:T(8,128)S(1)}, bf16[128,1024]{1,0:T(8,128)(2,1)}, bf16[128,1024]{1,0:T(8,128)(2,1)}) custom-call(f32[2]{0:T(128)S(1)} %pad_maximum_fusion.refs_0_, s32[1]{0:T(128)} %bitcast.refs_1_.refs_0_, bf16[512,1024]{1,0:T(8,128)(2,1)S(1)} %get-tuple-element.45.refs_2_.refs_4_.refs_1_, ...), custom_call_target="tpu_custom_call", output_to_operand_aliasing={{0}: (6, {})} | custom-call | flops 1 | bytes 1 | tf_op jit(solution)/shard_map/pallas_call | solution.py:103
  46.7 4.2 %shard_map.88 = (f32[512,1024]{1,0:T(8,128)S(1)}, f32[512,1]{1,0:T(8,128)S(1)}, bf16[528,512]{1,0:T(8,128)(2,1)S(1)}, bf16[256,512]{1,0:T(8,128)(2,1)}, bf16[512,128]{1,0:T(8,128)(2,1)S(1)}) custom-call(f32[2]{0:T(128)S(1)} %pad_maximum_fusion.refs_0_, s32[1]{0:T(128)} %bitcast.refs_1_.refs_0_, ...), custom_call_target="tpu_custom_call", output_to_operand_aliasing={{0}: (5, {})} | custom-call | flops 1 | bytes 1 | tf_op jit(solution)/shard_map/pallas_call | solution.py:103
  51.0 1.9 %collective-permute-done.12.refs_1_ = bf16[528,512]{1,0:T(8,128)(2,1)S(1)} collective-permute-done((bf16[528,512]{1,0:T(8,128)(2,1)S(1)}, bf16[528,512]{1,0:T(8,128)(2,1)S(1)}, u32[]{:S(2)}, u32[]{:S(2)}) %collective-permute-start.12) | collective-permute-done | bytes 540704 | tf_op jit(solution)/shard_map/ppermute | solution.py:37
  52.9 3.1 %shard_map.89 = (bf16[8,64,1152]{2,1,0:T(8,128)(2,1)}, f32[256,512]{1,0:T(8,128)}) custom-call(s32[1]{0:T(128)} %bitcast.refs_1_.refs_0_, bf16[528,512]{1,0:T(8,128)(2,1)S(1)} %collective-permute-done.12.refs_1_, f32[512,1024]{1,0:T(8,128)S(1)} %get-tuple-element.54.refs_2_.refs_3_, f32[512,1]{1,0:T(8,128)S(1)} %get-tuple-element.55.refs_3_, ...), custom_call_target="tpu_custom_call" | custom-call | flops 1 | bytes 1 | tf_op jit(solution)/shard_map/pallas_call | solution.py:103
  56.1 4.3 %all-to-all-start = ((bf16[8,64,1152]{2,1,0:T(8,128)(2,1)}), bf16[8,64,1152]{2,1,0:T(8,128)(2,1)}, u32[]{:S(2)}, u32[]{:S(2)}) async-start(bf16[8,64,1152]{2,1,0:T(8,128)(2,1)} %get-tuple-element.64), calls=%async_computation | async-start | bytes 2359296 | tf_op jit(solution)/shard_map/all_to_all | solution.py:372
  67.2 2.0 %shard_map.90 = (bf16[128,1024]{1,0:T(8,128)(2,1)}, f32[128,1024]{1,0:T(8,128)}) custom-call(s32[1]{0:T(128)} %bitcast.refs_1_.refs_0_, f32[256,512]{1,0:T(8,128)} %get-tuple-element.57.refs_1_, bf16[256,512]{1,0:T(8,128)(2,1)S(1)} %collective-permute-done.13.refs_2_, f32[512,1024]{1,0:T(8,128)S(1)} %get-tuple-element.54.refs_2_.refs_3_), custom_call_target="tpu_custom_call" | custom-call | flops 1 | bytes 1 | tf_op jit(solution)/shard_map/pallas_call | solution.py:103
  69.2 9.3 %all-to-all-done.refs_0_ = bf16[8,64,1152]{2,1,0:T(8,128)(2,1)} async-done(((bf16[8,64,1152]{2,1,0:T(8,128)(2,1)}), bf16[8,64,1152]{2,1,0:T(8,128)(2,1)}, u32[]{:S(2)}, u32[]{:S(2)}) %all-to-all-start) | async-done | bytes 1179680 | tf_op jit(solution)/shard_map/all_to_all | solution.py:372
  78.5 2.3 %shard_map.92 = bf16[32,18,128]{2,1,0:T(8,128)(2,1)} custom-call(bf16[8,64,1152]{2,1,0:T(8,128)(2,1)} %all-to-all-done.refs_0_), custom_call_target="tpu_custom_call" | custom-call | flops 1 | bytes 1 | tf_op jit(solution)/shard_map/pallas_call | solution.py:103
  80.9 5.8 %all-to-all-start.1 = ((bf16[32,18,128]{2,1,0:T(8,128)(2,1)}), bf16[32,18,128]{2,1,0:T(8,128)(2,1)S(1)}, u32[]{:S(2)}, u32[]{:S(2)}) async-start(bf16[32,18,128]{2,1,0:T(8,128)(2,1)} %shard_map.92), calls=%async_computation.1 | async-start | bytes 393216 | tf_op jit(solution)/shard_map/all_to_all | solution.py:379
  87.8 2.4 %collective-permute-start.20 = (bf16[128,1024]{1,0:T(8,128)(2,1)S(1)}, bf16[128,1024]{1,0:T(8,128)(2,1)S(1)}, u32[]{:S(2)}, u32[]{:S(2)}) collective-permute-start(bf16[128,1024]{1,0:T(8,128)(2,1)S(1)} %add_convert_fusion), channel_id=1, source_target_pairs={{0,192},{8,72},{16,208},{24,88},{32,224},{40,104},{48,240},{56,120... | collective-permute-start | bytes 786440 | tf_op jit(solution)/shard_map/ppermute | solution.py:33
  92.7 2.9 %collective-permute-start.21 = (bf16[128,1024]{1,0:T(8,128)(2,1)S(1)}, bf16[128,1024]{1,0:T(8,128)(2,1)S(1)}, u32[]{:S(2)}, u32[]{:S(2)}) collective-permute-start(bf16[128,1024]{1,0:T(8,128)(2,1)S(1)} %copy-done.13), channel_id=1, source_target_pairs={{0,16},{8,24},{16,0},{24,8},{32,48},{40,56},{48,32},{56,40},{64,80... | collective-permute-start | bytes 786440 | tf_op jit(solution)/shard_map/ppermute | solution.py:41
  96.6 2.0 %all-to-all-done.1.refs_0_ = bf16[32,18,128]{2,1,0:T(8,128)(2,1)S(1)} async-done(((bf16[32,18,128]{2,1,0:T(8,128)(2,1)}), bf16[32,18,128]{2,1,0:T(8,128)(2,1)S(1)}, u32[]{:S(2)}, u32[]{:S(2)}) %all-to-all-start.1) | async-done | bytes 147488 | tf_op jit(solution)/shard_map/all_to_all | solution.py:379
  99.3 3.4 %all-to-all-start.2 = ((f32[8,36,128]{2,1,0:T(8,128)}), f32[8,36,128]{2,1,0:T(8,128)S(1)}, u32[]{:S(2)}, u32[]{:S(2)}) async-start(f32[8,36,128]{2,1,0:T(8,128)} %shard_map.93), calls=%async_computation.2 | async-start | bytes 327680 | tf_op jit(solution)/shard_map/all_to_all | solution.py:394
  106.0 3.4 %fusion = bf16[1,128,1152]{2,1,0:T(8,128)(2,1)} fusion(bf16[1152,1024]{1,0:T(8,128)(2,1)} %refs_0_.1, f32[128,1024]{1,0:T(8,128)S(1)} %copy-done.8, bf16[128,1024]{1,0:T(8,128)(2,1)S(1)} %collective-permute-done.21, f32[128]{0:T(128)S(1)} %slice_reduce_fusion, f32[128]{0:T(128)S(1)} %fusion.7, bf16[512,1024]{1,0:T(8,128)(2,1)S(1)} %get-tuple-element.45.refs_2_.refs_4_.refs_1_), kind=kOutput, calls=%fused_computation.1 | convolution fusion | flops 303054848 | bytes 3703808 | tf_op jit(solution)/shard_map/dot_general | solution.py:45
  (76 shorter events, 26.5 us)
Async XLA Ops:
  0.6 9.8 %collective-permute-start = (bf16[128,1152]{1,0:T(8,128)(2,1)}, bf16[128,1152]{1,0:T(8,128)(2,1)S(1)}, u32[]{:S(2)}, u32[]{:S(2)}) collective-permute-start(bf16[128,1152]{1,0:T(8,128)(2,1)} %bitcast.15), channel_id=1, source_target_pairs={{0,16},{8,24},{16,0},{24,8},{32,48},{40,56},{48,32},{56,40},{64,80... | collective-permute-start | bytes 884744 | tf_op jit(solution)/shard_map/ppermute | solution.py:41
  4.5 9.6 %collective-permute-start.5 = (bf16[128,1024]{1,0:T(8,128)(2,1)}, bf16[128,1024]{1,0:T(8,128)(2,1)S(1)}, u32[]{:S(2)}, u32[]{:S(2)}) collective-permute-start(bf16[128,1024]{1,0:T(8,128)(2,1)} %bitcast.19), channel_id=1, source_target_pairs={{0,224},{8,40},{16,240},{24,56},{32,0},{40,72},{48,16},{56,88},{64... | collective-permute-start | bytes 786440 | tf_op jit(solution)/shard_map/ppermute | solution.py:33
  6.1 8.9 %collective-permute-start.6 = (bf16[128,1024]{1,0:T(8,128)(2,1)}, bf16[128,1024]{1,0:T(8,128)(2,1)S(1)}, u32[]{:S(2)}, u32[]{:S(2)}) collective-permute-start(bf16[128,1024]{1,0:T(8,128)(2,1)} %bitcast.20), channel_id=1, source_target_pairs={{0,32},{8,232},{16,48},{24,248},{32,64},{40,8},{48,80},{56,24},{64... | collective-permute-start | bytes 786440 | tf_op jit(solution)/shard_map/ppermute | solution.py:33
  10.0 4.0 %collective-permute-start.3 = (s32[1,128]{1,0:T(1,128)}, s32[1,128]{1,0:T(1,128)S(1)}, u32[]{:S(2)}, u32[]{:S(2)}) collective-permute-start(s32[1,128]{1,0:T(1,128)} %refs_5_.1), channel_id=1, source_target_pairs={{0,16},{8,24},{16,0},{24,8},{32,48},{40,56},{48,32},{56,40},{64,80... | collective-permute-start | bytes 1544 | tf_op jit(solution)/shard_map/ppermute | solution.py:41
  10.5 12.4 %collective-permute-start.1 = (bf16[128,1152]{1,0:T(8,128)(2,1)}, bf16[128,1152]{1,0:T(8,128)(2,1)S(1)}, u32[]{:S(2)}, u32[]{:S(2)}) collective-permute-start(bf16[128,1152]{1,0:T(8,128)(2,1)} %bitcast.16), channel_id=1, source_target_pairs={{0,8},{8,0},{16,24},{24,16},{32,40},{40,32},{48,56},{56,48},{64,72... | collective-permute-start | bytes 884744 | tf_op jit(solution)/shard_map/ppermute | solution.py:37
  15.0 13.1 %collective-permute-start.7 = (bf16[128,1024]{1,0:T(8,128)(2,1)S(1)}, bf16[128,1024]{1,0:T(8,128)(2,1)}, u32[]{:S(2)}, u32[]{:S(2)}) collective-permute-start(bf16[128,1024]{1,0:T(8,128)(2,1)S(1)} %collective-permute-done.5.refs_5_), channel_id=1, source_target_pairs={{0,224},{8,40},{16,240},{24,56},{32,0},{40,72},{48,16},{56,88},{64... | collective-permute-start | bytes 786440 | tf_op jit(solution)/shard_map/ppermute | solution.py:33
  16.1 12.1 %collective-permute-start.8 = (bf16[128,1024]{1,0:T(8,128)(2,1)S(1)}, bf16[128,1024]{1,0:T(8,128)(2,1)}, u32[]{:S(2)}, u32[]{:S(2)}) collective-permute-start(bf16[128,1024]{1,0:T(8,128)(2,1)S(1)} %collective-permute-done.6.refs_6_), channel_id=1, source_target_pairs={{0,32},{8,232},{16,48},{24,248},{32,64},{40,8},{48,80},{56,24},{64... | collective-permute-start | bytes 786440 | tf_op jit(solution)/shard_map/ppermute | solution.py:33
  18.5 4.4 %collective-permute-start.2 = (bf16[128,1152]{1,0:T(8,128)(2,1)S(1)}, bf16[128,1152]{1,0:T(8,128)(2,1)S(1)}, u32[]{:S(2)}, u32[]{:S(2)}) collective-permute-start(bf16[128,1152]{1,0:T(8,128)(2,1)S(1)} %collective-permute-done.refs_3_.refs_8_), channel_id=1, source_target_pairs={{0,8},{8,0},{16,24},{24,16},{32,40},{40,32},{48,56},{56,48},{64,72... | collective-permute-start | bytes 884744 | tf_op jit(solution)/shard_map/ppermute | solution.py:37
  28.2 10.6 %collective-permute-start.11 = (bf16[128,1024]{1,0:T(8,128)(2,1)}, bf16[128,1024]{1,0:T(8,128)(2,1)}, u32[]{:S(2)}, u32[]{:S(2)}) collective-permute-start(bf16[128,1024]{1,0:T(8,128)(2,1)} %collective-permute-done.8.refs_8_), channel_id=1, source_target_pairs={{0,32},{8,232},{16,48},{24,248},{32,64},{40,8},{48,80},{56,24},{64... | collective-permute-start | bytes 786440 | tf_op jit(solution)/shard_map/ppermute | solution.py:33
  30.6 12.1 %collective-permute-start.10 = (bf16[128,1024]{1,0:T(8,128)(2,1)}, bf16[128,1024]{1,0:T(8,128)(2,1)}, u32[]{:S(2)}, u32[]{:S(2)}) collective-permute-start(bf16[128,1024]{1,0:T(8,128)(2,1)} %collective-permute-done.7.refs_7_), channel_id=1, source_target_pairs={{0,224},{8,40},{16,240},{24,56},{32,0},{40,72},{48,16},{56,88},{64... | collective-permute-start | bytes 786440 | tf_op jit(solution)/shard_map/ppermute | solution.py:33
  30.6 16.1 %collective-permute-start.9 = (bf16[128,1024]{1,0:T(8,128)(2,1)}, bf16[128,1024]{1,0:T(8,128)(2,1)}, u32[]{:S(2)}, u32[]{:S(2)}) collective-permute-start(bf16[128,1024]{1,0:T(8,128)(2,1)} %collective-permute-done.8.refs_8_), channel_id=1, source_target_pairs={{0,64},{8,200},{16,80},{24,216},{32,96},{40,232},{48,112},{56,248}... | collective-permute-start | bytes 786440 | tf_op jit(solution)/shard_map/ppermute | solution.py:33
  50.9 2.0 %collective-permute-start.12 = (bf16[528,512]{1,0:T(8,128)(2,1)S(1)}, bf16[528,512]{1,0:T(8,128)(2,1)S(1)}, u32[]{:S(2)}, u32[]{:S(2)}) collective-permute-start(bf16[528,512]{1,0:T(8,128)(2,1)S(1)} %get-tuple-element.53), channel_id=1, source_target_pairs={{0,8},{8,0},{16,24},{24,16},{32,40},{40,32},{48,56},{56,48},{64,72... | collective-permute-start | bytes 1622024 | tf_op jit(solution)/shard_map/ppermute | solution.py:37
  56.1 22.5 %all-to-all-start = ((bf16[8,64,1152]{2,1,0:T(8,128)(2,1)}), bf16[8,64,1152]{2,1,0:T(8,128)(2,1)}, u32[]{:S(2)}, u32[]{:S(2)}) async-start(bf16[8,64,1152]{2,1,0:T(8,128)(2,1)} %get-tuple-element.64), calls=%async_computation | async-start | bytes 2359296 | tf_op jit(solution)/shard_map/all_to_all | solution.py:372
  60.3 5.7 %collective-permute-start.13 = (bf16[256,512]{1,0:T(8,128)(2,1)}, bf16[256,512]{1,0:T(8,128)(2,1)S(1)}, u32[]{:S(2)}, u32[]{:S(2)}) collective-permute-start(bf16[256,512]{1,0:T(8,128)(2,1)} %get-tuple-element.65), channel_id=1, source_target_pairs={{0,8},{8,0},{16,24},{24,16},{32,40},{40,32},{48,56},{56,48},{64,72... | collective-permute-start | bytes 786440 | tf_op jit(solution)/shard_map/ppermute | solution.py:37
  61.7 25.0 %collective-permute-start.16 = (bf16[128,1024]{1,0:T(8,128)(2,1)}, bf16[128,1024]{1,0:T(8,128)(2,1)}, u32[]{:S(2)}, u32[]{:S(2)}) collective-permute-start(bf16[128,1024]{1,0:T(8,128)(2,1)} %shard_map.91), channel_id=1, source_target_pairs={{0,64},{8,200},{16,80},{24,216},{32,96},{40,232},{48,112},{56,248}... | collective-permute-start | bytes 786440 | tf_op jit(solution)/shard_map/ppermute | solution.py:33
  61.8 24.9 %collective-permute-start.14 = (bf16[128,1024]{1,0:T(8,128)(2,1)}, bf16[128,1024]{1,0:T(8,128)(2,1)}, u32[]{:S(2)}, u32[]{:S(2)}) collective-permute-start(bf16[128,1024]{1,0:T(8,128)(2,1)} %get-tuple-element.68), channel_id=1, source_target_pairs={{0,32},{8,232},{16,48},{24,248},{32,64},{40,8},{48,80},{56,24},{64... | collective-permute-start | bytes 786440 | tf_op jit(solution)/shard_map/ppermute | solution.py:33
  63.4 23.4 %collective-permute-start.15 = (bf16[128,1024]{1,0:T(8,128)(2,1)}, bf16[128,1024]{1,0:T(8,128)(2,1)}, u32[]{:S(2)}, u32[]{:S(2)}) collective-permute-start(bf16[128,1024]{1,0:T(8,128)(2,1)} %get-tuple-element.69), channel_id=1, source_target_pairs={{0,224},{8,40},{16,240},{24,56},{32,0},{40,72},{48,16},{56,88},{64... | collective-permute-start | bytes 786440 | tf_op jit(solution)/shard_map/ppermute | solution.py:33
  64.5 22.2 %collective-permute-start.17 = (bf16[128,1024]{1,0:T(8,128)(2,1)}, bf16[128,1024]{1,0:T(8,128)(2,1)}, u32[]{:S(2)}, u32[]{:S(2)}) collective-permute-start(bf16[128,1024]{1,0:T(8,128)(2,1)} %get-tuple-element.71), channel_id=1, source_target_pairs={{0,32},{8,232},{16,48},{24,248},{32,64},{40,8},{48,80},{56,24},{64... | collective-permute-start | bytes 786440 | tf_op jit(solution)/shard_map/ppermute | solution.py:33
  66.0 20.7 %collective-permute-start.18 = (bf16[128,1024]{1,0:T(8,128)(2,1)}, bf16[128,1024]{1,0:T(8,128)(2,1)}, u32[]{:S(2)}, u32[]{:S(2)}) collective-permute-start(bf16[128,1024]{1,0:T(8,128)(2,1)} %get-tuple-element.72), channel_id=1, source_target_pairs={{0,224},{8,40},{16,240},{24,56},{32,0},{40,72},{48,16},{56,88},{64... | collective-permute-start | bytes 786440 | tf_op jit(solution)/shard_map/ppermute | solution.py:33
  80.9 17.7 %all-to-all-start.1 = ((bf16[32,18,128]{2,1,0:T(8,128)(2,1)}), bf16[32,18,128]{2,1,0:T(8,128)(2,1)S(1)}, u32[]{:S(2)}, u32[]{:S(2)}) async-start(bf16[32,18,128]{2,1,0:T(8,128)(2,1)} %shard_map.92), calls=%async_computation.1 | async-start | bytes 393216 | tf_op jit(solution)/shard_map/all_to_all | solution.py:379
  87.8 16.4 %collective-permute-start.20 = (bf16[128,1024]{1,0:T(8,128)(2,1)S(1)}, bf16[128,1024]{1,0:T(8,128)(2,1)S(1)}, u32[]{:S(2)}, u32[]{:S(2)}) collective-permute-start(bf16[128,1024]{1,0:T(8,128)(2,1)S(1)} %add_convert_fusion), channel_id=1, source_target_pairs={{0,192},{8,72},{16,208},{24,88},{32,224},{40,104},{48,240},{56,120... | collective-permute-start | bytes 786440 | tf_op jit(solution)/shard_map/ppermute | solution.py:33
  91.4 14.4 %collective-permute-start.19 = (bf16[128,1024]{1,0:T(8,128)(2,1)S(1)}, bf16[128,1024]{1,0:T(8,128)(2,1)S(1)}, u32[]{:S(2)}, u32[]{:S(2)}) collective-permute-start(bf16[128,1024]{1,0:T(8,128)(2,1)S(1)} %add_convert_fusion.1), channel_id=1, source_target_pairs={{0,64},{8,200},{16,80},{24,216},{32,96},{40,232},{48,112},{56,248}... | collective-permute-start | bytes 786440 | tf_op jit(solution)/shard_map/ppermute | solution.py:33
  92.7 13.0 %collective-permute-start.21 = (bf16[128,1024]{1,0:T(8,128)(2,1)S(1)}, bf16[128,1024]{1,0:T(8,128)(2,1)S(1)}, u32[]{:S(2)}, u32[]{:S(2)}) collective-permute-start(bf16[128,1024]{1,0:T(8,128)(2,1)S(1)} %copy-done.13), channel_id=1, source_target_pairs={{0,16},{8,24},{16,0},{24,8},{32,48},{40,56},{48,32},{56,40},{64,80... | collective-permute-start | bytes 786440 | tf_op jit(solution)/shard_map/ppermute | solution.py:41
  99.3 12.4 %all-to-all-start.2 = ((f32[8,36,128]{2,1,0:T(8,128)}), f32[8,36,128]{2,1,0:T(8,128)S(1)}, u32[]{:S(2)}, u32[]{:S(2)}) async-start(f32[8,36,128]{2,1,0:T(8,128)} %shard_map.93), calls=%async_computation.2 | async-start | bytes 327680 | tf_op jit(solution)/shard_map/all_to_all | solution.py:394
  (15 other events, 155.2 us)

commit v11 on v10

--- a/solution.py
+++ b/solution.py
@@ -143,7 +143,7 @@
     for n in range(count):
         moves.need(4 + n)
     emb, grad = block_grads(numbers, columns, image, match[...], moves.pack[...])
-    text_part = inner_cols(grad, image)
+    text_part = scale_of(numbers) * inner_cols(grad, image)
     for n in range(count):
         text_out[n][...] = text_part[n * rows : (n + 1) * rows].astype(text_out[n].dtype)
         moves.send(1 + n)
@@ -171,7 +171,7 @@
         match_out[n * rows : (n + 1) * rows, :] = match.T[:, 0:1]
 
 
-def last_kernel(moves, numbers, place, image_emb, match, text, acc_in, acc_out, dot_out, packet, extra, grad_out):
+def last_kernel(moves, numbers, place, image_emb, match, text, acc_in, acc_out, dot_out, packet, grad_out):
     columns = columns_of(place, 4, text.shape[0])
     emb, grad = block_grads(numbers, columns, image_emb[...], match[...], text[...])
     grad_out[...] = grad
@@ -182,11 +182,7 @@
     rows, width = acc.shape
     half, block = width // 2, rows // 4
     core = place[0] & 1
-    own = pl.ds(pl.multiple_of(core * half, half), half)
     other = pl.ds(pl.multiple_of((1 - core) * half, half), half)
-    for n, slot in enumerate((1, 3)):
-        extra[n * block : (n + 1) * block, :] = acc_out[slot * block : (slot + 1) * block, own].astype(BF16)
-    moves.send(3)
     packet[:rows, :] = acc_out[:, other].astype(BF16)
     lines = []
     for slot in range(4):
@@ -198,8 +194,8 @@
     packet[rows:, :] = jnp.concatenate(lines, 0).astype(BF16)
 
 
-def last_text_kernel(moves, grad, image_emb, out):
-    out[...] = inner_cols(grad[...], image_emb[...]).astype(out.dtype)
+def last_text_kernel(moves, numbers, grad, image_emb, out):
+    out[...] = (scale_of(numbers) * inner_cols(grad[...], image_emb[...])).astype(out.dtype)
     moves.send(0)
 
 
@@ -233,6 +229,14 @@
             moves.send(0, at)
 
 
+def extra_kernel(moves, place, acc, extra):
+    rows, width = acc.shape
+    half, block = width // 2, rows // 4
+    own = pl.ds(pl.multiple_of((place[0] & 1) * half, half), half)
+    for n, slot in enumerate((1, 3)):
+        extra[n * block : (n + 1) * block, :] = acc[slot * block : (slot + 1) * block, own].astype(BF16)
+
+
 def row_kernel(moves, place, row_half, extra, acc, row_send, row_keep):
     rows, width = acc.shape
     half, block = width // 2, rows // 4
@@ -248,6 +252,42 @@
         moves.send(1 - n)
 
 
+def sums_kernel(moves, text_2, below, far, text_m2, above, up, down):
+    for n in range(3):
+        moves.need(n)
+    up[...] = (text_2[...].astype(F32) + below[...].astype(F32) + far[...].astype(F32)).astype(BF16)
+    moves.send(0)
+    moves.need(3)
+    moves.need(4)
+    down[...] = (text_m2[...].astype(F32) + above[...].astype(F32)).astype(BF16)
+    moves.send(1)
+
+
+def text_kernel(moves, text, own, near_below, near_above, up, down, out):
+    for n in range(6):
+        moves.need(n)
+    total = own[...] + near_below[...].astype(F32) + near_above[...].astype(F32)
+    total = total + up[...].astype(F32) + down[...].astype(F32)
+    wide = text[...].astype(F32)
+    inv = lax.rsqrt(jnp.sum(wide * wide, -1, keepdims=True) + 1e-06)
+    unit = wide * inv
+    out[...] = (total - unit * jnp.sum(unit * total, -1, keepdims=True)) * inv
+    moves.send(0)
+
+
+def sensor_kernel(moves, row_keep, row_got, inv, proj_weight, image_emb, out):
+    rows = row_keep.shape[0]
+    for n in range(3):
+        moves.need(n)
+    image_grad = row_keep[...] + row_got[...].astype(F32)
+    unit = image_emb[:rows, :].astype(F32)
+    dot = jnp.sum(unit * image_grad, -1, keepdims=True)
+    proj_grad = ((image_grad - unit * dot) * inv[:rows, :]).astype(BF16)
+    moves.need(3)
+    out[...] = inner_rows(proj_grad, proj_weight[...]).astype(BF16)
+    moves.send(0)
+
+
 def chunk_kernel(moves, parts, out):
     total = parts[0].astype(F32)
     for n in range(1, parts.shape[0]):
@@ -292,7 +332,6 @@
     feat, width = proj_weight.shape
     loop_index = lax.axis_index("loop")
     place = loop_index.reshape(1)
-    logit_scale = jnp.exp(log_scale)
     numbers = jnp.stack([log_scale, logit_bias])
 
     slot = {0: texts}
@@ -335,13 +374,12 @@
     acc, text_0, text_1, text_m1, text_2, text_m2 = pairs((0, 1, -1, 2, -2), (F32, BF16, BF16, BF16, BF16), None)
     acc, text_3, text_m3 = pairs((3, -3), (BF16, BF16), acc)
     shapes = [((4 * rows, width), F32), ((4 * rows, 1), F32), ((4 * rows + 16, width // 2), BF16)]
-    shapes += [((2 * rows, width // 2), BF16), ((4 * rows, rows), BF16)]
-    acc, dot, packet, extra, last_grad = call(
+    shapes.append(((4 * rows, rows), BF16))
+    acc, dot, packet, last_grad = call(
         last_kernel,
         [jax.ShapeDtypeStruct(*s) for s in shapes],
         {5: 0},
         numbers, place, image_emb, match_rows, slot[4], acc,
-        far_out=(3,),
     )
 
     got = swap_core(packet)
@@ -354,11 +392,12 @@
         far_out=(0, 1),
         sends=DP + 1,
     )
-    last_grad, extra, text_1, text_m1, text_3, text_m3, _ = lax.optimization_barrier(
-        (last_grad, extra, text_1, text_m1, text_3, text_m3, weight_part)
-    )
+    last_grad, acc, text_1, text_m1, text_3, text_m3, _ = lax.optimization_barrier(
+        (last_grad, acc, text_1, text_m1, text_3, text_m3, weight_part)
+    )
+    (extra,) = call(extra_kernel, [jax.ShapeDtypeStruct((2 * rows, width // 2), BF16)], {}, place, acc)
     (text_4,) = call(
-        last_text_kernel, [jax.ShapeDtypeStruct((rows, width), BF16)], {}, last_grad, image_emb, far_out=(0,)
+        last_text_kernel, [jax.ShapeDtypeStruct((rows, width), BF16)], {}, numbers, last_grad, image_emb, far_out=(0,)
     )
     shapes = [((rows, width), BF16), ((rows, width), F32)]
     row_send, row_keep = call(
@@ -383,30 +422,42 @@
 
     from_below, from_above, far = shift_z(text_3, 1), shift_z(text_m3, -1), shift_z(text_4, 2)
     near_below, near_above = shift_z(text_1, 1), shift_z(text_m1, -1)
-    from_below, from_above, far, near_below, near_above, row_send, _ = lax.optimization_barrier(
-        (from_below, from_above, far, near_below, near_above, row_send, weight_chunks)
-    )
     row_got = swap_yh(row_send)
-    up = text_2.astype(F32) + from_below.astype(F32) + far.astype(F32)
-    down = text_m2.astype(F32) + from_above.astype(F32)
-    up, down = shift_z(up.astype(BF16), 2), shift_z(down.astype(BF16), -2)
-    up, down, row_got, _ = lax.optimization_barrier((up, down, row_got, shares))
+    from_below, from_above, far, near_below, near_above, row_got, _ = lax.optimization_barrier(
+        (from_below, from_above, far, near_below, near_above, row_got, weight_chunks)
+    )
+    up, down = call(
+        sums_kernel,
+        [jax.ShapeDtypeStruct((rows, width), BF16)] * 2,
+        {},
+        text_2, from_below, far, text_m2, from_above,
+        far=range(5),
+        far_out=range(2),
+    )
+    up, down = shift_z(up, 2), shift_z(down, -2)
+
+    (sensor_grad,) = call(
+        sensor_kernel,
+        [jax.ShapeDtypeStruct((rows, feat), BF16)],
+        {},
+        row_keep, row_got, image_inv, proj_weight, image_emb,
+        far=range(4),
+        far_out=(0,),
+    )
+    shares, _ = lax.optimization_barrier((shares, sensor_grad))
+    up, down, _ = lax.optimization_barrier((up, down, shares))
     shares = lax.all_to_all(shares, "dp", 0, 0, tiled=True)
     (weight_grad,) = call(
         layout_kernel, [jax.ShapeDtypeStruct((per_loop, width), F32)], {}, shares, far_out=(0,)
     )
-    text_sum = text_0 + near_below.astype(F32) + near_above.astype(F32)
-    text_sum = logit_scale * (text_sum + up.astype(F32) + down.astype(F32))
-    text_wide = texts.astype(F32)
-    text_inv = lax.rsqrt(jnp.sum(text_wide * text_wide, -1, keepdims=True) + 1e-06)
-    text_unit = text_wide * text_inv
-    text_grad = (text_sum - text_unit * jnp.sum(text_unit * text_sum, -1, keepdims=True)) * text_inv
-
-    image_grad = row_keep + row_got.astype(F32)
-    own_unit = image_emb[:rows].astype(F32)
-    own_dot = jnp.sum(own_unit * image_grad, -1, keepdims=True)
-    proj_grad = ((image_grad - own_unit * own_dot) * image_inv[:rows]).astype(BF16)
-    sensor_grad = inner_rows(proj_grad, proj_weight).astype(BF16)
+    (text_grad,) = call(
+        text_kernel,
+        [jax.ShapeDtypeStruct((rows, width), F32)],
+        {},
+        texts, text_0, near_below, near_above, up, down,
+        far=range(6),
+        far_out=(0,),
+    )
     return (sensor_grad[None], text_grad[None], weight_grad)
 
 

time: 113 us -> 109 us (0.965)
  Pallas kernels: 27.9 us -> 36.4 us
  other arithmetic: 6.62 us -> 0.74 us
  matrix products: 3.35 us -> 0 us
  waiting for transfers between devices: 24 us -> 20.9 us
    pallas_call x10 -> x14, Pallas kernels: 27.9 us -> 36.4 us  [call(): pl.pallas_call(body, out_shape=[pltpu.HBM(o.shape, o.dtype) if n in far_o...]
    all_to_all x1, waiting for transfers between devices: 9.33 us -> 5.27 us  [on_device(): weight_part = lax.all_to_all(weight_part, 'dp', 0, 0, tiled=True)]
    dot_general x1 -> x0, matrix products: 3.35 us -> none  [inner_rows(): lax.dot_general(left, right, (((1,), (1,)), ((), ())), preferred_element_...]
    reduce_sum x3 -> x0, other arithmetic: 2.6 us -> none  [the longest x1 1.35 us: on_device(): jnp.sum(text_unit * text_sum, -1, keepdims=True)]
    ppermute x3, waiting for transfers between devices: 1.66 us -> 3.94 us  [swap_yh(): return lax.ppermute(block, 'loop', route(lambda z, y, c: (z, 1 - y, c)))]
    convert_element_type x2 -> x0, other arithmetic: 2.25 us -> none  [on_device(): up, down = (shift_z(up.astype(BF16), 2), shift_z(down.astype(BF16), -2))]
    all_to_all x1, starting transfers between devices: 5.83 us -> 8.03 us  [on_device(): weight_part = lax.all_to_all(weight_chunks, 'loop', 0, 0, tiled=True)]
    ppermute x5, starting transfers between devices: 5.22 us -> 3.07 us  [swap_core(): return lax.ppermute(block, 'loop', route(lambda z, y, c: (z, y, 1 - c)))]
  transfers between devices with their start and end apart: 25 -> 25, of which waited for: 10 -> 11; matrix products, arithmetic and copies ran while one was open for 10% -> 1% of each run, Pallas kernels for 18% -> 27%
where the time goes in v11:
time: 109 us; the launch traced here: 108 us
  starting transfers between devices  46.1 us (42%)
  Pallas kernels  36.4 us (33%)
  waiting for transfers between devices  20.9 us (19%)
  between operations  2.44 us (2%)
  local copies, waits for them, and re-layouts  1.63 us (1%)
    pallas_call x14, Pallas kernels, call(): pl.pallas_call(body, out_shape=[pltpu.HBM(o.shape, o.dtype) if n in far_o...  36.4 us
    ppermute x14, starting transfers between devices, shift_z(): lax.ppermute(block, 'loop', route(lambda z, y, c: (z + (1 - 2 * c) * dist...  21.1 us
    all_to_all x1, starting transfers between devices, on_device(): weight_part = lax.all_to_all(weight_chunks, 'loop', 0, 0, tiled=True)  8.03 us
    ppermute x14, waiting for transfers between devices, shift_z(): lax.ppermute(block, 'loop', route(lambda z, y, c: (z + (1 - 2 * c) * dist...  6.68 us
    ppermute x3, starting transfers between devices, swap_yh(): return lax.ppermute(block, 'loop', route(lambda z, y, c: (z, 1 - y, c)))  6.21 us
    all_to_all x1, waiting for transfers between devices, on_device(): weight_part = lax.all_to_all(weight_part, 'dp', 0, 0, tiled=True)  5.27 us
    all_to_all x1, starting transfers between devices, on_device(): weight_part = lax.all_to_all(weight_part, 'dp', 0, 0, tiled=True)  4.27 us
    ppermute x3, waiting for transfers between devices, swap_yh(): return lax.ppermute(block, 'loop', route(lambda z, y, c: (z, 1 - y, c)))  3.94 us
  transfers between devices with their start and end apart: 25, of which 11 were waited for; matrix products, arithmetic and copies ran while one was open for 1% of the time, Pallas kernels for 27%

profile of v11, /device:TPU:1, one launch (start us, length us, event | category | flops | bytes accessed | tf_op | source)
XLA Modules:
  0.0 108.3 jit_solution(4203615293946440170)
XLA Ops:
  0.6 3.8 %collective-permute-start = (bf16[128,1152]{1,0:T(8,128)(2,1)}, bf16[128,1152]{1,0:T(8,128)(2,1)S(1)}, u32[]{:S(2)}, u32[]{:S(2)}) collective-permute-start(bf16[128,1152]{1,0:T(8,128)(2,1)} %bitcast.9), channel_id=1, source_target_pairs={{0,16},{8,24},{16,0},{24,8},{32,48},{40,56},{48,32},{56,40},{64,80... | collective-permute-start | bytes 884744 | tf_op jit(solution)/shard_map/ppermute | solution.py:41
  4.5 5.6 %collective-permute-start.6 = (bf16[128,1024]{1,0:T(8,128)(2,1)}, bf16[128,1024]{1,0:T(8,128)(2,1)S(1)}, u32[]{:S(2)}, u32[]{:S(2)}) collective-permute-start(bf16[128,1024]{1,0:T(8,128)(2,1)} %bitcast.13), channel_id=1, source_target_pairs={{0,32},{8,232},{16,48},{24,248},{32,64},{40,8},{48,80},{56,24},{64... | collective-permute-start | bytes 786440 | tf_op jit(solution)/shard_map/ppermute | solution.py:33
  10.1 3.9 %collective-permute-done.3.refs_7_ = s32[1,128]{1,0:T(1,128)S(1)} collective-permute-done((s32[1,128]{1,0:T(1,128)}, s32[1,128]{1,0:T(1,128)S(1)}, u32[]{:S(2)}, u32[]{:S(2)}) %collective-permute-start.3) | collective-permute-done | bytes 544 | tf_op jit(solution)/shard_map/ppermute | solution.py:41
  15.0 2.9 %collective-permute-done.5.refs_5_ = bf16[128,1024]{1,0:T(8,128)(2,1)S(1)} collective-permute-done((bf16[128,1024]{1,0:T(8,128)(2,1)}, bf16[128,1024]{1,0:T(8,128)(2,1)S(1)}, u32[]{:S(2)}, u32[]{:S(2)}) %collective-permute-start.5) | collective-permute-done | bytes 262176 | tf_op jit(solution)/shard_map/ppermute | solution.py:33
  18.0 2.7 %collective-permute-start.8 = (bf16[128,1024]{1,0:T(8,128)(2,1)S(1)}, bf16[128,1024]{1,0:T(8,128)(2,1)}, u32[]{:S(2)}, u32[]{:S(2)}) collective-permute-start(bf16[128,1024]{1,0:T(8,128)(2,1)S(1)} %collective-permute-done.6.refs_6_), channel_id=1, source_target_pairs={{0,32},{8,232},{16,48},{24,248},{32,64},{40,8},{48,80},{56,24},{64... | collective-permute-start | bytes 786440 | tf_op jit(solution)/shard_map/ppermute | solution.py:33
  23.8 4.4 %shard_map.85 = (bf16[512,1024]{1,0:T(8,128)(2,1)S(1)}, f32[512,1]{1,0:T(8,128)}, f32[512,1]{1,0:T(8,128)S(1)}) custom-call(bf16[1152,1024]{1,0:T(8,128)(2,1)} %refs_3_.1, bf16[128,1152]{1,0:T(8,128)(2,1)} %bitcast.11, bf16[128,1152]{1,0:T(8,128)(2,1)} %copy-done.3, bf16[128,1152]{1,0:T(8,128)(2,1)} %copy-done.1, bf16[128,1152]{1,0:T(8,128)(2,1)} %copy-done.5, ...), custom_call_target="tpu_custom_call" | custom-call | flops 1 | bytes 1 | tf_op jit(solution)/shard_map/pallas_call | solution.py:103
  28.4 2.7 %collective-permute-start.11 = (bf16[128,1024]{1,0:T(8,128)(2,1)}, bf16[128,1024]{1,0:T(8,128)(2,1)}, u32[]{:S(2)}, u32[]{:S(2)}) collective-permute-start(bf16[128,1024]{1,0:T(8,128)(2,1)} %collective-permute-done.8.refs_8_), channel_id=1, source_target_pairs={{0,32},{8,232},{16,48},{24,248},{32,64},{40,8},{48,80},{56,24},{64... | collective-permute-start | bytes 786440 | tf_op jit(solution)/shard_map/ppermute | solution.py:33
  33.4 5.5 %shard_map.86 = (f32[512,1024]{1,0:T(8,128)S(1)}, f32[128,1024]{1,0:T(8,128)}, bf16[128,1024]{1,0:T(8,128)(2,1)}, bf16[128,1024]{1,0:T(8,128)(2,1)}, bf16[128,10...) custom-call(f32[2]{0:T(128)S(1)} %pad_maximum_fusion.refs_0_, s32[1]{0:T(128)} %bitcast.refs_1_.refs_0_, ...), custom_call_target="tpu_custom_call" | custom-call | flops 1 | bytes 1 | tf_op jit(solution)/shard_map/pallas_call | solution.py:103
  39.3 3.9 %shard_map.87 = (f32[512,1024]{1,0:T(8,128)S(1)}, bf16[128,1024]{1,0:T(8,128)(2,1)}, bf16[128,1024]{1,0:T(8,128)(2,1)}) custom-call(f32[2]{0:T(128)S(1)} %pad_maximum_fusion.refs_0_, s32[1]{0:T(128)} %bitcast.refs_1_.refs_0_, bf16[512,1024]{1,0:T(8,128)(2,1)S(1)} %get-tuple-element.46.refs_2_.refs_4_, ...), custom_call_target="tpu_custom_call", output_to_operand_aliasing={{0}: (6, {})} | custom-call | flops 1 | bytes 1 | tf_op jit(solution)/shard_map/pallas_call | solution.py:103
  43.3 3.5 %shard_map.88 = (f32[512,1024]{1,0:T(8,128)S(1)}, f32[512,1]{1,0:T(8,128)S(1)}, bf16[528,512]{1,0:T(8,128)(2,1)S(1)}, bf16[512,128]{1,0:T(8,128)(2,1)S(1)}) custom-call(f32[2]{0:T(128)S(1)} %pad_maximum_fusion.refs_0_, s32[1]{0:T(128)} %bitcast.refs_1_.refs_0_, ...), custom_call_target="tpu_custom_call", output_to_operand_aliasing={{0}: (5, {})} | custom-call | flops 1 | bytes 1 | tf_op jit(solution)/shard_map/pallas_call | solution.py:103
  50.3 3.1 %shard_map.89 = (bf16[8,64,1152]{2,1,0:T(8,128)(2,1)}, f32[256,512]{1,0:T(8,128)}) custom-call(s32[1]{0:T(128)} %bitcast.refs_1_.refs_0_, bf16[528,512]{1,0:T(8,128)(2,1)S(1)} %collective-permute-done.12.refs_1_, f32[512,1024]{1,0:T(8,128)S(1)} %get-tuple-element.65.refs_2_.refs_1_.refs_3_, f32[512,1]{1,0:T(8,128)S(1)} %get-tuple-element.56.refs_3_, ...), custom_call_target="tpu_custom_call" | custom-call | flops 1 | bytes 1 | tf_op jit(solution)/shard_map/pallas_call | solution.py:103
  53.5 4.3 %all-to-all-start = ((bf16[8,64,1152]{2,1,0:T(8,128)(2,1)}), bf16[8,64,1152]{2,1,0:T(8,128)(2,1)}, u32[]{:S(2)}, u32[]{:S(2)}) async-start(bf16[8,64,1152]{2,1,0:T(8,128)(2,1)} %get-tuple-element.64), calls=%async_computation | async-start | bytes 2359296 | tf_op jit(solution)/shard_map/all_to_all | solution.py:411
  60.0 2.1 %collective-permute-start.16 = (bf16[128,1024]{1,0:T(8,128)(2,1)}, bf16[128,1024]{1,0:T(8,128)(2,1)}, u32[]{:S(2)}, u32[]{:S(2)}) collective-permute-start(bf16[128,1024]{1,0:T(8,128)(2,1)} %shard_map.92), channel_id=1, source_target_pairs={{0,64},{8,200},{16,80},{24,216},{32,96},{40,232},{48,112},{56,248}... | collective-permute-start | bytes 786440 | tf_op jit(solution)/shard_map/ppermute | solution.py:33
  65.5 2.0 %shard_map.91 = (bf16[128,1024]{1,0:T(8,128)(2,1)}, f32[128,1024]{1,0:T(8,128)}) custom-call(s32[1]{0:T(128)} %bitcast.refs_1_.refs_0_, f32[256,512]{1,0:T(8,128)} %get-tuple-element.58.refs_1_, bf16[256,512]{1,0:T(8,128)(2,1)S(1)} %collective-permute-done.13.refs_2_, f32[512,1024]{1,0:T(8,128)S(1)} %get-tuple-element.65.refs_2_.refs_1_.refs_3_), custom_call_target="tpu_custom_call" | custom-call | flops 1 | bytes 1 | tf_op jit(solution)/shard_map/pallas_call | solution.py:103
  68.0 2.3 %collective-permute-start.19 = (bf16[128,1024]{1,0:T(8,128)(2,1)}, bf16[128,1024]{1,0:T(8,128)(2,1)S(1)}, u32[]{:S(2)}, u32[]{:S(2)}) collective-permute-start(bf16[128,1024]{1,0:T(8,128)(2,1)} %get-tuple-element.72), channel_id=1, source_target_pairs={{0,16},{8,24},{16,0},{24,8},{32,48},{40,56},{48,32},{56,40},{64,80... | collective-permute-start | bytes 786440 | tf_op jit(solution)/shard_map/ppermute | solution.py:41
  70.3 5.3 %all-to-all-done.refs_0_ = bf16[8,64,1152]{2,1,0:T(8,128)(2,1)} async-done(((bf16[8,64,1152]{2,1,0:T(8,128)(2,1)}), bf16[8,64,1152]{2,1,0:T(8,128)(2,1)}, u32[]{:S(2)}, u32[]{:S(2)}) %all-to-all-start) | async-done | bytes 1179680 | tf_op jit(solution)/shard_map/all_to_all | solution.py:411
  75.6 2.3 %shard_map.93 = bf16[32,18,128]{2,1,0:T(8,128)(2,1)} custom-call(bf16[8,64,1152]{2,1,0:T(8,128)(2,1)} %all-to-all-done.refs_0_), custom_call_target="tpu_custom_call" | custom-call | flops 1 | bytes 1 | tf_op jit(solution)/shard_map/pallas_call | solution.py:103
  77.9 8.0 %all-to-all-start.1 = ((bf16[32,18,128]{2,1,0:T(8,128)(2,1)}), bf16[32,18,128]{2,1,0:T(8,128)(2,1)S(1)}, u32[]{:S(2)}, u32[]{:S(2)}) async-start(bf16[32,18,128]{2,1,0:T(8,128)(2,1)} %shard_map.93), calls=%async_computation.1 | async-start | bytes 393216 | tf_op jit(solution)/shard_map/all_to_all | solution.py:418
  86.0 2.3 %shard_map.95 = (bf16[128,1024]{1,0:T(8,128)(2,1)}, bf16[128,1024]{1,0:T(8,128)(2,1)}) custom-call(bf16[128,1024]{1,0:T(8,128)(2,1)} %get-tuple-element.77.refs_0_, bf16[128,1024]{1,0:T(8,128)(2,1)} %collective-permute-done.14.refs_1_, bf16[128,1024]{1,0:T(8,128)(2,1)} %collective-permute-done.16.refs_2_, bf16[128,1024]{1,0:T(8,128)(2,1)} %get-tuple-element.80.refs_3_, ...), custom_call_target="tpu_custom_call" | custom-call | flops 1 | bytes 1 | tf_op jit(solution)/shard_map/pallas_call | solution.py:103
  88.3 3.6 %collective-permute-start.20 = (bf16[128,1024]{1,0:T(8,128)(2,1)}, bf16[128,1024]{1,0:T(8,128)(2,1)S(1)}, u32[]{:S(2)}, u32[]{:S(2)}) collective-permute-start(bf16[128,1024]{1,0:T(8,128)(2,1)} %get-tuple-element.82), channel_id=1, source_target_pairs={{0,64},{8,200},{16,80},{24,216},{32,96},{40,232},{48,112},{56,248}... | collective-permute-start | bytes 786440 | tf_op jit(solution)/shard_map/ppermute | solution.py:33
  91.9 3.6 %shard_map.94 = bf16[128,1152]{1,0:T(8,128)(2,1)} custom-call(f32[128,1024]{1,0:T(8,128)} %get-tuple-element.66.refs_0_, bf16[128,1024]{1,0:T(8,128)(2,1)} %copy-done.10, f32[512,1]{1,0:T(8,128)} %get-tuple-element.57.refs_5_.refs_2_, bf16[1152,1024]{1,0:T(8,128)(2,1)} %refs_3_.1, bf16[512,1024]{1,0:T(8,128)(2,1)S(1)} %get-tuple-element.46.refs_2_.refs_4_), custom_call_target="tpu_custom_call" | custom-call | flops 1 | bytes 1 | tf_op jit(solution)/shard_map/pallas_call | solution.py:103
  95.5 2.2 %all-to-all-done.1.refs_0_ = bf16[32,18,128]{2,1,0:T(8,128)(2,1)S(1)} async-done(((bf16[32,18,128]{2,1,0:T(8,128)(2,1)}), bf16[32,18,128]{2,1,0:T(8,128)(2,1)S(1)}, u32[]{:S(2)}, u32[]{:S(2)}) %all-to-all-start.1) | async-done | bytes 147488 | tf_op jit(solution)/shard_map/all_to_all | solution.py:418
  98.5 3.4 %all-to-all-start.2 = ((f32[8,36,128]{2,1,0:T(8,128)}), f32[8,36,128]{2,1,0:T(8,128)S(1)}, u32[]{:S(2)}, u32[]{:S(2)}) async-start(f32[8,36,128]{2,1,0:T(8,128)} %shard_map.96), calls=%async_computation.2 | async-start | bytes 327680 | tf_op jit(solution)/shard_map/all_to_all | solution.py:449
  104.6 2.6 %shard_map.97 = f32[128,1024]{1,0:T(8,128)} custom-call(bf16[128,1024]{1,0:T(8,128)(2,1)} %bitcast.16, f32[128,1024]{1,0:T(8,128)} %get-tuple-element.74.refs_1_, bf16[128,1024]{1,0:T(8,128)(2,1)} %copy-done.8, bf16[128,1024]{1,0:T(8,128)(2,1)} %collective-permute-done.18.refs_3_, bf16[128,1024]{1,0:T(8,128)(2,1)} %copy-done.11, bf16[128,1024]{1,0:T(8,128)(2,1)} %copy-done.12), custom_call_target="tpu_custom_call" | custom-call | flops 1 | bytes 1 | tf_op jit(solution)/shard_map/pallas_call | solution.py:103
  (69 shorter events, 19.7 us)
Async XLA Ops:
  0.6 17.3 %collective-permute-start = (bf16[128,1152]{1,0:T(8,128)(2,1)}, bf16[128,1152]{1,0:T(8,128)(2,1)S(1)}, u32[]{:S(2)}, u32[]{:S(2)}) collective-permute-start(bf16[128,1152]{1,0:T(8,128)(2,1)} %bitcast.9), channel_id=1, source_target_pairs={{0,16},{8,24},{16,0},{24,8},{32,48},{40,56},{48,32},{56,40},{64,80... | collective-permute-start | bytes 884744 | tf_op jit(solution)/shard_map/ppermute | solution.py:41
  4.5 10.5 %collective-permute-start.6 = (bf16[128,1024]{1,0:T(8,128)(2,1)}, bf16[128,1024]{1,0:T(8,128)(2,1)S(1)}, u32[]{:S(2)}, u32[]{:S(2)}) collective-permute-start(bf16[128,1024]{1,0:T(8,128)(2,1)} %bitcast.13), channel_id=1, source_target_pairs={{0,32},{8,232},{16,48},{24,248},{32,64},{40,8},{48,80},{56,24},{64... | collective-permute-start | bytes 786440 | tf_op jit(solution)/shard_map/ppermute | solution.py:33
  10.0 7.9 %collective-permute-start.5 = (bf16[128,1024]{1,0:T(8,128)(2,1)}, bf16[128,1024]{1,0:T(8,128)(2,1)S(1)}, u32[]{:S(2)}, u32[]{:S(2)}) collective-permute-start(bf16[128,1024]{1,0:T(8,128)(2,1)} %bitcast.14), channel_id=1, source_target_pairs={{0,224},{8,40},{16,240},{24,56},{32,0},{40,72},{48,16},{56,88},{64... | collective-permute-start | bytes 786440 | tf_op jit(solution)/shard_map/ppermute | solution.py:33
  10.0 4.0 %collective-permute-start.3 = (s32[1,128]{1,0:T(1,128)}, s32[1,128]{1,0:T(1,128)S(1)}, u32[]{:S(2)}, u32[]{:S(2)}) collective-permute-start(s32[1,128]{1,0:T(1,128)} %refs_5_.1), channel_id=1, source_target_pairs={{0,16},{8,24},{16,0},{24,8},{32,48},{40,56},{48,32},{56,40},{64,80... | collective-permute-start | bytes 1544 | tf_op jit(solution)/shard_map/ppermute | solution.py:41
  18.0 10.3 %collective-permute-start.7 = (bf16[128,1024]{1,0:T(8,128)(2,1)S(1)}, bf16[128,1024]{1,0:T(8,128)(2,1)}, u32[]{:S(2)}, u32[]{:S(2)}) collective-permute-start(bf16[128,1024]{1,0:T(8,128)(2,1)S(1)} %collective-permute-done.5.refs_5_), channel_id=1, source_target_pairs={{0,224},{8,40},{16,240},{24,56},{32,0},{40,72},{48,16},{56,88},{64... | collective-permute-start | bytes 786440 | tf_op jit(solution)/shard_map/ppermute | solution.py:33
  18.0 10.2 %collective-permute-start.8 = (bf16[128,1024]{1,0:T(8,128)(2,1)S(1)}, bf16[128,1024]{1,0:T(8,128)(2,1)}, u32[]{:S(2)}, u32[]{:S(2)}) collective-permute-start(bf16[128,1024]{1,0:T(8,128)(2,1)S(1)} %collective-permute-done.6.refs_6_), channel_id=1, source_target_pairs={{0,32},{8,232},{16,48},{24,248},{32,64},{40,8},{48,80},{56,24},{64... | collective-permute-start | bytes 786440 | tf_op jit(solution)/shard_map/ppermute | solution.py:33
  20.7 2.3 %collective-permute-start.1 = (bf16[128,1152]{1,0:T(8,128)(2,1)}, bf16[128,1152]{1,0:T(8,128)(2,1)S(1)}, u32[]{:S(2)}, u32[]{:S(2)}) collective-permute-start(bf16[128,1152]{1,0:T(8,128)(2,1)} %bitcast.10), channel_id=1, source_target_pairs={{0,8},{8,0},{16,24},{24,16},{32,40},{40,32},{48,56},{56,48},{64,72... | collective-permute-start | bytes 884744 | tf_op jit(solution)/shard_map/ppermute | solution.py:37
  20.7 2.3 %collective-permute-start.2 = (bf16[128,1152]{1,0:T(8,128)(2,1)S(1)}, bf16[128,1152]{1,0:T(8,128)(2,1)S(1)}, u32[]{:S(2)}, u32[]{:S(2)}) collective-permute-start(bf16[128,1152]{1,0:T(8,128)(2,1)S(1)} %collective-permute-done.refs_3_.refs_8_), channel_id=1, source_target_pairs={{0,8},{8,0},{16,24},{24,16},{32,40},{40,32},{48,56},{56,48},{64,72... | collective-permute-start | bytes 884744 | tf_op jit(solution)/shard_map/ppermute | solution.py:37
  28.3 10.6 %collective-permute-start.10 = (bf16[128,1024]{1,0:T(8,128)(2,1)}, bf16[128,1024]{1,0:T(8,128)(2,1)}, u32[]{:S(2)}, u32[]{:S(2)}) collective-permute-start(bf16[128,1024]{1,0:T(8,128)(2,1)} %collective-permute-done.7.refs_7_), channel_id=1, source_target_pairs={{0,224},{8,40},{16,240},{24,56},{32,0},{40,72},{48,16},{56,88},{64... | collective-permute-start | bytes 786440 | tf_op jit(solution)/shard_map/ppermute | solution.py:33
  28.4 10.9 %collective-permute-start.11 = (bf16[128,1024]{1,0:T(8,128)(2,1)}, bf16[128,1024]{1,0:T(8,128)(2,1)}, u32[]{:S(2)}, u32[]{:S(2)}) collective-permute-start(bf16[128,1024]{1,0:T(8,128)(2,1)} %collective-permute-done.8.refs_8_), channel_id=1, source_target_pairs={{0,32},{8,232},{16,48},{24,248},{32,64},{40,8},{48,80},{56,24},{64... | collective-permute-start | bytes 786440 | tf_op jit(solution)/shard_map/ppermute | solution.py:33
  31.1 12.2 %collective-permute-start.9 = (bf16[128,1024]{1,0:T(8,128)(2,1)}, bf16[128,1024]{1,0:T(8,128)(2,1)}, u32[]{:S(2)}, u32[]{:S(2)}) collective-permute-start(bf16[128,1024]{1,0:T(8,128)(2,1)} %collective-permute-done.8.refs_8_), channel_id=1, source_target_pairs={{0,64},{8,200},{16,80},{24,216},{32,96},{40,232},{48,112},{56,248}... | collective-permute-start | bytes 786440 | tf_op jit(solution)/shard_map/ppermute | solution.py:33
  46.8 3.5 %collective-permute-start.12 = (bf16[528,512]{1,0:T(8,128)(2,1)S(1)}, bf16[528,512]{1,0:T(8,128)(2,1)S(1)}, u32[]{:S(2)}, u32[]{:S(2)}) collective-permute-start(bf16[528,512]{1,0:T(8,128)(2,1)S(1)} %get-tuple-element.54), channel_id=1, source_target_pairs={{0,8},{8,0},{16,24},{24,16},{32,40},{40,32},{48,56},{56,48},{64,72... | collective-permute-start | bytes 1622024 | tf_op jit(solution)/shard_map/ppermute | solution.py:37
  53.5 22.1 %all-to-all-start = ((bf16[8,64,1152]{2,1,0:T(8,128)(2,1)}), bf16[8,64,1152]{2,1,0:T(8,128)(2,1)}, u32[]{:S(2)}, u32[]{:S(2)}) async-start(bf16[8,64,1152]{2,1,0:T(8,128)(2,1)} %get-tuple-element.64), calls=%async_computation | async-start | bytes 2359296 | tf_op jit(solution)/shard_map/all_to_all | solution.py:411
  57.8 7.7 %collective-permute-start.13 = (bf16[256,512]{1,0:T(8,128)(2,1)S(1)}, bf16[256,512]{1,0:T(8,128)(2,1)S(1)}, u32[]{:S(2)}, u32[]{:S(2)}) collective-permute-start(bf16[256,512]{1,0:T(8,128)(2,1)S(1)} %shard_map.90), channel_id=1, source_target_pairs={{0,8},{8,0},{16,24},{24,16},{32,40},{40,32},{48,56},{56,48},{64,72... | collective-permute-start | bytes 786440 | tf_op jit(solution)/shard_map/ppermute | solution.py:37
  60.0 8.0 %collective-permute-start.16 = (bf16[128,1024]{1,0:T(8,128)(2,1)}, bf16[128,1024]{1,0:T(8,128)(2,1)}, u32[]{:S(2)}, u32[]{:S(2)}) collective-permute-start(bf16[128,1024]{1,0:T(8,128)(2,1)} %shard_map.92), channel_id=1, source_target_pairs={{0,64},{8,200},{16,80},{24,216},{32,96},{40,232},{48,112},{56,248}... | collective-permute-start | bytes 786440 | tf_op jit(solution)/shard_map/ppermute | solution.py:33
  62.1 23.8 %collective-permute-start.14 = (bf16[128,1024]{1,0:T(8,128)(2,1)}, bf16[128,1024]{1,0:T(8,128)(2,1)}, u32[]{:S(2)}, u32[]{:S(2)}) collective-permute-start(bf16[128,1024]{1,0:T(8,128)(2,1)} %get-tuple-element.67), channel_id=1, source_target_pairs={{0,32},{8,232},{16,48},{24,248},{32,64},{40,8},{48,80},{56,24},{64... | collective-permute-start | bytes 786440 | tf_op jit(solution)/shard_map/ppermute | solution.py:33
  62.8 23.1 %collective-permute-start.15 = (bf16[128,1024]{1,0:T(8,128)(2,1)}, bf16[128,1024]{1,0:T(8,128)(2,1)}, u32[]{:S(2)}, u32[]{:S(2)}) collective-permute-start(bf16[128,1024]{1,0:T(8,128)(2,1)} %get-tuple-element.68), channel_id=1, source_target_pairs={{0,224},{8,40},{16,240},{24,56},{32,0},{40,72},{48,16},{56,88},{64... | collective-permute-start | bytes 786440 | tf_op jit(solution)/shard_map/ppermute | solution.py:33
  63.6 22.4 %collective-permute-start.17 = (bf16[128,1024]{1,0:T(8,128)(2,1)}, bf16[128,1024]{1,0:T(8,128)(2,1)S(1)}, u32[]{:S(2)}, u32[]{:S(2)}) collective-permute-start(bf16[128,1024]{1,0:T(8,128)(2,1)} %get-tuple-element.70), channel_id=1, source_target_pairs={{0,32},{8,232},{16,48},{24,248},{32,64},{40,8},{48,80},{56,24},{64... | collective-permute-start | bytes 786440 | tf_op jit(solution)/shard_map/ppermute | solution.py:33
  65.5 20.4 %collective-permute-start.18 = (bf16[128,1024]{1,0:T(8,128)(2,1)}, bf16[128,1024]{1,0:T(8,128)(2,1)}, u32[]{:S(2)}, u32[]{:S(2)}) collective-permute-start(bf16[128,1024]{1,0:T(8,128)(2,1)} %get-tuple-element.71), channel_id=1, source_target_pairs={{0,224},{8,40},{16,240},{24,56},{32,0},{40,72},{48,16},{56,88},{64... | collective-permute-start | bytes 786440 | tf_op jit(solution)/shard_map/ppermute | solution.py:33
  68.0 18.0 %collective-permute-start.19 = (bf16[128,1024]{1,0:T(8,128)(2,1)}, bf16[128,1024]{1,0:T(8,128)(2,1)S(1)}, u32[]{:S(2)}, u32[]{:S(2)}) collective-permute-start(bf16[128,1024]{1,0:T(8,128)(2,1)} %get-tuple-element.72), channel_id=1, source_target_pairs={{0,16},{8,24},{16,0},{24,8},{32,48},{40,56},{48,32},{56,40},{64,80... | collective-permute-start | bytes 786440 | tf_op jit(solution)/shard_map/ppermute | solution.py:41
  77.9 19.9 %all-to-all-start.1 = ((bf16[32,18,128]{2,1,0:T(8,128)(2,1)}), bf16[32,18,128]{2,1,0:T(8,128)(2,1)S(1)}, u32[]{:S(2)}, u32[]{:S(2)}) async-start(bf16[32,18,128]{2,1,0:T(8,128)(2,1)} %shard_map.93), calls=%async_computation.1 | async-start | bytes 393216 | tf_op jit(solution)/shard_map/all_to_all | solution.py:418
  88.3 15.5 %collective-permute-start.20 = (bf16[128,1024]{1,0:T(8,128)(2,1)}, bf16[128,1024]{1,0:T(8,128)(2,1)S(1)}, u32[]{:S(2)}, u32[]{:S(2)}) collective-permute-start(bf16[128,1024]{1,0:T(8,128)(2,1)} %get-tuple-element.82), channel_id=1, source_target_pairs={{0,64},{8,200},{16,80},{24,216},{32,96},{40,232},{48,112},{56,248}... | collective-permute-start | bytes 786440 | tf_op jit(solution)/shard_map/ppermute | solution.py:33
  91.9 11.9 %collective-permute-start.21 = (bf16[128,1024]{1,0:T(8,128)(2,1)}, bf16[128,1024]{1,0:T(8,128)(2,1)S(1)}, u32[]{:S(2)}, u32[]{:S(2)}) collective-permute-start(bf16[128,1024]{1,0:T(8,128)(2,1)} %get-tuple-element.83), channel_id=1, source_target_pairs={{0,192},{8,72},{16,208},{24,88},{32,224},{40,104},{48,240},{56,120... | collective-permute-start | bytes 786440 | tf_op jit(solution)/shard_map/ppermute | solution.py:33
  98.5 8.8 %all-to-all-start.2 = ((f32[8,36,128]{2,1,0:T(8,128)}), f32[8,36,128]{2,1,0:T(8,128)S(1)}, u32[]{:S(2)}, u32[]{:S(2)}) async-start(f32[8,36,128]{2,1,0:T(8,128)} %shard_map.96), calls=%async_computation.2 | async-start | bytes 327680 | tf_op jit(solution)/shard_map/all_to_all | solution.py:449
  (14 other events, 87.0 us)

commit v12 on v11

--- a/solution.py
+++ b/solution.py
@@ -57,6 +57,11 @@
     def need(self, n):
         self.loads[n].wait()
 
+    def push(self, source, n, part):
+        copy = pltpu.make_async_copy(source, self.outs[n].at[part], self.sems.at[self.base + len(self.sent)])
+        copy.start()
+        self.sent.append(copy)
+
     def send(self, n, part=None):
         source, target = self.held[n], self.outs[n]
         if part is not None:
@@ -66,7 +71,7 @@
         self.sent.append(copy)
 
 
-def call(kernel, out, aliases, *operands, far=(), packed=(), far_out=(), sends=None, cuts=()):
+def call(kernel, out, aliases, *operands, far=(), packed=(), far_out=(), pushed=(), sends=None, cuts=()):
     cuts = dict(cuts)
     far, packed, far_out, total = list(far), list(packed), list(far_out), len(operands)
     sends = len(far_out) if sends is None else sends
@@ -91,7 +96,7 @@
         for copy in moves.sent:
             copy.wait()
 
-    in_hbm = far + packed
+    in_hbm, out_hbm = far + packed, far_out + list(pushed)
     in_specs = [SMEM if o.ndim == 1 else HBM if n in in_hbm else VMEM for n, o in enumerate(operands)]
     scratch = [pltpu.VMEM(operands[n].shape, operands[n].dtype) for n in far]
     scratch += [pltpu.VMEM(out[n].shape, out[n].dtype) for n in far_out]
@@ -102,9 +107,9 @@
     operands = [pltpu.with_memory_space_constraint(o, pltpu.HBM) if n in in_hbm else o for n, o in enumerate(operands)]
     return pl.pallas_call(
         body,
-        out_shape=[pltpu.HBM(o.shape, o.dtype) if n in far_out else o for n, o in enumerate(out)],
+        out_shape=[pltpu.HBM(o.shape, o.dtype) if n in out_hbm else o for n, o in enumerate(out)],
         in_specs=in_specs,
-        out_specs=[HBM if n in far_out else VMEM for n in range(len(out))],
+        out_specs=[HBM if n in out_hbm else VMEM for n in range(len(out))],
         scratch_shapes=scratch,
         input_output_aliases=aliases,
         cost_estimate=pl.CostEstimate(flops=1, bytes_accessed=1, transcendentals=0),
@@ -131,44 +136,49 @@
     return (lax.broadcasted_iota(jnp.int32, (1, rows), 1) + start).astype(F32)
 
 
-def pairs_kernel(keys, first, moves, numbers, place, image_emb, match, *refs):
+def pairs_body(keys, moves, first, numbers, place, image_emb, match, texts, acc_in, acc_out, text_out):
     count = len(keys)
-    texts, refs = refs[:count], refs[count:]
-    if not first:
-        acc_in, refs = refs[0], refs[1:]
-    acc_out, text_out = refs[0], refs[1:]
     image = image_emb[...]
     rows = texts[0].shape[0]
     columns = jnp.concatenate([columns_of(place, key, rows) for key in keys], 1)
     for n in range(count):
-        moves.need(4 + n)
+        moves.need(first + n)
     emb, grad = block_grads(numbers, columns, image, match[...], moves.pack[...])
     text_part = scale_of(numbers) * inner_cols(grad, image)
+    shift = 2 if acc_in is None else 1
     for n in range(count):
         text_out[n][...] = text_part[n * rows : (n + 1) * rows].astype(text_out[n].dtype)
-        moves.send(1 + n)
+        moves.send(shift + n)
     part = jnp.dot(grad, emb, preferred_element_type=F32)
-    acc_out[...] = part if first else acc_in[...] + part
-
-
-def project_kernel(moves, proj_weight, own, core, yh, both, *refs):
-    matches, (emb, inv_out, match_out) = refs[:4], refs[4:]
-    rows, cut = own.shape[0], CUT
+    acc_out[...] = part if acc_in is None else acc_in[...] + part
+
+
+def pairs_kernel(keys, moves, numbers, place, image_emb, match, *refs):
+    count = len(keys)
+    pairs_body(keys, moves, 4, numbers, place, image_emb, match, refs[:count], refs[count], refs[count + 1], refs[count + 2 :])
+
+
+def project_kernel(moves, proj_weight, own, core, yh, both, emb, inv_out):
     for n in range(4):
         moves.need(1 + n)
     sensor = moves.pack[...]
     moves.need((0, 0))
-    projected = jnp.dot(sensor[:, :cut], proj_weight[:cut], preferred_element_type=F32)
+    projected = jnp.dot(sensor[:, :CUT], proj_weight[:CUT], preferred_element_type=F32)
     moves.need((0, 1))
-    projected = projected + jnp.dot(sensor[:, cut:], proj_weight[cut:], preferred_element_type=F32)
+    projected = projected + jnp.dot(sensor[:, CUT:], proj_weight[CUT:], preferred_element_type=F32)
     inv = lax.rsqrt(jnp.sum(projected * projected, -1, keepdims=True) + 1e-06)
-    emb[...] = (projected * inv).astype(BF16)
     inv_out[...] = inv
     moves.send(1)
-    moves.need(5)
-    for n in range(4):
-        match = jnp.broadcast_to(matches[n][...].astype(F32), (rows, rows))
-        match_out[n * rows : (n + 1) * rows, :] = match.T[:, 0:1]
+    emb[...] = (projected * inv).astype(BF16)
+
+
+def first_pairs_kernel(keys, moves, numbers, place, image_emb, own, core, yh, both, *refs):
+    texts, match, outs = refs[: len(keys)], refs[len(keys)], refs[len(keys) + 1 :]
+    block = own.shape[1]
+    for n, line in enumerate((own, core, yh, both)):
+        turned = jnp.broadcast_to(line[...].astype(F32), (128, block)).T
+        match[n * block : (n + 1) * block, :] = turned[:, 0:1]
+    pairs_body(keys, moves, 7, numbers, place, image_emb, match, texts, None, outs[0], outs[1:])
 
 
 def last_kernel(moves, numbers, place, image_emb, match, text, acc_in, acc_out, dot_out, packet, grad_out):
@@ -199,10 +209,16 @@
     moves.send(0)
 
 
-def weight_kernel(moves, place, got, acc, dot, image_emb, inv, own_rows, core_rows, yh_rows, both_rows, weight, row_half):
+def weight_kernel(moves, place, got, acc, dot, image_emb, inv, own_rows, core_rows, yh_rows, both_rows, weight, row_half, row_other, extra):
     rows, width = acc.shape
     half, quarter, block = width // 2, width // 4, rows // 4
-    own = pl.ds(pl.multiple_of((place[0] & 1) * half, half), half)
+    core = place[0] & 1
+    own = pl.ds(pl.multiple_of(core * half, half), half)
+    other = pl.ds(pl.multiple_of((1 - core) * half, half), half)
+    for n in range(2):
+        here = pl.ds(n * block, block)
+        moves.push(acc.at[pl.ds((2 * n + 1) * block, block), own], 3, here)
+        moves.push(acc.at[pl.ds(2 * n * block, block), other], 2, here)
     digits = got[rows:, :256].astype(F32)
     moves.need(5)
     projs = []
@@ -229,26 +245,17 @@
             moves.send(0, at)
 
 
-def extra_kernel(moves, place, acc, extra):
-    rows, width = acc.shape
-    half, block = width // 2, rows // 4
-    own = pl.ds(pl.multiple_of((place[0] & 1) * half, half), half)
-    for n, slot in enumerate((1, 3)):
-        extra[n * block : (n + 1) * block, :] = acc[slot * block : (slot + 1) * block, own].astype(BF16)
-
-
-def row_kernel(moves, place, row_half, extra, acc, row_send, row_keep):
-    rows, width = acc.shape
-    half, block = width // 2, rows // 4
+def row_kernel(moves, place, row_half, row_other, extra, row_send, row_keep):
+    block, half = row_half.shape[0] // 2, row_half.shape[1]
     core = place[0] & 1
     own = pl.ds(pl.multiple_of(core * half, half), half)
     other = pl.ds(pl.multiple_of((1 - core) * half, half), half)
-    moves.need(1)
-    for n, target in enumerate((row_keep, row_send)):
+    for n in range(3):
+        moves.need(1 + n)
+    for n, target in ((1, row_send), (0, row_keep)):
         here = slice(n * block, (n + 1) * block)
         target[:, own] = row_half[here, :].astype(target.dtype)
-        rest = extra[here, :].astype(F32)
-        target[:, other] = (acc[2 * n * block : (2 * n + 1) * block, other] + rest).astype(target.dtype)
+        target[:, other] = (row_other[here, :] + extra[here, :]).astype(target.dtype)
         moves.send(1 - n)
 
 
@@ -346,13 +353,12 @@
     sensors = [sensor, swap_core(sensor_later), sensor_yh, swap_core(sensor_yh)]
     match_both = swap_core(jnp.concatenate([match, match_yh], 0))
     match = [match, match_both[:1], match_yh, match_both[1:]]
-    shapes = [((4 * rows, width), BF16), ((4 * rows, 1), F32), ((4 * rows, 1), F32)]
-    image_emb, image_inv, match_rows = call(
+    image_emb, image_inv = call(
         project_kernel,
-        [jax.ShapeDtypeStruct(*s) for s in shapes],
-        {},
-        proj_weight, *sensors, *match,
-        far=(0, 5),
+        [jax.ShapeDtypeStruct((4 * rows, width), BF16), jax.ShapeDtypeStruct((4 * rows, 1), F32)],
+        {},
+        proj_weight, *sensors,
+        far=(0,),
         packed=range(1, 5),
         far_out=(1,),
         cuts={0: CUT},
@@ -360,19 +366,26 @@
     up, down, _ = lax.optimization_barrier((slot[2], slot[-2], image_emb))
     slot[3], slot[-3], slot[4] = shift_z(up, -1), shift_z(down, 1), shift_z(down, 2)
 
-    def pairs(keys, dtypes, acc):
-        operands = [numbers, place, image_emb, match_rows, *(slot[k] for k in keys)]
-        out = [jax.ShapeDtypeStruct((4 * rows, width), F32)]
-        out += [jax.ShapeDtypeStruct((rows, width), d) for d in dtypes]
-        aliases = {}
-        if acc is not None:
-            aliases = {len(operands): 0}
-            operands.append(acc)
-        kernel = functools.partial(pairs_kernel, keys, acc is None)
-        return call(kernel, out, aliases, *operands, packed=range(4, 4 + len(keys)), far_out=range(1, len(out)))
-
-    acc, text_0, text_1, text_m1, text_2, text_m2 = pairs((0, 1, -1, 2, -2), (F32, BF16, BF16, BF16, BF16), None)
-    acc, text_3, text_m3 = pairs((3, -3), (BF16, BF16), acc)
+    text_shape = jax.ShapeDtypeStruct((rows, width), BF16)
+    acc_shape = jax.ShapeDtypeStruct((4 * rows, width), F32)
+    keys = (0, 1, -1, 2, -2)
+    match_rows, acc, text_0, text_1, text_m1, text_2, text_m2 = call(
+        functools.partial(first_pairs_kernel, keys),
+        [jax.ShapeDtypeStruct((4 * rows, 1), F32), acc_shape, jax.ShapeDtypeStruct((rows, width), F32)] + [text_shape] * 4,
+        {},
+        numbers, place, image_emb, *match, *(slot[k] for k in keys),
+        packed=range(7, 12),
+        far_out=range(2, 7),
+    )
+    keys = (3, -3)
+    acc, text_3, text_m3 = call(
+        functools.partial(pairs_kernel, keys),
+        [acc_shape] + [text_shape] * 2,
+        {6: 0},
+        numbers, place, image_emb, match_rows, *(slot[k] for k in keys), acc,
+        packed=range(4, 6),
+        far_out=range(1, 3),
+    )
     shapes = [((4 * rows, width), F32), ((4 * rows, 1), F32), ((4 * rows + 16, width // 2), BF16)]
     shapes.append(((4 * rows, rows), BF16))
     acc, dot, packet, last_grad = call(
@@ -383,19 +396,19 @@
     )
 
     got = swap_core(packet)
-    weight_part, row_half = call(
+    weight_part, row_half, row_other, extra = call(
         weight_kernel,
-        [jax.ShapeDtypeStruct((DP, width // 16, feat), BF16), jax.ShapeDtypeStruct((2 * rows, width // 2), F32)],
+        [jax.ShapeDtypeStruct((DP, width // 16, feat), BF16)] + [jax.ShapeDtypeStruct((2 * rows, width // 2), F32)] * 3,
         {},
         place, got, acc, dot, image_emb, image_inv, *sensors,
         far=(5,),
         far_out=(0, 1),
-        sends=DP + 1,
-    )
-    last_grad, acc, text_1, text_m1, text_3, text_m3, _ = lax.optimization_barrier(
-        (last_grad, acc, text_1, text_m1, text_3, text_m3, weight_part)
-    )
-    (extra,) = call(extra_kernel, [jax.ShapeDtypeStruct((2 * rows, width // 2), BF16)], {}, place, acc)
+        pushed=(2, 3),
+        sends=DP + 5,
+    )
+    last_grad, text_1, text_m1, text_3, text_m3, _ = lax.optimization_barrier(
+        (last_grad, text_1, text_m1, text_3, text_m3, weight_part)
+    )
     (text_4,) = call(
         last_text_kernel, [jax.ShapeDtypeStruct((rows, width), BF16)], {}, numbers, last_grad, image_emb, far_out=(0,)
     )
@@ -404,8 +417,8 @@
         row_kernel,
         [jax.ShapeDtypeStruct(*s) for s in shapes],
         {},
-        place, row_half, swap_core(extra), acc,
-        far=(1,),
+        place, row_half, row_other, swap_core(extra),
+        far=range(1, 4),
         far_out=(0, 1),
     )
     weight_part = lax.all_to_all(weight_part, "dp", 0, 0, tiled=True)

time: 109 us -> 115 us (1.055)
  starting transfers between devices: 46.1 us -> 56.9 us
  waiting for transfers between devices: 20.9 us -> 15 us
  local copies, waits for them, and re-layouts: 1.63 us -> 4.58 us
  Pallas kernels: 36.4 us -> 34.9 us
    ppermute x3, starting transfers between devices: 6.21 us -> 9.5 us  [swap_yh(): return lax.ppermute(block, 'loop', route(lambda z, y, c: (z, 1 - y, c)))]
    ppermute x5, starting transfers between devices: 3.07 us -> 6.19 us  [swap_core(): return lax.ppermute(block, 'loop', route(lambda z, y, c: (z, y, 1 - c)))]
    unnamed x26 -> x44, local copies, waits for them, and re-layouts: 1.62 us -> 4.58 us
    ppermute x14, starting transfers between devices: 21.1 us -> 23.9 us  [shift_z(): lax.ppermute(block, 'loop', route(lambda z, y, c: (z + (1 - 2 * c) * dist...]
    ppermute x3, waiting for transfers between devices: 3.94 us -> 1.48 us  [swap_yh(): return lax.ppermute(block, 'loop', route(lambda z, y, c: (z, 1 - y, c)))]
    all_to_all x1, waiting for transfers between devices: 5.27 us -> 3.7 us  [on_device(): weight_part = lax.all_to_all(weight_part, 'dp', 0, 0, tiled=True)]
    pallas_call x14 -> x13, Pallas kernels: 36.4 us -> 34.9 us  [call(): pl.pallas_call(body, out_shape=[pltpu.HBM(o.shape, o.dtype) if n in out_h...]
  transfers between devices with their start and end apart: 25 -> 25, of which waited for: 11 -> 8; matrix products, arithmetic and copies ran while one was open for 1% -> 1% of each run, Pallas kernels for 27% -> 24%
where the time goes in v12:
time: 115 us
  starting transfers between devices  56.9 us (49%)
  Pallas kernels  34.9 us (30%)
  waiting for transfers between devices  15 us (13%)
  local copies, waits for them, and re-layouts  4.58 us (4%)
  between operations  2.5 us (2%)
    pallas_call x13, Pallas kernels, call(): pl.pallas_call(body, out_shape=[pltpu.HBM(o.shape, o.dtype) if n in out_h...  34.9 us
    ppermute x14, starting transfers between devices, shift_z(): lax.ppermute(block, 'loop', route(lambda z, y, c: (z + (1 - 2 * c) * dist...  23.9 us
    ppermute x3, starting transfers between devices, swap_yh(): return lax.ppermute(block, 'loop', route(lambda z, y, c: (z, 1 - y, c)))  9.5 us
    all_to_all x1, starting transfers between devices, on_device(): weight_part = lax.all_to_all(weight_chunks, 'loop', 0, 0, tiled=True)  8.8 us
    ppermute x14, waiting for transfers between devices, shift_z(): lax.ppermute(block, 'loop', route(lambda z, y, c: (z + (1 - 2 * c) * dist...  6.54 us
    ppermute x5, starting transfers between devices, swap_core(): return lax.ppermute(block, 'loop', route(lambda z, y, c: (z, y, 1 - c)))  6.19 us
    all_to_all x1, starting transfers between devices, on_device(): weight_part = lax.all_to_all(weight_part, 'dp', 0, 0, tiled=True)  5.03 us
    unnamed x44, local copies, waits for them, and re-layouts  4.58 us
  transfers between devices with their start and end apart: 25, of which 8 were waited for; matrix products, arithmetic and copies ran while one was open for 1% of the time, Pallas kernels for 24%

profile of v12, /device:TPU:1, one launch (start us, length us, event | category | flops | bytes accessed | tf_op | source)
XLA Modules:
  0.0 114.5 jit_solution(3180673191062205004)
XLA Ops:
  0.6 3.8 %collective-permute-start = (bf16[128,1152]{1,0:T(8,128)(2,1)}, bf16[128,1152]{1,0:T(8,128)(2,1)S(1)}, u32[]{:S(2)}, u32[]{:S(2)}) collective-permute-start(bf16[128,1152]{1,0:T(8,128)(2,1)} %bitcast.9), channel_id=1, source_target_pairs={{0,16},{8,24},{16,0},{24,8},{32,48},{40,56},{48,32},{56,40},{64,80... | collective-permute-start | bytes 884744 | tf_op jit(solution)/shard_map/ppermute | solution.py:41
  4.5 5.6 %collective-permute-start.6 = (bf16[128,1024]{1,0:T(8,128)(2,1)}, bf16[128,1024]{1,0:T(8,128)(2,1)S(1)}, u32[]{:S(2)}, u32[]{:S(2)}) collective-permute-start(bf16[128,1024]{1,0:T(8,128)(2,1)} %bitcast.13), channel_id=1, source_target_pairs={{0,32},{8,232},{16,48},{24,248},{32,64},{40,8},{48,80},{56,24},{64... | collective-permute-start | bytes 786440 | tf_op jit(solution)/shard_map/ppermute | solution.py:33
  10.5 2.2 %collective-permute-start.1 = (bf16[128,1152]{1,0:T(8,128)(2,1)}, bf16[128,1152]{1,0:T(8,128)(2,1)S(1)}, u32[]{:S(2)}, u32[]{:S(2)}) collective-permute-start(bf16[128,1152]{1,0:T(8,128)(2,1)} %bitcast.10), channel_id=1, source_target_pairs={{0,8},{8,0},{16,24},{24,16},{32,40},{40,32},{48,56},{56,48},{64,72... | collective-permute-start | bytes 884744 | tf_op jit(solution)/shard_map/ppermute | solution.py:37
  12.7 3.0 %collective-permute-start.3 = (s32[1,128]{1,0:T(1,128)}, s32[1,128]{1,0:T(1,128)S(1)}, u32[]{:S(2)}, u32[]{:S(2)}) collective-permute-start(s32[1,128]{1,0:T(1,128)} %refs_3_.2), channel_id=1, source_target_pairs={{0,16},{8,24},{16,0},{24,8},{32,48},{40,56},{48,32},{56,40},{64,80... | collective-permute-start | bytes 1544 | tf_op jit(solution)/shard_map/ppermute | solution.py:41
  18.5 4.0 %collective-permute-start.8 = (bf16[128,1024]{1,0:T(8,128)(2,1)S(1)}, bf16[128,1024]{1,0:T(8,128)(2,1)S(1)}, u32[]{:S(2)}, u32[]{:S(2)}) collective-permute-start(bf16[128,1024]{1,0:T(8,128)(2,1)S(1)} %collective-permute-done.6.refs_9_), channel_id=1, source_target_pairs={{0,32},{8,232},{16,48},{24,248},{32,64},{40,8},{48,80},{56,24},{64... | collective-permute-start | bytes 786440 | tf_op jit(solution)/shard_map/ppermute | solution.py:33
  27.7 4.4 %shard_map.85 = (bf16[512,1024]{1,0:T(8,128)(2,1)S(1)}, f32[512,1]{1,0:T(8,128)}) custom-call(bf16[1152,1024]{1,0:T(8,128)(2,1)} %refs_3_.3, bf16[128,1152]{1,0:T(8,128)(2,1)} %bitcast.11, bf16[128,1152]{1,0:T(8,128)(2,1)} %copy-done.3, bf16[128,1152]{1,0:T(8,128)(2,1)} %copy-done.1, bf16[128,1152]{1,0:T(8,128)(2,1)} %copy-done.5), custom_call_target="tpu_custom_call" | custom-call | flops 1 | bytes 1 | tf_op jit(solution)/shard_map/pallas_call | solution.py:108
  32.2 3.0 %collective-permute-start.11 = (bf16[128,1024]{1,0:T(8,128)(2,1)S(1)}, bf16[128,1024]{1,0:T(8,128)(2,1)S(1)}, u32[]{:S(2)}, u32[]{:S(2)}) collective-permute-start(bf16[128,1024]{1,0:T(8,128)(2,1)S(1)} %collective-permute-done.8.refs_11_), channel_id=1, source_target_pairs={{0,32},{8,232},{16,48},{24,248},{32,64},{40,8},{48,80},{56,24},{64... | collective-permute-start | bytes 786440 | tf_op jit(solution)/shard_map/ppermute | solution.py:33
  36.6 5.5 %shard_map.86 = (f32[512,1]{1,0:T(8,128)S(1)}, f32[512,1024]{1,0:T(8,128)S(1)}, f32[128,1024]{1,0:T(8,128)}, bf16[128,1024]{1,0:T(8,128)(2,1)}, bf16[128,1024]{1...) custom-call(f32[2]{0:T(128)S(1)} %pad_maximum_fusion.refs_0_, s32[1]{0:T(128)} %bitcast.refs_1_.refs_0_, ...), custom_call_target="tpu_custom_call" | custom-call | flops 1 | bytes 1 | tf_op jit(solution)/shard_map/pallas_call | solution.py:108
  42.1 2.9 %collective-permute-done.10.refs_4_ = bf16[128,1024]{1,0:T(8,128)(2,1)S(1)} collective-permute-done((bf16[128,1024]{1,0:T(8,128)(2,1)S(1)}, bf16[128,1024]{1,0:T(8,128)(2,1)S(1)}, u32[]{:S(2)}, u32[]{:S(2)}) %collective-permute-start.10) | collective-permute-done | bytes 262176 | tf_op jit(solution)/shard_map/ppermute | solution.py:33
  45.8 4.0 %shard_map.87 = (f32[512,1024]{1,0:T(8,128)S(1)}, bf16[128,1024]{1,0:T(8,128)(2,1)}, bf16[128,1024]{1,0:T(8,128)(2,1)}) custom-call(f32[2]{0:T(128)S(1)} %pad_maximum_fusion.refs_0_, s32[1]{0:T(128)} %bitcast.refs_1_.refs_0_, bf16[512,1024]{1,0:T(8,128)(2,1)S(1)} %get-tuple-element.47.refs_2_.refs_4_, ...), custom_call_target="tpu_custom_call", output_to_operand_aliasing={{0}: (6, {})} | custom-call | flops 1 | bytes 1 | tf_op jit(solution)/shard_map/pallas_call | solution.py:108
  49.8 3.0 %shard_map.88 = (f32[512,1024]{1,0:T(8,128)S(1)}, f32[512,1]{1,0:T(8,128)S(1)}, bf16[528,512]{1,0:T(8,128)(2,1)S(1)}, bf16[512,128]{1,0:T(8,128)(2,1)S(1)}) custom-call(f32[2]{0:T(128)S(1)} %pad_maximum_fusion.refs_0_, s32[1]{0:T(128)} %bitcast.refs_1_.refs_0_, ...), custom_call_target="tpu_custom_call", output_to_operand_aliasing={{0}: (5, {})} | custom-call | flops 1 | bytes 1 | tf_op jit(solution)/shard_map/pallas_call | solution.py:108
  55.9 3.3 %shard_map.89 = (bf16[8,64,1152]{2,1,0:T(8,128)(2,1)}, f32[256,512]{1,0:T(8,128)}, f32[256,512]{1,0:T(8,128)}, f32[256,512]{1,0:T(8,128)}) custom-call(s32[1]{0:T(128)} %bitcast.refs_1_.refs_0_, bf16[528,512]{1,0:T(8,128)(2,1)S(1)} %collective-permute-done.12.refs_1_, f32[512,1024]{1,0:T(8,128)S(1)} %get-tuple-element.56.refs_2_, ...), custom_call_target="tpu_custom_call" | custom-call | flops 1 | bytes 1 | tf_op jit(solution)/shard_map/pallas_call | solution.py:108
  59.2 5.0 %all-to-all-start = ((bf16[8,64,1152]{2,1,0:T(8,128)(2,1)}), bf16[8,64,1152]{2,1,0:T(8,128)(2,1)S(1)}, u32[]{:S(2)}, u32[]{:S(2)}) async-start(bf16[8,64,1152]{2,1,0:T(8,128)(2,1)} %get-tuple-element.68), calls=%async_computation | async-start | bytes 2359296 | tf_op jit(solution)/shard_map/all_to_all | solution.py:424
  70.1 2.3 %collective-permute-start.17 = (bf16[128,1024]{1,0:T(8,128)(2,1)}, bf16[128,1024]{1,0:T(8,128)(2,1)S(1)}, u32[]{:S(2)}, u32[]{:S(2)}) collective-permute-start(bf16[128,1024]{1,0:T(8,128)(2,1)} %get-tuple-element.72), channel_id=1, source_target_pairs={{0,32},{8,232},{16,48},{24,248},{32,64},{40,8},{48,80},{56,24},{64... | collective-permute-start | bytes 786440 | tf_op jit(solution)/shard_map/ppermute | solution.py:33
  73.2 2.3 %shard_map.90 = (bf16[128,1024]{1,0:T(8,128)(2,1)}, f32[128,1024]{1,0:T(8,128)}) custom-call(s32[1]{0:T(128)} %bitcast.refs_1_.refs_0_, f32[256,512]{1,0:T(8,128)} %get-tuple-element.59.refs_1_, f32[256,512]{1,0:T(8,128)} %get-tuple-element.60.refs_2_, f32[256,512]{1,0:T(8,128)} %copy-done.8), custom_call_target="tpu_custom_call" | custom-call | flops 1 | bytes 1 | tf_op jit(solution)/shard_map/pallas_call | solution.py:108
  75.5 2.7 %collective-permute-start.19 = (bf16[128,1024]{1,0:T(8,128)(2,1)}, bf16[128,1024]{1,0:T(8,128)(2,1)}, u32[]{:S(2)}, u32[]{:S(2)}) collective-permute-start(bf16[128,1024]{1,0:T(8,128)(2,1)} %get-tuple-element.74), channel_id=1, source_target_pairs={{0,16},{8,24},{16,0},{24,8},{32,48},{40,56},{48,32},{56,40},{64,80... | collective-permute-start | bytes 786440 | tf_op jit(solution)/shard_map/ppermute | solution.py:41
  78.3 3.7 %all-to-all-done.refs_0_ = bf16[8,64,1152]{2,1,0:T(8,128)(2,1)S(1)} async-done(((bf16[8,64,1152]{2,1,0:T(8,128)(2,1)}), bf16[8,64,1152]{2,1,0:T(8,128)(2,1)S(1)}, u32[]{:S(2)}, u32[]{:S(2)}) %all-to-all-start) | async-done | bytes 1179680 | tf_op jit(solution)/shard_map/all_to_all | solution.py:424
  83.0 8.8 %all-to-all-start.1 = ((bf16[32,18,128]{2,1,0:T(8,128)(2,1)}), bf16[32,18,128]{2,1,0:T(8,128)(2,1)S(1)}, u32[]{:S(2)}, u32[]{:S(2)}) async-start(bf16[32,18,128]{2,1,0:T(8,128)(2,1)} %shard_map.92), calls=%async_computation.1 | async-start | bytes 393216 | tf_op jit(solution)/shard_map/all_to_all | solution.py:431
  92.6 2.1 %shard_map.94 = (bf16[128,1024]{1,0:T(8,128)(2,1)}, bf16[128,1024]{1,0:T(8,128)(2,1)}) custom-call(bf16[128,1024]{1,0:T(8,128)(2,1)} %get-tuple-element.79.refs_0_, bf16[128,1024]{1,0:T(8,128)(2,1)} %copy-done.16, bf16[128,1024]{1,0:T(8,128)(2,1)} %copy-done.14, bf16[128,1024]{1,0:T(8,128)(2,1)} %get-tuple-element.82.refs_3_, bf16[128,1024]{1,0:T(8,128)(2,1)} %copy-done.17), custom_call_target="tpu_custom_call" | custom-call | flops 1 | bytes 1 | tf_op jit(solution)/shard_map/pallas_call | solution.py:108
  94.7 3.6 %collective-permute-start.20 = (bf16[128,1024]{1,0:T(8,128)(2,1)}, bf16[128,1024]{1,0:T(8,128)(2,1)S(1)}, u32[]{:S(2)}, u32[]{:S(2)}) collective-permute-start(bf16[128,1024]{1,0:T(8,128)(2,1)} %get-tuple-element.84), channel_id=1, source_target_pairs={{0,64},{8,200},{16,80},{24,216},{32,96},{40,232},{48,112},{56,248}... | collective-permute-start | bytes 786440 | tf_op jit(solution)/shard_map/ppermute | solution.py:33
  98.3 3.6 %shard_map.93 = bf16[128,1152]{1,0:T(8,128)(2,1)} custom-call(f32[128,1024]{1,0:T(8,128)} %get-tuple-element.62.refs_0_, bf16[128,1024]{1,0:T(8,128)(2,1)} %collective-permute-done.19.refs_1_, f32[512,1]{1,0:T(8,128)} %get-tuple-element.58.refs_5_.refs_2_, bf16[1152,1024]{1,0:T(8,128)(2,1)} %refs_3_.3, bf16[512,1024]{1,0:T(8,128)(2,1)S(1)} %get-tuple-element.47.refs_2_.refs_4_), custom_call_target="tpu_custom_call" | custom-call | flops 1 | bytes 1 | tf_op jit(solution)/shard_map/pallas_call | solution.py:108
  104.4 3.4 %all-to-all-start.2 = ((f32[8,36,128]{2,1,0:T(8,128)}), f32[8,36,128]{2,1,0:T(8,128)S(1)}, u32[]{:S(2)}, u32[]{:S(2)}) async-start(f32[8,36,128]{2,1,0:T(8,128)} %shard_map.95), calls=%async_computation.2 | async-start | bytes 327680 | tf_op jit(solution)/shard_map/all_to_all | solution.py:462
  107.8 2.4 %collective-permute-done.20.refs_4_ = bf16[128,1024]{1,0:T(8,128)(2,1)S(1)} collective-permute-done((bf16[128,1024]{1,0:T(8,128)(2,1)}, bf16[128,1024]{1,0:T(8,128)(2,1)S(1)}, u32[]{:S(2)}, u32[]{:S(2)}) %collective-permute-start.20) | collective-permute-done | bytes 262176 | tf_op jit(solution)/shard_map/ppermute | solution.py:33
  110.9 2.6 %shard_map.96 = f32[128,1024]{1,0:T(8,128)} custom-call(bf16[128,1024]{1,0:T(8,128)(2,1)} %bitcast.16, f32[128,1024]{1,0:T(8,128)} %get-tuple-element.76.refs_1_, bf16[128,1024]{1,0:T(8,128)(2,1)} %copy-done.9, bf16[128,1024]{1,0:T(8,128)(2,1)} %copy-done.12, bf16[128,1024]{1,0:T(8,128)(2,1)} %copy-done.20, bf16[128,1024]{1,0:T(8,128)(2,1)} %copy-done.21), custom_call_target="tpu_custom_call" | custom-call | flops 1 | bytes 1 | tf_op jit(solution)/shard_map/pallas_call | solution.py:108
  (86 shorter events, 24.9 us)
Async XLA Ops:
  0.6 9.8 %collective-permute-start = (bf16[128,1152]{1,0:T(8,128)(2,1)}, bf16[128,1152]{1,0:T(8,128)(2,1)S(1)}, u32[]{:S(2)}, u32[]{:S(2)}) collective-permute-start(bf16[128,1152]{1,0:T(8,128)(2,1)} %bitcast.9), channel_id=1, source_target_pairs={{0,16},{8,24},{16,0},{24,8},{32,48},{40,56},{48,32},{56,40},{64,80... | collective-permute-start | bytes 884744 | tf_op jit(solution)/shard_map/ppermute | solution.py:41
  4.5 12.2 %collective-permute-start.6 = (bf16[128,1024]{1,0:T(8,128)(2,1)}, bf16[128,1024]{1,0:T(8,128)(2,1)S(1)}, u32[]{:S(2)}, u32[]{:S(2)}) collective-permute-start(bf16[128,1024]{1,0:T(8,128)(2,1)} %bitcast.13), channel_id=1, source_target_pairs={{0,32},{8,232},{16,48},{24,248},{32,64},{40,8},{48,80},{56,24},{64... | collective-permute-start | bytes 786440 | tf_op jit(solution)/shard_map/ppermute | solution.py:33
  10.0 7.9 %collective-permute-start.5 = (bf16[128,1024]{1,0:T(8,128)(2,1)}, bf16[128,1024]{1,0:T(8,128)(2,1)S(1)}, u32[]{:S(2)}, u32[]{:S(2)}) collective-permute-start(bf16[128,1024]{1,0:T(8,128)(2,1)} %bitcast.14), channel_id=1, source_target_pairs={{0,224},{8,40},{16,240},{24,56},{32,0},{40,72},{48,16},{56,88},{64... | collective-permute-start | bytes 786440 | tf_op jit(solution)/shard_map/ppermute | solution.py:33
  10.5 15.8 %collective-permute-start.1 = (bf16[128,1152]{1,0:T(8,128)(2,1)}, bf16[128,1152]{1,0:T(8,128)(2,1)S(1)}, u32[]{:S(2)}, u32[]{:S(2)}) collective-permute-start(bf16[128,1152]{1,0:T(8,128)(2,1)} %bitcast.10), channel_id=1, source_target_pairs={{0,8},{8,0},{16,24},{24,16},{32,40},{40,32},{48,56},{56,48},{64,72... | collective-permute-start | bytes 884744 | tf_op jit(solution)/shard_map/ppermute | solution.py:37
  12.7 13.7 %collective-permute-start.2 = (bf16[128,1152]{1,0:T(8,128)(2,1)S(1)}, bf16[128,1152]{1,0:T(8,128)(2,1)S(1)}, u32[]{:S(2)}, u32[]{:S(2)}) collective-permute-start(bf16[128,1152]{1,0:T(8,128)(2,1)S(1)} %collective-permute-done.refs_3_.refs_8_), channel_id=1, source_target_pairs={{0,8},{8,0},{16,24},{24,16},{32,40},{40,32},{48,56},{56,48},{64,72... | collective-permute-start | bytes 884744 | tf_op jit(solution)/shard_map/ppermute | solution.py:37
  12.7 4.0 %collective-permute-start.3 = (s32[1,128]{1,0:T(1,128)}, s32[1,128]{1,0:T(1,128)S(1)}, u32[]{:S(2)}, u32[]{:S(2)}) collective-permute-start(s32[1,128]{1,0:T(1,128)} %refs_3_.2), channel_id=1, source_target_pairs={{0,16},{8,24},{16,0},{24,8},{32,48},{40,56},{48,32},{56,40},{64,80... | collective-permute-start | bytes 1544 | tf_op jit(solution)/shard_map/ppermute | solution.py:41
  18.0 14.2 %collective-permute-start.7 = (bf16[128,1024]{1,0:T(8,128)(2,1)S(1)}, bf16[128,1024]{1,0:T(8,128)(2,1)S(1)}, u32[]{:S(2)}, u32[]{:S(2)}) collective-permute-start(bf16[128,1024]{1,0:T(8,128)(2,1)S(1)} %collective-permute-done.5.refs_8_), channel_id=1, source_target_pairs={{0,224},{8,40},{16,240},{24,56},{32,0},{40,72},{48,16},{56,88},{64... | collective-permute-start | bytes 786440 | tf_op jit(solution)/shard_map/ppermute | solution.py:33
  18.5 13.7 %collective-permute-start.8 = (bf16[128,1024]{1,0:T(8,128)(2,1)S(1)}, bf16[128,1024]{1,0:T(8,128)(2,1)S(1)}, u32[]{:S(2)}, u32[]{:S(2)}) collective-permute-start(bf16[128,1024]{1,0:T(8,128)(2,1)S(1)} %collective-permute-done.6.refs_9_), channel_id=1, source_target_pairs={{0,32},{8,232},{16,48},{24,248},{32,64},{40,8},{48,80},{56,24},{64... | collective-permute-start | bytes 786440 | tf_op jit(solution)/shard_map/ppermute | solution.py:33
  24.5 12.1 %collective-permute-start.4 = (s32[2,128]{1,0:T(2,128)S(1)}, s32[2,128]{1,0:T(2,128)S(1)}, u32[]{:S(2)}, u32[]{:S(2)}) collective-permute-start(s32[2,128]{1,0:T(2,128)S(1)} %pad_add_fusion), channel_id=1, source_target_pairs={{0,8},{8,0},{16,24},{24,16},{32,40},{40,32},{48,56},{56,48},{64,72... | collective-permute-start | bytes 3080 | tf_op jit(solution)/shard_map/ppermute | solution.py:37
  32.2 12.8 %collective-permute-start.11 = (bf16[128,1024]{1,0:T(8,128)(2,1)S(1)}, bf16[128,1024]{1,0:T(8,128)(2,1)S(1)}, u32[]{:S(2)}, u32[]{:S(2)}) collective-permute-start(bf16[128,1024]{1,0:T(8,128)(2,1)S(1)} %collective-permute-done.8.refs_11_), channel_id=1, source_target_pairs={{0,32},{8,232},{16,48},{24,248},{32,64},{40,8},{48,80},{56,24},{64... | collective-permute-start | bytes 786440 | tf_op jit(solution)/shard_map/ppermute | solution.py:33
  35.2 14.6 %collective-permute-start.9 = (bf16[128,1024]{1,0:T(8,128)(2,1)S(1)}, bf16[128,1024]{1,0:T(8,128)(2,1)S(1)}, u32[]{:S(2)}, u32[]{:S(2)}) collective-permute-start(bf16[128,1024]{1,0:T(8,128)(2,1)S(1)} %collective-permute-done.8.refs_11_), channel_id=1, source_target_pairs={{0,64},{8,200},{16,80},{24,216},{32,96},{40,232},{48,112},{56,248}... | collective-permute-start | bytes 786440 | tf_op jit(solution)/shard_map/ppermute | solution.py:33
  35.2 9.7 %collective-permute-start.10 = (bf16[128,1024]{1,0:T(8,128)(2,1)S(1)}, bf16[128,1024]{1,0:T(8,128)(2,1)S(1)}, u32[]{:S(2)}, u32[]{:S(2)}) collective-permute-start(bf16[128,1024]{1,0:T(8,128)(2,1)S(1)} %collective-permute-done.7.refs_10_), channel_id=1, source_target_pairs={{0,224},{8,40},{16,240},{24,56},{32,0},{40,72},{48,16},{56,88},{64... | collective-permute-start | bytes 786440 | tf_op jit(solution)/shard_map/ppermute | solution.py:33
  59.2 22.8 %all-to-all-start = ((bf16[8,64,1152]{2,1,0:T(8,128)(2,1)}), bf16[8,64,1152]{2,1,0:T(8,128)(2,1)S(1)}, u32[]{:S(2)}, u32[]{:S(2)}) async-start(bf16[8,64,1152]{2,1,0:T(8,128)(2,1)} %get-tuple-element.68), calls=%async_computation | async-start | bytes 2359296 | tf_op jit(solution)/shard_map/all_to_all | solution.py:424
  64.2 8.2 %collective-permute-start.13 = (f32[256,512]{1,0:T(8,128)}, f32[256,512]{1,0:T(8,128)S(1)}, u32[]{:S(2)}, u32[]{:S(2)}) collective-permute-start(f32[256,512]{1,0:T(8,128)} %get-tuple-element.61), channel_id=1, source_target_pairs={{0,8},{8,0},{16,24},{24,16},{32,40},{40,32},{48,56},{56,48},{64,72... | collective-permute-start | bytes 1572872 | tf_op jit(solution)/shard_map/ppermute | solution.py:37
  66.5 9.0 %collective-permute-start.16 = (bf16[128,1024]{1,0:T(8,128)(2,1)}, bf16[128,1024]{1,0:T(8,128)(2,1)S(1)}, u32[]{:S(2)}, u32[]{:S(2)}) collective-permute-start(bf16[128,1024]{1,0:T(8,128)(2,1)} %shard_map.91), channel_id=1, source_target_pairs={{0,64},{8,200},{16,80},{24,216},{32,96},{40,232},{48,112},{56,248}... | collective-permute-start | bytes 786440 | tf_op jit(solution)/shard_map/ppermute | solution.py:33
  67.9 23.9 %collective-permute-start.14 = (bf16[128,1024]{1,0:T(8,128)(2,1)}, bf16[128,1024]{1,0:T(8,128)(2,1)S(1)}, u32[]{:S(2)}, u32[]{:S(2)}) collective-permute-start(bf16[128,1024]{1,0:T(8,128)(2,1)} %get-tuple-element.69), channel_id=1, source_target_pairs={{0,32},{8,232},{16,48},{24,248},{32,64},{40,8},{48,80},{56,24},{64... | collective-permute-start | bytes 786440 | tf_op jit(solution)/shard_map/ppermute | solution.py:33
  69.7 22.1 %collective-permute-start.15 = (bf16[128,1024]{1,0:T(8,128)(2,1)}, bf16[128,1024]{1,0:T(8,128)(2,1)S(1)}, u32[]{:S(2)}, u32[]{:S(2)}) collective-permute-start(bf16[128,1024]{1,0:T(8,128)(2,1)} %get-tuple-element.70), channel_id=1, source_target_pairs={{0,224},{8,40},{16,240},{24,56},{32,0},{40,72},{48,16},{56,88},{64... | collective-permute-start | bytes 786440 | tf_op jit(solution)/shard_map/ppermute | solution.py:33
  70.1 21.7 %collective-permute-start.17 = (bf16[128,1024]{1,0:T(8,128)(2,1)}, bf16[128,1024]{1,0:T(8,128)(2,1)S(1)}, u32[]{:S(2)}, u32[]{:S(2)}) collective-permute-start(bf16[128,1024]{1,0:T(8,128)(2,1)} %get-tuple-element.72), channel_id=1, source_target_pairs={{0,32},{8,232},{16,48},{24,248},{32,64},{40,8},{48,80},{56,24},{64... | collective-permute-start | bytes 786440 | tf_op jit(solution)/shard_map/ppermute | solution.py:33
  72.4 19.5 %collective-permute-start.18 = (bf16[128,1024]{1,0:T(8,128)(2,1)}, bf16[128,1024]{1,0:T(8,128)(2,1)S(1)}, u32[]{:S(2)}, u32[]{:S(2)}) collective-permute-start(bf16[128,1024]{1,0:T(8,128)(2,1)} %get-tuple-element.73), channel_id=1, source_target_pairs={{0,224},{8,40},{16,240},{24,56},{32,0},{40,72},{48,16},{56,88},{64... | collective-permute-start | bytes 786440 | tf_op jit(solution)/shard_map/ppermute | solution.py:33
  75.5 16.3 %collective-permute-start.19 = (bf16[128,1024]{1,0:T(8,128)(2,1)}, bf16[128,1024]{1,0:T(8,128)(2,1)}, u32[]{:S(2)}, u32[]{:S(2)}) collective-permute-start(bf16[128,1024]{1,0:T(8,128)(2,1)} %get-tuple-element.74), channel_id=1, source_target_pairs={{0,16},{8,24},{16,0},{24,8},{32,48},{40,56},{48,32},{56,40},{64,80... | collective-permute-start | bytes 786440 | tf_op jit(solution)/shard_map/ppermute | solution.py:41
  83.0 20.7 %all-to-all-start.1 = ((bf16[32,18,128]{2,1,0:T(8,128)(2,1)}), bf16[32,18,128]{2,1,0:T(8,128)(2,1)S(1)}, u32[]{:S(2)}, u32[]{:S(2)}) async-start(bf16[32,18,128]{2,1,0:T(8,128)(2,1)} %shard_map.92), calls=%async_computation.1 | async-start | bytes 393216 | tf_op jit(solution)/shard_map/all_to_all | solution.py:431
  94.7 15.4 %collective-permute-start.20 = (bf16[128,1024]{1,0:T(8,128)(2,1)}, bf16[128,1024]{1,0:T(8,128)(2,1)S(1)}, u32[]{:S(2)}, u32[]{:S(2)}) collective-permute-start(bf16[128,1024]{1,0:T(8,128)(2,1)} %get-tuple-element.84), channel_id=1, source_target_pairs={{0,64},{8,200},{16,80},{24,216},{32,96},{40,232},{48,112},{56,248}... | collective-permute-start | bytes 786440 | tf_op jit(solution)/shard_map/ppermute | solution.py:33
  98.3 11.8 %collective-permute-start.21 = (bf16[128,1024]{1,0:T(8,128)(2,1)}, bf16[128,1024]{1,0:T(8,128)(2,1)S(1)}, u32[]{:S(2)}, u32[]{:S(2)}) collective-permute-start(bf16[128,1024]{1,0:T(8,128)(2,1)} %get-tuple-element.85), channel_id=1, source_target_pairs={{0,192},{8,72},{16,208},{24,88},{32,224},{40,104},{48,240},{56,120... | collective-permute-start | bytes 786440 | tf_op jit(solution)/shard_map/ppermute | solution.py:33
  104.4 9.2 %all-to-all-start.2 = ((f32[8,36,128]{2,1,0:T(8,128)}), f32[8,36,128]{2,1,0:T(8,128)S(1)}, u32[]{:S(2)}, u32[]{:S(2)}) async-start(f32[8,36,128]{2,1,0:T(8,128)} %shard_map.95), calls=%async_computation.2 | async-start | bytes 327680 | tf_op jit(solution)/shard_map/all_to_all | solution.py:462
  (23 other events, 170.1 us)

commit v13 on v12

--- a/solution.py
+++ b/solution.py
@@ -15,6 +15,7 @@
 F32 = jnp.float32
 VMEM = pl.BlockSpec(memory_space=pltpu.VMEM)
 HBM = pl.BlockSpec(memory_space=pltpu.HBM)
+ANY = pl.BlockSpec(memory_space=pl.ANY)
 SMEM = pl.BlockSpec(memory_space=pltpu.SMEM)
 
 
@@ -71,7 +72,7 @@
         self.sent.append(copy)
 
 
-def call(kernel, out, aliases, *operands, far=(), packed=(), far_out=(), pushed=(), sends=None, cuts=()):
+def call(kernel, out, aliases, *operands, far=(), packed=(), far_out=(), pushed=(), sends=None, cuts=(), loose=()):
     cuts = dict(cuts)
     far, packed, far_out, total = list(far), list(packed), list(far_out), len(operands)
     sends = len(far_out) if sends is None else sends
@@ -98,13 +99,14 @@
 
     in_hbm, out_hbm = far + packed, far_out + list(pushed)
     in_specs = [SMEM if o.ndim == 1 else HBM if n in in_hbm else VMEM for n, o in enumerate(operands)]
+    in_specs = [ANY if n in loose else spec for n, spec in enumerate(in_specs)]
     scratch = [pltpu.VMEM(operands[n].shape, operands[n].dtype) for n in far]
     scratch += [pltpu.VMEM(out[n].shape, out[n].dtype) for n in far_out]
     if packed:
         height, width = operands[packed[0]].shape
         scratch.append(pltpu.VMEM((len(packed) * height, width), operands[packed[0]].dtype))
     scratch.append(pltpu.SemaphoreType.DMA((len(in_hbm) + sends + 1,)))
-    operands = [pltpu.with_memory_space_constraint(o, pltpu.HBM) if n in in_hbm else o for n, o in enumerate(operands)]
+    operands = [o if n in loose or n not in in_hbm else pltpu.with_memory_space_constraint(o, pltpu.HBM) for n, o in enumerate(operands)]
     return pl.pallas_call(
         body,
         out_shape=[pltpu.HBM(o.shape, o.dtype) if n in out_hbm else o for n, o in enumerate(out)],
@@ -349,8 +351,8 @@
     match_yh = swap_yh(match)
     up, down, _, _ = lax.optimization_barrier((slot[1], slot[-1], sensor_yh, match_yh))
     slot[2], slot[-2] = shift_z(up, -1), shift_z(down, 1)
-    sensor_later, _ = lax.optimization_barrier((sensor, sensor_yh))
-    sensors = [sensor, swap_core(sensor_later), sensor_yh, swap_core(sensor_yh)]
+    sensor_later, sensor_yh_later, _, _, _ = lax.optimization_barrier((sensor, sensor_yh, match_yh, slot[1], slot[-1]))
+    sensors = [sensor, swap_core(sensor_later), sensor_yh, swap_core(sensor_yh_later)]
     match_both = swap_core(jnp.concatenate([match, match_yh], 0))
     match = [match, match_both[:1], match_yh, match_both[1:]]
     image_emb, image_inv = call(
@@ -385,6 +387,7 @@
         numbers, place, image_emb, match_rows, *(slot[k] for k in keys), acc,
         packed=range(4, 6),
         far_out=range(1, 3),
+        loose=range(4, 6),
     )
     shapes = [((4 * rows, width), F32), ((4 * rows, 1), F32), ((4 * rows + 16, width // 2), BF16)]
     shapes.append(((4 * rows, rows), BF16))
@@ -446,6 +449,7 @@
         text_2, from_below, far, text_m2, from_above,
         far=range(5),
         far_out=range(2),
+        loose=(1, 2, 4),
     )
     up, down = shift_z(up, 2), shift_z(down, -2)
 
@@ -470,6 +474,7 @@
         texts, text_0, near_below, near_above, up, down,
         far=range(6),
         far_out=(0,),
+        loose=(4, 5),
     )
     return (sensor_grad[None], text_grad[None], weight_grad)
 

time: 115 us -> 109 us (0.948)
  starting transfers between devices: 56.9 us -> 45.8 us
  waiting for transfers between devices: 15 us -> 22.9 us
  local copies, waits for them, and re-layouts: 4.58 us -> 2.25 us
    ppermute x3, starting transfers between devices: 9.5 us -> 5.68 us  [swap_yh(): return lax.ppermute(block, 'loop', route(lambda z, y, c: (z, 1 - y, c)))]
    ppermute x5, starting transfers between devices: 6.19 us -> 2.74 us  [swap_core(): return lax.ppermute(block, 'loop', route(lambda z, y, c: (z, y, 1 - c)))]
    ppermute x14, waiting for transfers between devices: 6.54 us -> 9.16 us  [shift_z(): lax.ppermute(block, 'loop', route(lambda z, y, c: (z + (1 - 2 * c) * dist...]
    ppermute x3, waiting for transfers between devices: 1.48 us -> 3.94 us  [swap_yh(): return lax.ppermute(block, 'loop', route(lambda z, y, c: (z, 1 - y, c)))]
    unnamed x44 -> x30, local copies, waits for them, and re-layouts: 4.58 us -> 2.25 us
    ppermute x14, starting transfers between devices: 23.9 us -> 21.9 us  [shift_z(): lax.ppermute(block, 'loop', route(lambda z, y, c: (z + (1 - 2 * c) * dist...]
    all_to_all x1, waiting for transfers between devices: 0.01 us -> 1.18 us  [on_device(): shares = lax.all_to_all(shares, 'dp', 0, 0, tiled=True)]
  transfers between devices with their start and end apart: 25 -> 25, of which waited for: 8 -> 9; matrix products, arithmetic and copies ran while one was open for 1% -> 1% of each run, Pallas kernels for 24% -> 25%
where the time goes in v13:
time: 109 us; the launch traced here: 108 us
  starting transfers between devices  45.8 us (42%)
  Pallas kernels  33.8 us (31%)
  waiting for transfers between devices  22.9 us (21%)
  between operations  2.47 us (2%)
  local copies, waits for them, and re-layouts  2.25 us (2%)
    pallas_call x13, Pallas kernels, call(): pl.pallas_call(body, out_shape=[pltpu.HBM(o.shape, o.dtype) if n in out_h...  33.8 us
    ppermute x14, starting transfers between devices, shift_z(): lax.ppermute(block, 'loop', route(lambda z, y, c: (z + (1 - 2 * c) * dist...  21.9 us
    ppermute x14, waiting for transfers between devices, shift_z(): lax.ppermute(block, 'loop', route(lambda z, y, c: (z + (1 - 2 * c) * dist...  9.16 us
    all_to_all x1, starting transfers between devices, on_device(): weight_part = lax.all_to_all(weight_chunks, 'loop', 0, 0, tiled=True)  7.9 us
    ppermute x3, starting transfers between devices, swap_yh(): return lax.ppermute(block, 'loop', route(lambda z, y, c: (z, 1 - y, c)))  5.68 us
    all_to_all x1, waiting for transfers between devices, on_device(): weight_part = lax.all_to_all(weight_part, 'dp', 0, 0, tiled=True)  4.67 us
    all_to_all x1, starting transfers between devices, on_device(): weight_part = lax.all_to_all(weight_part, 'dp', 0, 0, tiled=True)  4.15 us
    ppermute x3, waiting for transfers between devices, swap_yh(): return lax.ppermute(block, 'loop', route(lambda z, y, c: (z, 1 - y, c)))  3.94 us
  transfers between devices with their start and end apart: 25, of which 9 were waited for; matrix products, arithmetic and copies ran while one was open for 1% of the time, Pallas kernels for 25%

profile of v13, /device:TPU:1, one launch (start us, length us, event | category | flops | bytes accessed | tf_op | source)
XLA Modules:
  0.0 108.1 jit_solution(10073970337276015634)
XLA Ops:
  0.6 3.8 %collective-permute-start = (bf16[128,1152]{1,0:T(8,128)(2,1)}, bf16[128,1152]{1,0:T(8,128)(2,1)S(1)}, u32[]{:S(2)}, u32[]{:S(2)}) collective-permute-start(bf16[128,1152]{1,0:T(8,128)(2,1)} %bitcast.9), channel_id=1, source_target_pairs={{0,16},{8,24},{16,0},{24,8},{32,48},{40,56},{48,32},{56,40},{64,80... | collective-permute-start | bytes 884744 | tf_op jit(solution)/shard_map/ppermute | solution.py:42
  4.5 5.6 %collective-permute-start.3 = (bf16[128,1024]{1,0:T(8,128)(2,1)}, bf16[128,1024]{1,0:T(8,128)(2,1)S(1)}, u32[]{:S(2)}, u32[]{:S(2)}) collective-permute-start(bf16[128,1024]{1,0:T(8,128)(2,1)} %bitcast.13), channel_id=1, source_target_pairs={{0,32},{8,232},{16,48},{24,248},{32,64},{40,8},{48,80},{56,24},{64... | collective-permute-start | bytes 786440 | tf_op jit(solution)/shard_map/ppermute | solution.py:34
  10.1 3.9 %collective-permute-done.1.refs_5_ = s32[1,128]{1,0:T(1,128)S(1)} collective-permute-done((s32[1,128]{1,0:T(1,128)}, s32[1,128]{1,0:T(1,128)S(1)}, u32[]{:S(2)}, u32[]{:S(2)}) %collective-permute-start.1) | collective-permute-done | bytes 544 | tf_op jit(solution)/shard_map/ppermute | solution.py:42
  15.0 2.9 %collective-permute-done.2.refs_8_ = bf16[128,1024]{1,0:T(8,128)(2,1)S(1)} collective-permute-done((bf16[128,1024]{1,0:T(8,128)(2,1)}, bf16[128,1024]{1,0:T(8,128)(2,1)S(1)}, u32[]{:S(2)}, u32[]{:S(2)}) %collective-permute-start.2) | collective-permute-done | bytes 262176 | tf_op jit(solution)/shard_map/ppermute | solution.py:34
  18.6 2.7 %collective-permute-start.8 = (bf16[128,1024]{1,0:T(8,128)(2,1)S(1)}, bf16[128,1024]{1,0:T(8,128)(2,1)S(1)}, u32[]{:S(2)}, u32[]{:S(2)}) collective-permute-start(bf16[128,1024]{1,0:T(8,128)(2,1)S(1)} %collective-permute-done.3.refs_9_), channel_id=1, source_target_pairs={{0,32},{8,232},{16,48},{24,248},{32,64},{40,8},{48,80},{56,24},{64... | collective-permute-start | bytes 786440 | tf_op jit(solution)/shard_map/ppermute | solution.py:34
  24.6 4.4 %shard_map.85 = (bf16[512,1024]{1,0:T(8,128)(2,1)S(1)}, f32[512,1]{1,0:T(8,128)}) custom-call(bf16[1152,1024]{1,0:T(8,128)(2,1)} %refs_3_.3, bf16[128,1152]{1,0:T(8,128)(2,1)} %bitcast.11, bf16[128,1152]{1,0:T(8,128)(2,1)} %copy-done.3, bf16[128,1152]{1,0:T(8,128)(2,1)} %copy-done.1, bf16[128,1152]{1,0:T(8,128)(2,1)} %copy-done.5), custom_call_target="tpu_custom_call" | custom-call | flops 1 | bytes 1 | tf_op jit(solution)/shard_map/pallas_call | solution.py:110
  29.1 2.9 %collective-permute-start.11 = (bf16[128,1024]{1,0:T(8,128)(2,1)S(1)}, bf16[128,1024]{1,0:T(8,128)(2,1)S(1)}, u32[]{:S(2)}, u32[]{:S(2)}) collective-permute-start(bf16[128,1024]{1,0:T(8,128)(2,1)S(1)} %collective-permute-done.8.refs_11_), channel_id=1, source_target_pairs={{0,32},{8,232},{16,48},{24,248},{32,64},{40,8},{48,80},{56,24},{64... | collective-permute-start | bytes 786440 | tf_op jit(solution)/shard_map/ppermute | solution.py:34
  33.3 5.4 %shard_map.86 = (f32[512,1]{1,0:T(8,128)S(1)}, f32[512,1024]{1,0:T(8,128)S(1)}, f32[128,1024]{1,0:T(8,128)}, bf16[128,1024]{1,0:T(8,128)(2,1)}, bf16[128,1024]{1...) custom-call(f32[2]{0:T(128)S(1)} %pad_maximum_fusion.refs_0_, s32[1]{0:T(128)} %bitcast.refs_1_.refs_0_, ...), custom_call_target="tpu_custom_call" | custom-call | flops 1 | bytes 1 | tf_op jit(solution)/shard_map/pallas_call | solution.py:110
  38.8 3.3 %collective-permute-done.10.refs_4_ = bf16[128,1024]{1,0:T(8,128)(2,1)S(1)} collective-permute-done((bf16[128,1024]{1,0:T(8,128)(2,1)S(1)}, bf16[128,1024]{1,0:T(8,128)(2,1)S(1)}, u32[]{:S(2)}, u32[]{:S(2)}) %collective-permute-start.10) | collective-permute-done | bytes 262176 | tf_op jit(solution)/shard_map/ppermute | solution.py:34
  42.1 3.0 %shard_map.87 = (f32[512,1024]{1,0:T(8,128)S(1)}, bf16[128,1024]{1,0:T(8,128)(2,1)}, bf16[128,1024]{1,0:T(8,128)(2,1)}) custom-call(f32[2]{0:T(128)S(1)} %pad_maximum_fusion.refs_0_, s32[1]{0:T(128)} %bitcast.refs_1_.refs_0_, bf16[512,1024]{1,0:T(8,128)(2,1)S(1)} %get-tuple-element.49.refs_2_.refs_4_, ...), custom_call_target="tpu_custom_call", output_to_operand_aliasing={{0}: (6, {})} | custom-call | flops 1 | bytes 1 | tf_op jit(solution)/shard_map/pallas_call | solution.py:110
  45.2 3.0 %shard_map.88 = (f32[512,1024]{1,0:T(8,128)S(1)}, f32[512,1]{1,0:T(8,128)S(1)}, bf16[528,512]{1,0:T(8,128)(2,1)S(1)}, bf16[512,128]{1,0:T(8,128)(2,1)S(1)}) custom-call(f32[2]{0:T(128)S(1)} %pad_maximum_fusion.refs_0_, s32[1]{0:T(128)} %bitcast.refs_1_.refs_0_, ...), custom_call_target="tpu_custom_call", output_to_operand_aliasing={{0}: (5, {})} | custom-call | flops 1 | bytes 1 | tf_op jit(solution)/shard_map/pallas_call | solution.py:110
  51.3 3.3 %shard_map.89 = (bf16[8,64,1152]{2,1,0:T(8,128)(2,1)}, f32[256,512]{1,0:T(8,128)}, f32[256,512]{1,0:T(8,128)}, f32[256,512]{1,0:T(8,128)}) custom-call(s32[1]{0:T(128)} %bitcast.refs_1_.refs_0_, bf16[528,512]{1,0:T(8,128)(2,1)S(1)} %collective-permute-done.12.refs_1_, f32[512,1024]{1,0:T(8,128)S(1)} %get-tuple-element.58.refs_2_, ...), custom_call_target="tpu_custom_call" | custom-call | flops 1 | bytes 1 | tf_op jit(solution)/shard_map/pallas_call | solution.py:110
  54.6 4.1 %all-to-all-start = ((bf16[8,64,1152]{2,1,0:T(8,128)(2,1)}), bf16[8,64,1152]{2,1,0:T(8,128)(2,1)S(1)}, u32[]{:S(2)}, u32[]{:S(2)}) async-start(bf16[8,64,1152]{2,1,0:T(8,128)(2,1)} %get-tuple-element.70), calls=%async_computation | async-start | bytes 2359296 | tf_op jit(solution)/shard_map/all_to_all | solution.py:427
  64.8 2.1 %collective-permute-start.17 = (bf16[128,1024]{1,0:T(8,128)(2,1)}, bf16[128,1024]{1,0:T(8,128)(2,1)S(1)}, u32[]{:S(2)}, u32[]{:S(2)}) collective-permute-start(bf16[128,1024]{1,0:T(8,128)(2,1)} %get-tuple-element.74), channel_id=1, source_target_pairs={{0,32},{8,232},{16,48},{24,248},{32,64},{40,8},{48,80},{56,24},{64... | collective-permute-start | bytes 786440 | tf_op jit(solution)/shard_map/ppermute | solution.py:34
  67.7 2.3 %shard_map.90 = (bf16[128,1024]{1,0:T(8,128)(2,1)}, f32[128,1024]{1,0:T(8,128)}) custom-call(s32[1]{0:T(128)} %bitcast.refs_1_.refs_0_, f32[256,512]{1,0:T(8,128)} %get-tuple-element.61.refs_1_, f32[256,512]{1,0:T(8,128)} %get-tuple-element.62.refs_2_, f32[256,512]{1,0:T(8,128)} %copy-done.8), custom_call_target="tpu_custom_call" | custom-call | flops 1 | bytes 1 | tf_op jit(solution)/shard_map/pallas_call | solution.py:110
  71.8 4.7 %all-to-all-done.refs_0_ = bf16[8,64,1152]{2,1,0:T(8,128)(2,1)S(1)} async-done(((bf16[8,64,1152]{2,1,0:T(8,128)(2,1)}), bf16[8,64,1152]{2,1,0:T(8,128)(2,1)S(1)}, u32[]{:S(2)}, u32[]{:S(2)}) %all-to-all-start) | async-done | bytes 1179680 | tf_op jit(solution)/shard_map/all_to_all | solution.py:427
  77.5 7.9 %all-to-all-start.1 = ((bf16[32,18,128]{2,1,0:T(8,128)(2,1)}), bf16[32,18,128]{2,1,0:T(8,128)(2,1)S(1)}, u32[]{:S(2)}, u32[]{:S(2)}) async-start(bf16[32,18,128]{2,1,0:T(8,128)(2,1)} %shard_map.92), calls=%async_computation.1 | async-start | bytes 393216 | tf_op jit(solution)/shard_map/all_to_all | solution.py:434
  85.5 2.1 %shard_map.94 = (bf16[128,1024]{1,0:T(8,128)(2,1)}, bf16[128,1024]{1,0:T(8,128)(2,1)}) custom-call(bf16[128,1024]{1,0:T(8,128)(2,1)} %get-tuple-element.81.refs_0_, bf16[128,1024]{1,0:T(8,128)(2,1)S(1)} %collective-permute-done.14.refs_1_, bf16[128,1024]{1,0:T(8,128)(2,1)S(1)} %collective-permute-done.16.refs_2_, ...), custom_call_target="tpu_custom_call" | custom-call | flops 1 | bytes 1 | tf_op jit(solution)/shard_map/pallas_call | solution.py:110
  87.6 3.6 %collective-permute-start.20 = (bf16[128,1024]{1,0:T(8,128)(2,1)}, bf16[128,1024]{1,0:T(8,128)(2,1)S(1)}, u32[]{:S(2)}, u32[]{:S(2)}) collective-permute-start(bf16[128,1024]{1,0:T(8,128)(2,1)} %get-tuple-element.86), channel_id=1, source_target_pairs={{0,64},{8,200},{16,80},{24,216},{32,96},{40,232},{48,112},{56,248}... | collective-permute-start | bytes 786440 | tf_op jit(solution)/shard_map/ppermute | solution.py:34
  91.2 3.6 %shard_map.93 = bf16[128,1152]{1,0:T(8,128)(2,1)} custom-call(f32[128,1024]{1,0:T(8,128)} %get-tuple-element.64.refs_0_, bf16[128,1024]{1,0:T(8,128)(2,1)} %collective-permute-done.19.refs_1_, f32[512,1]{1,0:T(8,128)} %get-tuple-element.60.refs_5_.refs_2_, bf16[1152,1024]{1,0:T(8,128)(2,1)} %refs_3_.3, bf16[512,1024]{1,0:T(8,128)(2,1)S(1)} %get-tuple-element.49.refs_2_.refs_4_), custom_call_target="tpu_custom_call" | custom-call | flops 1 | bytes 1 | tf_op jit(solution)/shard_map/pallas_call | solution.py:110
  94.9 2.4 %all-to-all-done.1.refs_0_ = bf16[32,18,128]{2,1,0:T(8,128)(2,1)S(1)} async-done(((bf16[32,18,128]{2,1,0:T(8,128)(2,1)}), bf16[32,18,128]{2,1,0:T(8,128)(2,1)S(1)}, u32[]{:S(2)}, u32[]{:S(2)}) %all-to-all-start.1) | async-done | bytes 147488 | tf_op jit(solution)/shard_map/all_to_all | solution.py:434
  98.0 3.5 %all-to-all-start.2 = ((f32[8,36,128]{2,1,0:T(8,128)}), f32[8,36,128]{2,1,0:T(8,128)S(1)}, u32[]{:S(2)}, u32[]{:S(2)}) async-start(f32[8,36,128]{2,1,0:T(8,128)} %shard_map.95), calls=%async_computation.2 | async-start | bytes 327680 | tf_op jit(solution)/shard_map/all_to_all | solution.py:466
  101.5 2.0 %collective-permute-done.20.refs_4_ = bf16[128,1024]{1,0:T(8,128)(2,1)S(1)} collective-permute-done((bf16[128,1024]{1,0:T(8,128)(2,1)}, bf16[128,1024]{1,0:T(8,128)(2,1)S(1)}, u32[]{:S(2)}, u32[]{:S(2)}) %collective-permute-start.20) | collective-permute-done | bytes 262176 | tf_op jit(solution)/shard_map/ppermute | solution.py:34
  103.4 2.5 %shard_map.96 = f32[128,1024]{1,0:T(8,128)} custom-call(bf16[128,1024]{1,0:T(8,128)(2,1)} %bitcast.16, f32[128,1024]{1,0:T(8,128)} %get-tuple-element.78.refs_1_, bf16[128,1024]{1,0:T(8,128)(2,1)} %copy-done.9, bf16[128,1024]{1,0:T(8,128)(2,1)} %copy-done.12, bf16[128,1024]{1,0:T(8,128)(2,1)S(1)} %collective-permute-done.20.refs_4_, ...), custom_call_target="tpu_custom_call" | custom-call | flops 1 | bytes 1 | tf_op jit(solution)/shard_map/pallas_call | solution.py:110
  (72 shorter events, 20.6 us)
Async XLA Ops:
  0.6 17.3 %collective-permute-start = (bf16[128,1152]{1,0:T(8,128)(2,1)}, bf16[128,1152]{1,0:T(8,128)(2,1)S(1)}, u32[]{:S(2)}, u32[]{:S(2)}) collective-permute-start(bf16[128,1152]{1,0:T(8,128)(2,1)} %bitcast.9), channel_id=1, source_target_pairs={{0,16},{8,24},{16,0},{24,8},{32,48},{40,56},{48,32},{56,40},{64,80... | collective-permute-start | bytes 884744 | tf_op jit(solution)/shard_map/ppermute | solution.py:42
  4.5 10.5 %collective-permute-start.3 = (bf16[128,1024]{1,0:T(8,128)(2,1)}, bf16[128,1024]{1,0:T(8,128)(2,1)S(1)}, u32[]{:S(2)}, u32[]{:S(2)}) collective-permute-start(bf16[128,1024]{1,0:T(8,128)(2,1)} %bitcast.13), channel_id=1, source_target_pairs={{0,32},{8,232},{16,48},{24,248},{32,64},{40,8},{48,80},{56,24},{64... | collective-permute-start | bytes 786440 | tf_op jit(solution)/shard_map/ppermute | solution.py:34
  10.0 7.9 %collective-permute-start.2 = (bf16[128,1024]{1,0:T(8,128)(2,1)}, bf16[128,1024]{1,0:T(8,128)(2,1)S(1)}, u32[]{:S(2)}, u32[]{:S(2)}) collective-permute-start(bf16[128,1024]{1,0:T(8,128)(2,1)} %bitcast.14), channel_id=1, source_target_pairs={{0,224},{8,40},{16,240},{24,56},{32,0},{40,72},{48,16},{56,88},{64... | collective-permute-start | bytes 786440 | tf_op jit(solution)/shard_map/ppermute | solution.py:34
  10.1 4.0 %collective-permute-start.1 = (s32[1,128]{1,0:T(1,128)}, s32[1,128]{1,0:T(1,128)S(1)}, u32[]{:S(2)}, u32[]{:S(2)}) collective-permute-start(s32[1,128]{1,0:T(1,128)} %refs_3_.2), channel_id=1, source_target_pairs={{0,16},{8,24},{16,0},{24,8},{32,48},{40,56},{48,32},{56,40},{64,80... | collective-permute-start | bytes 1544 | tf_op jit(solution)/shard_map/ppermute | solution.py:42
  18.0 5.2 %collective-permute-start.4 = (bf16[128,1152]{1,0:T(8,128)(2,1)}, bf16[128,1152]{1,0:T(8,128)(2,1)S(1)}, u32[]{:S(2)}, u32[]{:S(2)}) collective-permute-start(bf16[128,1152]{1,0:T(8,128)(2,1)} %bitcast.10), channel_id=1, source_target_pairs={{0,8},{8,0},{16,24},{24,16},{32,40},{40,32},{48,56},{56,48},{64,72... | collective-permute-start | bytes 884744 | tf_op jit(solution)/shard_map/ppermute | solution.py:38
  18.1 5.2 %collective-permute-start.5 = (bf16[128,1152]{1,0:T(8,128)(2,1)S(1)}, bf16[128,1152]{1,0:T(8,128)(2,1)S(1)}, u32[]{:S(2)}, u32[]{:S(2)}) collective-permute-start(bf16[128,1152]{1,0:T(8,128)(2,1)S(1)} %collective-permute-done.refs_3_.refs_8_), channel_id=1, source_target_pairs={{0,8},{8,0},{16,24},{24,16},{32,40},{40,32},{48,56},{56,48},{64,72... | collective-permute-start | bytes 884744 | tf_op jit(solution)/shard_map/ppermute | solution.py:38
  18.6 10.5 %collective-permute-start.7 = (bf16[128,1024]{1,0:T(8,128)(2,1)S(1)}, bf16[128,1024]{1,0:T(8,128)(2,1)S(1)}, u32[]{:S(2)}, u32[]{:S(2)}) collective-permute-start(bf16[128,1024]{1,0:T(8,128)(2,1)S(1)} %collective-permute-done.2.refs_8_), channel_id=1, source_target_pairs={{0,224},{8,40},{16,240},{24,56},{32,0},{40,72},{48,16},{56,88},{64... | collective-permute-start | bytes 786440 | tf_op jit(solution)/shard_map/ppermute | solution.py:34
  18.6 10.5 %collective-permute-start.8 = (bf16[128,1024]{1,0:T(8,128)(2,1)S(1)}, bf16[128,1024]{1,0:T(8,128)(2,1)S(1)}, u32[]{:S(2)}, u32[]{:S(2)}) collective-permute-start(bf16[128,1024]{1,0:T(8,128)(2,1)S(1)} %collective-permute-done.3.refs_9_), channel_id=1, source_target_pairs={{0,32},{8,232},{16,48},{24,248},{32,64},{40,8},{48,80},{56,24},{64... | collective-permute-start | bytes 786440 | tf_op jit(solution)/shard_map/ppermute | solution.py:34
  23.2 10.1 %collective-permute-start.6 = (s32[2,128]{1,0:T(2,128)S(1)}, s32[2,128]{1,0:T(2,128)S(1)}, u32[]{:S(2)}, u32[]{:S(2)}) collective-permute-start(s32[2,128]{1,0:T(2,128)S(1)} %pad_add_fusion), channel_id=1, source_target_pairs={{0,8},{8,0},{16,24},{24,16},{32,40},{40,32},{48,56},{56,48},{64,72... | collective-permute-start | bytes 3080 | tf_op jit(solution)/shard_map/ppermute | solution.py:38
  29.1 13.0 %collective-permute-start.11 = (bf16[128,1024]{1,0:T(8,128)(2,1)S(1)}, bf16[128,1024]{1,0:T(8,128)(2,1)S(1)}, u32[]{:S(2)}, u32[]{:S(2)}) collective-permute-start(bf16[128,1024]{1,0:T(8,128)(2,1)S(1)} %collective-permute-done.8.refs_11_), channel_id=1, source_target_pairs={{0,32},{8,232},{16,48},{24,248},{32,64},{40,8},{48,80},{56,24},{64... | collective-permute-start | bytes 786440 | tf_op jit(solution)/shard_map/ppermute | solution.py:34
  31.9 13.2 %collective-permute-start.9 = (bf16[128,1024]{1,0:T(8,128)(2,1)S(1)}, bf16[128,1024]{1,0:T(8,128)(2,1)S(1)}, u32[]{:S(2)}, u32[]{:S(2)}) collective-permute-start(bf16[128,1024]{1,0:T(8,128)(2,1)S(1)} %collective-permute-done.8.refs_11_), channel_id=1, source_target_pairs={{0,64},{8,200},{16,80},{24,216},{32,96},{40,232},{48,112},{56,248}... | collective-permute-start | bytes 786440 | tf_op jit(solution)/shard_map/ppermute | solution.py:34
  31.9 10.1 %collective-permute-start.10 = (bf16[128,1024]{1,0:T(8,128)(2,1)S(1)}, bf16[128,1024]{1,0:T(8,128)(2,1)S(1)}, u32[]{:S(2)}, u32[]{:S(2)}) collective-permute-start(bf16[128,1024]{1,0:T(8,128)(2,1)S(1)} %collective-permute-done.7.refs_10_), channel_id=1, source_target_pairs={{0,224},{8,40},{16,240},{24,56},{32,0},{40,72},{48,16},{56,88},{64... | collective-permute-start | bytes 786440 | tf_op jit(solution)/shard_map/ppermute | solution.py:34
  54.6 21.9 %all-to-all-start = ((bf16[8,64,1152]{2,1,0:T(8,128)(2,1)}), bf16[8,64,1152]{2,1,0:T(8,128)(2,1)S(1)}, u32[]{:S(2)}, u32[]{:S(2)}) async-start(bf16[8,64,1152]{2,1,0:T(8,128)(2,1)} %get-tuple-element.70), calls=%async_computation | async-start | bytes 2359296 | tf_op jit(solution)/shard_map/all_to_all | solution.py:427
  58.7 8.2 %collective-permute-start.13 = (f32[256,512]{1,0:T(8,128)}, f32[256,512]{1,0:T(8,128)S(1)}, u32[]{:S(2)}, u32[]{:S(2)}) collective-permute-start(f32[256,512]{1,0:T(8,128)} %get-tuple-element.63), channel_id=1, source_target_pairs={{0,8},{8,0},{16,24},{24,16},{32,40},{40,32},{48,56},{56,48},{64,72... | collective-permute-start | bytes 1572872 | tf_op jit(solution)/shard_map/ppermute | solution.py:38
  61.0 9.1 %collective-permute-start.16 = (bf16[128,1024]{1,0:T(8,128)(2,1)}, bf16[128,1024]{1,0:T(8,128)(2,1)S(1)}, u32[]{:S(2)}, u32[]{:S(2)}) collective-permute-start(bf16[128,1024]{1,0:T(8,128)(2,1)} %shard_map.91), channel_id=1, source_target_pairs={{0,64},{8,200},{16,80},{24,216},{32,96},{40,232},{48,112},{56,248}... | collective-permute-start | bytes 786440 | tf_op jit(solution)/shard_map/ppermute | solution.py:34
  62.5 22.9 %collective-permute-start.14 = (bf16[128,1024]{1,0:T(8,128)(2,1)}, bf16[128,1024]{1,0:T(8,128)(2,1)S(1)}, u32[]{:S(2)}, u32[]{:S(2)}) collective-permute-start(bf16[128,1024]{1,0:T(8,128)(2,1)} %get-tuple-element.71), channel_id=1, source_target_pairs={{0,32},{8,232},{16,48},{24,248},{32,64},{40,8},{48,80},{56,24},{64... | collective-permute-start | bytes 786440 | tf_op jit(solution)/shard_map/ppermute | solution.py:34
  64.2 21.2 %collective-permute-start.15 = (bf16[128,1024]{1,0:T(8,128)(2,1)}, bf16[128,1024]{1,0:T(8,128)(2,1)S(1)}, u32[]{:S(2)}, u32[]{:S(2)}) collective-permute-start(bf16[128,1024]{1,0:T(8,128)(2,1)} %get-tuple-element.72), channel_id=1, source_target_pairs={{0,224},{8,40},{16,240},{24,56},{32,0},{40,72},{48,16},{56,88},{64... | collective-permute-start | bytes 786440 | tf_op jit(solution)/shard_map/ppermute | solution.py:34
  64.8 20.7 %collective-permute-start.17 = (bf16[128,1024]{1,0:T(8,128)(2,1)}, bf16[128,1024]{1,0:T(8,128)(2,1)S(1)}, u32[]{:S(2)}, u32[]{:S(2)}) collective-permute-start(bf16[128,1024]{1,0:T(8,128)(2,1)} %get-tuple-element.74), channel_id=1, source_target_pairs={{0,32},{8,232},{16,48},{24,248},{32,64},{40,8},{48,80},{56,24},{64... | collective-permute-start | bytes 786440 | tf_op jit(solution)/shard_map/ppermute | solution.py:34
  66.9 18.6 %collective-permute-start.18 = (bf16[128,1024]{1,0:T(8,128)(2,1)}, bf16[128,1024]{1,0:T(8,128)(2,1)S(1)}, u32[]{:S(2)}, u32[]{:S(2)}) collective-permute-start(bf16[128,1024]{1,0:T(8,128)(2,1)} %get-tuple-element.75), channel_id=1, source_target_pairs={{0,224},{8,40},{16,240},{24,56},{32,0},{40,72},{48,16},{56,88},{64... | collective-permute-start | bytes 786440 | tf_op jit(solution)/shard_map/ppermute | solution.py:34
  70.1 15.5 %collective-permute-start.19 = (bf16[128,1024]{1,0:T(8,128)(2,1)}, bf16[128,1024]{1,0:T(8,128)(2,1)}, u32[]{:S(2)}, u32[]{:S(2)}) collective-permute-start(bf16[128,1024]{1,0:T(8,128)(2,1)} %get-tuple-element.76), channel_id=1, source_target_pairs={{0,16},{8,24},{16,0},{24,8},{32,48},{40,56},{48,32},{56,40},{64,80... | collective-permute-start | bytes 786440 | tf_op jit(solution)/shard_map/ppermute | solution.py:42
  77.5 19.8 %all-to-all-start.1 = ((bf16[32,18,128]{2,1,0:T(8,128)(2,1)}), bf16[32,18,128]{2,1,0:T(8,128)(2,1)S(1)}, u32[]{:S(2)}, u32[]{:S(2)}) async-start(bf16[32,18,128]{2,1,0:T(8,128)(2,1)} %shard_map.92), calls=%async_computation.1 | async-start | bytes 393216 | tf_op jit(solution)/shard_map/all_to_all | solution.py:434
  87.6 15.8 %collective-permute-start.20 = (bf16[128,1024]{1,0:T(8,128)(2,1)}, bf16[128,1024]{1,0:T(8,128)(2,1)S(1)}, u32[]{:S(2)}, u32[]{:S(2)}) collective-permute-start(bf16[128,1024]{1,0:T(8,128)(2,1)} %get-tuple-element.86), channel_id=1, source_target_pairs={{0,64},{8,200},{16,80},{24,216},{32,96},{40,232},{48,112},{56,248}... | collective-permute-start | bytes 786440 | tf_op jit(solution)/shard_map/ppermute | solution.py:34
  91.2 12.2 %collective-permute-start.21 = (bf16[128,1024]{1,0:T(8,128)(2,1)}, bf16[128,1024]{1,0:T(8,128)(2,1)S(1)}, u32[]{:S(2)}, u32[]{:S(2)}) collective-permute-start(bf16[128,1024]{1,0:T(8,128)(2,1)} %get-tuple-element.87), channel_id=1, source_target_pairs={{0,192},{8,72},{16,208},{24,88},{32,224},{40,104},{48,240},{56,120... | collective-permute-start | bytes 786440 | tf_op jit(solution)/shard_map/ppermute | solution.py:34
  98.0 9.1 %all-to-all-start.2 = ((f32[8,36,128]{2,1,0:T(8,128)}), f32[8,36,128]{2,1,0:T(8,128)S(1)}, u32[]{:S(2)}, u32[]{:S(2)}) async-start(f32[8,36,128]{2,1,0:T(8,128)} %shard_map.95), calls=%async_computation.2 | async-start | bytes 327680 | tf_op jit(solution)/shard_map/all_to_all | solution.py:466
  (16 other events, 128.8 us)

commit v14 on v13

--- a/solution.py
+++ b/solution.py
@@ -364,9 +364,12 @@
         packed=range(1, 5),
         far_out=(1,),
         cuts={0: CUT},
+        loose=range(2, 5),
     )
     up, down, _ = lax.optimization_barrier((slot[2], slot[-2], image_emb))
-    slot[3], slot[-3], slot[4] = shift_z(up, -1), shift_z(down, 1), shift_z(down, 2)
+    slot[3], slot[-3] = shift_z(up, -1), shift_z(down, 1)
+    far, _ = lax.optimization_barrier((down, match_both))
+    slot[4] = shift_z(far, 2)
 
     text_shape = jax.ShapeDtypeStruct((rows, width), BF16)
     acc_shape = jax.ShapeDtypeStruct((4 * rows, width), F32)
@@ -379,16 +382,18 @@
         packed=range(7, 12),
         far_out=range(2, 7),
     )
-    keys = (3, -3)
-    acc, text_3, text_m3 = call(
-        functools.partial(pairs_kernel, keys),
-        [acc_shape] + [text_shape] * 2,
-        {6: 0},
-        numbers, place, image_emb, match_rows, *(slot[k] for k in keys), acc,
-        packed=range(4, 6),
-        far_out=range(1, 3),
-        loose=range(4, 6),
-    )
+    text_far = {}
+    for key in (-3, 3):
+        acc, text_far[key] = call(
+            functools.partial(pairs_kernel, (key,)),
+            [acc_shape, text_shape],
+            {5: 0},
+            numbers, place, image_emb, match_rows, slot[key], acc,
+            packed=(4,),
+            far_out=(1,),
+            loose=(4,),
+        )
+    text_3, text_m3 = text_far[3], text_far[-3]
     shapes = [((4 * rows, width), F32), ((4 * rows, 1), F32), ((4 * rows + 16, width // 2), BF16)]
     shapes.append(((4 * rows, rows), BF16))
     acc, dot, packet, last_grad = call(

time: 109 us -> 107 us (0.982)
  starting transfers between devices: 45.8 us -> 43.2 us
  Pallas kernels: 33.8 us -> 35.8 us
  local copies, waits for them, and re-layouts: 2.25 us -> 0.82 us
    pallas_call x13 -> x14, Pallas kernels: 33.8 us -> 35.8 us  [call(): pl.pallas_call(body, out_shape=[pltpu.HBM(o.shape, o.dtype) if n in out_h...]
    ppermute x3, starting transfers between devices: 5.68 us -> 3.92 us  [swap_yh(): return lax.ppermute(block, 'loop', route(lambda z, y, c: (z, 1 - y, c)))]
    unnamed x30 -> x12, local copies, waits for them, and re-layouts: 2.25 us -> 0.81 us
    ppermute x14, waiting for transfers between devices: 9.16 us -> 10.2 us  [shift_z(): lax.ppermute(block, 'loop', route(lambda z, y, c: (z + (1 - 2 * c) * dist...]
  transfers between devices with their start and end apart: 25 -> 25, of which waited for: 9 -> 10; matrix products, arithmetic and copies ran while one was open for 1% -> 1% of each run, Pallas kernels for 25% -> 27%
where the time goes in v14:
time: 107 us
  starting transfers between devices  43.2 us (40%)
  Pallas kernels  35.8 us (33%)
  waiting for transfers between devices  23.6 us (22%)
  between operations  2.39 us (2%)
    pallas_call x14, Pallas kernels, call(): pl.pallas_call(body, out_shape=[pltpu.HBM(o.shape, o.dtype) if n in out_h...  35.8 us
    ppermute x14, starting transfers between devices, shift_z(): lax.ppermute(block, 'loop', route(lambda z, y, c: (z + (1 - 2 * c) * dist...  21.4 us
    ppermute x14, waiting for transfers between devices, shift_z(): lax.ppermute(block, 'loop', route(lambda z, y, c: (z + (1 - 2 * c) * dist...  10.2 us
    all_to_all x1, starting transfers between devices, on_device(): weight_part = lax.all_to_all(weight_chunks, 'loop', 0, 0, tiled=True)  7.35 us
    all_to_all x1, waiting for transfers between devices, on_device(): weight_part = lax.all_to_all(weight_part, 'dp', 0, 0, tiled=True)  4.45 us
    all_to_all x1, starting transfers between devices, on_device(): weight_part = lax.all_to_all(weight_part, 'dp', 0, 0, tiled=True)  4.14 us
    ppermute x3, waiting for transfers between devices, swap_yh(): return lax.ppermute(block, 'loop', route(lambda z, y, c: (z, 1 - y, c)))  3.94 us
    ppermute x3, starting transfers between devices, swap_yh(): return lax.ppermute(block, 'loop', route(lambda z, y, c: (z, 1 - y, c)))  3.92 us
  transfers between devices with their start and end apart: 25, of which 10 were waited for; matrix products, arithmetic and copies ran while one was open for 1% of the time, Pallas kernels for 27%

profile of v14, /device:TPU:1, one launch (start us, length us, event | category | flops | bytes accessed | tf_op | source)
XLA Modules:
  0.0 106.5 jit_solution(10113511278866531036)
XLA Ops:
  0.6 3.8 %collective-permute-start = (bf16[128,1152]{1,0:T(8,128)(2,1)}, bf16[128,1152]{1,0:T(8,128)(2,1)S(1)}, u32[]{:S(2)}, u32[]{:S(2)}) collective-permute-start(bf16[128,1152]{1,0:T(8,128)(2,1)} %bitcast.9), channel_id=1, source_target_pairs={{0,16},{8,24},{16,0},{24,8},{32,48},{40,56},{48,32},{56,40},{64,80... | collective-permute-start | bytes 884744 | tf_op jit(solution)/shard_map/ppermute | solution.py:42
  4.5 5.6 %collective-permute-start.3 = (bf16[128,1024]{1,0:T(8,128)(2,1)}, bf16[128,1024]{1,0:T(8,128)(2,1)S(1)}, u32[]{:S(2)}, u32[]{:S(2)}) collective-permute-start(bf16[128,1024]{1,0:T(8,128)(2,1)} %bitcast.13), channel_id=1, source_target_pairs={{0,32},{8,232},{16,48},{24,248},{32,64},{40,8},{48,80},{56,24},{64... | collective-permute-start | bytes 786440 | tf_op jit(solution)/shard_map/ppermute | solution.py:34
  10.1 3.9 %collective-permute-done.1.refs_5_ = s32[1,128]{1,0:T(1,128)S(1)} collective-permute-done((s32[1,128]{1,0:T(1,128)}, s32[1,128]{1,0:T(1,128)S(1)}, u32[]{:S(2)}, u32[]{:S(2)}) %collective-permute-start.1) | collective-permute-done | bytes 544 | tf_op jit(solution)/shard_map/ppermute | solution.py:42
  15.0 2.9 %collective-permute-done.2.refs_8_ = bf16[128,1024]{1,0:T(8,128)(2,1)S(1)} collective-permute-done((bf16[128,1024]{1,0:T(8,128)(2,1)}, bf16[128,1024]{1,0:T(8,128)(2,1)S(1)}, u32[]{:S(2)}, u32[]{:S(2)}) %collective-permute-start.2) | collective-permute-done | bytes 262176 | tf_op jit(solution)/shard_map/ppermute | solution.py:34
  18.5 2.7 %collective-permute-start.8 = (bf16[128,1024]{1,0:T(8,128)(2,1)S(1)}, bf16[128,1024]{1,0:T(8,128)(2,1)}, u32[]{:S(2)}, u32[]{:S(2)}) collective-permute-start(bf16[128,1024]{1,0:T(8,128)(2,1)S(1)} %collective-permute-done.3.refs_9_), channel_id=1, source_target_pairs={{0,32},{8,232},{16,48},{24,248},{32,64},{40,8},{48,80},{56,24},{64... | collective-permute-start | bytes 786440 | tf_op jit(solution)/shard_map/ppermute | solution.py:34
  23.1 4.2 %shard_map.85 = (bf16[512,1024]{1,0:T(8,128)(2,1)S(1)}, f32[512,1]{1,0:T(8,128)}) custom-call(bf16[1152,1024]{1,0:T(8,128)(2,1)} %refs_3_.3, bf16[128,1152]{1,0:T(8,128)(2,1)} %bitcast.11, bf16[128,1152]{1,0:T(8,128)(2,1)S(1)} %collective-permute-done.4.refs_2_.refs_7_, bf16[128,1152]{1,0:T(8,128)(2,1)S(1)} %collective-permute-done.refs_3_.refs_8_, ...), custom_call_target="tpu_custom_call" | custom-call | flops 1 | bytes 1 | tf_op jit(solution)/shard_map/pallas_call | solution.py:110
  27.4 3.4 %collective-permute-start.11 = (bf16[128,1024]{1,0:T(8,128)(2,1)}, bf16[128,1024]{1,0:T(8,128)(2,1)S(1)}, u32[]{:S(2)}, u32[]{:S(2)}) collective-permute-start(bf16[128,1024]{1,0:T(8,128)(2,1)} %collective-permute-done.8.refs_11_), channel_id=1, source_target_pairs={{0,32},{8,232},{16,48},{24,248},{32,64},{40,8},{48,80},{56,24},{64... | collective-permute-start | bytes 786440 | tf_op jit(solution)/shard_map/ppermute | solution.py:34
  32.1 5.4 %shard_map.86 = (f32[512,1]{1,0:T(8,128)S(1)}, f32[512,1024]{1,0:T(8,128)S(1)}, f32[128,1024]{1,0:T(8,128)}, bf16[128,1024]{1,0:T(8,128)(2,1)}, bf16[128,1024]{1...) custom-call(f32[2]{0:T(128)S(1)} %pad_maximum_fusion.refs_0_, s32[1]{0:T(128)} %bitcast.refs_1_.refs_0_, ...), custom_call_target="tpu_custom_call" | custom-call | flops 1 | bytes 1 | tf_op jit(solution)/shard_map/pallas_call | solution.py:110
  38.8 2.6 %shard_map.87 = (f32[512,1024]{1,0:T(8,128)S(1)}, bf16[128,1024]{1,0:T(8,128)(2,1)}) custom-call(f32[2]{0:T(128)S(1)} %pad_maximum_fusion.refs_0_, s32[1]{0:T(128)} %bitcast.refs_1_.refs_0_, bf16[512,1024]{1,0:T(8,128)(2,1)S(1)} %get-tuple-element.51.refs_2_.refs_4_, f32[512,1]{1,0:T(8,128)S(1)} %get-tuple-element.54.refs_3_, ...), custom_call_target="tpu_custom_call", output_to_operand_aliasing={{0}: (5, {})} | custom-call | flops 1 | bytes 1 | tf_op jit(solution)/shard_map/pallas_call | solution.py:110
  41.4 2.6 %shard_map.88 = (f32[512,1024]{1,0:T(8,128)S(1)}, bf16[128,1024]{1,0:T(8,128)(2,1)}) custom-call(f32[2]{0:T(128)S(1)} %pad_maximum_fusion.refs_0_, s32[1]{0:T(128)} %bitcast.refs_1_.refs_0_, bf16[512,1024]{1,0:T(8,128)(2,1)S(1)} %get-tuple-element.51.refs_2_.refs_4_, f32[512,1]{1,0:T(8,128)S(1)} %get-tuple-element.54.refs_3_, ...), custom_call_target="tpu_custom_call", output_to_operand_aliasing={{0}: (5, {})} | custom-call | flops 1 | bytes 1 | tf_op jit(solution)/shard_map/pallas_call | solution.py:110
  44.1 3.0 %shard_map.89 = (f32[512,1024]{1,0:T(8,128)S(1)}, f32[512,1]{1,0:T(8,128)S(1)}, bf16[528,512]{1,0:T(8,128)(2,1)S(1)}, bf16[512,128]{1,0:T(8,128)(2,1)S(1)}) custom-call(f32[2]{0:T(128)S(1)} %pad_maximum_fusion.refs_0_, s32[1]{0:T(128)} %bitcast.refs_1_.refs_0_, ...), custom_call_target="tpu_custom_call", output_to_operand_aliasing={{0}: (5, {})} | custom-call | flops 1 | bytes 1 | tf_op jit(solution)/shard_map/pallas_call | solution.py:110
  50.6 3.3 %shard_map.90 = (bf16[8,64,1152]{2,1,0:T(8,128)(2,1)}, f32[256,512]{1,0:T(8,128)}, f32[256,512]{1,0:T(8,128)}, f32[256,512]{1,0:T(8,128)}) custom-call(s32[1]{0:T(128)} %bitcast.refs_1_.refs_0_, bf16[528,512]{1,0:T(8,128)(2,1)S(1)} %collective-permute-done.12.refs_1_, f32[512,1024]{1,0:T(8,128)S(1)} %get-tuple-element.62.refs_2_, ...), custom_call_target="tpu_custom_call" | custom-call | flops 1 | bytes 1 | tf_op jit(solution)/shard_map/pallas_call | solution.py:110
  53.9 4.1 %all-to-all-start = ((bf16[8,64,1152]{2,1,0:T(8,128)(2,1)}), bf16[8,64,1152]{2,1,0:T(8,128)(2,1)S(1)}, u32[]{:S(2)}, u32[]{:S(2)}) async-start(bf16[8,64,1152]{2,1,0:T(8,128)(2,1)} %get-tuple-element.74), calls=%async_computation | async-start | bytes 2359296 | tf_op jit(solution)/shard_map/all_to_all | solution.py:432
  66.0 2.3 %shard_map.91 = (bf16[128,1024]{1,0:T(8,128)(2,1)}, f32[128,1024]{1,0:T(8,128)}) custom-call(s32[1]{0:T(128)} %bitcast.refs_1_.refs_0_, f32[256,512]{1,0:T(8,128)} %get-tuple-element.65.refs_1_, f32[256,512]{1,0:T(8,128)} %get-tuple-element.66.refs_2_, f32[256,512]{1,0:T(8,128)} %copy-done.2), custom_call_target="tpu_custom_call" | custom-call | flops 1 | bytes 1 | tf_op jit(solution)/shard_map/pallas_call | solution.py:110
  68.3 3.0 %collective-permute-done.16.refs_2_ = bf16[128,1024]{1,0:T(8,128)(2,1)S(1)} collective-permute-done((bf16[128,1024]{1,0:T(8,128)(2,1)}, bf16[128,1024]{1,0:T(8,128)(2,1)S(1)}, u32[]{:S(2)}, u32[]{:S(2)}) %collective-permute-start.16) | collective-permute-done | bytes 262176 | tf_op jit(solution)/shard_map/ppermute | solution.py:34
  71.3 4.5 %all-to-all-done.refs_0_ = bf16[8,64,1152]{2,1,0:T(8,128)(2,1)S(1)} async-done(((bf16[8,64,1152]{2,1,0:T(8,128)(2,1)}), bf16[8,64,1152]{2,1,0:T(8,128)(2,1)S(1)}, u32[]{:S(2)}, u32[]{:S(2)}) %all-to-all-start) | async-done | bytes 1179680 | tf_op jit(solution)/shard_map/all_to_all | solution.py:432
  76.8 7.3 %all-to-all-start.1 = ((bf16[32,18,128]{2,1,0:T(8,128)(2,1)}), bf16[32,18,128]{2,1,0:T(8,128)(2,1)S(1)}, u32[]{:S(2)}, u32[]{:S(2)}) async-start(bf16[32,18,128]{2,1,0:T(8,128)(2,1)} %shard_map.93), calls=%async_computation.1 | async-start | bytes 393216 | tf_op jit(solution)/shard_map/all_to_all | solution.py:439
  84.2 2.0 %shard_map.95 = (bf16[128,1024]{1,0:T(8,128)(2,1)}, bf16[128,1024]{1,0:T(8,128)(2,1)}) custom-call(bf16[128,1024]{1,0:T(8,128)(2,1)} %get-tuple-element.85.refs_0_, bf16[128,1024]{1,0:T(8,128)(2,1)S(1)} %collective-permute-done.14.refs_1_, bf16[128,1024]{1,0:T(8,128)(2,1)S(1)} %collective-permute-done.16.refs_2_, ...), custom_call_target="tpu_custom_call" | custom-call | flops 1 | bytes 1 | tf_op jit(solution)/shard_map/pallas_call | solution.py:110
  86.2 3.6 %collective-permute-start.20 = (bf16[128,1024]{1,0:T(8,128)(2,1)}, bf16[128,1024]{1,0:T(8,128)(2,1)S(1)}, u32[]{:S(2)}, u32[]{:S(2)}) collective-permute-start(bf16[128,1024]{1,0:T(8,128)(2,1)} %get-tuple-element.90), channel_id=1, source_target_pairs={{0,64},{8,200},{16,80},{24,216},{32,96},{40,232},{48,112},{56,248}... | collective-permute-start | bytes 786440 | tf_op jit(solution)/shard_map/ppermute | solution.py:34
  89.8 3.6 %shard_map.94 = bf16[128,1152]{1,0:T(8,128)(2,1)} custom-call(f32[128,1024]{1,0:T(8,128)} %get-tuple-element.68.refs_0_, bf16[128,1024]{1,0:T(8,128)(2,1)} %collective-permute-done.19.refs_1_, f32[512,1]{1,0:T(8,128)} %get-tuple-element.64.refs_5_.refs_2_, bf16[1152,1024]{1,0:T(8,128)(2,1)} %refs_3_.3, bf16[512,1024]{1,0:T(8,128)(2,1)S(1)} %get-tuple-element.51.refs_2_.refs_4_), custom_call_target="tpu_custom_call" | custom-call | flops 1 | bytes 1 | tf_op jit(solution)/shard_map/pallas_call | solution.py:110
  93.5 2.5 %all-to-all-done.1.refs_0_ = bf16[32,18,128]{2,1,0:T(8,128)(2,1)S(1)} async-done(((bf16[32,18,128]{2,1,0:T(8,128)(2,1)}), bf16[32,18,128]{2,1,0:T(8,128)(2,1)S(1)}, u32[]{:S(2)}, u32[]{:S(2)}) %all-to-all-start.1) | async-done | bytes 147488 | tf_op jit(solution)/shard_map/all_to_all | solution.py:439
  96.7 3.4 %all-to-all-start.2 = ((f32[8,36,128]{2,1,0:T(8,128)}), f32[8,36,128]{2,1,0:T(8,128)S(1)}, u32[]{:S(2)}, u32[]{:S(2)}) async-start(f32[8,36,128]{2,1,0:T(8,128)} %shard_map.96), calls=%async_computation.2 | async-start | bytes 327680 | tf_op jit(solution)/shard_map/all_to_all | solution.py:471
  100.1 2.1 %collective-permute-done.20.refs_4_ = bf16[128,1024]{1,0:T(8,128)(2,1)S(1)} collective-permute-done((bf16[128,1024]{1,0:T(8,128)(2,1)}, bf16[128,1024]{1,0:T(8,128)(2,1)S(1)}, u32[]{:S(2)}, u32[]{:S(2)}) %collective-permute-start.20) | collective-permute-done | bytes 262176 | tf_op jit(solution)/shard_map/ppermute | solution.py:34
  102.2 2.5 %shard_map.97 = f32[128,1024]{1,0:T(8,128)} custom-call(bf16[128,1024]{1,0:T(8,128)(2,1)} %bitcast.16, f32[128,1024]{1,0:T(8,128)} %get-tuple-element.82.refs_1_, bf16[128,1024]{1,0:T(8,128)(2,1)} %copy-done.3, bf16[128,1024]{1,0:T(8,128)(2,1)} %collective-permute-done.18.refs_3_, bf16[128,1024]{1,0:T(8,128)(2,1)S(1)} %collective-permute-done.20.refs_4_, ...), custom_call_target="tpu_custom_call" | custom-call | flops 1 | bytes 1 | tf_op jit(solution)/shard_map/pallas_call | solution.py:110
  (55 shorter events, 19.7 us)
Async XLA Ops:
  0.6 17.3 %collective-permute-start = (bf16[128,1152]{1,0:T(8,128)(2,1)}, bf16[128,1152]{1,0:T(8,128)(2,1)S(1)}, u32[]{:S(2)}, u32[]{:S(2)}) collective-permute-start(bf16[128,1152]{1,0:T(8,128)(2,1)} %bitcast.9), channel_id=1, source_target_pairs={{0,16},{8,24},{16,0},{24,8},{32,48},{40,56},{48,32},{56,40},{64,80... | collective-permute-start | bytes 884744 | tf_op jit(solution)/shard_map/ppermute | solution.py:42
  4.5 10.5 %collective-permute-start.3 = (bf16[128,1024]{1,0:T(8,128)(2,1)}, bf16[128,1024]{1,0:T(8,128)(2,1)S(1)}, u32[]{:S(2)}, u32[]{:S(2)}) collective-permute-start(bf16[128,1024]{1,0:T(8,128)(2,1)} %bitcast.13), channel_id=1, source_target_pairs={{0,32},{8,232},{16,48},{24,248},{32,64},{40,8},{48,80},{56,24},{64... | collective-permute-start | bytes 786440 | tf_op jit(solution)/shard_map/ppermute | solution.py:34
  10.0 7.9 %collective-permute-start.2 = (bf16[128,1024]{1,0:T(8,128)(2,1)}, bf16[128,1024]{1,0:T(8,128)(2,1)S(1)}, u32[]{:S(2)}, u32[]{:S(2)}) collective-permute-start(bf16[128,1024]{1,0:T(8,128)(2,1)} %bitcast.14), channel_id=1, source_target_pairs={{0,224},{8,40},{16,240},{24,56},{32,0},{40,72},{48,16},{56,88},{64... | collective-permute-start | bytes 786440 | tf_op jit(solution)/shard_map/ppermute | solution.py:34
  10.1 4.0 %collective-permute-start.1 = (s32[1,128]{1,0:T(1,128)}, s32[1,128]{1,0:T(1,128)S(1)}, u32[]{:S(2)}, u32[]{:S(2)}) collective-permute-start(s32[1,128]{1,0:T(1,128)} %refs_3_.2), channel_id=1, source_target_pairs={{0,16},{8,24},{16,0},{24,8},{32,48},{40,56},{48,32},{56,40},{64,80... | collective-permute-start | bytes 1544 | tf_op jit(solution)/shard_map/ppermute | solution.py:42
  18.0 5.2 %collective-permute-start.4 = (bf16[128,1152]{1,0:T(8,128)(2,1)}, bf16[128,1152]{1,0:T(8,128)(2,1)S(1)}, u32[]{:S(2)}, u32[]{:S(2)}) collective-permute-start(bf16[128,1152]{1,0:T(8,128)(2,1)} %bitcast.10), channel_id=1, source_target_pairs={{0,8},{8,0},{16,24},{24,16},{32,40},{40,32},{48,56},{56,48},{64,72... | collective-permute-start | bytes 884744 | tf_op jit(solution)/shard_map/ppermute | solution.py:38
  18.0 5.2 %collective-permute-start.5 = (bf16[128,1152]{1,0:T(8,128)(2,1)S(1)}, bf16[128,1152]{1,0:T(8,128)(2,1)S(1)}, u32[]{:S(2)}, u32[]{:S(2)}) collective-permute-start(bf16[128,1152]{1,0:T(8,128)(2,1)S(1)} %collective-permute-done.refs_3_.refs_8_), channel_id=1, source_target_pairs={{0,8},{8,0},{16,24},{24,16},{32,40},{40,32},{48,56},{56,48},{64,72... | collective-permute-start | bytes 884744 | tf_op jit(solution)/shard_map/ppermute | solution.py:38
  18.5 8.9 %collective-permute-start.7 = (bf16[128,1024]{1,0:T(8,128)(2,1)S(1)}, bf16[128,1024]{1,0:T(8,128)(2,1)}, u32[]{:S(2)}, u32[]{:S(2)}) collective-permute-start(bf16[128,1024]{1,0:T(8,128)(2,1)S(1)} %collective-permute-done.2.refs_8_), channel_id=1, source_target_pairs={{0,224},{8,40},{16,240},{24,56},{32,0},{40,72},{48,16},{56,88},{64... | collective-permute-start | bytes 786440 | tf_op jit(solution)/shard_map/ppermute | solution.py:34
  18.5 8.9 %collective-permute-start.8 = (bf16[128,1024]{1,0:T(8,128)(2,1)S(1)}, bf16[128,1024]{1,0:T(8,128)(2,1)}, u32[]{:S(2)}, u32[]{:S(2)}) collective-permute-start(bf16[128,1024]{1,0:T(8,128)(2,1)S(1)} %collective-permute-done.3.refs_9_), channel_id=1, source_target_pairs={{0,32},{8,232},{16,48},{24,248},{32,64},{40,8},{48,80},{56,24},{64... | collective-permute-start | bytes 786440 | tf_op jit(solution)/shard_map/ppermute | solution.py:34
  21.8 9.0 %collective-permute-start.6 = (s32[2,128]{1,0:T(2,128)S(1)}, s32[2,128]{1,0:T(2,128)S(1)}, u32[]{:S(2)}, u32[]{:S(2)}) collective-permute-start(s32[2,128]{1,0:T(2,128)S(1)} %pad_add_fusion), channel_id=1, source_target_pairs={{0,8},{8,0},{16,24},{24,16},{32,40},{40,32},{48,56},{56,48},{64,72... | collective-permute-start | bytes 3080 | tf_op jit(solution)/shard_map/ppermute | solution.py:38
  27.4 11.4 %collective-permute-start.11 = (bf16[128,1024]{1,0:T(8,128)(2,1)}, bf16[128,1024]{1,0:T(8,128)(2,1)S(1)}, u32[]{:S(2)}, u32[]{:S(2)}) collective-permute-start(bf16[128,1024]{1,0:T(8,128)(2,1)} %collective-permute-done.8.refs_11_), channel_id=1, source_target_pairs={{0,32},{8,232},{16,48},{24,248},{32,64},{40,8},{48,80},{56,24},{64... | collective-permute-start | bytes 786440 | tf_op jit(solution)/shard_map/ppermute | solution.py:34
  30.8 13.3 %collective-permute-start.9 = (bf16[128,1024]{1,0:T(8,128)(2,1)}, bf16[128,1024]{1,0:T(8,128)(2,1)S(1)}, u32[]{:S(2)}, u32[]{:S(2)}) collective-permute-start(bf16[128,1024]{1,0:T(8,128)(2,1)} %collective-permute-done.8.refs_11_), channel_id=1, source_target_pairs={{0,64},{8,200},{16,80},{24,216},{32,96},{40,232},{48,112},{56,248}... | collective-permute-start | bytes 786440 | tf_op jit(solution)/shard_map/ppermute | solution.py:34
  30.8 10.6 %collective-permute-start.10 = (bf16[128,1024]{1,0:T(8,128)(2,1)}, bf16[128,1024]{1,0:T(8,128)(2,1)S(1)}, u32[]{:S(2)}, u32[]{:S(2)}) collective-permute-start(bf16[128,1024]{1,0:T(8,128)(2,1)} %collective-permute-done.7.refs_10_), channel_id=1, source_target_pairs={{0,224},{8,40},{16,240},{24,56},{32,0},{40,72},{48,16},{56,88},{64... | collective-permute-start | bytes 786440 | tf_op jit(solution)/shard_map/ppermute | solution.py:34
  53.9 21.9 %all-to-all-start = ((bf16[8,64,1152]{2,1,0:T(8,128)(2,1)}), bf16[8,64,1152]{2,1,0:T(8,128)(2,1)S(1)}, u32[]{:S(2)}, u32[]{:S(2)}) async-start(bf16[8,64,1152]{2,1,0:T(8,128)(2,1)} %get-tuple-element.74), calls=%async_computation | async-start | bytes 2359296 | tf_op jit(solution)/shard_map/all_to_all | solution.py:432
  58.0 7.2 %collective-permute-start.13 = (f32[256,512]{1,0:T(8,128)}, f32[256,512]{1,0:T(8,128)S(1)}, u32[]{:S(2)}, u32[]{:S(2)}) collective-permute-start(f32[256,512]{1,0:T(8,128)} %get-tuple-element.67), channel_id=1, source_target_pairs={{0,8},{8,0},{16,24},{24,16},{32,40},{40,32},{48,56},{56,48},{64,72... | collective-permute-start | bytes 1572872 | tf_op jit(solution)/shard_map/ppermute | solution.py:38
  60.3 11.0 %collective-permute-start.16 = (bf16[128,1024]{1,0:T(8,128)(2,1)}, bf16[128,1024]{1,0:T(8,128)(2,1)S(1)}, u32[]{:S(2)}, u32[]{:S(2)}) collective-permute-start(bf16[128,1024]{1,0:T(8,128)(2,1)} %shard_map.92), channel_id=1, source_target_pairs={{0,64},{8,200},{16,80},{24,216},{32,96},{40,232},{48,112},{56,248}... | collective-permute-start | bytes 786440 | tf_op jit(solution)/shard_map/ppermute | solution.py:34
  61.3 22.8 %collective-permute-start.14 = (bf16[128,1024]{1,0:T(8,128)(2,1)}, bf16[128,1024]{1,0:T(8,128)(2,1)S(1)}, u32[]{:S(2)}, u32[]{:S(2)}) collective-permute-start(bf16[128,1024]{1,0:T(8,128)(2,1)} %get-tuple-element.75), channel_id=1, source_target_pairs={{0,32},{8,232},{16,48},{24,248},{32,64},{40,8},{48,80},{56,24},{64... | collective-permute-start | bytes 786440 | tf_op jit(solution)/shard_map/ppermute | solution.py:34
  62.5 21.7 %collective-permute-start.15 = (bf16[128,1024]{1,0:T(8,128)(2,1)}, bf16[128,1024]{1,0:T(8,128)(2,1)S(1)}, u32[]{:S(2)}, u32[]{:S(2)}) collective-permute-start(bf16[128,1024]{1,0:T(8,128)(2,1)} %get-tuple-element.76), channel_id=1, source_target_pairs={{0,224},{8,40},{16,240},{24,56},{32,0},{40,72},{48,16},{56,88},{64... | collective-permute-start | bytes 786440 | tf_op jit(solution)/shard_map/ppermute | solution.py:34
  63.3 20.9 %collective-permute-start.17 = (bf16[128,1024]{1,0:T(8,128)(2,1)}, bf16[128,1024]{1,0:T(8,128)(2,1)S(1)}, u32[]{:S(2)}, u32[]{:S(2)}) collective-permute-start(bf16[128,1024]{1,0:T(8,128)(2,1)} %get-tuple-element.78), channel_id=1, source_target_pairs={{0,32},{8,232},{16,48},{24,248},{32,64},{40,8},{48,80},{56,24},{64... | collective-permute-start | bytes 786440 | tf_op jit(solution)/shard_map/ppermute | solution.py:34
  65.2 19.0 %collective-permute-start.18 = (bf16[128,1024]{1,0:T(8,128)(2,1)}, bf16[128,1024]{1,0:T(8,128)(2,1)}, u32[]{:S(2)}, u32[]{:S(2)}) collective-permute-start(bf16[128,1024]{1,0:T(8,128)(2,1)} %get-tuple-element.79), channel_id=1, source_target_pairs={{0,224},{8,40},{16,240},{24,56},{32,0},{40,72},{48,16},{56,88},{64... | collective-permute-start | bytes 786440 | tf_op jit(solution)/shard_map/ppermute | solution.py:34
  71.3 12.9 %collective-permute-start.19 = (bf16[128,1024]{1,0:T(8,128)(2,1)}, bf16[128,1024]{1,0:T(8,128)(2,1)}, u32[]{:S(2)}, u32[]{:S(2)}) collective-permute-start(bf16[128,1024]{1,0:T(8,128)(2,1)} %get-tuple-element.80), channel_id=1, source_target_pairs={{0,16},{8,24},{16,0},{24,8},{32,48},{40,56},{48,32},{56,40},{64,80... | collective-permute-start | bytes 786440 | tf_op jit(solution)/shard_map/ppermute | solution.py:42
  76.8 19.2 %all-to-all-start.1 = ((bf16[32,18,128]{2,1,0:T(8,128)(2,1)}), bf16[32,18,128]{2,1,0:T(8,128)(2,1)S(1)}, u32[]{:S(2)}, u32[]{:S(2)}) async-start(bf16[32,18,128]{2,1,0:T(8,128)(2,1)} %shard_map.93), calls=%async_computation.1 | async-start | bytes 393216 | tf_op jit(solution)/shard_map/all_to_all | solution.py:439
  86.2 16.0 %collective-permute-start.20 = (bf16[128,1024]{1,0:T(8,128)(2,1)}, bf16[128,1024]{1,0:T(8,128)(2,1)S(1)}, u32[]{:S(2)}, u32[]{:S(2)}) collective-permute-start(bf16[128,1024]{1,0:T(8,128)(2,1)} %get-tuple-element.90), channel_id=1, source_target_pairs={{0,64},{8,200},{16,80},{24,216},{32,96},{40,232},{48,112},{56,248}... | collective-permute-start | bytes 786440 | tf_op jit(solution)/shard_map/ppermute | solution.py:34
  89.8 12.4 %collective-permute-start.21 = (bf16[128,1024]{1,0:T(8,128)(2,1)}, bf16[128,1024]{1,0:T(8,128)(2,1)S(1)}, u32[]{:S(2)}, u32[]{:S(2)}) collective-permute-start(bf16[128,1024]{1,0:T(8,128)(2,1)} %get-tuple-element.91), channel_id=1, source_target_pairs={{0,192},{8,72},{16,208},{24,88},{32,224},{40,104},{48,240},{56,120... | collective-permute-start | bytes 786440 | tf_op jit(solution)/shard_map/ppermute | solution.py:34
  96.7 8.8 %all-to-all-start.2 = ((f32[8,36,128]{2,1,0:T(8,128)}), f32[8,36,128]{2,1,0:T(8,128)S(1)}, u32[]{:S(2)}, u32[]{:S(2)}) async-start(f32[8,36,128]{2,1,0:T(8,128)} %shard_map.96), calls=%async_computation.2 | async-start | bytes 327680 | tf_op jit(solution)/shard_map/all_to_all | solution.py:471
  (7 other events, 82.7 us)

commit v15 on v14

--- a/solution.py
+++ b/solution.py
@@ -120,14 +120,14 @@
 
 
 def scale_of(numbers):
-    return jnp.exp(jnp.full((1, 128), numbers[0], F32))[:, 0:1]
+    return numbers[0:1, 0:1]
 
 
 def block_grads(numbers, columns, image_emb, match, text):
     wide = text.astype(F32)
     inv = lax.rsqrt(jnp.sum(wide * wide, -1, keepdims=True) + 1e-06)
     emb = (wide * inv).astype(BF16)
-    logits = scale_of(numbers) * inner_rows(image_emb, emb) + numbers[1]
+    logits = scale_of(numbers) * inner_rows(image_emb, emb) + numbers[1:2, 0:1]
     positive = (match == columns).astype(F32)
     return emb, (jax.nn.sigmoid(logits) - positive).astype(BF16)
 
@@ -160,7 +160,7 @@
     pairs_body(keys, moves, 4, numbers, place, image_emb, match, refs[:count], refs[count], refs[count + 1], refs[count + 2 :])
 
 
-def project_kernel(moves, proj_weight, own, core, yh, both, emb, inv_out):
+def project_kernel(moves, proj_weight, own, core, yh, both, log_scale, bias, emb, inv_out, numbers):
     for n in range(4):
         moves.need(1 + n)
     sensor = moves.pack[...]
@@ -172,6 +172,9 @@
     inv_out[...] = inv
     moves.send(1)
     emb[...] = (projected * inv).astype(BF16)
+    row = lax.broadcasted_iota(jnp.int32, numbers.shape, 0)
+    scale = jnp.exp(jnp.full(numbers.shape, log_scale[0], F32))
+    numbers[...] = jnp.where(row == 0, scale, bias[0])
 
 
 def first_pairs_kernel(keys, moves, numbers, place, image_emb, own, core, yh, both, *refs):
@@ -341,7 +344,6 @@
     feat, width = proj_weight.shape
     loop_index = lax.axis_index("loop")
     place = loop_index.reshape(1)
-    numbers = jnp.stack([log_scale, logit_bias])
 
     slot = {0: texts}
     slot[1], slot[-1] = shift_z(texts, -1), shift_z(texts, 1)
@@ -355,11 +357,11 @@
     sensors = [sensor, swap_core(sensor_later), sensor_yh, swap_core(sensor_yh_later)]
     match_both = swap_core(jnp.concatenate([match, match_yh], 0))
     match = [match, match_both[:1], match_yh, match_both[1:]]
-    image_emb, image_inv = call(
+    image_emb, image_inv, numbers = call(
         project_kernel,
-        [jax.ShapeDtypeStruct((4 * rows, width), BF16), jax.ShapeDtypeStruct((4 * rows, 1), F32)],
-        {},
-        proj_weight, *sensors,
+        [jax.ShapeDtypeStruct(*s) for s in (((4 * rows, width), BF16), ((4 * rows, 1), F32), ((8, 128), F32))],
+        {},
+        proj_weight, *sensors, log_scale.reshape(1), logit_bias.reshape(1),
         far=(0,),
         packed=range(1, 5),
         far_out=(1,),

time: 107 us -> 106 us (level)
  Pallas kernels: 35.8 us -> 33 us
  waiting for transfers between devices: 23.6 us -> 25.1 us
    pallas_call x14, Pallas kernels: 35.8 us -> 33 us  [call(): pl.pallas_call(body, out_shape=[pltpu.HBM(o.shape, o.dtype) if n in out_h...]
  transfers between devices with their start and end apart: 25 -> 25, of which waited for: 10 -> 10; matrix products, arithmetic and copies ran while one was open for 1% -> 1% of each run, Pallas kernels for 27% -> 25%
where the time goes in v15:
time: 106 us
  starting transfers between devices  43.7 us (41%)
  Pallas kernels  33 us (31%)
  waiting for transfers between devices  25.1 us (24%)
  between operations  2.41 us (2%)
    pallas_call x14, Pallas kernels, call(): pl.pallas_call(body, out_shape=[pltpu.HBM(o.shape, o.dtype) if n in out_h...  33 us
    ppermute x14, starting transfers between devices, shift_z(): lax.ppermute(block, 'loop', route(lambda z, y, c: (z + (1 - 2 * c) * dist...  22.2 us
    ppermute x14, waiting for transfers between devices, shift_z(): lax.ppermute(block, 'loop', route(lambda z, y, c: (z + (1 - 2 * c) * dist...  10.5 us
    all_to_all x1, starting transfers between devices, on_device(): weight_part = lax.all_to_all(weight_chunks, 'loop', 0, 0, tiled=True)  7.28 us
    all_to_all x1, waiting for transfers between devices, on_device(): weight_part = lax.all_to_all(weight_part, 'dp', 0, 0, tiled=True)  5.27 us
    all_to_all x1, starting transfers between devices, on_device(): weight_part = lax.all_to_all(weight_part, 'dp', 0, 0, tiled=True)  4.28 us
    ppermute x3, waiting for transfers between devices, swap_yh(): return lax.ppermute(block, 'loop', route(lambda z, y, c: (z, 1 - y, c)))  3.94 us
    ppermute x3, starting transfers between devices, swap_yh(): return lax.ppermute(block, 'loop', route(lambda z, y, c: (z, 1 - y, c)))  3.92 us
  transfers between devices with their start and end apart: 25, of which 10 were waited for; matrix products, arithmetic and copies ran while one was open for 1% of the time, Pallas kernels for 25%

profile of v15, /device:TPU:1, one launch (start us, length us, event | category | flops | bytes accessed | tf_op | source)
XLA Modules:
  0.0 105.7 jit_solution(4857018180827100613)
XLA Ops:
  0.6 3.8 %collective-permute-start = (bf16[128,1152]{1,0:T(8,128)(2,1)}, bf16[128,1152]{1,0:T(8,128)(2,1)S(1)}, u32[]{:S(2)}, u32[]{:S(2)}) collective-permute-start(bf16[128,1152]{1,0:T(8,128)(2,1)} %bitcast.9), channel_id=1, source_target_pairs={{0,16},{8,24},{16,0},{24,8},{32,48},{40,56},{48,32},{56,40},{64,80... | collective-permute-start | bytes 884744 | tf_op jit(solution)/shard_map/ppermute | solution.py:42
  4.5 5.6 %collective-permute-start.3 = (bf16[128,1024]{1,0:T(8,128)(2,1)}, bf16[128,1024]{1,0:T(8,128)(2,1)S(1)}, u32[]{:S(2)}, u32[]{:S(2)}) collective-permute-start(bf16[128,1024]{1,0:T(8,128)(2,1)} %bitcast.13), channel_id=1, source_target_pairs={{0,32},{8,232},{16,48},{24,248},{32,64},{40,8},{48,80},{56,24},{64... | collective-permute-start | bytes 786440 | tf_op jit(solution)/shard_map/ppermute | solution.py:34
  10.1 3.9 %collective-permute-done.1.refs_5_ = s32[1,128]{1,0:T(1,128)S(1)} collective-permute-done((s32[1,128]{1,0:T(1,128)}, s32[1,128]{1,0:T(1,128)S(1)}, u32[]{:S(2)}, u32[]{:S(2)}) %collective-permute-start.1) | collective-permute-done | bytes 544 | tf_op jit(solution)/shard_map/ppermute | solution.py:42
  15.0 2.9 %collective-permute-done.2.refs_8_ = bf16[128,1024]{1,0:T(8,128)(2,1)S(1)} collective-permute-done((bf16[128,1024]{1,0:T(8,128)(2,1)}, bf16[128,1024]{1,0:T(8,128)(2,1)S(1)}, u32[]{:S(2)}, u32[]{:S(2)}) %collective-permute-start.2) | collective-permute-done | bytes 262176 | tf_op jit(solution)/shard_map/ppermute | solution.py:34
  18.5 2.7 %collective-permute-start.8 = (bf16[128,1024]{1,0:T(8,128)(2,1)S(1)}, bf16[128,1024]{1,0:T(8,128)(2,1)S(1)}, u32[]{:S(2)}, u32[]{:S(2)}) collective-permute-start(bf16[128,1024]{1,0:T(8,128)(2,1)S(1)} %collective-permute-done.3.refs_9_), channel_id=1, source_target_pairs={{0,32},{8,232},{16,48},{24,248},{32,64},{40,8},{48,80},{56,24},{64... | collective-permute-start | bytes 786440 | tf_op jit(solution)/shard_map/ppermute | solution.py:34
  23.1 4.2 %shard_map.85 = (bf16[512,1024]{1,0:T(8,128)(2,1)S(1)}, f32[512,1]{1,0:T(8,128)}, f32[8,128]{1,0:T(8,128)S(1)}) custom-call(bf16[1152,1024]{1,0:T(8,128)(2,1)} %refs_3_.3, bf16[128,1152]{1,0:T(8,128)(2,1)} %bitcast.11, bf16[128,1152]{1,0:T(8,128)(2,1)S(1)} %collective-permute-done.4.refs_2_.refs_7_, ...), custom_call_target="tpu_custom_call" | custom-call | flops 1 | bytes 1 | tf_op jit(solution)/shard_map/pallas_call | solution.py:110
  27.4 3.4 %collective-permute-start.11 = (bf16[128,1024]{1,0:T(8,128)(2,1)S(1)}, bf16[128,1024]{1,0:T(8,128)(2,1)S(1)}, u32[]{:S(2)}, u32[]{:S(2)}) collective-permute-start(bf16[128,1024]{1,0:T(8,128)(2,1)S(1)} %collective-permute-done.8.refs_11_), channel_id=1, source_target_pairs={{0,32},{8,232},{16,48},{24,248},{32,64},{40,8},{48,80},{56,24},{64... | collective-permute-start | bytes 786440 | tf_op jit(solution)/shard_map/ppermute | solution.py:34
  32.0 4.9 %shard_map.86 = (f32[512,1]{1,0:T(8,128)S(1)}, f32[512,1024]{1,0:T(8,128)S(1)}, f32[128,1024]{1,0:T(8,128)}, bf16[128,1024]{1,0:T(8,128)(2,1)}, bf16[128,1024]{1...) custom-call(f32[8,128]{1,0:T(8,128)S(1)} %get-tuple-element.52.refs_0_, s32[1]{0:T(128)} %bitcast.refs_1_.refs_0_, ...), custom_call_target="tpu_custom_call" | custom-call | flops 1 | bytes 1 | tf_op jit(solution)/shard_map/pallas_call | solution.py:110
  36.9 2.0 %shard_map.87 = (f32[512,1024]{1,0:T(8,128)S(1)}, bf16[128,1024]{1,0:T(8,128)(2,1)}) custom-call(f32[8,128]{1,0:T(8,128)S(1)} %get-tuple-element.52.refs_0_, s32[1]{0:T(128)} %bitcast.refs_1_.refs_0_, bf16[512,1024]{1,0:T(8,128)(2,1)S(1)} %get-tuple-element.53.refs_2_.refs_4_, ...), custom_call_target="tpu_custom_call", output_to_operand_aliasing={{0}: (5, {})} | custom-call | flops 1 | bytes 1 | tf_op jit(solution)/shard_map/pallas_call | solution.py:110
  39.0 2.8 %collective-permute-done.10.refs_4_ = bf16[128,1024]{1,0:T(8,128)(2,1)S(1)} collective-permute-done((bf16[128,1024]{1,0:T(8,128)(2,1)}, bf16[128,1024]{1,0:T(8,128)(2,1)S(1)}, u32[]{:S(2)}, u32[]{:S(2)}) %collective-permute-start.10) | collective-permute-done | bytes 262176 | tf_op jit(solution)/shard_map/ppermute | solution.py:34
  41.8 2.0 %shard_map.88 = (f32[512,1024]{1,0:T(8,128)S(1)}, bf16[128,1024]{1,0:T(8,128)(2,1)}) custom-call(f32[8,128]{1,0:T(8,128)S(1)} %get-tuple-element.52.refs_0_, s32[1]{0:T(128)} %bitcast.refs_1_.refs_0_, bf16[512,1024]{1,0:T(8,128)(2,1)S(1)} %get-tuple-element.53.refs_2_.refs_4_, ...), custom_call_target="tpu_custom_call", output_to_operand_aliasing={{0}: (5, {})} | custom-call | flops 1 | bytes 1 | tf_op jit(solution)/shard_map/pallas_call | solution.py:110
  43.9 2.5 %shard_map.89 = (f32[512,1024]{1,0:T(8,128)S(1)}, f32[512,1]{1,0:T(8,128)S(1)}, bf16[528,512]{1,0:T(8,128)(2,1)S(1)}, bf16[512,128]{1,0:T(8,128)(2,1)S(1)}) custom-call(f32[8,128]{1,0:T(8,128)S(1)} %get-tuple-element.52.refs_0_, s32[1]{0:T(128)} %bitcast.refs_1_.refs_0_, ...), custom_call_target="tpu_custom_call", output_to_operand_aliasing={{0}: (5, {})} | custom-call | flops 1 | bytes 1 | tf_op jit(solution)/shard_map/pallas_call | solution.py:110
  49.2 3.3 %shard_map.90 = (bf16[8,64,1152]{2,1,0:T(8,128)(2,1)}, f32[256,512]{1,0:T(8,128)}, f32[256,512]{1,0:T(8,128)}, f32[256,512]{1,0:T(8,128)}) custom-call(s32[1]{0:T(128)} %bitcast.refs_1_.refs_0_, bf16[528,512]{1,0:T(8,128)(2,1)S(1)} %collective-permute-done.12.refs_1_, f32[512,1024]{1,0:T(8,128)S(1)} %get-tuple-element.64.refs_2_, ...), custom_call_target="tpu_custom_call" | custom-call | flops 1 | bytes 1 | tf_op jit(solution)/shard_map/pallas_call | solution.py:110
  52.5 4.3 %all-to-all-start = ((bf16[8,64,1152]{2,1,0:T(8,128)(2,1)}), bf16[8,64,1152]{2,1,0:T(8,128)(2,1)S(1)}, u32[]{:S(2)}, u32[]{:S(2)}) async-start(bf16[8,64,1152]{2,1,0:T(8,128)(2,1)} %get-tuple-element.76), calls=%async_computation | async-start | bytes 2359296 | tf_op jit(solution)/shard_map/all_to_all | solution.py:434
  61.8 2.4 %collective-permute-start.17 = (bf16[128,1024]{1,0:T(8,128)(2,1)}, bf16[128,1024]{1,0:T(8,128)(2,1)S(1)}, u32[]{:S(2)}, u32[]{:S(2)}) collective-permute-start(bf16[128,1024]{1,0:T(8,128)(2,1)} %get-tuple-element.80), channel_id=1, source_target_pairs={{0,32},{8,232},{16,48},{24,248},{32,64},{40,8},{48,80},{56,24},{64... | collective-permute-start | bytes 786440 | tf_op jit(solution)/shard_map/ppermute | solution.py:34
  64.9 2.4 %shard_map.91 = (bf16[128,1024]{1,0:T(8,128)(2,1)}, f32[128,1024]{1,0:T(8,128)}) custom-call(s32[1]{0:T(128)} %bitcast.refs_1_.refs_0_, f32[256,512]{1,0:T(8,128)} %get-tuple-element.67.refs_1_, f32[256,512]{1,0:T(8,128)} %get-tuple-element.68.refs_2_, f32[256,512]{1,0:T(8,128)} %copy-done.2), custom_call_target="tpu_custom_call" | custom-call | flops 1 | bytes 1 | tf_op jit(solution)/shard_map/pallas_call | solution.py:110
  69.2 5.3 %all-to-all-done.refs_0_ = bf16[8,64,1152]{2,1,0:T(8,128)(2,1)S(1)} async-done(((bf16[8,64,1152]{2,1,0:T(8,128)(2,1)}), bf16[8,64,1152]{2,1,0:T(8,128)(2,1)S(1)}, u32[]{:S(2)}, u32[]{:S(2)}) %all-to-all-start) | async-done | bytes 1179680 | tf_op jit(solution)/shard_map/all_to_all | solution.py:434
  75.6 7.3 %all-to-all-start.1 = ((bf16[32,18,128]{2,1,0:T(8,128)(2,1)}), bf16[32,18,128]{2,1,0:T(8,128)(2,1)S(1)}, u32[]{:S(2)}, u32[]{:S(2)}) async-start(bf16[32,18,128]{2,1,0:T(8,128)(2,1)} %shard_map.93), calls=%async_computation.1 | async-start | bytes 393216 | tf_op jit(solution)/shard_map/all_to_all | solution.py:441
  82.9 2.0 %shard_map.95 = (bf16[128,1024]{1,0:T(8,128)(2,1)}, bf16[128,1024]{1,0:T(8,128)(2,1)}) custom-call(bf16[128,1024]{1,0:T(8,128)(2,1)} %get-tuple-element.87.refs_0_, bf16[128,1024]{1,0:T(8,128)(2,1)S(1)} %collective-permute-done.14.refs_1_, bf16[128,1024]{1,0:T(8,128)(2,1)S(1)} %collective-permute-done.16.refs_2_, ...), custom_call_target="tpu_custom_call" | custom-call | flops 1 | bytes 1 | tf_op jit(solution)/shard_map/pallas_call | solution.py:110
  84.9 3.6 %collective-permute-start.20 = (bf16[128,1024]{1,0:T(8,128)(2,1)}, bf16[128,1024]{1,0:T(8,128)(2,1)S(1)}, u32[]{:S(2)}, u32[]{:S(2)}) collective-permute-start(bf16[128,1024]{1,0:T(8,128)(2,1)} %get-tuple-element.92), channel_id=1, source_target_pairs={{0,64},{8,200},{16,80},{24,216},{32,96},{40,232},{48,112},{56,248}... | collective-permute-start | bytes 786440 | tf_op jit(solution)/shard_map/ppermute | solution.py:34
  88.5 3.6 %shard_map.94 = bf16[128,1152]{1,0:T(8,128)(2,1)} custom-call(f32[128,1024]{1,0:T(8,128)} %get-tuple-element.70.refs_0_, bf16[128,1024]{1,0:T(8,128)(2,1)} %collective-permute-done.19.refs_1_, f32[512,1]{1,0:T(8,128)} %get-tuple-element.66.refs_5_.refs_2_, bf16[1152,1024]{1,0:T(8,128)(2,1)} %refs_3_.3, bf16[512,1024]{1,0:T(8,128)(2,1)S(1)} %get-tuple-element.53.refs_2_.refs_4_), custom_call_target="tpu_custom_call" | custom-call | flops 1 | bytes 1 | tf_op jit(solution)/shard_map/pallas_call | solution.py:110
  92.2 2.5 %all-to-all-done.1.refs_0_ = bf16[32,18,128]{2,1,0:T(8,128)(2,1)S(1)} async-done(((bf16[32,18,128]{2,1,0:T(8,128)(2,1)}), bf16[32,18,128]{2,1,0:T(8,128)(2,1)S(1)}, u32[]{:S(2)}, u32[]{:S(2)}) %all-to-all-start.1) | async-done | bytes 147488 | tf_op jit(solution)/shard_map/all_to_all | solution.py:441
  95.4 3.7 %all-to-all-start.2 = ((f32[8,36,128]{2,1,0:T(8,128)}), f32[8,36,128]{2,1,0:T(8,128)S(1)}, u32[]{:S(2)}, u32[]{:S(2)}) async-start(f32[8,36,128]{2,1,0:T(8,128)} %shard_map.96), calls=%async_computation.2 | async-start | bytes 327680 | tf_op jit(solution)/shard_map/all_to_all | solution.py:473
  100.9 2.5 %shard_map.97 = f32[128,1024]{1,0:T(8,128)} custom-call(bf16[128,1024]{1,0:T(8,128)(2,1)} %bitcast.16, f32[128,1024]{1,0:T(8,128)} %get-tuple-element.84.refs_1_, bf16[128,1024]{1,0:T(8,128)(2,1)} %copy-done.3, bf16[128,1024]{1,0:T(8,128)(2,1)} %collective-permute-done.18.refs_3_, bf16[128,1024]{1,0:T(8,128)(2,1)S(1)} %collective-permute-done.20.refs_4_, ...), custom_call_target="tpu_custom_call" | custom-call | flops 1 | bytes 1 | tf_op jit(solution)/shard_map/pallas_call | solution.py:110
  (58 shorter events, 19.7 us)
Async XLA Ops:
  0.6 17.3 %collective-permute-start = (bf16[128,1152]{1,0:T(8,128)(2,1)}, bf16[128,1152]{1,0:T(8,128)(2,1)S(1)}, u32[]{:S(2)}, u32[]{:S(2)}) collective-permute-start(bf16[128,1152]{1,0:T(8,128)(2,1)} %bitcast.9), channel_id=1, source_target_pairs={{0,16},{8,24},{16,0},{24,8},{32,48},{40,56},{48,32},{56,40},{64,80... | collective-permute-start | bytes 884744 | tf_op jit(solution)/shard_map/ppermute | solution.py:42
  4.5 10.5 %collective-permute-start.3 = (bf16[128,1024]{1,0:T(8,128)(2,1)}, bf16[128,1024]{1,0:T(8,128)(2,1)S(1)}, u32[]{:S(2)}, u32[]{:S(2)}) collective-permute-start(bf16[128,1024]{1,0:T(8,128)(2,1)} %bitcast.13), channel_id=1, source_target_pairs={{0,32},{8,232},{16,48},{24,248},{32,64},{40,8},{48,80},{56,24},{64... | collective-permute-start | bytes 786440 | tf_op jit(solution)/shard_map/ppermute | solution.py:34
  10.0 7.9 %collective-permute-start.2 = (bf16[128,1024]{1,0:T(8,128)(2,1)}, bf16[128,1024]{1,0:T(8,128)(2,1)S(1)}, u32[]{:S(2)}, u32[]{:S(2)}) collective-permute-start(bf16[128,1024]{1,0:T(8,128)(2,1)} %bitcast.14), channel_id=1, source_target_pairs={{0,224},{8,40},{16,240},{24,56},{32,0},{40,72},{48,16},{56,88},{64... | collective-permute-start | bytes 786440 | tf_op jit(solution)/shard_map/ppermute | solution.py:34
  10.1 4.0 %collective-permute-start.1 = (s32[1,128]{1,0:T(1,128)}, s32[1,128]{1,0:T(1,128)S(1)}, u32[]{:S(2)}, u32[]{:S(2)}) collective-permute-start(s32[1,128]{1,0:T(1,128)} %refs_3_.2), channel_id=1, source_target_pairs={{0,16},{8,24},{16,0},{24,8},{32,48},{40,56},{48,32},{56,40},{64,80... | collective-permute-start | bytes 1544 | tf_op jit(solution)/shard_map/ppermute | solution.py:42
  18.0 5.2 %collective-permute-start.4 = (bf16[128,1152]{1,0:T(8,128)(2,1)}, bf16[128,1152]{1,0:T(8,128)(2,1)S(1)}, u32[]{:S(2)}, u32[]{:S(2)}) collective-permute-start(bf16[128,1152]{1,0:T(8,128)(2,1)} %bitcast.10), channel_id=1, source_target_pairs={{0,8},{8,0},{16,24},{24,16},{32,40},{40,32},{48,56},{56,48},{64,72... | collective-permute-start | bytes 884744 | tf_op jit(solution)/shard_map/ppermute | solution.py:38
  18.0 5.2 %collective-permute-start.5 = (bf16[128,1152]{1,0:T(8,128)(2,1)S(1)}, bf16[128,1152]{1,0:T(8,128)(2,1)S(1)}, u32[]{:S(2)}, u32[]{:S(2)}) collective-permute-start(bf16[128,1152]{1,0:T(8,128)(2,1)S(1)} %collective-permute-done.refs_3_.refs_8_), channel_id=1, source_target_pairs={{0,8},{8,0},{16,24},{24,16},{32,40},{40,32},{48,56},{56,48},{64,72... | collective-permute-start | bytes 884744 | tf_op jit(solution)/shard_map/ppermute | solution.py:38
  18.5 8.9 %collective-permute-start.7 = (bf16[128,1024]{1,0:T(8,128)(2,1)S(1)}, bf16[128,1024]{1,0:T(8,128)(2,1)}, u32[]{:S(2)}, u32[]{:S(2)}) collective-permute-start(bf16[128,1024]{1,0:T(8,128)(2,1)S(1)} %collective-permute-done.2.refs_8_), channel_id=1, source_target_pairs={{0,224},{8,40},{16,240},{24,56},{32,0},{40,72},{48,16},{56,88},{64... | collective-permute-start | bytes 786440 | tf_op jit(solution)/shard_map/ppermute | solution.py:34
  18.5 8.9 %collective-permute-start.8 = (bf16[128,1024]{1,0:T(8,128)(2,1)S(1)}, bf16[128,1024]{1,0:T(8,128)(2,1)S(1)}, u32[]{:S(2)}, u32[]{:S(2)}) collective-permute-start(bf16[128,1024]{1,0:T(8,128)(2,1)S(1)} %collective-permute-done.3.refs_9_), channel_id=1, source_target_pairs={{0,32},{8,232},{16,48},{24,248},{32,64},{40,8},{48,80},{56,24},{64... | collective-permute-start | bytes 786440 | tf_op jit(solution)/shard_map/ppermute | solution.py:34
  21.8 9.0 %collective-permute-start.6 = (s32[2,128]{1,0:T(2,128)S(1)}, s32[2,128]{1,0:T(2,128)S(1)}, u32[]{:S(2)}, u32[]{:S(2)}) collective-permute-start(s32[2,128]{1,0:T(2,128)S(1)} %pad_add_fusion), channel_id=1, source_target_pairs={{0,8},{8,0},{16,24},{24,16},{32,40},{40,32},{48,56},{56,48},{64,72... | collective-permute-start | bytes 3080 | tf_op jit(solution)/shard_map/ppermute | solution.py:38
  27.4 9.5 %collective-permute-start.11 = (bf16[128,1024]{1,0:T(8,128)(2,1)S(1)}, bf16[128,1024]{1,0:T(8,128)(2,1)S(1)}, u32[]{:S(2)}, u32[]{:S(2)}) collective-permute-start(bf16[128,1024]{1,0:T(8,128)(2,1)S(1)} %collective-permute-done.8.refs_11_), channel_id=1, source_target_pairs={{0,32},{8,232},{16,48},{24,248},{32,64},{40,8},{48,80},{56,24},{64... | collective-permute-start | bytes 786440 | tf_op jit(solution)/shard_map/ppermute | solution.py:34
  30.8 11.0 %collective-permute-start.10 = (bf16[128,1024]{1,0:T(8,128)(2,1)}, bf16[128,1024]{1,0:T(8,128)(2,1)S(1)}, u32[]{:S(2)}, u32[]{:S(2)}) collective-permute-start(bf16[128,1024]{1,0:T(8,128)(2,1)} %collective-permute-done.7.refs_10_), channel_id=1, source_target_pairs={{0,224},{8,40},{16,240},{24,56},{32,0},{40,72},{48,16},{56,88},{64... | collective-permute-start | bytes 786440 | tf_op jit(solution)/shard_map/ppermute | solution.py:34
  30.8 13.1 %collective-permute-start.9 = (bf16[128,1024]{1,0:T(8,128)(2,1)S(1)}, bf16[128,1024]{1,0:T(8,128)(2,1)S(1)}, u32[]{:S(2)}, u32[]{:S(2)}) collective-permute-start(bf16[128,1024]{1,0:T(8,128)(2,1)S(1)} %collective-permute-done.8.refs_11_), channel_id=1, source_target_pairs={{0,64},{8,200},{16,80},{24,216},{32,96},{40,232},{48,112},{56,248}... | collective-permute-start | bytes 786440 | tf_op jit(solution)/shard_map/ppermute | solution.py:34
  52.5 22.0 %all-to-all-start = ((bf16[8,64,1152]{2,1,0:T(8,128)(2,1)}), bf16[8,64,1152]{2,1,0:T(8,128)(2,1)S(1)}, u32[]{:S(2)}, u32[]{:S(2)}) async-start(bf16[8,64,1152]{2,1,0:T(8,128)(2,1)} %get-tuple-element.76), calls=%async_computation | async-start | bytes 2359296 | tf_op jit(solution)/shard_map/all_to_all | solution.py:434
  56.8 7.4 %collective-permute-start.13 = (f32[256,512]{1,0:T(8,128)}, f32[256,512]{1,0:T(8,128)S(1)}, u32[]{:S(2)}, u32[]{:S(2)}) collective-permute-start(f32[256,512]{1,0:T(8,128)} %get-tuple-element.69), channel_id=1, source_target_pairs={{0,8},{8,0},{16,24},{24,16},{32,40},{40,32},{48,56},{56,48},{64,72... | collective-permute-start | bytes 1572872 | tf_op jit(solution)/shard_map/ppermute | solution.py:38
  58.5 10.8 %collective-permute-start.16 = (bf16[128,1024]{1,0:T(8,128)(2,1)}, bf16[128,1024]{1,0:T(8,128)(2,1)S(1)}, u32[]{:S(2)}, u32[]{:S(2)}) collective-permute-start(bf16[128,1024]{1,0:T(8,128)(2,1)} %shard_map.92), channel_id=1, source_target_pairs={{0,64},{8,200},{16,80},{24,216},{32,96},{40,232},{48,112},{56,248}... | collective-permute-start | bytes 786440 | tf_op jit(solution)/shard_map/ppermute | solution.py:34
  60.2 22.6 %collective-permute-start.14 = (bf16[128,1024]{1,0:T(8,128)(2,1)}, bf16[128,1024]{1,0:T(8,128)(2,1)S(1)}, u32[]{:S(2)}, u32[]{:S(2)}) collective-permute-start(bf16[128,1024]{1,0:T(8,128)(2,1)} %get-tuple-element.77), channel_id=1, source_target_pairs={{0,32},{8,232},{16,48},{24,248},{32,64},{40,8},{48,80},{56,24},{64... | collective-permute-start | bytes 786440 | tf_op jit(solution)/shard_map/ppermute | solution.py:34
  61.4 21.4 %collective-permute-start.15 = (bf16[128,1024]{1,0:T(8,128)(2,1)}, bf16[128,1024]{1,0:T(8,128)(2,1)S(1)}, u32[]{:S(2)}, u32[]{:S(2)}) collective-permute-start(bf16[128,1024]{1,0:T(8,128)(2,1)} %get-tuple-element.78), channel_id=1, source_target_pairs={{0,224},{8,40},{16,240},{24,56},{32,0},{40,72},{48,16},{56,88},{64... | collective-permute-start | bytes 786440 | tf_op jit(solution)/shard_map/ppermute | solution.py:34
  61.8 21.1 %collective-permute-start.17 = (bf16[128,1024]{1,0:T(8,128)(2,1)}, bf16[128,1024]{1,0:T(8,128)(2,1)S(1)}, u32[]{:S(2)}, u32[]{:S(2)}) collective-permute-start(bf16[128,1024]{1,0:T(8,128)(2,1)} %get-tuple-element.80), channel_id=1, source_target_pairs={{0,32},{8,232},{16,48},{24,248},{32,64},{40,8},{48,80},{56,24},{64... | collective-permute-start | bytes 786440 | tf_op jit(solution)/shard_map/ppermute | solution.py:34
  64.1 18.8 %collective-permute-start.18 = (bf16[128,1024]{1,0:T(8,128)(2,1)S(1)}, bf16[128,1024]{1,0:T(8,128)(2,1)}, u32[]{:S(2)}, u32[]{:S(2)}) collective-permute-start(bf16[128,1024]{1,0:T(8,128)(2,1)S(1)} %copy-done.7), channel_id=1, source_target_pairs={{0,224},{8,40},{16,240},{24,56},{32,0},{40,72},{48,16},{56,88},{64... | collective-permute-start | bytes 786440 | tf_op jit(solution)/shard_map/ppermute | solution.py:34
  69.2 13.7 %collective-permute-start.19 = (bf16[128,1024]{1,0:T(8,128)(2,1)}, bf16[128,1024]{1,0:T(8,128)(2,1)}, u32[]{:S(2)}, u32[]{:S(2)}) collective-permute-start(bf16[128,1024]{1,0:T(8,128)(2,1)} %get-tuple-element.82), channel_id=1, source_target_pairs={{0,16},{8,24},{16,0},{24,8},{32,48},{40,56},{48,32},{56,40},{64,80... | collective-permute-start | bytes 786440 | tf_op jit(solution)/shard_map/ppermute | solution.py:42
  75.6 19.1 %all-to-all-start.1 = ((bf16[32,18,128]{2,1,0:T(8,128)(2,1)}), bf16[32,18,128]{2,1,0:T(8,128)(2,1)S(1)}, u32[]{:S(2)}, u32[]{:S(2)}) async-start(bf16[32,18,128]{2,1,0:T(8,128)(2,1)} %shard_map.93), calls=%async_computation.1 | async-start | bytes 393216 | tf_op jit(solution)/shard_map/all_to_all | solution.py:441
  84.9 16.0 %collective-permute-start.20 = (bf16[128,1024]{1,0:T(8,128)(2,1)}, bf16[128,1024]{1,0:T(8,128)(2,1)S(1)}, u32[]{:S(2)}, u32[]{:S(2)}) collective-permute-start(bf16[128,1024]{1,0:T(8,128)(2,1)} %get-tuple-element.92), channel_id=1, source_target_pairs={{0,64},{8,200},{16,80},{24,216},{32,96},{40,232},{48,112},{56,248}... | collective-permute-start | bytes 786440 | tf_op jit(solution)/shard_map/ppermute | solution.py:34
  88.5 12.4 %collective-permute-start.21 = (bf16[128,1024]{1,0:T(8,128)(2,1)}, bf16[128,1024]{1,0:T(8,128)(2,1)S(1)}, u32[]{:S(2)}, u32[]{:S(2)}) collective-permute-start(bf16[128,1024]{1,0:T(8,128)(2,1)} %get-tuple-element.93), channel_id=1, source_target_pairs={{0,192},{8,72},{16,208},{24,88},{32,224},{40,104},{48,240},{56,120... | collective-permute-start | bytes 786440 | tf_op jit(solution)/shard_map/ppermute | solution.py:34
  95.4 9.3 %all-to-all-start.2 = ((f32[8,36,128]{2,1,0:T(8,128)}), f32[8,36,128]{2,1,0:T(8,128)S(1)}, u32[]{:S(2)}, u32[]{:S(2)}) async-start(f32[8,36,128]{2,1,0:T(8,128)} %shard_map.96), calls=%async_computation.2 | async-start | bytes 327680 | tf_op jit(solution)/shard_map/all_to_all | solution.py:473
  (9 other events, 96.8 us)

commit v16 on v15

--- a/solution.py
+++ b/solution.py
@@ -355,8 +355,6 @@
     slot[2], slot[-2] = shift_z(up, -1), shift_z(down, 1)
     sensor_later, sensor_yh_later, _, _, _ = lax.optimization_barrier((sensor, sensor_yh, match_yh, slot[1], slot[-1]))
     sensors = [sensor, swap_core(sensor_later), sensor_yh, swap_core(sensor_yh_later)]
-    match_both = swap_core(jnp.concatenate([match, match_yh], 0))
-    match = [match, match_both[:1], match_yh, match_both[1:]]
     image_emb, image_inv, numbers = call(
         project_kernel,
         [jax.ShapeDtypeStruct(*s) for s in (((4 * rows, width), BF16), ((4 * rows, 1), F32), ((8, 128), F32))],
@@ -370,6 +368,9 @@
     )
     up, down, _ = lax.optimization_barrier((slot[2], slot[-2], image_emb))
     slot[3], slot[-3] = shift_z(up, -1), shift_z(down, 1)
+    match_pair, _ = lax.optimization_barrier((jnp.concatenate([match, match_yh], 0), image_emb))
+    match_both = swap_core(match_pair)
+    match = [match, match_both[:1], match_yh, match_both[1:]]
     far, _ = lax.optimization_barrier((down, match_both))
     slot[4] = shift_z(far, 2)
 

time: 106 us -> 106 us (level)
  no operation moved by 1% of the time
where the time goes in v16:
time: 106 us
  starting transfers between devices  43.5 us (41%)
  Pallas kernels  33.1 us (31%)
  waiting for transfers between devices  25.2 us (24%)
  between operations  2.37 us (2%)
    pallas_call x14, Pallas kernels, call(): pl.pallas_call(body, out_shape=[pltpu.HBM(o.shape, o.dtype) if n in out_h...  33.1 us
    ppermute x14, starting transfers between devices, shift_z(): lax.ppermute(block, 'loop', route(lambda z, y, c: (z + (1 - 2 * c) * dist...  22.3 us
    ppermute x14, waiting for transfers between devices, shift_z(): lax.ppermute(block, 'loop', route(lambda z, y, c: (z + (1 - 2 * c) * dist...  10.9 us
    all_to_all x1, starting transfers between devices, on_device(): weight_part = lax.all_to_all(weight_chunks, 'loop', 0, 0, tiled=True)  7.5 us
    all_to_all x1, waiting for transfers between devices, on_device(): weight_part = lax.all_to_all(weight_part, 'dp', 0, 0, tiled=True)  5.08 us
    all_to_all x1, starting transfers between devices, on_device(): weight_part = lax.all_to_all(weight_part, 'dp', 0, 0, tiled=True)  4.15 us
    ppermute x3, starting transfers between devices, swap_yh(): return lax.ppermute(block, 'loop', route(lambda z, y, c: (z, 1 - y, c)))  4 us
    ppermute x3, waiting for transfers between devices, swap_yh(): return lax.ppermute(block, 'loop', route(lambda z, y, c: (z, 1 - y, c)))  3.94 us
  transfers between devices with their start and end apart: 25, of which 10 were waited for; matrix products, arithmetic and copies ran while one was open for 1% of the time, Pallas kernels for 25%

profile of v16, /device:TPU:1, one launch (start us, length us, event | category | flops | bytes accessed | tf_op | source)
XLA Modules:
  0.0 105.6 jit_solution(3139996331489996116)
XLA Ops:
  0.6 3.8 %collective-permute-start = (bf16[128,1152]{1,0:T(8,128)(2,1)}, bf16[128,1152]{1,0:T(8,128)(2,1)S(1)}, u32[]{:S(2)}, u32[]{:S(2)}) collective-permute-start(bf16[128,1152]{1,0:T(8,128)(2,1)} %bitcast.9), channel_id=1, source_target_pairs={{0,16},{8,24},{16,0},{24,8},{32,48},{40,56},{48,32},{56,40},{64,80... | collective-permute-start | bytes 884744 | tf_op jit(solution)/shard_map/ppermute | solution.py:42
  4.5 5.6 %collective-permute-start.3 = (bf16[128,1024]{1,0:T(8,128)(2,1)}, bf16[128,1024]{1,0:T(8,128)(2,1)S(1)}, u32[]{:S(2)}, u32[]{:S(2)}) collective-permute-start(bf16[128,1024]{1,0:T(8,128)(2,1)} %bitcast.13), channel_id=1, source_target_pairs={{0,32},{8,232},{16,48},{24,248},{32,64},{40,8},{48,80},{56,24},{64... | collective-permute-start | bytes 786440 | tf_op jit(solution)/shard_map/ppermute | solution.py:34
  10.1 3.9 %collective-permute-done.1.refs_5_ = s32[1,128]{1,0:T(1,128)S(1)} collective-permute-done((s32[1,128]{1,0:T(1,128)}, s32[1,128]{1,0:T(1,128)S(1)}, u32[]{:S(2)}, u32[]{:S(2)}) %collective-permute-start.1) | collective-permute-done | bytes 544 | tf_op jit(solution)/shard_map/ppermute | solution.py:42
  15.0 2.9 %collective-permute-done.2.refs_8_ = bf16[128,1024]{1,0:T(8,128)(2,1)S(1)} collective-permute-done((bf16[128,1024]{1,0:T(8,128)(2,1)}, bf16[128,1024]{1,0:T(8,128)(2,1)S(1)}, u32[]{:S(2)}, u32[]{:S(2)}) %collective-permute-start.2) | collective-permute-done | bytes 262176 | tf_op jit(solution)/shard_map/ppermute | solution.py:34
  18.5 2.7 %collective-permute-start.8 = (bf16[128,1024]{1,0:T(8,128)(2,1)S(1)}, bf16[128,1024]{1,0:T(8,128)(2,1)}, u32[]{:S(2)}, u32[]{:S(2)}) collective-permute-start(bf16[128,1024]{1,0:T(8,128)(2,1)S(1)} %collective-permute-done.3.refs_9_), channel_id=1, source_target_pairs={{0,32},{8,232},{16,48},{24,248},{32,64},{40,8},{48,80},{56,24},{64... | collective-permute-start | bytes 786440 | tf_op jit(solution)/shard_map/ppermute | solution.py:34
  23.1 4.3 %shard_map.85 = (bf16[512,1024]{1,0:T(8,128)(2,1)S(1)}, f32[512,1]{1,0:T(8,128)}, f32[8,128]{1,0:T(8,128)S(1)}) custom-call(bf16[1152,1024]{1,0:T(8,128)(2,1)} %refs_3_.3, bf16[128,1152]{1,0:T(8,128)(2,1)} %bitcast.11, bf16[128,1152]{1,0:T(8,128)(2,1)S(1)} %collective-permute-done.4.refs_2_.refs_7_, ...), custom_call_target="tpu_custom_call" | custom-call | flops 1 | bytes 1 | tf_op jit(solution)/shard_map/pallas_call | solution.py:110
  27.5 3.3 %collective-permute-start.11 = (bf16[128,1024]{1,0:T(8,128)(2,1)}, bf16[128,1024]{1,0:T(8,128)(2,1)S(1)}, u32[]{:S(2)}, u32[]{:S(2)}) collective-permute-start(bf16[128,1024]{1,0:T(8,128)(2,1)} %collective-permute-done.8.refs_11_), channel_id=1, source_target_pairs={{0,32},{8,232},{16,48},{24,248},{32,64},{40,8},{48,80},{56,24},{64... | collective-permute-start | bytes 786440 | tf_op jit(solution)/shard_map/ppermute | solution.py:34
  32.0 4.9 %shard_map.86 = (f32[512,1]{1,0:T(8,128)S(1)}, f32[512,1024]{1,0:T(8,128)S(1)}, f32[128,1024]{1,0:T(8,128)}, bf16[128,1024]{1,0:T(8,128)(2,1)}, bf16[128,1024]{1...) custom-call(f32[8,128]{1,0:T(8,128)S(1)} %get-tuple-element.53.refs_0_, s32[1]{0:T(128)} %bitcast.refs_1_.refs_0_, ...), custom_call_target="tpu_custom_call" | custom-call | flops 1 | bytes 1 | tf_op jit(solution)/shard_map/pallas_call | solution.py:110
  36.9 2.1 %shard_map.87 = (f32[512,1024]{1,0:T(8,128)S(1)}, bf16[128,1024]{1,0:T(8,128)(2,1)}) custom-call(f32[8,128]{1,0:T(8,128)S(1)} %get-tuple-element.53.refs_0_, s32[1]{0:T(128)} %bitcast.refs_1_.refs_0_, bf16[512,1024]{1,0:T(8,128)(2,1)S(1)} %get-tuple-element.54.refs_2_.refs_4_, ...), custom_call_target="tpu_custom_call", output_to_operand_aliasing={{0}: (5, {})} | custom-call | flops 1 | bytes 1 | tf_op jit(solution)/shard_map/pallas_call | solution.py:110
  39.0 3.3 %collective-permute-done.10.refs_4_ = bf16[128,1024]{1,0:T(8,128)(2,1)S(1)} collective-permute-done((bf16[128,1024]{1,0:T(8,128)(2,1)}, bf16[128,1024]{1,0:T(8,128)(2,1)S(1)}, u32[]{:S(2)}, u32[]{:S(2)}) %collective-permute-start.10) | collective-permute-done | bytes 262176 | tf_op jit(solution)/shard_map/ppermute | solution.py:34
  42.3 2.1 %shard_map.88 = (f32[512,1024]{1,0:T(8,128)S(1)}, bf16[128,1024]{1,0:T(8,128)(2,1)}) custom-call(f32[8,128]{1,0:T(8,128)S(1)} %get-tuple-element.53.refs_0_, s32[1]{0:T(128)} %bitcast.refs_1_.refs_0_, bf16[512,1024]{1,0:T(8,128)(2,1)S(1)} %get-tuple-element.54.refs_2_.refs_4_, ...), custom_call_target="tpu_custom_call", output_to_operand_aliasing={{0}: (5, {})} | custom-call | flops 1 | bytes 1 | tf_op jit(solution)/shard_map/pallas_call | solution.py:110
  44.4 2.5 %shard_map.89 = (f32[512,1024]{1,0:T(8,128)S(1)}, f32[512,1]{1,0:T(8,128)S(1)}, bf16[528,512]{1,0:T(8,128)(2,1)S(1)}, bf16[512,128]{1,0:T(8,128)(2,1)S(1)}) custom-call(f32[8,128]{1,0:T(8,128)S(1)} %get-tuple-element.53.refs_0_, s32[1]{0:T(128)} %bitcast.refs_1_.refs_0_, ...), custom_call_target="tpu_custom_call", output_to_operand_aliasing={{0}: (5, {})} | custom-call | flops 1 | bytes 1 | tf_op jit(solution)/shard_map/pallas_call | solution.py:110
  49.2 3.3 %shard_map.90 = (bf16[8,64,1152]{2,1,0:T(8,128)(2,1)}, f32[256,512]{1,0:T(8,128)}, f32[256,512]{1,0:T(8,128)}, f32[256,512]{1,0:T(8,128)}) custom-call(s32[1]{0:T(128)} %bitcast.refs_1_.refs_0_, bf16[528,512]{1,0:T(8,128)(2,1)S(1)} %collective-permute-done.12.refs_1_, f32[512,1024]{1,0:T(8,128)S(1)} %get-tuple-element.66.refs_2_, ...), custom_call_target="tpu_custom_call" | custom-call | flops 1 | bytes 1 | tf_op jit(solution)/shard_map/pallas_call | solution.py:110
  52.5 4.1 %all-to-all-start = ((bf16[8,64,1152]{2,1,0:T(8,128)(2,1)}), bf16[8,64,1152]{2,1,0:T(8,128)(2,1)S(1)}, u32[]{:S(2)}, u32[]{:S(2)}) async-start(bf16[8,64,1152]{2,1,0:T(8,128)(2,1)} %get-tuple-element.78), calls=%async_computation | async-start | bytes 2359296 | tf_op jit(solution)/shard_map/all_to_all | solution.py:435
  61.8 2.6 %collective-permute-start.17 = (bf16[128,1024]{1,0:T(8,128)(2,1)}, bf16[128,1024]{1,0:T(8,128)(2,1)S(1)}, u32[]{:S(2)}, u32[]{:S(2)}) collective-permute-start(bf16[128,1024]{1,0:T(8,128)(2,1)} %get-tuple-element.82), channel_id=1, source_target_pairs={{0,32},{8,232},{16,48},{24,248},{32,64},{40,8},{48,80},{56,24},{64... | collective-permute-start | bytes 786440 | tf_op jit(solution)/shard_map/ppermute | solution.py:34
  65.2 2.3 %shard_map.91 = (bf16[128,1024]{1,0:T(8,128)(2,1)}, f32[128,1024]{1,0:T(8,128)}) custom-call(s32[1]{0:T(128)} %bitcast.refs_1_.refs_0_, f32[256,512]{1,0:T(8,128)} %get-tuple-element.69.refs_1_, f32[256,512]{1,0:T(8,128)} %get-tuple-element.70.refs_2_, f32[256,512]{1,0:T(8,128)} %copy-done.2), custom_call_target="tpu_custom_call" | custom-call | flops 1 | bytes 1 | tf_op jit(solution)/shard_map/pallas_call | solution.py:110
  69.3 5.1 %all-to-all-done.refs_0_ = bf16[8,64,1152]{2,1,0:T(8,128)(2,1)S(1)} async-done(((bf16[8,64,1152]{2,1,0:T(8,128)(2,1)}), bf16[8,64,1152]{2,1,0:T(8,128)(2,1)S(1)}, u32[]{:S(2)}, u32[]{:S(2)}) %all-to-all-start) | async-done | bytes 1179680 | tf_op jit(solution)/shard_map/all_to_all | solution.py:435
  75.4 7.5 %all-to-all-start.1 = ((bf16[32,18,128]{2,1,0:T(8,128)(2,1)}), bf16[32,18,128]{2,1,0:T(8,128)(2,1)S(1)}, u32[]{:S(2)}, u32[]{:S(2)}) async-start(bf16[32,18,128]{2,1,0:T(8,128)(2,1)} %shard_map.93), calls=%async_computation.1 | async-start | bytes 393216 | tf_op jit(solution)/shard_map/all_to_all | solution.py:442
  83.0 2.0 %shard_map.95 = (bf16[128,1024]{1,0:T(8,128)(2,1)}, bf16[128,1024]{1,0:T(8,128)(2,1)}) custom-call(bf16[128,1024]{1,0:T(8,128)(2,1)} %get-tuple-element.89.refs_0_, bf16[128,1024]{1,0:T(8,128)(2,1)S(1)} %collective-permute-done.14.refs_1_, bf16[128,1024]{1,0:T(8,128)(2,1)S(1)} %collective-permute-done.16.refs_2_, ...), custom_call_target="tpu_custom_call" | custom-call | flops 1 | bytes 1 | tf_op jit(solution)/shard_map/pallas_call | solution.py:110
  85.0 3.6 %collective-permute-start.20 = (bf16[128,1024]{1,0:T(8,128)(2,1)}, bf16[128,1024]{1,0:T(8,128)(2,1)S(1)}, u32[]{:S(2)}, u32[]{:S(2)}) collective-permute-start(bf16[128,1024]{1,0:T(8,128)(2,1)} %get-tuple-element.94), channel_id=1, source_target_pairs={{0,64},{8,200},{16,80},{24,216},{32,96},{40,232},{48,112},{56,248}... | collective-permute-start | bytes 786440 | tf_op jit(solution)/shard_map/ppermute | solution.py:34
  88.6 3.6 %shard_map.94 = bf16[128,1152]{1,0:T(8,128)(2,1)} custom-call(f32[128,1024]{1,0:T(8,128)} %get-tuple-element.72.refs_0_, bf16[128,1024]{1,0:T(8,128)(2,1)} %collective-permute-done.19.refs_1_, f32[512,1]{1,0:T(8,128)} %get-tuple-element.68.refs_5_.refs_2_, bf16[1152,1024]{1,0:T(8,128)(2,1)} %refs_3_.3, bf16[512,1024]{1,0:T(8,128)(2,1)S(1)} %get-tuple-element.54.refs_2_.refs_4_), custom_call_target="tpu_custom_call" | custom-call | flops 1 | bytes 1 | tf_op jit(solution)/shard_map/pallas_call | solution.py:110
  92.2 2.5 %all-to-all-done.1.refs_0_ = bf16[32,18,128]{2,1,0:T(8,128)(2,1)S(1)} async-done(((bf16[32,18,128]{2,1,0:T(8,128)(2,1)}), bf16[32,18,128]{2,1,0:T(8,128)(2,1)S(1)}, u32[]{:S(2)}, u32[]{:S(2)}) %all-to-all-start.1) | async-done | bytes 147488 | tf_op jit(solution)/shard_map/all_to_all | solution.py:442
  95.5 3.6 %all-to-all-start.2 = ((f32[8,36,128]{2,1,0:T(8,128)}), f32[8,36,128]{2,1,0:T(8,128)S(1)}, u32[]{:S(2)}, u32[]{:S(2)}) async-start(f32[8,36,128]{2,1,0:T(8,128)} %shard_map.96), calls=%async_computation.2 | async-start | bytes 327680 | tf_op jit(solution)/shard_map/all_to_all | solution.py:474
  101.0 2.5 %shard_map.97 = f32[128,1024]{1,0:T(8,128)} custom-call(bf16[128,1024]{1,0:T(8,128)(2,1)} %bitcast.16, f32[128,1024]{1,0:T(8,128)} %get-tuple-element.86.refs_1_, bf16[128,1024]{1,0:T(8,128)(2,1)} %copy-done.3, bf16[128,1024]{1,0:T(8,128)(2,1)} %collective-permute-done.18.refs_3_, bf16[128,1024]{1,0:T(8,128)(2,1)S(1)} %collective-permute-done.20.refs_4_, ...), custom_call_target="tpu_custom_call" | custom-call | flops 1 | bytes 1 | tf_op jit(solution)/shard_map/pallas_call | solution.py:110
  (54 shorter events, 19.2 us)
Async XLA Ops:
  0.6 17.3 %collective-permute-start = (bf16[128,1152]{1,0:T(8,128)(2,1)}, bf16[128,1152]{1,0:T(8,128)(2,1)S(1)}, u32[]{:S(2)}, u32[]{:S(2)}) collective-permute-start(bf16[128,1152]{1,0:T(8,128)(2,1)} %bitcast.9), channel_id=1, source_target_pairs={{0,16},{8,24},{16,0},{24,8},{32,48},{40,56},{48,32},{56,40},{64,80... | collective-permute-start | bytes 884744 | tf_op jit(solution)/shard_map/ppermute | solution.py:42
  4.5 10.5 %collective-permute-start.3 = (bf16[128,1024]{1,0:T(8,128)(2,1)}, bf16[128,1024]{1,0:T(8,128)(2,1)S(1)}, u32[]{:S(2)}, u32[]{:S(2)}) collective-permute-start(bf16[128,1024]{1,0:T(8,128)(2,1)} %bitcast.13), channel_id=1, source_target_pairs={{0,32},{8,232},{16,48},{24,248},{32,64},{40,8},{48,80},{56,24},{64... | collective-permute-start | bytes 786440 | tf_op jit(solution)/shard_map/ppermute | solution.py:34
  10.0 7.9 %collective-permute-start.2 = (bf16[128,1024]{1,0:T(8,128)(2,1)}, bf16[128,1024]{1,0:T(8,128)(2,1)S(1)}, u32[]{:S(2)}, u32[]{:S(2)}) collective-permute-start(bf16[128,1024]{1,0:T(8,128)(2,1)} %bitcast.14), channel_id=1, source_target_pairs={{0,224},{8,40},{16,240},{24,56},{32,0},{40,72},{48,16},{56,88},{64... | collective-permute-start | bytes 786440 | tf_op jit(solution)/shard_map/ppermute | solution.py:34
  10.1 4.0 %collective-permute-start.1 = (s32[1,128]{1,0:T(1,128)}, s32[1,128]{1,0:T(1,128)S(1)}, u32[]{:S(2)}, u32[]{:S(2)}) collective-permute-start(s32[1,128]{1,0:T(1,128)} %refs_3_.2), channel_id=1, source_target_pairs={{0,16},{8,24},{16,0},{24,8},{32,48},{40,56},{48,32},{56,40},{64,80... | collective-permute-start | bytes 1544 | tf_op jit(solution)/shard_map/ppermute | solution.py:42
  18.0 5.2 %collective-permute-start.4 = (bf16[128,1152]{1,0:T(8,128)(2,1)}, bf16[128,1152]{1,0:T(8,128)(2,1)S(1)}, u32[]{:S(2)}, u32[]{:S(2)}) collective-permute-start(bf16[128,1152]{1,0:T(8,128)(2,1)} %bitcast.10), channel_id=1, source_target_pairs={{0,8},{8,0},{16,24},{24,16},{32,40},{40,32},{48,56},{56,48},{64,72... | collective-permute-start | bytes 884744 | tf_op jit(solution)/shard_map/ppermute | solution.py:38
  18.0 5.2 %collective-permute-start.5 = (bf16[128,1152]{1,0:T(8,128)(2,1)S(1)}, bf16[128,1152]{1,0:T(8,128)(2,1)S(1)}, u32[]{:S(2)}, u32[]{:S(2)}) collective-permute-start(bf16[128,1152]{1,0:T(8,128)(2,1)S(1)} %collective-permute-done.refs_3_.refs_8_), channel_id=1, source_target_pairs={{0,8},{8,0},{16,24},{24,16},{32,40},{40,32},{48,56},{56,48},{64,72... | collective-permute-start | bytes 884744 | tf_op jit(solution)/shard_map/ppermute | solution.py:38
  18.5 9.0 %collective-permute-start.7 = (bf16[128,1024]{1,0:T(8,128)(2,1)S(1)}, bf16[128,1024]{1,0:T(8,128)(2,1)}, u32[]{:S(2)}, u32[]{:S(2)}) collective-permute-start(bf16[128,1024]{1,0:T(8,128)(2,1)S(1)} %collective-permute-done.2.refs_8_), channel_id=1, source_target_pairs={{0,224},{8,40},{16,240},{24,56},{32,0},{40,72},{48,16},{56,88},{64... | collective-permute-start | bytes 786440 | tf_op jit(solution)/shard_map/ppermute | solution.py:34
  18.5 9.0 %collective-permute-start.8 = (bf16[128,1024]{1,0:T(8,128)(2,1)S(1)}, bf16[128,1024]{1,0:T(8,128)(2,1)}, u32[]{:S(2)}, u32[]{:S(2)}) collective-permute-start(bf16[128,1024]{1,0:T(8,128)(2,1)S(1)} %collective-permute-done.3.refs_9_), channel_id=1, source_target_pairs={{0,32},{8,232},{16,48},{24,248},{32,64},{40,8},{48,80},{56,24},{64... | collective-permute-start | bytes 786440 | tf_op jit(solution)/shard_map/ppermute | solution.py:34
  27.4 3.4 %collective-permute-start.6 = (s32[2,128]{1,0:T(2,128)S(1)}, s32[2,128]{1,0:T(2,128)S(1)}, u32[]{:S(2)}, u32[]{:S(2)}) collective-permute-start(s32[2,128]{1,0:T(2,128)S(1)} %pad_add_fusion), channel_id=1, source_target_pairs={{0,8},{8,0},{16,24},{24,16},{32,40},{40,32},{48,56},{56,48},{64,72... | collective-permute-start | bytes 3080 | tf_op jit(solution)/shard_map/ppermute | solution.py:38
  27.5 9.4 %collective-permute-start.11 = (bf16[128,1024]{1,0:T(8,128)(2,1)}, bf16[128,1024]{1,0:T(8,128)(2,1)S(1)}, u32[]{:S(2)}, u32[]{:S(2)}) collective-permute-start(bf16[128,1024]{1,0:T(8,128)(2,1)} %collective-permute-done.8.refs_11_), channel_id=1, source_target_pairs={{0,32},{8,232},{16,48},{24,248},{32,64},{40,8},{48,80},{56,24},{64... | collective-permute-start | bytes 786440 | tf_op jit(solution)/shard_map/ppermute | solution.py:34
  30.8 11.5 %collective-permute-start.10 = (bf16[128,1024]{1,0:T(8,128)(2,1)}, bf16[128,1024]{1,0:T(8,128)(2,1)S(1)}, u32[]{:S(2)}, u32[]{:S(2)}) collective-permute-start(bf16[128,1024]{1,0:T(8,128)(2,1)} %collective-permute-done.7.refs_10_), channel_id=1, source_target_pairs={{0,224},{8,40},{16,240},{24,56},{32,0},{40,72},{48,16},{56,88},{64... | collective-permute-start | bytes 786440 | tf_op jit(solution)/shard_map/ppermute | solution.py:34
  30.8 13.6 %collective-permute-start.9 = (bf16[128,1024]{1,0:T(8,128)(2,1)}, bf16[128,1024]{1,0:T(8,128)(2,1)S(1)}, u32[]{:S(2)}, u32[]{:S(2)}) collective-permute-start(bf16[128,1024]{1,0:T(8,128)(2,1)} %collective-permute-done.8.refs_11_), channel_id=1, source_target_pairs={{0,64},{8,200},{16,80},{24,216},{32,96},{40,232},{48,112},{56,248}... | collective-permute-start | bytes 786440 | tf_op jit(solution)/shard_map/ppermute | solution.py:34
  52.5 21.9 %all-to-all-start = ((bf16[8,64,1152]{2,1,0:T(8,128)(2,1)}), bf16[8,64,1152]{2,1,0:T(8,128)(2,1)S(1)}, u32[]{:S(2)}, u32[]{:S(2)}) async-start(bf16[8,64,1152]{2,1,0:T(8,128)(2,1)} %get-tuple-element.78), calls=%async_computation | async-start | bytes 2359296 | tf_op jit(solution)/shard_map/all_to_all | solution.py:435
  56.6 7.7 %collective-permute-start.13 = (f32[256,512]{1,0:T(8,128)}, f32[256,512]{1,0:T(8,128)S(1)}, u32[]{:S(2)}, u32[]{:S(2)}) collective-permute-start(f32[256,512]{1,0:T(8,128)} %get-tuple-element.71), channel_id=1, source_target_pairs={{0,8},{8,0},{16,24},{24,16},{32,40},{40,32},{48,56},{56,48},{64,72... | collective-permute-start | bytes 1572872 | tf_op jit(solution)/shard_map/ppermute | solution.py:38
  58.4 10.8 %collective-permute-start.16 = (bf16[128,1024]{1,0:T(8,128)(2,1)}, bf16[128,1024]{1,0:T(8,128)(2,1)S(1)}, u32[]{:S(2)}, u32[]{:S(2)}) collective-permute-start(bf16[128,1024]{1,0:T(8,128)(2,1)} %shard_map.92), channel_id=1, source_target_pairs={{0,64},{8,200},{16,80},{24,216},{32,96},{40,232},{48,112},{56,248}... | collective-permute-start | bytes 786440 | tf_op jit(solution)/shard_map/ppermute | solution.py:34
  60.3 22.6 %collective-permute-start.14 = (bf16[128,1024]{1,0:T(8,128)(2,1)}, bf16[128,1024]{1,0:T(8,128)(2,1)S(1)}, u32[]{:S(2)}, u32[]{:S(2)}) collective-permute-start(bf16[128,1024]{1,0:T(8,128)(2,1)} %get-tuple-element.79), channel_id=1, source_target_pairs={{0,32},{8,232},{16,48},{24,248},{32,64},{40,8},{48,80},{56,24},{64... | collective-permute-start | bytes 786440 | tf_op jit(solution)/shard_map/ppermute | solution.py:34
  61.7 21.3 %collective-permute-start.15 = (bf16[128,1024]{1,0:T(8,128)(2,1)}, bf16[128,1024]{1,0:T(8,128)(2,1)S(1)}, u32[]{:S(2)}, u32[]{:S(2)}) collective-permute-start(bf16[128,1024]{1,0:T(8,128)(2,1)} %get-tuple-element.80), channel_id=1, source_target_pairs={{0,224},{8,40},{16,240},{24,56},{32,0},{40,72},{48,16},{56,88},{64... | collective-permute-start | bytes 786440 | tf_op jit(solution)/shard_map/ppermute | solution.py:34
  61.8 21.2 %collective-permute-start.17 = (bf16[128,1024]{1,0:T(8,128)(2,1)}, bf16[128,1024]{1,0:T(8,128)(2,1)S(1)}, u32[]{:S(2)}, u32[]{:S(2)}) collective-permute-start(bf16[128,1024]{1,0:T(8,128)(2,1)} %get-tuple-element.82), channel_id=1, source_target_pairs={{0,32},{8,232},{16,48},{24,248},{32,64},{40,8},{48,80},{56,24},{64... | collective-permute-start | bytes 786440 | tf_op jit(solution)/shard_map/ppermute | solution.py:34
  64.4 18.6 %collective-permute-start.18 = (bf16[128,1024]{1,0:T(8,128)(2,1)}, bf16[128,1024]{1,0:T(8,128)(2,1)}, u32[]{:S(2)}, u32[]{:S(2)}) collective-permute-start(bf16[128,1024]{1,0:T(8,128)(2,1)} %get-tuple-element.83), channel_id=1, source_target_pairs={{0,224},{8,40},{16,240},{24,56},{32,0},{40,72},{48,16},{56,88},{64... | collective-permute-start | bytes 786440 | tf_op jit(solution)/shard_map/ppermute | solution.py:34
  69.2 13.8 %collective-permute-start.19 = (bf16[128,1024]{1,0:T(8,128)(2,1)}, bf16[128,1024]{1,0:T(8,128)(2,1)}, u32[]{:S(2)}, u32[]{:S(2)}) collective-permute-start(bf16[128,1024]{1,0:T(8,128)(2,1)} %get-tuple-element.84), channel_id=1, source_target_pairs={{0,16},{8,24},{16,0},{24,8},{32,48},{40,56},{48,32},{56,40},{64,80... | collective-permute-start | bytes 786440 | tf_op jit(solution)/shard_map/ppermute | solution.py:42
  75.4 19.4 %all-to-all-start.1 = ((bf16[32,18,128]{2,1,0:T(8,128)(2,1)}), bf16[32,18,128]{2,1,0:T(8,128)(2,1)S(1)}, u32[]{:S(2)}, u32[]{:S(2)}) async-start(bf16[32,18,128]{2,1,0:T(8,128)(2,1)} %shard_map.93), calls=%async_computation.1 | async-start | bytes 393216 | tf_op jit(solution)/shard_map/all_to_all | solution.py:442
  85.0 16.0 %collective-permute-start.20 = (bf16[128,1024]{1,0:T(8,128)(2,1)}, bf16[128,1024]{1,0:T(8,128)(2,1)S(1)}, u32[]{:S(2)}, u32[]{:S(2)}) collective-permute-start(bf16[128,1024]{1,0:T(8,128)(2,1)} %get-tuple-element.94), channel_id=1, source_target_pairs={{0,64},{8,200},{16,80},{24,216},{32,96},{40,232},{48,112},{56,248}... | collective-permute-start | bytes 786440 | tf_op jit(solution)/shard_map/ppermute | solution.py:34
  88.6 12.4 %collective-permute-start.21 = (bf16[128,1024]{1,0:T(8,128)(2,1)}, bf16[128,1024]{1,0:T(8,128)(2,1)S(1)}, u32[]{:S(2)}, u32[]{:S(2)}) collective-permute-start(bf16[128,1024]{1,0:T(8,128)(2,1)} %get-tuple-element.95), channel_id=1, source_target_pairs={{0,192},{8,72},{16,208},{24,88},{32,224},{40,104},{48,240},{56,120... | collective-permute-start | bytes 786440 | tf_op jit(solution)/shard_map/ppermute | solution.py:34
  95.5 9.2 %all-to-all-start.2 = ((f32[8,36,128]{2,1,0:T(8,128)}), f32[8,36,128]{2,1,0:T(8,128)S(1)}, u32[]{:S(2)}, u32[]{:S(2)}) async-start(f32[8,36,128]{2,1,0:T(8,128)} %shard_map.96), calls=%async_computation.2 | async-start | bytes 327680 | tf_op jit(solution)/shard_map/all_to_all | solution.py:474
  (7 other events, 79.5 us)
